TPU v7x, 32 devices: a whole 2x2x4 slice. The times are simulated.
32 devices in a mesh: gx: 4 (over x, core), gy: 2 (over y), gz: 4 (over z).
Axes of the slice: x: 2, y: 2, z: 4, core: 2. Of those that a mesh axis runs over, the one named last changes fastest.
Arguments:
- primal_states: float32 [2, 19, 16, 32, 512], P(None, None, 'gx', 'gy', 'gz'), as said below
- adjoint_last: float32 [19, 16, 32, 512], P(None, 'gx', 'gy', 'gz'), may hold values from -6 to 6
- porosity: float32 [16, 32, 512], P('gx', 'gy', 'gz'), may hold values from 0 to 0.9
- solid_mask: int32 [16, 32, 512], P('gx', 'gy', 'gz'), may hold values from 0 to 1, as said below
Outputs:
- adjoint_first: float32 [19, 16, 32, 512], P(None, 'gx', 'gy', 'gz')
- porosity_grad: float32 [16, 32, 512], P('gx', 'gy', 'gz')
- drag: float32 [], replicated
Inputs may be any that keep to these rules, and one draw needn't show every extreme that they name: `primal_states`: every population is positive. `solid_mask`: every cell on the planes y = 0 and y = 31 is solid; elsewhere cells are solid at random.
All inputs are finite; a program needn't handle non-finite values.
Results may differ from a plain program's by a relative error of at most 0.00013.
Values sent between devices are 32-bit elements; how exact they have to be, the bound alone decides.
No kernel may reach another device: no remote copies, remote signals or barrier semaphores. Data moves between devices by JAX's collectives and lax.ppermute only.
A program may use at most 128 MiB of HBM per device.

v0:
```python
import jax
import jax.numpy as jnp
import numpy as np
from jax import lax
from jax.sharding import PartitionSpec as P


def extended(cells, sides, width):
    for axis, dim in sides:
        count = lax.axis_size(axis)
        head = lax.slice_in_dim(cells, 0, width, axis=dim)
        tail = lax.slice_in_dim(cells, cells.shape[dim] - width, cells.shape[dim], axis=dim)
        cells = jnp.concatenate(
            [
                lax.ppermute(tail, axis, [(i, (i + 1) % count) for i in range(count)]),
                cells,
                lax.ppermute(head, axis, [((i + 1) % count, i) for i in range(count)]),
            ],
            axis=dim,
        )
    return cells


def orthonormal_rows(monomials):
    rows = []
    for column in range(monomials.shape[1]):
        vector = monomials[:, column] * 1.0
        for sweep in range(2):
            for earlier in rows:
                vector = vector - np.dot(earlier, vector) * earlier
        vector = vector / np.sqrt(np.dot(vector, vector))
        rows.append(vector)
    return np.stack(rows)


def lattice_tables():
    velocity = (
        np.array(
            [
                (0, 0, 0),
                (1, 0, 0),
                (-1, 0, 0),
                (0, 1, 0),
                (0, -1, 0),
                (0, 0, 1),
                (0, 0, -1),
                (1, 1, 0),
                (-1, -1, 0),
                (1, -1, 0),
                (-1, 1, 0),
                (1, 0, 1),
                (-1, 0, -1),
                (1, 0, -1),
                (-1, 0, 1),
                (0, 1, 1),
                (0, -1, -1),
                (0, 1, -1),
                (0, -1, 1),
            ]
        )
        * 1.0
    )
    speeds = np.sum(np.abs(velocity), axis=1)
    weights = np.where(speeds == 0, 1.0 / 3.0, np.where(speeds == 1, 1.0 / 18.0, 1.0 / 36.0))
    opposite = np.zeros((19, 19))
    for member in range(19):
        for other in range(19):
            if np.all(velocity[other] == -velocity[member]):
                opposite[member, other] = 1.0
    vx = velocity[:, 0]
    vy = velocity[:, 1]
    vz = velocity[:, 2]
    columns = [
        np.ones(19),
        vx,
        vy,
        vz,
        vx * vx,
        vy * vy,
        vz * vz,
        vx * vy,
        vx * vz,
        vy * vz,
        vx * vy * vy,
        vx * vz * vz,
        vy * vx * vx,
        vy * vz * vz,
        vz * vx * vx,
        vz * vy * vy,
        vx * vx * vy * vy,
        vx * vx * vz * vz,
        vy * vy * vz * vz,
    ]
    monomials = np.stack(columns, axis=1)
    basis = orthonormal_rows(monomials)
    rates = np.array([0.0] * 4 + [1.6] * 6 + [1.2] * 9)
    return (velocity, weights, opposite, basis, rates)


def collide(state, blocking):
    velocity, weights, opposite, basis, rates = lattice_tables()
    highest = lax.Precision.HIGHEST
    vel = jnp.asarray(velocity, jnp.float32)
    density = jnp.sum(state, axis=0)
    momentum = jnp.dot(vel.T, state, precision=highest)
    speed = momentum / density[None, :]
    along = jnp.dot(vel, speed, precision=highest)
    usquare = jnp.sum(speed * speed, axis=0)
    equilibrium = (
        jnp.asarray(weights, jnp.float32)[:, None]
        * density[None, :]
        * (1.0 + 3.0 * along + 4.5 * along * along - 1.5 * usquare[None, :])
    )
    basis_rows = jnp.asarray(basis, jnp.float32)
    moments = jnp.dot(basis_rows, state - equilibrium, precision=highest)
    relaxed = jnp.asarray(rates, jnp.float32)[:, None] * moments
    post = state - jnp.dot(basis_rows.T, relaxed, precision=highest)
    bounced = jnp.dot(jnp.asarray(opposite, jnp.float32), state, precision=highest)
    return (1.0 - blocking[None, :]) * post + blocking[None, :] * bounced


def adjoint_step(read, state, blocking):
    velocity = jnp.asarray(lattice_tables()[0], jnp.float32)
    unused, pull = jax.vjp(collide, state, blocking)
    d_state, d_block = pull(read)
    flux_x = jnp.dot(velocity[:, 0], state, precision=lax.Precision.HIGHEST)
    adjoint = d_state + velocity[:, 0:1] * blocking[None, :]
    return (adjoint, d_block + flux_x, jnp.sum(blocking * flux_x))


def stream_back(adjoint):
    velocity = lattice_tables()[0]
    extent = adjoint.shape
    padded = extended(adjoint, (("gx", 1), ("gy", 2), ("gz", 3)), 1)
    pieces = []
    for member in range(19):
        start_x = 1 + int(velocity[member, 0])
        start_y = 1 + int(velocity[member, 1])
        start_z = 1 + int(velocity[member, 2])
        pieces.append(
            padded[
                member,
                start_x : start_x + extent[1],
                start_y : start_y + extent[2],
                start_z : start_z + extent[3],
            ]
        )
    return jnp.stack(pieces)


def body(primal_states, adjoint_last, porosity, solid_mask):
    extent = porosity.shape
    cell_count = extent[0] * extent[1] * extent[2]
    fluid = solid_mask == 0
    blocking = jnp.where(fluid, porosity, jnp.ones_like(porosity)).reshape(cell_count)
    adjoint = adjoint_last
    gradient = jnp.zeros((cell_count,), jnp.float32)
    drag_totals = []
    for instant in (1, 0):
        read = stream_back(adjoint).reshape(19, cell_count)
        state = primal_states[instant].reshape(19, cell_count)
        fresh, d_block, drag_part = adjoint_step(read, state, blocking)
        adjoint = fresh.reshape(19, extent[0], extent[1], extent[2])
        gradient = gradient + d_block
        drag_totals.append(lax.psum(drag_part, ("gx", "gy", "gz")))
    total = drag_totals[0] + drag_totals[1]
    whole_cells = cell_count * lax.axis_size("gx") * lax.axis_size("gy") * lax.axis_size("gz")
    gradient = gradient.reshape(extent)
    porosity_grad = jnp.where(fluid, gradient, jnp.zeros_like(gradient))
    return (adjoint, porosity_grad, total / whole_cells)


def solution(mesh):
    return jax.shard_map(
        body,
        mesh=mesh,
        in_specs=(
            P(None, None, "gx", "gy", "gz"),
            P(None, "gx", "gy", "gz"),
            P("gx", "gy", "gz"),
            P("gx", "gy", "gz"),
        ),
        out_specs=(P(None, "gx", "gy", "gz"), P("gx", "gy", "gz"), P()),
        check_vma=False,
    )
```

profile of v0, /device:TPU:0, one launch (start us, length us, event | category | flops | bytes accessed | tf_op | source)
XLA Modules:
  0.0 181.3 jit_solution(8925617094191820125)
XLA Ops:
  2.8 1.9 %collective-permute-start = (f32[19,1,16,128]{3,2,1,0:T(8,128)}, f32[19,1,16,128]{3,2,1,0:T(8,128)}, u32[]{:S(2)}, u32[]{:S(2)}) collective-permute-start(f32[19,1,16,128]{3,2,1,0:T(8,128)} %get-tuple-element.64), channel_id=1, source_target_pairs={{8,0},{16,8},{24,16},{0,24},{9,1},{17,9},{25,17},{1,25},{10,2},{18... | collective-permute-start | bytes 466952 | tf_op jit(solution)/shard_map/ppermute | solution.py:17
  13.6 2.0 %convolution_multiply_fusion = f32[8192,19]{0,1:T(8,128)} fusion(f32[19,19]{1,0:T(8,128)S(1)} %copy-done.16, f32[19,8192]{1,0:T(8,128)S(1)} %reshape_squeeze.7, f32[19,8192]{1,0:T(8,128)S(1)} %fusion.81, f32[8192]{0:T(1024)S(1)} %broadcast_multiply_fusion, f32[8192]{0:T(1024)S(1)} %bitcast.111, f32[19]{0:T(128)S(1)} %copy-done.34, f32[19]{0:T(128)S(1)} %copy-done.33), kind=kOutput, calls=%fused_computation.3 | convolution fusion | flops 37044224 | bytes 1934908 | tf_op jit(solution)/shard_map/jvp()/dot_general | solution.py:115
  15.6 2.0 %convolution_multiply_fusion.2 = f32[8192,19]{0,1:T(8,128)} fusion(f32[19,19]{1,0:T(8,128)S(1)} %copy-done.16, f32[19,8192]{1,0:T(8,128)S(1)} %reshape_squeeze.6, f32[19,8192]{1,0:T(8,128)S(1)} %fusion.80, f32[8192]{0:T(1024)S(1)} %broadcast_multiply_fusion.1, f32[8192]{0:T(1024)S(1)} %bitcast.117, f32[19]{0:T(128)S(1)} %copy-done.34, f32[19]{0:T(128)S(1)} %copy-done.33), kind=kOutput, calls=%fused_computation.7 | convolution fusion | flops 37044224 | bytes 1934908 | tf_op jit(solution)/shard_map/jvp()/dot_general | solution.py:115
  19.3 5.6 %copy.76 = f32[19,6,16,128]{2,0,3,1:T(8,128)} copy(f32[19,6,16,128]{3,2,1,0:T(8,128)S(1)} %constant_dynamic-update-slice_fusion) | data formatting | bytes 1867776 | tf_op jit(solution)/shard_map/concatenate | solution.py:13
  25.0 2.4 %collective-permute-start.3 = (f32[19,6,1,128]{3,0,2,1:T(8,128)S(1)}, f32[19,6,1,128]{3,0,2,1:T(8,128)S(1)}, u32[]{:S(2)}, u32[]{:S(2)}) collective-permute-start(f32[19,6,1,128]{3,0,2,1:T(8,128)S(1)} %copy.108), channel_id=1, source_target_pairs={{0,4},{4,0},{1,5},{5,1},{2,6},{6,2},{3,7},{7,3},{8,12},{12,8},{9,1... | collective-permute-start | bytes 175112 | tf_op jit(solution)/shard_map/ppermute | solution.py:15
  30.8 5.6 %copy.75 = f32[19,6,1,128]{2,0,3,1:T(8,128)} copy(f32[19,6,1,128]{3,0,2,1:T(8,128)S(1)} %collective-permute-done.3) | data formatting | bytes 116736 | tf_op jit(solution)/shard_map/ppermute | solution.py:15
  36.4 6.5 %copy.77 = f32[19,6,1,128]{2,0,3,1:T(8,128)} copy(f32[19,6,1,128]{3,0,2,1:T(8,128)} %collective-permute-done.2) | data formatting | bytes 116736 | tf_op jit(solution)/shard_map/ppermute | solution.py:17
  42.8 11.1 %pad_maximum_fusion = f32[19,6,18,128]{2,0,3,1:T(8,128)S(1)} fusion(f32[19,6,1,128]{2,0,3,1:T(8,128)} %copy.77, f32[19,6,16,128]{2,0,3,1:T(8,128)} %copy.76, f32[19,6,1,128]{2,0,3,1:T(8,128)} %copy.75), kind=kLoop, calls=%fused_computation | loop fusion | flops 525312 | bytes 2101248 | tf_op jit(solution)/shard_map/concatenate | solution.py:13
  53.9 3.7 %copy-done = f32[19,6,18,128]{2,0,3,1:T(8,128)} copy-done((f32[19,6,18,128]{2,0,3,1:T(8,128)}, f32[19,6,18,128]{2,0,3,1:T(8,128)S(1)}, u32[]{:S(2)}) %copy-start) | copy-done | bytes 1050648
  58.2 4.1 %collective-permute-start.4 = (f32[19,6,18,1]{2,0,3,1:T(8,128)S(1)}, f32[19,6,18,1]{2,0,3,1:T(8,128)S(1)}, u32[]{:S(2)}, u32[]{:S(2)}) collective-permute-start(f32[19,6,18,1]{2,0,3,1:T(8,128)S(1)} %get-tuple-element.14), channel_id=1, source_target_pairs={{1,0},{2,1},{3,2},{0,3},{5,4},{6,5},{7,6},{4,7},{9,8},{10,9},{11,1... | collective-permute-start | bytes 24632 | tf_op jit(solution)/shard_map/ppermute | solution.py:17
  65.8 6.4 %copy.78 = f32[19,6,18,128]{3,0,2,1:T(8,128)S(1)} copy(f32[19,6,18,128]{2,0,3,1:T(8,128)} %copy-done) | data formatting | bytes 2101248 | tf_op jit(solution)/shard_map/concatenate | solution.py:13
  72.2 2.0 %copy.79 = f32[19,6,18,1]{3,0,2,1:T(8,128)} copy(f32[19,6,18,1]{2,0,3,1:T(8,128)S(1)} %collective-permute-done.4) | data formatting | bytes 16416 | tf_op jit(solution)/shard_map/ppermute | solution.py:17
  74.3 2.6 %pad_maximum_fusion.24 = (f32[1,4,16,128]{3,0,2,1:T(1,128)S(1)}, f32[1,4,16,128]{3,0,2,1:T(1,128)S(1)}, f32[1,4,16,128]{3,0,2,1:T(1,128)S(1)}, f32[1,4,16,128]{3,0,2,1:T(1,128)S(1)}, f32[1,4,16,128]{3,0,2,1:T(1,128)S(1)}) fusion(f32[19,6,18,1]{3,0,2,1:T(8,128)} %copy.79, f32[19,6,18,128]{3,0,2,1:T(8,128)S(1)} %copy.78), kind=kLoop, calls=%fused_computation.147 | loop fusion | flops 40960 | bytes 1222672 | tf_op jit(solution)/shard_map/concatenate | solution.py:13
  76.9 2.9 %copy.80 = f32[19,6,18,1]{3,0,2,1:T(8,128)} copy(f32[19,6,18,1]{2,0,3,1:T(8,128)} %collective-permute-done.5) | data formatting | bytes 16416 | tf_op jit(solution)/shard_map/ppermute | solution.py:15
  79.8 2.2 %pad_maximum_fusion.25 = (f32[1,4,16,128]{3,0,2,1:T(1,128)S(1)}, f32[1,4,16,128]{3,0,2,1:T(1,128)S(1)}, f32[1,4,16,128]{3,0,2,1:T(1,128)S(1)}, f32[1,4,16,128]{3,0,2,1:T(1,128)S(1)}, f32[1,4,16,128]{3,0,2,1:T(1,128)S(1)}) fusion(f32[19,6,18,128]{3,0,2,1:T(8,128)S(1)} %copy.78, f32[19,6,18,1]{3,0,2,1:T(8,128)} %copy.80), kind=kLoop, calls=%fused_computation.148 | loop fusion | flops 40960 | bytes 1222672 | tf_op jit(solution)/shard_map/concatenate | solution.py:13
  97.5 1.7 collective-permute-start.6
  109.2 2.0 %fusion.83 = (f32[19,6,18,1]{3,2,1,0:T(8,128)}, f32[19,6,18,1]{3,2,1,0:T(8,128)}) fusion(f32[19,6,18,128]{3,2,1,0:T(8,128)S(1)} %pad_maximum_fusion.1), kind=kLoop, calls=%fused_computation.189 | loop fusion | bytes 32832 | tf_op jit(solution)/shard_map/slice | solution.py:12
  111.2 2.1 %copy.98 = f32[19,6,18,1]{0,3,2,1:T(1,128)S(1)} copy(f32[19,6,18,1]{3,2,1,0:T(8,128)} %get-tuple-element.34) | data formatting | bytes 16416 | tf_op jit(solution)/shard_map/slice | solution.py:11
  113.3 4.1 %collective-permute-start.10 = (f32[19,6,18,1]{0,3,2,1:T(1,128)S(1)}, f32[19,6,18,1]{0,3,2,1:T(1,128)S(1)}, u32[]{:S(2)}, u32[]{:S(2)}) collective-permute-start(f32[19,6,18,1]{0,3,2,1:T(1,128)S(1)} %copy.98), channel_id=1, source_target_pairs={{1,0},{2,1},{3,2},{0,3},{5,4},{6,5},{7,6},{4,7},{9,8},{10,9},{11,1... | collective-permute-start | bytes 24632 | tf_op jit(solution)/shard_map/ppermute | solution.py:17
  118.0 2.1 %copy.100 = f32[19,6,18,1]{0,3,2,1:T(1,128)S(1)} copy(f32[19,6,18,1]{3,2,1,0:T(8,128)} %get-tuple-element.33) | data formatting | bytes 16416 | tf_op jit(solution)/shard_map/slice | solution.py:12
  120.1 2.1 %copy.99 = f32[19,6,18,1]{3,2,1,0:T(8,128)} copy(f32[19,6,18,1]{0,3,2,1:T(1,128)S(1)} %collective-permute-done.10) | data formatting | bytes 16416 | tf_op jit(solution)/shard_map/ppermute | solution.py:17
  123.3 2.8 %collective-permute-done.11 = f32[19,6,18,1]{0,3,2,1:T(1,128)S(1)} collective-permute-done((f32[19,6,18,1]{0,3,2,1:T(1,128)S(1)}, f32[19,6,18,1]{0,3,2,1:T(1,128)S(1)}, u32[]{:S(2)}, u32[]{:S(2)}) %collective-permute-start.11) | collective-permute-done | bytes 8240 | tf_op jit(solution)/shard_map/ppermute | solution.py:15
  126.1 2.1 %copy.101 = f32[19,6,18,1]{3,2,1,0:T(8,128)} copy(f32[19,6,18,1]{0,3,2,1:T(1,128)S(1)} %collective-permute-done.11) | data formatting | bytes 16416 | tf_op jit(solution)/shard_map/ppermute | solution.py:15
  136.2 37.7 %psum.16 = f32[]{:T(128)} all-reduce(f32[]{:T(128)S(6)} %add.43), channel_id=1, replica_groups=mesh['gx'=4,'gy'=2,'gz'=4] {'gx','gy','gz'}, use_global_device_ids=true, to_apply=%region_15.16 | all-reduce | flops 1 | bytes 8 | tf_op jit(solution)/shard_map/psum | solution.py:165
  (181 shorter events, 58.9 us)
Async XLA Ops:
  2.3 15.3 %collective-permute-start.1 = (f32[19,1,16,128]{3,2,1,0:T(8,128)S(1)}, f32[19,1,16,128]{3,2,1,0:T(8,128)S(1)}, u32[]{:S(2)}, u32[]{:S(2)}) collective-permute-start(f32[19,1,16,128]{3,2,1,0:T(8,128)S(1)} %get-tuple-element.63), channel_id=1, source_target_pairs={{0,8},{8,16},{16,24},{24,0},{1,9},{9,17},{17,25},{25,1},{2,10},{10... | collective-permute-start | bytes 466952 | tf_op jit(solution)/shard_map/ppermute | solution.py:15
  2.8 14.9 %collective-permute-start = (f32[19,1,16,128]{3,2,1,0:T(8,128)}, f32[19,1,16,128]{3,2,1,0:T(8,128)}, u32[]{:S(2)}, u32[]{:S(2)}) collective-permute-start(f32[19,1,16,128]{3,2,1,0:T(8,128)} %get-tuple-element.64), channel_id=1, source_target_pairs={{8,0},{16,8},{24,16},{0,24},{9,1},{17,9},{25,17},{1,25},{10,2},{18... | collective-permute-start | bytes 466952 | tf_op jit(solution)/shard_map/ppermute | solution.py:17
  9.0 3.7 %copy-start.11 = (f32[3,8192]{1,0:T(4,128)}, f32[3,8192]{1,0:T(4,128)S(1)}, u32[]{:S(2)}) copy-start(f32[3,8192]{1,0:T(4,128)S(1)} %get-tuple-element.72) | copy-start | bytes 294916
  12.6 2.9 %copy-start.7 = (f32[19,8192]{1,0:T(8,128)}, f32[19,8192]{1,0:T(8,128)S(1)}, u32[]{:S(2)}) copy-start(f32[19,8192]{1,0:T(8,128)S(1)} %fusion.80) | copy-start | bytes 1867780
  12.7 2.9 %copy-start.20 = (f32[8192]{0:T(1024)}, f32[8192]{0:T(1024)S(1)}, u32[]{:S(2)}) copy-start(f32[8192]{0:T(1024)S(1)} %broadcast_multiply_fusion.1) | copy-start | bytes 98308
  13.4 4.1 %copy-start.3 = (f32[19,8192]{1,0:T(8,128)}, f32[19,8192]{1,0:T(8,128)S(1)}, u32[]{:S(2)}) copy-start(f32[19,8192]{1,0:T(8,128)S(1)} %fusion.81) | copy-start | bytes 1867780
  13.5 4.1 %copy-start.18 = (f32[8192]{0:T(1024)}, f32[8192]{0:T(1024)S(1)}, u32[]{:S(2)}) copy-start(f32[8192]{0:T(1024)S(1)} %broadcast_multiply_fusion) | copy-start | bytes 98308
  25.0 5.8 %collective-permute-start.3 = (f32[19,6,1,128]{3,0,2,1:T(8,128)S(1)}, f32[19,6,1,128]{3,0,2,1:T(8,128)S(1)}, u32[]{:S(2)}, u32[]{:S(2)}) collective-permute-start(f32[19,6,1,128]{3,0,2,1:T(8,128)S(1)} %copy.108), channel_id=1, source_target_pairs={{0,4},{4,0},{1,5},{5,1},{2,6},{6,2},{3,7},{7,3},{8,12},{12,8},{9,1... | collective-permute-start | bytes 175112 | tf_op jit(solution)/shard_map/ppermute | solution.py:15
  28.8 7.5 %collective-permute-start.2 = (f32[19,6,1,128]{3,0,2,1:T(8,128)}, f32[19,6,1,128]{3,0,2,1:T(8,128)}, u32[]{:S(2)}, u32[]{:S(2)}) collective-permute-start(f32[19,6,1,128]{3,0,2,1:T(8,128)} %copy.107), channel_id=1, source_target_pairs={{4,0},{0,4},{5,1},{1,5},{6,2},{2,6},{7,3},{3,7},{12,8},{8,12},{13,... | collective-permute-start | bytes 175112 | tf_op jit(solution)/shard_map/ppermute | solution.py:17
  53.9 3.7 %copy-start = (f32[19,6,18,128]{2,0,3,1:T(8,128)}, f32[19,6,18,128]{2,0,3,1:T(8,128)S(1)}, u32[]{:S(2)}) copy-start(f32[19,6,18,128]{2,0,3,1:T(8,128)S(1)} %pad_maximum_fusion) | copy-start | bytes 3151876
  58.2 14.0 %collective-permute-start.4 = (f32[19,6,18,1]{2,0,3,1:T(8,128)S(1)}, f32[19,6,18,1]{2,0,3,1:T(8,128)S(1)}, u32[]{:S(2)}, u32[]{:S(2)}) collective-permute-start(f32[19,6,18,1]{2,0,3,1:T(8,128)S(1)} %get-tuple-element.14), channel_id=1, source_target_pairs={{1,0},{2,1},{3,2},{0,3},{5,4},{6,5},{7,6},{4,7},{9,8},{10,9},{11,1... | collective-permute-start | bytes 24632 | tf_op jit(solution)/shard_map/ppermute | solution.py:17
  64.6 12.3 %collective-permute-start.5 = (f32[19,6,18,1]{2,0,3,1:T(8,128)}, f32[19,6,18,1]{2,0,3,1:T(8,128)}, u32[]{:S(2)}, u32[]{:S(2)}) collective-permute-start(f32[19,6,18,1]{2,0,3,1:T(8,128)} %get-tuple-element.13), channel_id=1, source_target_pairs={{0,1},{1,2},{2,3},{3,0},{4,5},{5,6},{6,7},{7,4},{8,9},{9,10},{10,1... | collective-permute-start | bytes 24632 | tf_op jit(solution)/shard_map/ppermute | solution.py:15
  79.8 4.1 %copy-start.26 = (f32[1,4,16,128]{3,0,2,1:T(1,128)S(1)}, f32[1,4,16,128]{3,0,2,1:T(1,128)}, u32[]{:S(2)}) copy-start(f32[1,4,16,128]{3,0,2,1:T(1,128)} %get-tuple-element.39) | copy-start | bytes 98308
  97.4 4.7 %collective-permute-start.7 = (f32[19,1,16,128]{3,2,1,0:T(8,128)S(1)}, f32[19,1,16,128]{3,2,1,0:T(8,128)S(1)}, u32[]{:S(2)}, u32[]{:S(2)}) collective-permute-start(f32[19,1,16,128]{3,2,1,0:T(8,128)S(1)} %get-tuple-element.61), channel_id=1, source_target_pairs={{0,8},{8,16},{16,24},{24,0},{1,9},{9,17},{17,25},{25,1},{2,10},{10... | collective-permute-start | bytes 466952 | tf_op jit(solution)/shard_map/ppermute | solution.py:15
  97.5 5.3 %collective-permute-start.6 = (f32[19,1,16,128]{3,2,1,0:T(8,128)S(1)}, f32[19,1,16,128]{3,2,1,0:T(8,128)S(1)}, u32[]{:S(2)}, u32[]{:S(2)}) collective-permute-start(f32[19,1,16,128]{3,2,1,0:T(8,128)S(1)} %get-tuple-element.62), channel_id=1, source_target_pairs={{8,0},{16,8},{24,16},{0,24},{9,1},{17,9},{25,17},{1,25},{10,2},{18... | collective-permute-start | bytes 466952 | tf_op jit(solution)/shard_map/ppermute | solution.py:17
  102.8 4.9 %copy-start.9 = (f32[19,1,16,128]{3,2,1,0:T(8,128)}, f32[19,1,16,128]{3,2,1,0:T(8,128)S(1)}, u32[]{:S(2)}) copy-start(f32[19,1,16,128]{3,2,1,0:T(8,128)S(1)} %collective-permute-done.6) | copy-start | bytes 466948
  102.9 4.8 %collective-permute-start.8 = (f32[19,6,1,128]{3,2,1,0:T(1,128)S(1)}, f32[19,6,1,128]{3,2,1,0:T(1,128)S(1)}, u32[]{:S(2)}, u32[]{:S(2)}) collective-permute-start(f32[19,6,1,128]{3,2,1,0:T(1,128)S(1)} %get-tuple-element.54), channel_id=1, source_target_pairs={{4,0},{0,4},{5,1},{1,5},{6,2},{2,6},{7,3},{3,7},{12,8},{8,12},{13,... | collective-permute-start | bytes 175112 | tf_op jit(solution)/shard_map/ppermute | solution.py:17
  104.5 4.5 %collective-permute-start.9 = (f32[19,6,1,128]{3,2,1,0:T(1,128)S(1)}, f32[19,6,1,128]{3,2,1,0:T(1,128)S(1)}, u32[]{:S(2)}, u32[]{:S(2)}) collective-permute-start(f32[19,6,1,128]{3,2,1,0:T(1,128)S(1)} %get-tuple-element.53), channel_id=1, source_target_pairs={{0,4},{4,0},{1,5},{5,1},{2,6},{6,2},{3,7},{7,3},{8,12},{12,8},{9,1... | collective-permute-start | bytes 175112 | tf_op jit(solution)/shard_map/ppermute | solution.py:15
  111.2 6.2 %copy-start.10 = (f32[19,1,16,128]{3,2,1,0:T(8,128)S(1)}, f32[19,1,16,128]{3,2,1,0:T(8,128)}, u32[]{:S(2)}) copy-start(f32[19,1,16,128]{3,2,1,0:T(8,128)} %copy-done.9) | copy-start | bytes 466948
  113.3 6.8 %collective-permute-start.10 = (f32[19,6,18,1]{0,3,2,1:T(1,128)S(1)}, f32[19,6,18,1]{0,3,2,1:T(1,128)S(1)}, u32[]{:S(2)}, u32[]{:S(2)}) collective-permute-start(f32[19,6,18,1]{0,3,2,1:T(1,128)S(1)} %copy.98), channel_id=1, source_target_pairs={{1,0},{2,1},{3,2},{0,3},{5,4},{6,5},{7,6},{4,7},{9,8},{10,9},{11,1... | collective-permute-start | bytes 24632 | tf_op jit(solution)/shard_map/ppermute | solution.py:17
  120.1 6.0 %collective-permute-start.11 = (f32[19,6,18,1]{0,3,2,1:T(1,128)S(1)}, f32[19,6,18,1]{0,3,2,1:T(1,128)S(1)}, u32[]{:S(2)}, u32[]{:S(2)}) collective-permute-start(f32[19,6,18,1]{0,3,2,1:T(1,128)S(1)} %copy.100), channel_id=1, source_target_pairs={{0,1},{1,2},{2,3},{3,0},{4,5},{5,6},{6,7},{7,4},{8,9},{9,10},{10,1... | collective-permute-start | bytes 24632 | tf_op jit(solution)/shard_map/ppermute | solution.py:15
  133.3 40.6 %copy-start.4 = (f32[19,8192]{1,0:T(8,128)S(1)}, f32[19,8192]{1,0:T(8,128)}, u32[]{:S(2)}) copy-start(f32[19,8192]{1,0:T(8,128)} %copy-done.3) | copy-start | bytes 1867780
  133.3 40.6 %copy-start.19 = (f32[8192]{0:T(1024)S(1)}, f32[8192]{0:T(1024)}, u32[]{:S(2)}) copy-start(f32[8192]{0:T(1024)} %copy-done.18) | copy-start | bytes 98308
  133.3 40.6 %copy-start.36 = (f32[19]{0:T(128)S(1)}, f32[19]{0:T(128)}, u32[]{:S(2)}) copy-start(f32[19]{0:T(128)} %constant.11.clone) | copy-start | bytes 232
  (28 other events, 39.4 us)
where the time goes:
time: 183 us; the launch traced here: 181 us
  local copies, waits for them, and re-layouts  67.4 us (37%)
  blocking collectives  37.7 us (21%)
  other arithmetic  25 us (14%)
  matrix products  23.1 us (13%)
  starting transfers between devices  16.9 us (9%)
  waiting for transfers between devices  6.71 us (4%)
  between operations  4.59 us (3%)
    psum x1, blocking collectives, body(): drag_totals.append(lax.psum(drag_part, ('gx', 'gy', 'gz')))  37.7 us
    concatenate x8, other arithmetic, extended(): jnp.concatenate([lax.ppermute(tail, axis, [(i, (i + 1) % count) for i in...  19.8 us
    unnamed x109, local copies, waits for them, and re-layouts  19.2 us
    concatenate x6, local copies, waits for them, and re-layouts, extended(): jnp.concatenate([lax.ppermute(tail, axis, [(i, (i + 1) % count) for i in...  14.4 us
    ppermute x6, starting transfers between devices, extended(): lax.ppermute(head, axis, [((i + 1) % count, i) for i in range(count)])  13.4 us
    ppermute x3, local copies, waits for them, and re-layouts, extended(): lax.ppermute(head, axis, [((i + 1) % count, i) for i in range(count)])  10.6 us
    ppermute x3, local copies, waits for them, and re-layouts, extended(): lax.ppermute(tail, axis, [(i, (i + 1) % count) for i in range(count)])  10.6 us
    slice x7, local copies, waits for them, and re-layouts, extended(): lax.slice_in_dim(cells, cells.shape[dim] - width, cells.shape[dim], axis=...  7.19 us
  transfers between devices with their start and end apart: 12, of which 5 were waited for; matrix products, arithmetic and copies ran while one was open for 25% of the time, Pallas kernels for 0%

commit v1 on v0

v1 whole, which is shorter than its diff:
```python
import functools

import jax
import jax.numpy as jnp
import numpy as np
from jax import lax
from jax.experimental import pallas as pl
from jax.experimental.pallas import tpu as pltpu
from jax.sharding import PartitionSpec as P

VEL = (
    (0, 0, 0),
    (1, 0, 0),
    (-1, 0, 0),
    (0, 1, 0),
    (0, -1, 0),
    (0, 0, 1),
    (0, 0, -1),
    (1, 1, 0),
    (-1, -1, 0),
    (1, -1, 0),
    (-1, 1, 0),
    (1, 0, 1),
    (-1, 0, -1),
    (1, 0, -1),
    (-1, 0, 1),
    (0, 1, 1),
    (0, -1, -1),
    (0, 1, -1),
    (0, -1, 1),
)
PAIRS = tuple((i, i + 1) for i in range(1, 19, 2))
AXES = ("gx", "gy", "gz")
UB = (19, 20, 21, 22)


def near(axis, sign):
    return tuple(i for i in range(19) if VEL[i][axis] * sign >= 0) + UB


def far(axis, sign):
    return tuple(i for i in range(19) if VEL[i][axis] == sign)


NSLOT = 23
ZGROUPS = (
    tuple(i for i in range(19) if VEL[i][2] == -1),
    tuple(i for i in range(19) if VEL[i][2] == 1),
    tuple(i for i in range(19) if VEL[i][2] == 0)[:8],
    tuple(i for i in range(19) if VEL[i][2] == 0)[8:] + UB,
)
ZSLOT = {q: (g, k) for g, group in enumerate(ZGROUPS) for k, q in enumerate(group)}


def pairs_of(values):
    s = [values[a] + values[b] for a, b in PAIRS]
    d = [values[a] - values[b] for a, b in PAIRS]
    return s, d


def moments(v0, s, d):
    sx, sy, sz, sp, sq, sr, ss, st, su = s
    dx, dy, dz, dp, dq, dr, ds, dt, du = d
    ex = sp + sq
    ez = sr + ss
    ey = st + su
    faces = sx + sy + sz
    edges = ex + ez + ey
    exx = ex + ez
    eyy = ex + ey
    ezz = ez + ey
    fx = (dp + dq) + (dr + ds)
    fy = (dp - dq) + (dt + du)
    fz = (dr - ds) + (dt - du)
    return dict(
        rest=v0,
        faces=faces,
        edges=edges,
        total=v0 + faces + edges,
        face1=(dx, dy, dz),
        edge1=(fx, fy, fz),
        one=(dx + fx, dy + fy, dz + fz),
        face2=(sx, sy, sz),
        edge2=(exx, eyy, ezz),
        two=(sx + exx, sy + eyy, sz + ezz),
        cross=(sp - sq, sr - ss, st - su),
    )


def adjoint_cell(g, u, b, drive):
    s, d = pairs_of(g)
    m = moments(g[0], s, d)
    total = m["total"]
    trace = m["faces"] + 2.0 * m["edges"] - (30.0 / 19.0) * total
    p0 = (-1.2 / 19.0) * total - (2.0 / 21.0) * trace
    q = [
        (0.4 / 6.0) * (two - (10.0 / 19.0) * total) + (0.8 / 21.0) * trace
        for two in m["two"]
    ]
    qsum = q[0] + q[1] + q[2]
    qab = [0.1 * c for c in m["cross"]]
    p1 = [-0.12 * one for one in m["one"]]
    h0 = (
        0.4 * m["rest"]
        + (1.2 / 18.0) * m["faces"]
        + (1.2 / 36.0) * m["edges"]
        + p0
        + (1.0 / 3.0) * qsum
    )
    h1 = [
        (1.2 / 18.0) * f + (1.2 / 36.0) * e + (1.0 / 3.0) * p
        for f, e, p in zip(m["face1"], m["edge1"], p1)
    ]
    base = (1.0 / 3.0) * p0 + (1.0 / 9.0) * qsum
    haa = [
        (1.2 / 18.0) * f + (1.2 / 36.0) * e + (2.0 / 9.0) * qa + base
        for f, e, qa in zip(m["face2"], m["edge2"], q)
    ]
    hxy, hxz, hyz = [(2.0 / 45.0) * c for c in m["cross"]]
    ux, uy, uz = u
    v = (
        haa[0] * ux + hxy * uy + hxz * uz,
        hxy * ux + haa[1] * uy + hyz * uz,
        hxz * ux + hyz * uy + haa[2] * uz,
    )
    uv = ux * v[0] + uy * v[1] + uz * v[2]
    uu = ux * ux + uy * uy + uz * uz
    uuh = 1.5 * uu * h0
    a = h0 + uuh - 4.5 * uv
    nb = 1.0 - b
    e0 = nb * (a - p0)
    nq = [nb * x for x in q]
    nxy, nxz, nyz = [nb * x for x in qab]
    o = [
        nb * (3.0 * h1[k] + 9.0 * v[k] - 3.0 * u[k] * h0 - p1[k]) for k in range(3)
    ]
    o[0] = o[0] + b * drive
    alpha = -0.2 * nb
    half_s = 0.5 * (alpha + b)
    half_d = 0.5 * (alpha - b)
    exy = e0 - nq[0] - nq[1]
    exz = e0 - nq[0] - nq[2]
    eyz = e0 - nq[1] - nq[2]
    even = (
        e0 - nq[0],
        e0 - nq[1],
        e0 - nq[2],
        exy - nxy,
        exy + nxy,
        exz - nxz,
        exz + nxz,
        eyz - nyz,
        eyz + nyz,
    )
    odd = (
        o[0],
        o[1],
        o[2],
        o[0] + o[1],
        o[0] - o[1],
        o[0] + o[2],
        o[0] - o[2],
        o[1] + o[2],
        o[1] - o[2],
    )
    out = [(alpha + b) * g[0] + e0]
    for k in range(9):
        even_k = half_s * s[k] + even[k]
        odd_k = half_d * d[k] + odd[k]
        out.append(even_k + odd_k)
        out.append(even_k - odd_k)
    kept = dict(
        s=s, d=d, g0=g[0], p0=p0, p1=p1, q=q, qab=qab, h0=h0, h1=h1, uv=uv, uuh=uuh
    )
    return out, kept


def gradient_cell(kept, f0, fs, fd, fm, u):
    rho = fm["total"]
    even = fs[0] * kept["s"][0]
    odd = fd[0] * kept["d"][0]
    for k in range(1, 9):
        even = even + fs[k] * kept["s"][k]
        odd = odd + fd[k] * kept["d"][k]
    hf = kept["p0"] * rho
    for k in range(3):
        hf = hf + kept["p1"][k] * fm["one"][k] + kept["q"][k] * fm["two"][k]
        hf = hf + kept["qab"][k] * fm["cross"][k]
    uh1 = u[0] * kept["h1"][0] + u[1] * kept["h1"][1] + u[2] * kept["h1"][2]
    hfeq = rho * (kept["h0"] - kept["uuh"] + 3.0 * uh1 + 4.5 * kept["uv"])
    pairs = 1.2 * f0 * kept["g0"] + 0.6 * even - 0.4 * odd
    return pairs + hf - hfeq + fm["one"][0]


def state_of(ref, index):
    f = [ref[(index[0], i) + index[1:]] for i in range(19)]
    s, d = pairs_of(f)
    m = moments(f[0], s, d)
    inverse = 1.0 / m["total"]
    u = [one * inverse for one in m["one"]]
    return f[0], s, d, m, u


def pack_x_kernel(
    par_ref, states_ref, adj_ref, por_ref, mask_ref, a_ref, b_ref, ub_ref, drag_ref
):
    nx, ny, nz = por_ref.shape
    tiles = ny // 8

    def cells(n, drag):
        x = n // tiles
        rows = pl.ds(pl.multiple_of((n % tiles) * 8, 8), 8)
        blocking = jnp.where(mask_ref[x, rows, :] == 0, por_ref[x, rows, :], 1.0)
        f0, s, d, m, u = state_of(states_ref, (1, x, rows))
        flux = m["one"][0]
        for a, b in PAIRS:
            if VEL[a][0]:
                flux = flux + (states_ref[0, a, x, rows, :] - states_ref[0, b, x, rows, :])
        for k in range(3):
            ub_ref[k, x, rows, :] = u[k]
        ub_ref[3, x, rows, :] = blocking
        return drag + blocking * flux

    drag = lax.fori_loop(0, nx * tiles, cells, jnp.zeros((8, nz), jnp.float32))
    drag_ref[...] = drag

    def fill(out_ref, sign):
        first, second = (0, 1) if sign > 0 else (nx - 1, nx - 2)
        for k, q in enumerate(near(0, sign)):
            out_ref[k * ny : (k + 1) * ny] = (
                adj_ref[q, first] if q < 19 else ub_ref[q - 19, first]
            )
        for k, q in enumerate(far(0, sign)):
            k += 18
            out_ref[k * ny : (k + 1) * ny] = adj_ref[q, second]
        out_ref[NSLOT * ny : NSLOT * ny + 8] = drag

    @pl.when(par_ref[0] == 0)
    def _():
        fill(a_ref, -1)
        fill(b_ref, 1)

    @pl.when(par_ref[0] == 1)
    def _():
        fill(a_ref, 1)
        fill(b_ref, -1)


def total_of(mode, tiles):
    if mode == "pair":
        return tiles[0] + tiles[1]
    if mode == "four":
        return (tiles[0] + tiles[1]) + (tiles[2] + tiles[3])
    return tiles[3]


def pack_y_kernel(
    mode,
    par_ref,
    adj_ref,
    ub_ref,
    xa_ref,
    xb_ref,
    drag_ref,
    extra_ref,
    out_ref,
):
    nx, ny = adj_ref.shape[1:3]
    even = par_ref[0] == 0
    row_sets = {
        1: (near(1, 1), 0, far(1, 1), 1),
        -1: (near(1, -1), ny - 1, far(1, -1), ny - 2),
    }

    def fill(place, sign):
        first_q, first_row, second_q, second_row = row_sets[sign]
        entries = [(q, first_row) for q in first_q] + [(q, second_row) for q in second_q]
        for k, (q, row) in enumerate(entries):
            where = slice(k * 8, k * 8 + 8)
            rows = []
            for s in range(nx + 4):
                if 2 <= s < nx + 2:
                    rows.append(
                        adj_ref[q, s - 2, row : row + 1, :]
                        if q < 19
                        else ub_ref[q - 19, s - 2, row : row + 1, :]
                    )
                    continue
                side = -1 if s < 2 else 1
                if s in (1, nx + 2):
                    names, offset = near(0, side), 0
                else:
                    names, offset = far(0, side), 18
                if q in names:
                    start = (names.index(q) + offset) * ny + row
                    va = xa_ref[start : start + 1, :]
                    vb = xb_ref[start : start + 1, :]
                    rows.append(
                        jnp.where(even, va, vb) if side > 0 else jnp.where(even, vb, va)
                    )
                else:
                    rows.append(None)
            for s, value in enumerate(rows):
                if value is not None:
                    out_ref[place, k * 8 + s : k * 8 + s + 1, :] = value
                else:
                    out_ref[place, k * 8 + s : k * 8 + s + 1, :] = jnp.zeros(
                        (1, out_ref.shape[2]), jnp.float32
                    )

    @pl.when(par_ref[1] == 0)
    def _():
        fill(0, -1)
        fill(1, 1)

    @pl.when(par_ref[1] == 1)
    def _():
        fill(0, 1)
        fill(1, -1)

    last = slice(NSLOT * ny, NSLOT * ny + 8)
    drag = total_of(
        mode, (drag_ref[...], xa_ref[last], xb_ref[last], extra_ref[...])
    )
    out_ref[0, NSLOT * 8 : NSLOT * 8 + 8, :] = drag
    out_ref[1, NSLOT * 8 : NSLOT * 8 + 8, :] = drag


def pack_z_kernel(
    mode,
    par_ref,
    adj_ref,
    ub_ref,
    xa_ref,
    xb_ref,
    ya_ref,
    yb_ref,
    ysent_ref,
    extra_ref,
    read_ref,
    zmsg_ref,
    drag_ref,
    ext,
):
    nx, ny, nz = adj_ref.shape[1:]
    even_x = par_ref[0] == 0
    even_y = par_ref[1] == 0
    base = 16

    def copy(q, carry):
        return carry

    for q in range(NSLOT):
        for x in range(nx):
            ext[q, x + 2, base : base + ny, :] = (
                adj_ref[q, x] if q < 19 else ub_ref[q - 19, x]
            )
    for sign in (1, -1):
        one, two = (nx + 2, nx + 3) if sign > 0 else (1, 0)
        for names, plane, offset in ((near(0, sign), one, 0), (far(0, sign), two, 18)):
            for k, q in enumerate(names):
                rows = slice((k + offset) * ny, (k + offset + 1) * ny)
                first, second = (xa_ref, xb_ref) if sign > 0 else (xb_ref, xa_ref)
                ext[q, plane, base : base + ny, :] = jnp.where(
                    even_x, first[rows], second[rows]
                )
        one, two = (base + ny, base + ny + 1) if sign > 0 else (base - 1, base - 2)
        first, second = (ya_ref, yb_ref) if sign > 0 else (yb_ref, ya_ref)
        for names, row, offset in ((near(1, sign), one, 0), (far(1, sign), two, 18)):
            for k, q in enumerate(names):
                start = (k + offset) * 8
                tile = jnp.where(
                    even_y, first[start : start + 8], second[start : start + 8]
                )
                for s in range(nx + 4):
                    ext[q, s, row : row + 1, :] = tile[s : s + 1]

    lane = lax.broadcasted_iota(jnp.int32, (8, nz), 1)
    sub = lax.broadcasted_iota(jnp.int32, (8, nz), 0)
    pair = lane // 2
    tiles = ny // 8
    for g, group in enumerate(ZGROUPS):
        acc = [jnp.zeros((8, nz), jnp.float32) for t in range(tiles + 1)]
        for k, q in enumerate(group):
            cx, cy, cz = VEL[q] if q < 19 else (0, 0, 0)
            for p in range(nx + 2):
                plane = p + 1 + cx
                start = 16 * k + 2 * p
                mask = pair == start // 2
                for t in range(tiles + 1):
                    if t < tiles:
                        low = base + 8 * t + cy
                        value = ext[q, plane, low : low + 8, :]
                    else:
                        high = base + ny + cy
                        low = base - 8 + cy
                        value = jnp.where(
                            sub < 4,
                            ext[q, plane, high : high + 8, :],
                            ext[q, plane, low : low + 8, :],
                        )
                    read_ref[q, p, 8 * t : 8 * t + 8, :] = value
                    shift = start + (2 if cz < 0 else 1 if cz == 0 else 0)
                    moved = pltpu.roll(value, shift % nz, 1)
                    acc[t] = jnp.where(mask, moved, acc[t])
        for t in range(tiles + 1):
            row = (g * (tiles + 1) + t) * 8
            zmsg_ref[row : row + 8, :] = acc[t]
    last = slice(NSLOT * 8, NSLOT * 8 + 8)
    drag = total_of(mode, (ysent_ref[0, last, :], ya_ref[last], yb_ref[last], extra_ref[...]))
    drag_ref[...] = drag
    row = 4 * (tiles + 1) * 8
    zmsg_ref[row : row + 8, :] = drag


def levels_kernel(
    mode,
    whole_cells,
    par_ref,
    states_ref,
    mask_ref,
    read_ref,
    zown_ref,
    za_ref,
    zb_ref,
    extra_ref,
    out_ref,
    grad_ref,
    drag_ref,
    lo_ref,
    hi_ref,
    slab_ref,
    mid,
    zmid,
):
    nx, ny, nz = mask_ref.shape
    tiles = ny // 8
    height = (tiles + 1) * 8
    even = par_ref[2] == 0
    lane = lax.broadcasted_iota(jnp.int32, (8, nz), 1)
    side = lane % 2
    first_lane = lane == 0
    last_lane = lane == nz - 1

    for g in range(4):
        for t in range(tiles + 1):
            rows = slice((g * (tiles + 1) + t) * 8, (g * (tiles + 1) + t) * 8 + 8)
            va = za_ref[rows]
            vb = zb_ref[rows]
            high = jnp.where(even, va, vb)
            low = jnp.where(even, vb, va)
            lo_ref[rows] = low
            hi_ref[rows] = high
            own = zown_ref[rows]
            slab_ref[rows] = jnp.where(
                side == 0, own if g == 1 else low, own if g == 0 else high
            )

    last = slice(4 * height, 4 * height + 8)
    drag = total_of(mode, (zown_ref[last], za_ref[last], zb_ref[last], extra_ref[...]))
    summed = jnp.sum(jnp.sum(drag, axis=1, keepdims=True), axis=0, keepdims=True)
    drag_ref[...] = summed / whole_cells

    def rolled(value, shift):
        return pltpu.roll(value, lax.rem(shift + 2 * nz, nz), 1)

    def z_slab(t, carry):
        row = pl.multiple_of(t * 8, 8)
        got = []
        for q in range(NSLOT):
            g, k = ZSLOT[q]
            tile = slab_ref[pl.ds(pl.multiple_of(g * height + row, 8), 8), :]
            got.append(tile if k == 0 else pltpu.roll(tile, nz - 16 * k, 1))
        out, kept = adjoint_cell(got[:19], got[19:22], got[22], 1.0)
        for n, i in enumerate(ZGROUPS[0] + ZGROUPS[1]):
            if_last = t == tiles

            zmid[n, pl.ds(pl.multiple_of(row + 8, 8), 8), :] = out[i]

            @pl.when(if_last)
            def _():
                zmid[n, 0:8, :] = out[i]

        return carry

    lax.fori_loop(0, tiles + 1, z_slab, 0)

    def first_reads(p, t):
        rows = pl.ds(pl.multiple_of(t * 8, 8), 8)
        got = []
        for i in range(19):
            value = read_ref[i, p, rows, :]
            cz = VEL[i][2]
            if cz:
                g, k = ZSLOT[i]
                zrows = pl.ds(pl.multiple_of(g * height + t * 8, 8), 8)
                value = pltpu.roll(value, 1 if cz < 0 else nz - 1, 1)
                if cz < 0:
                    edge = rolled(lo_ref[zrows, :], -(16 * k + 2 * p + 1))
                    value = jnp.where(first_lane, edge, value)
                else:
                    edge = rolled(hi_ref[zrows, :], nz - 1 - 16 * k - 2 * p)
                    value = jnp.where(last_lane, edge, value)
            got.append(value)
        ub = [read_ref[19 + k, p, rows, :] for k in range(4)]
        return got, ub[:3], ub[3]

    def store_mid(out, p, t):
        for i in range(19):
            mid[i, p, pl.ds(pl.multiple_of(t * 8 + 8, 8), 8), :] = out[i]

    def inner(n, carry):
        x = n // tiles
        t = n % tiles
        got, u, b = first_reads(x + 1, t)
        out, kept = adjoint_cell(got, u, b, 1.0)
        store_mid(out, x + 1, t)
        rows = pl.ds(pl.multiple_of(t * 8, 8), 8)
        f0, fs, fd, fm, _ = state_of(states_ref, (1, x, rows))
        grad_ref[x, rows, :] = gradient_cell(kept, f0, fs, fd, fm, u)
        return carry

    lax.fori_loop(0, nx * tiles, inner, 0)

    def outer(n, carry):
        faces = 2 * (tiles + 1)
        p = jnp.where(n < faces, (nx + 1) * (n // (tiles + 1)), n - faces + 1)
        t = jnp.where(n < faces, n % (tiles + 1), tiles)
        got, u, b = first_reads(p, t)
        out, kept = adjoint_cell(got, u, b, 1.0)
        store_mid(out, p, t)

        @pl.when(t == tiles)
        def _():
            for i in range(19):
                mid[i, p, 0:8, :] = out[i]

        return carry

    lax.fori_loop(0, 2 * (tiles + 1) + nx, outer, 0)

    edge_pops = ZGROUPS[0] + ZGROUPS[1]

    def second(x, carry):
        for t in range(tiles):
            rows = slice(t * 8, t * 8 + 8)
            got = []
            for i in range(19):
                cx, cy, cz = VEL[i]
                low = 8 + 8 * t + cy
                value = mid[i, x + 1 + cx, low : low + 8, :]
                if cz:
                    value = pltpu.roll(value, 1 if cz < 0 else nz - 1, 1)
                    edge = zmid[edge_pops.index(i), low : low + 8, :]
                    at = 2 * (x + 1 + cx)
                    if cz < 0:
                        value = jnp.where(first_lane, rolled(edge, -at), value)
                    else:
                        value = jnp.where(
                            last_lane, rolled(edge, nz - 2 - at), value
                        )
                got.append(value)
            f0, fs, fd, fm, u = state_of(states_ref, (0, x, rows))
            b = read_ref[22, x + 1, rows, :]
            out, kept = adjoint_cell(got, u, b, 1.0)
            for i in range(19):
                out_ref[i, x, rows, :] = out[i]
            grad = grad_ref[x, rows, :] + gradient_cell(kept, f0, fs, fd, fm, u)
            grad_ref[x, rows, :] = jnp.where(mask_ref[x, rows, :] == 0, grad, 0.0)
        return carry

    lax.fori_loop(0, nx, second, 0)


def swaps(count):
    first = [(i, i ^ 1) for i in range(count)]
    second = [(i, (((i + 1) % count) ^ 1) - 1) for i in range(count)]
    second = [(i, j % count) for i, j in second]
    return first, second


def drag_extra(tile, axis, count):
    if count == 2:
        return "pair", tile
    if count == 4:
        return "four", lax.ppermute(tile, axis, [(i, (i + 2) % 4) for i in range(4)])
    return "whole", lax.psum(tile, axis)


VMEM = pl.BlockSpec(memory_space=pltpu.VMEM)
SMEM = pl.BlockSpec(memory_space=pltpu.SMEM)
PARAMS = pltpu.CompilerParams(vmem_limit_bytes=48 * 2**20)


def call(kernel, inputs, shapes, scratch=()):
    return pl.pallas_call(
        kernel,
        out_shape=[jax.ShapeDtypeStruct(s, jnp.float32) for s in shapes],
        in_specs=[SMEM] + [VMEM] * (len(inputs) - 1),
        out_specs=[VMEM] * len(shapes),
        scratch_shapes=[pltpu.VMEM(s, jnp.float32) for s in scratch],
        compiler_params=PARAMS,
    )(*inputs)


def body(primal_states, adjoint_last, porosity, solid_mask):
    nx, ny, nz = porosity.shape
    counts = [lax.axis_size(axis) for axis in AXES]
    pairings = [swaps(count) for count in counts]
    parity = jnp.stack([lax.axis_index(axis) & 1 for axis in AXES]).astype(jnp.int32)
    tiles = ny // 8
    height = (tiles + 1) * 8

    rows_x = NSLOT * ny + 8
    xa, xb, ub, drag = call(
        pack_x_kernel,
        (parity, primal_states, adjoint_last, porosity, solid_mask),
        [(rows_x, nz), (rows_x, nz), (4, nx, ny, nz), (8, nz)],
    )
    xb = lax.ppermute(xb, "gx", pairings[0][1])
    xa = lax.ppermute(xa, "gx", pairings[0][0])
    mode, extra = drag_extra(drag, "gx", counts[0])

    rows_y = NSLOT * 8 + 8
    (ysent,) = call(
        functools.partial(pack_y_kernel, mode),
        (parity, adjoint_last, ub, xa, xb, drag, extra),
        [(2, rows_y, nz)],
    )
    drag_y = ysent[0, NSLOT * 8 :] if counts[1] > 2 else drag
    if counts[1] == 2:
        ygot = lax.ppermute(ysent, "gy", pairings[1][0])
        ya, yb = ygot[0], ygot[1]
    else:
        ya = lax.ppermute(ysent[0], "gy", pairings[1][0])
        yb = lax.ppermute(ysent[1], "gy", pairings[1][1])
    mode, extra = drag_extra(drag_y, "gy", counts[1])

    read, zmsg, drag = call(
        functools.partial(pack_z_kernel, mode),
        (parity, adjoint_last, ub, xa, xb, ya, yb, ysent, extra),
        [(NSLOT, nx + 2, height, nz), (4 * height + 8, nz), (8, nz)],
        [(NSLOT, nx + 4, ny + 32, nz)],
    )
    zb = lax.ppermute(zmsg, "gz", pairings[2][1])
    za = lax.ppermute(zmsg, "gz", pairings[2][0])
    mode, extra = drag_extra(drag, "gz", counts[2])
    whole_cells = nx * ny * nz * counts[0] * counts[1] * counts[2]

    first, gradient, total = call(
        functools.partial(levels_kernel, mode, float(whole_cells)),
        (parity, primal_states, solid_mask, read, zmsg, za, zb, extra),
        [(19, nx, ny, nz), (nx, ny, nz), (1, 1)],
        [
            (4 * height, nz),
            (4 * height, nz),
            (4 * height, nz),
            (19, nx + 2, height + 8, nz),
            (10, height + 8, nz),
        ],
    )
    return (first, gradient, total.reshape(()))


def solution(mesh):
    return jax.shard_map(
        body,
        mesh=mesh,
        in_specs=(
            P(None, None, "gx", "gy", "gz"),
            P(None, "gx", "gy", "gz"),
            P("gx", "gy", "gz"),
            P("gx", "gy", "gz"),
        ),
        out_specs=(P(None, "gx", "gy", "gz"), P("gx", "gy", "gz"), P()),
        check_vma=False,
    )
```

time: 183 us -> 36.3 us (0.20)
  local copies, waits for them, and re-layouts: 67.4 us -> 3.91 us
  blocking collectives: 37.7 us -> 0 us
  other arithmetic: 25 us -> 0.08 us
  matrix products: 23.1 us -> 0 us
  Pallas kernels: 0 us -> 7.7 us
  starting transfers between devices: 16.9 us -> 9.5 us
  waiting for transfers between devices: 6.71 us -> 14.1 us
  between operations: 4.59 us -> 0.69 us
    psum x1 -> x0, blocking collectives: 37.7 us -> none  [body(): drag_totals.append(lax.psum(drag_part, ('gx', 'gy', 'gz')))]
    dot_general x22 -> x0, matrix products: 23.1 us -> none  [the longest x4 6.44 us: collide(): moments = jnp.dot(basis_rows, state - equilibrium, precision=highest)]
    ppermute x6 -> x0, local copies, waits for them, and re-layouts: 21.3 us -> none  [the longest x3 10.6 us: extended(): lax.ppermute(head, axis, [((i + 1) % count, i) for i in range(count)])]
    concatenate x8 -> x0, other arithmetic: 19.8 us -> none  [extended(): jnp.concatenate([lax.ppermute(tail, axis, [(i, (i + 1) % count) for i in...]
    unnamed x109 -> x12, local copies, waits for them, and re-layouts: 19.2 us -> 3.89 us
    concatenate x6 -> x0, local copies, waits for them, and re-layouts: 14.4 us -> none  [extended(): jnp.concatenate([lax.ppermute(tail, axis, [(i, (i + 1) % count) for i in...]
    slice x11 -> x0, local copies, waits for them, and re-layouts: 10.7 us -> none  [the longest x7 7.19 us: extended(): lax.slice_in_dim(cells, cells.shape[dim] - width, cells.shape[dim], axis=...]
    pallas_call x0 -> x4, Pallas kernels: none -> 7.7 us  [call(): pl.pallas_call(kernel, out_shape=[jax.ShapeDtypeStruct(s, jnp.float32) fo...]
  transfers between devices with their start and end apart: 12 -> 7, of which waited for: 5 -> 3; matrix products, arithmetic and copies ran while one was open for 25% -> 0% of each run, Pallas kernels for 0% -> 0%
where the time goes in v1:
time: 36.3 us; the launch traced here: 36 us
  waiting for transfers between devices  14.1 us (39%)
  starting transfers between devices  9.5 us (26%)
  Pallas kernels  7.7 us (21%)
  local copies, waits for them, and re-layouts  3.91 us (11%)
  between operations  0.69 us (2%)
    ppermute x2, waiting for transfers between devices, drag_extra(): lax.ppermute(tile, axis, [(i, (i + 2) % 4) for i in range(4)])  9.27 us
    pallas_call x4, Pallas kernels, call(): pl.pallas_call(kernel, out_shape=[jax.ShapeDtypeStruct(s, jnp.float32) fo...  7.7 us
    ppermute x1, waiting for transfers between devices, body(): ygot = lax.ppermute(ysent, 'gy', pairings[1][0])  4.83 us
    unnamed x12, local copies, waits for them, and re-layouts  3.89 us
    ppermute x1, starting transfers between devices, body(): zb = lax.ppermute(zmsg, 'gz', pairings[2][1])  3.88 us
    ppermute x1, starting transfers between devices, body(): xb = lax.ppermute(xb, 'gx', pairings[0][1])  2.62 us
    ppermute x1, starting transfers between devices, body(): ygot = lax.ppermute(ysent, 'gy', pairings[1][0])  1.8 us
  transfers between devices with their start and end apart: 7, of which 3 were waited for; matrix products, arithmetic and copies ran while one was open for 0% of the time, Pallas kernels for 0%

profile of v1, /device:TPU:0, one launch (start us, length us, event | category | flops | bytes accessed | tf_op | source)
XLA Modules:
  0.0 36.0 jit_solution(2584357501239898906)
XLA Ops:
  0.6 0.1 pad_add_fusion.par_ref
  0.7 1.1 %copy-done = f32[19,4,16,128]{3,2,1,0:T(8,128)S(1)} copy-done((f32[19,4,16,128]{3,2,1,0:T(8,128)S(1)}, f32[19,4,16,128]{3,2,1,0:T(8,128)}, u32[]{:S(2)}) %copy-start) | copy-done | bytes 622616
  1.8 1.3 %copy-done.2 = f32[2,19,4,16,128]{4,3,2,1,0:T(8,128)S(1)} copy-done((f32[2,19,4,16,128]{4,3,2,1,0:T(8,128)S(1)}, f32[2,19,4,16,128]{4,3,2,1,0:T(8,128)}, u32[]{:S(2)}) %copy-start.2) | copy-done | bytes 1245208
  3.1 0.8 %copy-done.4 = s32[4,16,128]{2,1,0:T(8,128)S(1)} copy-done((s32[4,16,128]{2,1,0:T(8,128)S(1)}, s32[4,16,128]{2,1,0:T(8,128)}, u32[]{:S(2)}) %copy-start.4) | copy-done | bytes 32792
  3.8 0.8 %copy-done.5 = f32[4,16,128]{2,1,0:T(8,128)S(1)} copy-done((f32[4,16,128]{2,1,0:T(8,128)S(1)}, f32[4,16,128]{2,1,0:T(8,128)}, u32[]{:S(2)}) %copy-start.5) | copy-done | bytes 32792
  4.6 0.8 %shard_map.67 = (f32[376,128]{1,0:T(8,128)S(1)}, f32[376,128]{1,0:T(8,128)S(1)}, f32[4,4,16,128]{3,2,1,0:T(8,128)S(1)}, f32[8,128]{1,0:T(8,128)S(1)}) custom-call(s32[3]{0:T(128)S(1)} %pad_add_fusion.par_ref, f32[2,19,4,16,128]{4,3,2,1,0:T(8,128)S(1)} %copy-done.2, f32[19,4,16,128]{3,2,1,0:T(8,128)S(1)} %copy-done, f32[4,16,128]{2,1,0:T(8,128)S(1)} %copy-done.5, ...), custom_call_target="tpu_custom_call" | custom-call | tf_op jit(solution)/shard_map/pallas_call | solution.py:596
  5.4 0.0 copy-start.3
  5.4 0.5 %collective-permute-start = (f32[376,128]{1,0:T(8,128)S(1)}, f32[376,128]{1,0:T(8,128)S(1)}, u32[]{:S(2)}, u32[]{:S(2)}) collective-permute-start(f32[376,128]{1,0:T(8,128)S(1)} %get-tuple-element.14), channel_id=1, source_target_pairs={{0,8},{8,0},{16,24},{24,16},{1,9},{9,1},{17,25},{25,17},{2,10},{10... | collective-permute-start | bytes 577544 | tf_op jit(solution)/shard_map/ppermute | solution.py:621
  5.9 2.6 %collective-permute-start.1 = (f32[376,128]{1,0:T(8,128)S(1)}, f32[376,128]{1,0:T(8,128)S(1)}, u32[]{:S(2)}, u32[]{:S(2)}) collective-permute-start(f32[376,128]{1,0:T(8,128)S(1)} %get-tuple-element.15), channel_id=1, source_target_pairs={{0,24},{8,16},{16,8},{24,0},{1,25},{9,17},{17,9},{25,1},{2,26},{10... | collective-permute-start | bytes 577544 | tf_op jit(solution)/shard_map/ppermute | solution.py:620
  8.6 0.0 collective-permute-start.2
  8.6 5.4 %collective-permute-done.2.extra_ref = f32[8,128]{1,0:T(8,128)S(1)} collective-permute-done((f32[8,128]{1,0:T(8,128)S(1)}, f32[8,128]{1,0:T(8,128)S(1)}, u32[]{:S(2)}, u32[]{:S(2)}) %collective-permute-start.2) | collective-permute-done | bytes 4128 | tf_op jit(solution)/shard_map/ppermute | solution.py:586
  14.0 0.0 collective-permute-done.xa_ref
  14.0 0.0 collective-permute-done.1.xb_ref
  14.0 0.7 %shard_map.68.ysent_ref = f32[2,192,128]{2,1,0:T(8,128)S(1)} custom-call(s32[3]{0:T(128)S(1)} %pad_add_fusion.par_ref, f32[19,4,16,128]{3,2,1,0:T(8,128)S(1)} %copy-done.1, f32[4,4,16,128]{3,2,1,0:T(8,128)S(1)} %get-tuple-element.13.ub_ref, f32[376,128]{1,0:T(8,128)S(1)} %collective-permute-done.xa_ref, f32[376,128]{1,0:T(8,128)S(1)} %collective-permute-done.1.xb_ref, ...), custom_call_target="tpu_custom_call" | custom-call | tf_op jit(solution)/shard_map/pallas_call | solution.py:596
  14.7 1.8 %collective-permute-start.3 = (f32[2,192,128]{2,1,0:T(8,128)S(1)}, f32[2,192,128]{2,1,0:T(8,128)S(1)}, u32[]{:S(2)}, u32[]{:S(2)}) collective-permute-start(f32[2,192,128]{2,1,0:T(8,128)S(1)} %shard_map.68.ysent_ref), channel_id=1, source_target_pairs={{0,4},{4,0},{1,5},{5,1},{2,6},{6,2},{3,7},{7,3},{8,12},{12,8},{9,1... | collective-permute-start | bytes 589832 | tf_op jit(solution)/shard_map/ppermute | solution.py:632
  16.5 4.8 %collective-permute-done.3 = f32[2,192,128]{2,1,0:T(8,128)S(1)} collective-permute-done((f32[2,192,128]{2,1,0:T(8,128)S(1)}, f32[2,192,128]{2,1,0:T(8,128)S(1)}, u32[]{:S(2)}, u32[]{:S(2)}) %collective-permute-start.3) | collective-permute-done | bytes 196640 | tf_op jit(solution)/shard_map/ppermute | solution.py:632
  21.4 1.1 %shard_map.69 = (f32[23,6,24,128]{3,2,1,0:T(8,128)S(1)}, f32[104,128]{1,0:T(8,128)S(1)}, f32[8,128]{1,0:T(8,128)S(1)}) custom-call(s32[3]{0:T(128)S(1)} %pad_add_fusion.par_ref, f32[19,4,16,128]{3,2,1,0:T(8,128)S(1)} %copy-done.1, f32[4,4,16,128]{3,2,1,0:T(8,128)S(1)} %get-tuple-element.13.ub_ref, f32[376,128]{1,0:T(8,128)S(1)} %collective-permute-done.xa_ref, ...), custom_call_target="tpu_custom_call" | custom-call | tf_op jit(solution)/shard_map/pallas_call | solution.py:596
  22.5 3.9 %collective-permute-start.5 = (f32[104,128]{1,0:T(8,128)S(1)}, f32[104,128]{1,0:T(8,128)S(1)}, u32[]{:S(2)}, u32[]{:S(2)}) collective-permute-start(f32[104,128]{1,0:T(8,128)S(1)} %get-tuple-element.18.zown_ref), channel_id=1, source_target_pairs={{0,3},{1,2},{2,1},{3,0},{4,7},{5,6},{6,5},{7,4},{8,11},{9,10},{10,... | collective-permute-start | bytes 159752 | tf_op jit(solution)/shard_map/ppermute | solution.py:645
  26.4 0.0 collective-permute-start.4
  26.4 0.6 %collective-permute-start.6 = (f32[8,128]{1,0:T(8,128)S(1)}, f32[8,128]{1,0:T(8,128)S(1)}, u32[]{:S(2)}, u32[]{:S(2)}) collective-permute-start(f32[8,128]{1,0:T(8,128)S(1)} %get-tuple-element.19), channel_id=1, source_target_pairs={{0,2},{1,3},{2,0},{3,1},{4,6},{5,7},{6,4},{7,5},{8,10},{9,11},{10,... | collective-permute-start | bytes 12296 | tf_op jit(solution)/shard_map/ppermute | solution.py:586
  27.0 3.9 %collective-permute-done.6.extra_ref = f32[8,128]{1,0:T(8,128)S(1)} collective-permute-done((f32[8,128]{1,0:T(8,128)S(1)}, f32[8,128]{1,0:T(8,128)S(1)}, u32[]{:S(2)}, u32[]{:S(2)}) %collective-permute-start.6) | collective-permute-done | bytes 4128 | tf_op jit(solution)/shard_map/ppermute | solution.py:586
  30.9 0.0 collective-permute-done.5.zb_ref
  30.9 0.0 collective-permute-done.4.za_ref
  30.9 5.1 %shard_map.70 = (f32[19,4,16,128]{3,2,1,0:T(8,128)}, f32[4,16,128]{2,1,0:T(8,128)}, f32[1,1]{1,0:T(1,128)}) custom-call(s32[3]{0:T(128)S(1)} %pad_add_fusion.par_ref, f32[2,19,4,16,128]{4,3,2,1,0:T(8,128)S(1)} %copy-done.3, s32[4,16,128]{2,1,0:T(8,128)S(1)} %copy-done.4, f32[23,6,24,128]{3,2,1,0:T(8,128)S(1)} %get-tuple-element.17.read_ref, ...), custom_call_target="tpu_custom_call" | custom-call | tf_op jit(solution)/shard_map/pallas_call | solution.py:596
  (8 shorter events, 0.0 us)
Async XLA Ops:
  0.7 1.1 %copy-start = (f32[19,4,16,128]{3,2,1,0:T(8,128)S(1)}, f32[19,4,16,128]{3,2,1,0:T(8,128)}, u32[]{:S(2)}) copy-start(f32[19,4,16,128]{3,2,1,0:T(8,128)} %adj_ref.5) | copy-start | bytes 1867780
  1.8 1.3 %copy-start.2 = (f32[2,19,4,16,128]{4,3,2,1,0:T(8,128)S(1)}, f32[2,19,4,16,128]{4,3,2,1,0:T(8,128)}, u32[]{:S(2)}) copy-start(f32[2,19,4,16,128]{4,3,2,1,0:T(8,128)} %states_ref.3) | copy-start | bytes 3735556
  3.1 0.8 %copy-start.4 = (s32[4,16,128]{2,1,0:T(8,128)S(1)}, s32[4,16,128]{2,1,0:T(8,128)}, u32[]{:S(2)}) copy-start(s32[4,16,128]{2,1,0:T(8,128)} %mask_ref.3) | copy-start | bytes 98308
  3.8 0.8 %copy-start.5 = (f32[4,16,128]{2,1,0:T(8,128)S(1)}, f32[4,16,128]{2,1,0:T(8,128)}, u32[]{:S(2)}) copy-start(f32[4,16,128]{2,1,0:T(8,128)} %por_ref.1) | copy-start | bytes 98308
  4.6 9.4 %copy-start.1 = (f32[19,4,16,128]{3,2,1,0:T(8,128)S(1)}, f32[19,4,16,128]{3,2,1,0:T(8,128)}, u32[]{:S(2)}) copy-start(f32[19,4,16,128]{3,2,1,0:T(8,128)} %adj_ref.5) | copy-start | bytes 1867780
  5.4 25.5 %copy-start.3 = (f32[2,19,4,16,128]{4,3,2,1,0:T(8,128)S(1)}, f32[2,19,4,16,128]{4,3,2,1,0:T(8,128)}, u32[]{:S(2)}) copy-start(f32[2,19,4,16,128]{4,3,2,1,0:T(8,128)} %states_ref.3) | copy-start | bytes 3735556
  5.4 8.6 %collective-permute-start = (f32[376,128]{1,0:T(8,128)S(1)}, f32[376,128]{1,0:T(8,128)S(1)}, u32[]{:S(2)}, u32[]{:S(2)}) collective-permute-start(f32[376,128]{1,0:T(8,128)S(1)} %get-tuple-element.14), channel_id=1, source_target_pairs={{0,8},{8,0},{16,24},{24,16},{1,9},{9,1},{17,25},{25,17},{2,10},{10... | collective-permute-start | bytes 577544 | tf_op jit(solution)/shard_map/ppermute | solution.py:621
  5.9 8.1 %collective-permute-start.1 = (f32[376,128]{1,0:T(8,128)S(1)}, f32[376,128]{1,0:T(8,128)S(1)}, u32[]{:S(2)}, u32[]{:S(2)}) collective-permute-start(f32[376,128]{1,0:T(8,128)S(1)} %get-tuple-element.15), channel_id=1, source_target_pairs={{0,24},{8,16},{16,8},{24,0},{1,25},{9,17},{17,9},{25,1},{2,26},{10... | collective-permute-start | bytes 577544 | tf_op jit(solution)/shard_map/ppermute | solution.py:620
  8.6 5.4 %collective-permute-start.2 = (f32[8,128]{1,0:T(8,128)S(1)}, f32[8,128]{1,0:T(8,128)S(1)}, u32[]{:S(2)}, u32[]{:S(2)}) collective-permute-start(f32[8,128]{1,0:T(8,128)S(1)} %get-tuple-element.16.drag_ref.extra_ref), channel_id=1, source_target_pairs={{0,16},{8,24},{16,0},{24,8},{1,17},{9,25},{17,1},{25,9},{2,18},{10... | collective-permute-start | bytes 12296 | tf_op jit(solution)/shard_map/ppermute | solution.py:586
  14.7 6.6 %collective-permute-start.3 = (f32[2,192,128]{2,1,0:T(8,128)S(1)}, f32[2,192,128]{2,1,0:T(8,128)S(1)}, u32[]{:S(2)}, u32[]{:S(2)}) collective-permute-start(f32[2,192,128]{2,1,0:T(8,128)S(1)} %shard_map.68.ysent_ref), channel_id=1, source_target_pairs={{0,4},{4,0},{1,5},{5,1},{2,6},{6,2},{3,7},{7,3},{8,12},{12,8},{9,1... | collective-permute-start | bytes 589832 | tf_op jit(solution)/shard_map/ppermute | solution.py:632
  22.5 8.4 %collective-permute-start.5 = (f32[104,128]{1,0:T(8,128)S(1)}, f32[104,128]{1,0:T(8,128)S(1)}, u32[]{:S(2)}, u32[]{:S(2)}) collective-permute-start(f32[104,128]{1,0:T(8,128)S(1)} %get-tuple-element.18.zown_ref), channel_id=1, source_target_pairs={{0,3},{1,2},{2,1},{3,0},{4,7},{5,6},{6,5},{7,4},{8,11},{9,10},{10,... | collective-permute-start | bytes 159752 | tf_op jit(solution)/shard_map/ppermute | solution.py:645
  26.4 4.5 %collective-permute-start.4 = (f32[104,128]{1,0:T(8,128)S(1)}, f32[104,128]{1,0:T(8,128)S(1)}, u32[]{:S(2)}, u32[]{:S(2)}) collective-permute-start(f32[104,128]{1,0:T(8,128)S(1)} %get-tuple-element.18.zown_ref), channel_id=1, source_target_pairs={{0,1},{1,0},{2,3},{3,2},{4,5},{5,4},{6,7},{7,6},{8,9},{9,8},{10,11... | collective-permute-start | bytes 159752 | tf_op jit(solution)/shard_map/ppermute | solution.py:646
  26.4 4.5 %collective-permute-start.6 = (f32[8,128]{1,0:T(8,128)S(1)}, f32[8,128]{1,0:T(8,128)S(1)}, u32[]{:S(2)}, u32[]{:S(2)}) collective-permute-start(f32[8,128]{1,0:T(8,128)S(1)} %get-tuple-element.19), channel_id=1, source_target_pairs={{0,2},{1,3},{2,0},{3,1},{4,6},{5,7},{6,4},{7,5},{8,10},{9,11},{10,... | collective-permute-start | bytes 12296 | tf_op jit(solution)/shard_map/ppermute | solution.py:586

commit v2 on v1

--- a/solution.py
+++ b/solution.py
@@ -43,6 +43,13 @@
 
 
 NSLOT = 23
+CORNER = 24
+
+
+def y_rows(nx):
+    return -(-NSLOT * nx // 8) * 8
+
+
 ZGROUPS = (
     tuple(i for i in range(19) if VEL[i][2] == -1),
     tuple(i for i in range(19) if VEL[i][2] == 1),
@@ -201,13 +208,56 @@
     return f[0], s, d, m, u
 
 
+def corner_rows(sx, sy):
+    rows = []
+    for dx, dy in ((0, 0), (1, 0), (0, 1), (1, 1)):
+        for i in near(0, sx) if dx == 0 else far(0, sx):
+            if i in (near(1, sy) if dy == 0 else far(1, sy)):
+                rows.append((i, dx, dy))
+    return rows
+
+
+def cell_rows(adj_ref, ub_ref, q, x, rows):
+    return adj_ref[q, x, rows, :] if q < 19 else ub_ref[q - 19, x, rows, :]
+
+
 def pack_x_kernel(
-    par_ref, states_ref, adj_ref, por_ref, mask_ref, a_ref, b_ref, ub_ref, drag_ref
+    par_ref,
+    states_hbm,
+    adj_hbm,
+    por_hbm,
+    mask_hbm,
+    a_ref,
+    b_ref,
+    ub_ref,
+    drag_ref,
+    states_ref,
+    adj_ref,
+    por_ref,
+    mask_ref,
+    sems,
 ):
     nx, ny, nz = por_ref.shape
     tiles = ny // 8
-
-    def cells(n, drag):
+    copies = [
+        pltpu.make_async_copy(src, dst, sems.at[k])
+        for k, (src, dst) in enumerate(
+            (
+                (states_hbm.at[1], states_ref.at[1]),
+                (por_hbm, por_ref),
+                (mask_hbm, mask_ref),
+                (states_hbm.at[0, 1:3], states_ref.at[0, 1:3]),
+                (states_hbm.at[0, 7:15], states_ref.at[0, 7:15]),
+                (adj_hbm, adj_ref),
+            )
+        )
+    ]
+    for copy in copies:
+        copy.start()
+    for copy in copies[:5]:
+        copy.wait()
+
+    def cells(n, carry):
         x = n // tiles
         rows = pl.ds(pl.multiple_of((n % tiles) * 8, 8), 8)
         blocking = jnp.where(mask_ref[x, rows, :] == 0, por_ref[x, rows, :], 1.0)
@@ -219,124 +269,95 @@
         for k in range(3):
             ub_ref[k, x, rows, :] = u[k]
         ub_ref[3, x, rows, :] = blocking
-        return drag + blocking * flux
+        return carry + blocking * flux
 
     drag = lax.fori_loop(0, nx * tiles, cells, jnp.zeros((8, nz), jnp.float32))
     drag_ref[...] = drag
-
-    def fill(out_ref, sign):
-        first, second = (0, 1) if sign > 0 else (nx - 1, nx - 2)
-        for k, q in enumerate(near(0, sign)):
-            out_ref[k * ny : (k + 1) * ny] = (
-                adj_ref[q, first] if q < 19 else ub_ref[q - 19, first]
-            )
-        for k, q in enumerate(far(0, sign)):
-            k += 18
-            out_ref[k * ny : (k + 1) * ny] = adj_ref[q, second]
-        out_ref[NSLOT * ny : NSLOT * ny + 8] = drag
-
-    @pl.when(par_ref[0] == 0)
-    def _():
-        fill(a_ref, -1)
-        fill(b_ref, 1)
-
-    @pl.when(par_ref[0] == 1)
-    def _():
-        fill(a_ref, 1)
-        fill(b_ref, -1)
-
-
-def total_of(mode, tiles):
-    if mode == "pair":
-        return tiles[0] + tiles[1]
-    if mode == "four":
-        return (tiles[0] + tiles[1]) + (tiles[2] + tiles[3])
-    return tiles[3]
-
-
-def pack_y_kernel(
-    mode,
+    a_ref[NSLOT * ny :] = drag
+    b_ref[NSLOT * ny :] = drag
+    copies[5].wait()
+
+    def fill_x(out_ref, sign):
+        for names, offset, x in (
+            (near(0, sign), 0, 0 if sign > 0 else nx - 1),
+            (far(0, sign), 18, 1 if sign > 0 else nx - 2),
+        ):
+            for k, q in enumerate(names):
+                k += offset
+                out_ref[k * ny : (k + 1) * ny] = cell_rows(
+                    adj_ref, ub_ref, q, x, slice(0, ny)
+                )
+
+    for px in (0, 1):
+
+        @pl.when(par_ref[0] == px)
+        def _():
+            sa = 1 if px else -1
+            fill_x(a_ref, sa)
+            fill_x(b_ref, -sa)
+
+
+def pack_y_kernel(par_ref, adj_ref, ub_ref, drag_ref, y_ref, ya_ref, yb_ref):
+    nx, ny, nz = adj_ref.shape[1:]
+
+    def fill_y(place, sign):
+        for names, offset, y in (
+            (near(1, sign), 0, 0 if sign > 0 else ny - 1),
+            (far(1, sign), 18, 1 if sign > 0 else ny - 2),
+        ):
+            for k, q in enumerate(names):
+                for x in range(nx):
+                    row = place * y_rows(nx) + (k + offset) * nx + x
+                    y_ref[row : row + 1] = cell_rows(
+                        adj_ref, ub_ref, q, x, slice(y, y + 1)
+                    )
+
+    def fill_corner(out_ref, place, sx, sy):
+        names = corner_rows(sx, sy)
+        for k, (q, dx, dy) in enumerate(names):
+            x = dx if sx > 0 else nx - 1 - dx
+            y = dy if sy > 0 else ny - 1 - dy
+            row = place * CORNER + k
+            out_ref[row : row + 1] = cell_rows(adj_ref, ub_ref, q, x, slice(y, y + 1))
+        row = place * CORNER + len(names)
+        out_ref[row : (place + 1) * CORNER] = jnp.zeros(
+            ((place + 1) * CORNER - row, nz), jnp.float32
+        )
+
+    drag = drag_ref[...]
+    y_ref[2 * y_rows(nx) :] = drag
+    ya_ref[2 * CORNER :] = drag
+    yb_ref[2 * CORNER :] = drag
+    for py in (0, 1):
+
+        @pl.when(par_ref[1] == py)
+        def _():
+            s0 = 1 if py else -1
+            fill_y(0, s0)
+            fill_y(1, -s0)
+
+    for px in (0, 1):
+        for py in (0, 1):
+
+            @pl.when((par_ref[0] == px) & (par_ref[1] == py))
+            def _():
+                sa = 1 if px else -1
+                s0 = 1 if py else -1
+                for out_ref, sx in ((ya_ref, sa), (yb_ref, -sa)):
+                    fill_corner(out_ref, 0, sx, s0)
+                    fill_corner(out_ref, 1, sx, -s0)
+
+
+def pack_z_kernel(
     par_ref,
     adj_ref,
     ub_ref,
     xa_ref,
     xb_ref,
-    drag_ref,
-    extra_ref,
-    out_ref,
-):
-    nx, ny = adj_ref.shape[1:3]
-    even = par_ref[0] == 0
-    row_sets = {
-        1: (near(1, 1), 0, far(1, 1), 1),
-        -1: (near(1, -1), ny - 1, far(1, -1), ny - 2),
-    }
-
-    def fill(place, sign):
-        first_q, first_row, second_q, second_row = row_sets[sign]
-        entries = [(q, first_row) for q in first_q] + [(q, second_row) for q in second_q]
-        for k, (q, row) in enumerate(entries):
-            where = slice(k * 8, k * 8 + 8)
-            rows = []
-            for s in range(nx + 4):
-                if 2 <= s < nx + 2:
-                    rows.append(
-                        adj_ref[q, s - 2, row : row + 1, :]
-                        if q < 19
-                        else ub_ref[q - 19, s - 2, row : row + 1, :]
-                    )
-                    continue
-                side = -1 if s < 2 else 1
-                if s in (1, nx + 2):
-                    names, offset = near(0, side), 0
-                else:
-                    names, offset = far(0, side), 18
-                if q in names:
-                    start = (names.index(q) + offset) * ny + row
-                    va = xa_ref[start : start + 1, :]
-                    vb = xb_ref[start : start + 1, :]
-                    rows.append(
-                        jnp.where(even, va, vb) if side > 0 else jnp.where(even, vb, va)
-                    )
-                else:
-                    rows.append(None)
-            for s, value in enumerate(rows):
-                if value is not None:
-                    out_ref[place, k * 8 + s : k * 8 + s + 1, :] = value
-                else:
-                    out_ref[place, k * 8 + s : k * 8 + s + 1, :] = jnp.zeros(
-                        (1, out_ref.shape[2]), jnp.float32
-                    )
-
-    @pl.when(par_ref[1] == 0)
-    def _():
-        fill(0, -1)
-        fill(1, 1)
-
-    @pl.when(par_ref[1] == 1)
-    def _():
-        fill(0, 1)
-        fill(1, -1)
-
-    last = slice(NSLOT * ny, NSLOT * ny + 8)
-    drag = total_of(
-        mode, (drag_ref[...], xa_ref[last], xb_ref[last], extra_ref[...])
-    )
-    out_ref[0, NSLOT * 8 : NSLOT * 8 + 8, :] = drag
-    out_ref[1, NSLOT * 8 : NSLOT * 8 + 8, :] = drag
-
-
-def pack_z_kernel(
-    mode,
-    par_ref,
-    adj_ref,
-    ub_ref,
-    xa_ref,
-    xb_ref,
+    y_ref,
     ya_ref,
     yb_ref,
-    ysent_ref,
-    extra_ref,
+    own_ref,
     read_ref,
     zmsg_ref,
     drag_ref,
@@ -347,33 +368,46 @@
     even_y = par_ref[1] == 0
     base = 16
 
-    def copy(q, carry):
-        return carry
-
     for q in range(NSLOT):
         for x in range(nx):
             ext[q, x + 2, base : base + ny, :] = (
                 adj_ref[q, x] if q < 19 else ub_ref[q - 19, x]
             )
+    planes = {1: (nx + 2, nx + 3), -1: (1, 0)}
+    lines = {1: (base + ny, base + ny + 1), -1: (base - 1, base - 2)}
     for sign in (1, -1):
-        one, two = (nx + 2, nx + 3) if sign > 0 else (1, 0)
-        for names, plane, offset in ((near(0, sign), one, 0), (far(0, sign), two, 18)):
+        first, second = (xa_ref, xb_ref) if sign > 0 else (xb_ref, xa_ref)
+        for names, depth, offset in ((near(0, sign), 0, 0), (far(0, sign), 1, 18)):
             for k, q in enumerate(names):
                 rows = slice((k + offset) * ny, (k + offset + 1) * ny)
-                first, second = (xa_ref, xb_ref) if sign > 0 else (xb_ref, xa_ref)
-                ext[q, plane, base : base + ny, :] = jnp.where(
+                ext[q, planes[sign][depth], base : base + ny, :] = jnp.where(
                     even_x, first[rows], second[rows]
                 )
-        one, two = (base + ny, base + ny + 1) if sign > 0 else (base - 1, base - 2)
-        first, second = (ya_ref, yb_ref) if sign > 0 else (yb_ref, ya_ref)
-        for names, row, offset in ((near(1, sign), one, 0), (far(1, sign), two, 18)):
+        block = y_rows(nx)
+        first, second = (0, block) if sign > 0 else (block, 0)
+        per = 8 // nx if nx < 8 else 1
+        for names, depth, offset in ((near(1, sign), 0, 0), (far(1, sign), 1, 18)):
+            line = lines[sign][depth]
             for k, q in enumerate(names):
-                start = (k + offset) * 8
-                tile = jnp.where(
-                    even_y, first[start : start + 8], second[start : start + 8]
+                row = (k + offset) * nx
+                got = jnp.where(
+                    even_y,
+                    y_ref[first + row : first + row + nx],
+                    y_ref[second + row : second + row + nx],
                 )
-                for s in range(nx + 4):
-                    ext[q, s, row : row + 1, :] = tile[s : s + 1]
+                for x in range(nx):
+                    ext[q, x + 2, line : line + 1, :] = got[x : x + 1]
+        for sx in (1, -1):
+            xs = (ya_ref, yb_ref) if sx > 0 else (yb_ref, ya_ref)
+            ys = (0, CORNER) if sign > 0 else (CORNER, 0)
+            low, high = [
+                jnp.where(even_x, xs[0][r : r + CORNER], xs[1][r : r + CORNER])
+                for r in ys
+            ]
+            got = jnp.where(even_y, low, high)
+            for k, (q, dx, dy) in enumerate(corner_rows(sx, sign)):
+                line = lines[sign][dy]
+                ext[q, planes[sx][dx], line : line + 1, :] = got[k : k + 1]
 
     lane = lax.broadcasted_iota(jnp.int32, (8, nz), 1)
     sub = lax.broadcasted_iota(jnp.int32, (8, nz), 0)
@@ -406,16 +440,18 @@
         for t in range(tiles + 1):
             row = (g * (tiles + 1) + t) * 8
             zmsg_ref[row : row + 8, :] = acc[t]
-    last = slice(NSLOT * 8, NSLOT * 8 + 8)
-    drag = total_of(mode, (ysent_ref[0, last, :], ya_ref[last], yb_ref[last], extra_ref[...]))
-    drag_ref[...] = drag
+    drags = [
+        own_ref[...] + y_ref[2 * y_rows(nx) :],
+        xa_ref[NSLOT * ny :] + ya_ref[2 * CORNER :],
+        xb_ref[NSLOT * ny :] + yb_ref[2 * CORNER :],
+    ]
     row = 4 * (tiles + 1) * 8
-    zmsg_ref[row : row + 8, :] = drag
+    for k, drag in enumerate(drags):
+        drag_ref[8 * k : 8 * k + 8, :] = drag
+        zmsg_ref[row + 8 * k : row + 8 * k + 8, :] = drag
 
 
 def levels_kernel(
-    mode,
-    whole_cells,
     par_ref,
     states_ref,
     mask_ref,
@@ -423,10 +459,8 @@
     zown_ref,
     za_ref,
     zb_ref,
-    extra_ref,
     out_ref,
     grad_ref,
-    drag_ref,
     lo_ref,
     hi_ref,
     slab_ref,
@@ -455,11 +489,6 @@
             slab_ref[rows] = jnp.where(
                 side == 0, own if g == 1 else low, own if g == 0 else high
             )
-
-    last = slice(4 * height, 4 * height + 8)
-    drag = total_of(mode, (zown_ref[last], za_ref[last], zb_ref[last], extra_ref[...]))
-    summed = jnp.sum(jnp.sum(drag, axis=1, keepdims=True), axis=0, keepdims=True)
-    drag_ref[...] = summed / whole_cells
 
     def rolled(value, shift):
         return pltpu.roll(value, lax.rem(shift + 2 * nz, nz), 1)
@@ -579,87 +608,115 @@
     return first, second
 
 
-def drag_extra(tile, axis, count):
-    if count == 2:
-        return "pair", tile
-    if count == 4:
-        return "four", lax.ppermute(tile, axis, [(i, (i + 2) % 4) for i in range(4)])
-    return "whole", lax.psum(tile, axis)
-
-
 VMEM = pl.BlockSpec(memory_space=pltpu.VMEM)
 SMEM = pl.BlockSpec(memory_space=pltpu.SMEM)
+HBM = pl.BlockSpec(memory_space=pltpu.HBM)
 PARAMS = pltpu.CompilerParams(vmem_limit_bytes=48 * 2**20)
 
 
-def call(kernel, inputs, shapes, scratch=()):
+def call(kernel, inputs, shapes, scratch=(), space=VMEM, micros=1):
+    if space is HBM:
+        inputs = inputs[:1] + tuple(
+            pltpu.with_memory_space_constraint(x, pltpu.HBM) for x in inputs[1:]
+        )
     return pl.pallas_call(
         kernel,
         out_shape=[jax.ShapeDtypeStruct(s, jnp.float32) for s in shapes],
-        in_specs=[SMEM] + [VMEM] * (len(inputs) - 1),
+        in_specs=[SMEM] + [space] * (len(inputs) - 1),
         out_specs=[VMEM] * len(shapes),
-        scratch_shapes=[pltpu.VMEM(s, jnp.float32) for s in scratch],
+        scratch_shapes=list(scratch),
         compiler_params=PARAMS,
+        cost_estimate=pl.CostEstimate(
+            flops=0, bytes_accessed=int(3.6e6 * micros), transcendentals=0
+        ),
     )(*inputs)
 
 
 def body(primal_states, adjoint_last, porosity, solid_mask):
     nx, ny, nz = porosity.shape
-    counts = [lax.axis_size(axis) for axis in AXES]
-    pairings = [swaps(count) for count in counts]
+    gx, gy, gz = [lax.axis_size(axis) for axis in AXES]
+    x_first, x_second = swaps(gx)
+    y_first, y_second = swaps(gy)
+    z_first, z_second = swaps(gz)
     parity = jnp.stack([lax.axis_index(axis) & 1 for axis in AXES]).astype(jnp.int32)
     tiles = ny // 8
     height = (tiles + 1) * 8
+    f32 = jnp.float32
+
+    def diagonal(message, x_pairs, y_pairs):
+        pairs = [(a * gy + c, b * gy + d) for a, b in x_pairs for c, d in y_pairs]
+        return lax.ppermute(message, ("gx", "gy"), pairs)
 
     rows_x = NSLOT * ny + 8
+    rows_y = 2 * y_rows(nx) + 8
+    rows_c = 2 * CORNER + 8
     xa, xb, ub, drag = call(
         pack_x_kernel,
         (parity, primal_states, adjoint_last, porosity, solid_mask),
         [(rows_x, nz), (rows_x, nz), (4, nx, ny, nz), (8, nz)],
-    )
-    xb = lax.ppermute(xb, "gx", pairings[0][1])
-    xa = lax.ppermute(xa, "gx", pairings[0][0])
-    mode, extra = drag_extra(drag, "gx", counts[0])
-
-    rows_y = NSLOT * 8 + 8
-    (ysent,) = call(
-        functools.partial(pack_y_kernel, mode),
-        (parity, adjoint_last, ub, xa, xb, drag, extra),
-        [(2, rows_y, nz)],
-    )
-    drag_y = ysent[0, NSLOT * 8 :] if counts[1] > 2 else drag
-    if counts[1] == 2:
-        ygot = lax.ppermute(ysent, "gy", pairings[1][0])
-        ya, yb = ygot[0], ygot[1]
+        [
+            pltpu.VMEM((2, 19, nx, ny, nz), f32),
+            pltpu.VMEM((19, nx, ny, nz), f32),
+            pltpu.VMEM((nx, ny, nz), f32),
+            pltpu.VMEM((nx, ny, nz), jnp.int32),
+            pltpu.SemaphoreType.DMA((6,)),
+        ],
+        HBM,
+    )
+    y, ya, yb = call(
+        pack_y_kernel,
+        (parity, adjoint_last, ub, drag),
+        [(rows_y, nz), (rows_c, nz), (rows_c, nz)],
+        micros=4,
+    )
+    xb = lax.ppermute(xb, "gx", x_second)
+    if gy == 2:
+        y = lax.ppermute(y, "gy", y_first)
+        yb = diagonal(yb, x_second, y_first)
+        ya = diagonal(ya, x_first, y_first)
     else:
-        ya = lax.ppermute(ysent[0], "gy", pairings[1][0])
-        yb = lax.ppermute(ysent[1], "gy", pairings[1][1])
-    mode, extra = drag_extra(drag_y, "gy", counts[1])
-
-    read, zmsg, drag = call(
-        functools.partial(pack_z_kernel, mode),
-        (parity, adjoint_last, ub, xa, xb, ya, yb, ysent, extra),
-        [(NSLOT, nx + 2, height, nz), (4 * height + 8, nz), (8, nz)],
-        [(NSLOT, nx + 4, ny + 32, nz)],
-    )
-    zb = lax.ppermute(zmsg, "gz", pairings[2][1])
-    za = lax.ppermute(zmsg, "gz", pairings[2][0])
-    mode, extra = drag_extra(drag, "gz", counts[2])
-    whole_cells = nx * ny * nz * counts[0] * counts[1] * counts[2]
-
-    first, gradient, total = call(
-        functools.partial(levels_kernel, mode, float(whole_cells)),
-        (parity, primal_states, solid_mask, read, zmsg, za, zb, extra),
-        [(19, nx, ny, nz), (nx, ny, nz), (1, 1)],
+
+        def both(message, block, send):
+            parts = [message[:block], message[block : 2 * block], message[2 * block :]]
+            return jnp.concatenate(
+                [send(parts[0], y_first), send(parts[1], y_second), parts[2]]
+            )
+
+        y = both(y, y_rows(nx), lambda m, pairs: lax.ppermute(m, "gy", pairs))
+        yb = both(yb, CORNER, lambda m, pairs: diagonal(m, x_second, pairs))
+        ya = both(ya, CORNER, lambda m, pairs: diagonal(m, x_first, pairs))
+    xa = lax.ppermute(xa, "gx", x_first)
+
+    read, zmsg, drags = call(
+        pack_z_kernel,
+        (parity, adjoint_last, ub, xa, xb, y, ya, yb, drag),
+        [(NSLOT, nx + 2, height, nz), (4 * height + 24, nz), (24, nz)],
+        [pltpu.VMEM((NSLOT, nx + 4, ny + 32, nz), f32)],
+    )
+    zb = lax.ppermute(zmsg, "gz", z_second)
+    za = lax.ppermute(zmsg, "gz", z_first)
+    if (gx, gy, gz) == (4, 2, 4):
+        across = lax.ppermute(drags, "gz", [(i, i ^ 2) for i in range(gz)])
+        drags = (drags + across) + (za[4 * height :] + zb[4 * height :])
+        fourth = lax.ppermute(drags[16:], "gx", x_first)
+        drag = jnp.sum(drags[:8] + drags[8:16] + drags[16:] + fourth)
+    else:
+        drag = lax.psum(jnp.sum(drag), AXES)
+
+    first, gradient = call(
+        levels_kernel,
+        (parity, primal_states, solid_mask, read, zmsg, za, zb),
+        [(19, nx, ny, nz), (nx, ny, nz)],
         [
-            (4 * height, nz),
-            (4 * height, nz),
-            (4 * height, nz),
-            (19, nx + 2, height + 8, nz),
-            (10, height + 8, nz),
+            pltpu.VMEM((4 * height, nz), f32),
+            pltpu.VMEM((4 * height, nz), f32),
+            pltpu.VMEM((4 * height, nz), f32),
+            pltpu.VMEM((19, nx + 2, height + 8, nz), f32),
+            pltpu.VMEM((10, height + 8, nz), f32),
         ],
-    )
-    return (first, gradient, total.reshape(()))
+        micros=4,
+    )
+    return (first, gradient, drag / (nx * ny * nz * gx * gy * gz))
 
 
 def solution(mesh):

time: 36.3 us -> 30.3 us (0.83)
  waiting for transfers between devices: 14.1 us -> 7.34 us
  local copies, waits for them, and re-layouts: 3.91 us -> 0.02 us
  between operations: 0.69 us -> 2.49 us
  starting transfers between devices: 9.5 us -> 10.7 us
  Pallas kernels: 7.7 us -> 8.87 us
  other arithmetic: 0.08 us -> 0.68 us
    ppermute x7 -> x9, waiting for transfers between devices: 14.1 us -> 7.34 us  [the longest x1 4.49 us: body(): across = lax.ppermute(drags, 'gz', [(i, i ^ 2) for i in range(gz)])]
    unnamed x12 -> x6, local copies, waits for them, and re-layouts: 3.89 us -> 0.01 us
    ppermute x7 -> x9, starting transfers between devices: 9.5 us -> 10.7 us  [the longest x1 2.61 us: body(): xb = lax.ppermute(xb, 'gx', x_second)]
    pallas_call x4, Pallas kernels: 7.7 us -> 8.87 us  [call(): pl.pallas_call(kernel, out_shape=[jax.ShapeDtypeStruct(s, jnp.float32) fo...]
    reduce_sum x0 -> x1, other arithmetic: none -> 0.6 us  [body(): drag = jnp.sum(drags[:8] + drags[8:16] + drags[16:] + fourth)]
  transfers between devices with their start and end apart: 7 -> 9, of which waited for: 3 -> 3; matrix products, arithmetic and copies ran while one was open for 0% -> 0% of each run, Pallas kernels for 0% -> 19%
where the time goes in v2:
time: 30.3 us; the launch traced here: 30.1 us
  starting transfers between devices  10.7 us (35%)
  Pallas kernels  8.87 us (29%)
  waiting for transfers between devices  7.34 us (24%)
  between operations  2.49 us (8%)
  other arithmetic  0.68 us (2%)
    pallas_call x4, Pallas kernels, call(): pl.pallas_call(kernel, out_shape=[jax.ShapeDtypeStruct(s, jnp.float32) fo...  8.87 us
    ppermute x1, waiting for transfers between devices, body(): across = lax.ppermute(drags, 'gz', [(i, i ^ 2) for i in range(gz)])  4.49 us
    ppermute x2, waiting for transfers between devices, diagonal(): return lax.ppermute(message, ('gx', 'gy'), pairs)  2.84 us
    ppermute x1, starting transfers between devices, body(): xb = lax.ppermute(xb, 'gx', x_second)  2.61 us
    ppermute x1, starting transfers between devices, body(): zb = lax.ppermute(zmsg, 'gz', z_second)  2.47 us
    ppermute x2, starting transfers between devices, diagonal(): return lax.ppermute(message, ('gx', 'gy'), pairs)  1.72 us
    ppermute x1, starting transfers between devices, body(): za = lax.ppermute(zmsg, 'gz', z_first)  1.64 us
    ppermute x1, starting transfers between devices, body(): y = lax.ppermute(y, 'gy', y_first)  1.58 us
  transfers between devices with their start and end apart: 9, of which 3 were waited for; matrix products, arithmetic and copies ran while one was open for 0% of the time, Pallas kernels for 19%

profile of v2, /device:TPU:0, one launch (start us, length us, event | category | flops | bytes accessed | tf_op | source)
XLA Modules:
  0.0 30.1 jit_solution(2998932884034912030)
XLA Ops:
  0.6 0.0 copy-start
  0.6 0.1 pad_add_fusion.par_ref
  0.7 2.0 %shard_map.67 = (f32[376,128]{1,0:T(8,128)S(1)}, f32[376,128]{1,0:T(8,128)S(1)}, f32[4,4,16,128]{3,2,1,0:T(8,128)S(1)}, f32[8,128]{1,0:T(8,128)S(1)}) custom-call(s32[3]{0:T(128)S(1)} %pad_add_fusion.par_ref, f32[2,19,4,16,128]{4,3,2,1,0:T(8,128)} %states_ref.1, f32[19,4,16,128]{3,2,1,0:T(8,128)} %adj_ref.3, f32[4,16,128]{2,1,0:T(8,128)} %por_hbm.1, ...), custom_call_target="tpu_custom_call" | custom-call | bytes 3600000 | tf_op jit(solution)/shard_map/pallas_call | solution.py:622
  2.8 0.5 %collective-permute-start = (f32[376,128]{1,0:T(8,128)S(1)}, f32[376,128]{1,0:T(8,128)S(1)}, u32[]{:S(2)}, u32[]{:S(2)}) collective-permute-start(f32[376,128]{1,0:T(8,128)S(1)} %get-tuple-element.16), channel_id=1, source_target_pairs={{0,8},{8,0},{16,24},{24,16},{1,9},{9,1},{17,25},{25,17},{2,10},{10... | collective-permute-start | bytes 577544 | tf_op jit(solution)/shard_map/ppermute | solution.py:688
  3.3 2.6 %collective-permute-start.1 = (f32[376,128]{1,0:T(8,128)S(1)}, f32[376,128]{1,0:T(8,128)S(1)}, u32[]{:S(2)}, u32[]{:S(2)}) collective-permute-start(f32[376,128]{1,0:T(8,128)S(1)} %get-tuple-element.17), channel_id=1, source_target_pairs={{0,24},{8,16},{16,8},{24,0},{1,25},{9,17},{17,9},{25,1},{2,26},{10... | collective-permute-start | bytes 577544 | tf_op jit(solution)/shard_map/ppermute | solution.py:672
  5.9 0.7 %shard_map.68 = (f32[200,128]{1,0:T(8,128)S(1)}, f32[56,128]{1,0:T(8,128)S(1)}, f32[56,128]{1,0:T(8,128)S(1)}) custom-call(s32[3]{0:T(128)S(1)} %pad_add_fusion.par_ref, f32[19,4,16,128]{3,2,1,0:T(8,128)S(1)} %copy-done, f32[4,4,16,128]{3,2,1,0:T(8,128)S(1)} %get-tuple-element.15.ub_ref, f32[8,128]{1,0:T(8,128)S(1)} %get-tuple-element.18.drag_ref.own_ref), custom_call_target="tpu_custom_call" | custom-call | bytes 14400000 | tf_op jit(solution)/shard_map/pallas_call | solution.py:622
  6.6 1.6 %collective-permute-start.2 = (f32[200,128]{1,0:T(8,128)S(1)}, f32[200,128]{1,0:T(8,128)S(1)}, u32[]{:S(2)}, u32[]{:S(2)}) collective-permute-start(f32[200,128]{1,0:T(8,128)S(1)} %get-tuple-element.19), channel_id=1, source_target_pairs={{0,4},{4,0},{1,5},{5,1},{2,6},{6,2},{3,7},{7,3},{8,12},{12,8},{9,1... | collective-permute-start | bytes 307208 | tf_op jit(solution)/shard_map/ppermute | solution.py:674
  8.2 0.0 collective-permute-start.3
  8.2 1.7 %collective-permute-start.4 = (f32[56,128]{1,0:T(8,128)S(1)}, f32[56,128]{1,0:T(8,128)S(1)}, u32[]{:S(2)}, u32[]{:S(2)}) collective-permute-start(f32[56,128]{1,0:T(8,128)S(1)} %get-tuple-element.21), channel_id=1, source_target_pairs={{0,28},{4,24},{8,20},{12,16},{16,12},{20,8},{24,4},{28,0},{1,29},{... | collective-permute-start | bytes 86024 | tf_op jit(solution)/shard_map/ppermute | solution.py:648
  9.9 1.9 %collective-permute-done.3.ya_ref = f32[56,128]{1,0:T(8,128)S(1)} collective-permute-done((f32[56,128]{1,0:T(8,128)S(1)}, f32[56,128]{1,0:T(8,128)S(1)}, u32[]{:S(2)}, u32[]{:S(2)}) %collective-permute-start.3) | collective-permute-done | bytes 28704 | tf_op jit(solution)/shard_map/ppermute | solution.py:648
  11.8 1.0 %collective-permute-done.4.yb_ref = f32[56,128]{1,0:T(8,128)S(1)} collective-permute-done((f32[56,128]{1,0:T(8,128)S(1)}, f32[56,128]{1,0:T(8,128)S(1)}, u32[]{:S(2)}, u32[]{:S(2)}) %collective-permute-start.4) | collective-permute-done | bytes 28704 | tf_op jit(solution)/shard_map/ppermute | solution.py:648
  12.7 0.0 collective-permute-done.2.y_ref
  12.7 0.0 collective-permute-done.xa_ref
  12.8 0.0 collective-permute-done.1.xb_ref
  12.8 1.2 %shard_map.69 = (f32[23,6,24,128]{3,2,1,0:T(8,128)S(1)}, f32[120,128]{1,0:T(8,128)S(1)}, f32[24,128]{1,0:T(8,128)S(1)}) custom-call(s32[3]{0:T(128)S(1)} %pad_add_fusion.par_ref, f32[19,4,16,128]{3,2,1,0:T(8,128)S(1)} %copy-done, f32[4,4,16,128]{3,2,1,0:T(8,128)S(1)} %get-tuple-element.15.ub_ref, f32[376,128]{1,0:T(8,128)S(1)} %collective-permute-done.xa_ref, ...), custom_call_target="tpu_custom_call" | custom-call | bytes 3600000 | tf_op jit(solution)/shard_map/pallas_call | solution.py:622
  13.9 1.6 %collective-permute-start.5 = (f32[120,128]{1,0:T(8,128)S(1)}, f32[120,128]{1,0:T(8,128)S(1)}, u32[]{:S(2)}, u32[]{:S(2)}) collective-permute-start(f32[120,128]{1,0:T(8,128)S(1)} %get-tuple-element.23.zown_ref), channel_id=1, source_target_pairs={{0,1},{1,0},{2,3},{3,2},{4,5},{5,4},{6,7},{7,6},{8,9},{9,8},{10,11... | collective-permute-start | bytes 184328 | tf_op jit(solution)/shard_map/ppermute | solution.py:697
  15.6 2.5 %collective-permute-start.6 = (f32[120,128]{1,0:T(8,128)S(1)}, f32[120,128]{1,0:T(8,128)S(1)}, u32[]{:S(2)}, u32[]{:S(2)}) collective-permute-start(f32[120,128]{1,0:T(8,128)S(1)} %get-tuple-element.23.zown_ref), channel_id=1, source_target_pairs={{0,3},{1,2},{2,1},{3,0},{4,7},{5,6},{6,5},{7,4},{8,11},{9,10},{10,... | collective-permute-start | bytes 184328 | tf_op jit(solution)/shard_map/ppermute | solution.py:696
  18.1 0.1 collective-permute-start.7
  18.2 4.5 %collective-permute-done.7 = f32[24,128]{1,0:T(8,128)S(1)} collective-permute-done((f32[24,128]{1,0:T(8,128)S(1)}, f32[24,128]{1,0:T(8,128)S(1)}, u32[]{:S(2)}, u32[]{:S(2)}) %collective-permute-start.7) | collective-permute-done | bytes 12320 | tf_op jit(solution)/shard_map/ppermute | solution.py:699
  22.7 0.0 collective-permute-done.5.za_ref
  22.7 0.0 collective-permute-done.6.zb_ref
  22.7 0.1 collective-permute-start.8
  22.8 5.0 %shard_map.70 = (f32[19,4,16,128]{3,2,1,0:T(8,128)}, f32[4,16,128]{2,1,0:T(8,128)}) custom-call(s32[3]{0:T(128)S(1)} %pad_add_fusion.par_ref, f32[2,19,4,16,128]{4,3,2,1,0:T(8,128)S(1)} %copy-done.1, s32[4,16,128]{2,1,0:T(8,128)S(1)} %copy-done.2, f32[23,6,24,128]{3,2,1,0:T(8,128)S(1)} %get-tuple-element.22.read_ref, ...), custom_call_target="tpu_custom_call" | custom-call | bytes 14400000 | tf_op jit(solution)/shard_map/pallas_call | solution.py:622
  27.8 0.6 %fusion.3 = f32[]{:T(128)} fusion(f32[8,128]{1,0:T(8,128)S(1)} %collective-permute-done.8, f32[24,128]{1,0:T(8,128)S(1)} %fusion), kind=kLoop, calls=%fused_computation.5 | loop fusion | flops 4095 | bytes 16388 | tf_op jit(solution)/shard_map/reduce_sum | solution.py:702
  (8 shorter events, 0.0 us)
Async XLA Ops:
  0.6 5.3 %copy-start = (f32[19,4,16,128]{3,2,1,0:T(8,128)S(1)}, f32[19,4,16,128]{3,2,1,0:T(8,128)}, u32[]{:S(2)}) copy-start(f32[19,4,16,128]{3,2,1,0:T(8,128)} %adj_ref.3) | copy-start | bytes 1867780
  0.7 22.0 %copy-start.1 = (f32[2,19,4,16,128]{4,3,2,1,0:T(8,128)S(1)}, f32[2,19,4,16,128]{4,3,2,1,0:T(8,128)}, u32[]{:S(2)}) copy-start(f32[2,19,4,16,128]{4,3,2,1,0:T(8,128)} %states_ref.1) | copy-start | bytes 3735556
  0.7 22.1 %copy-start.2 = (s32[4,16,128]{2,1,0:T(8,128)S(1)}, s32[4,16,128]{2,1,0:T(8,128)}, u32[]{:S(2)}) copy-start(s32[4,16,128]{2,1,0:T(8,128)} %mask_ref.1) | copy-start | bytes 98308
  2.8 10.0 %collective-permute-start = (f32[376,128]{1,0:T(8,128)S(1)}, f32[376,128]{1,0:T(8,128)S(1)}, u32[]{:S(2)}, u32[]{:S(2)}) collective-permute-start(f32[376,128]{1,0:T(8,128)S(1)} %get-tuple-element.16), channel_id=1, source_target_pairs={{0,8},{8,0},{16,24},{24,16},{1,9},{9,1},{17,25},{25,17},{2,10},{10... | collective-permute-start | bytes 577544 | tf_op jit(solution)/shard_map/ppermute | solution.py:688
  3.3 9.5 %collective-permute-start.1 = (f32[376,128]{1,0:T(8,128)S(1)}, f32[376,128]{1,0:T(8,128)S(1)}, u32[]{:S(2)}, u32[]{:S(2)}) collective-permute-start(f32[376,128]{1,0:T(8,128)S(1)} %get-tuple-element.17), channel_id=1, source_target_pairs={{0,24},{8,16},{16,8},{24,0},{1,25},{9,17},{17,9},{25,1},{2,26},{10... | collective-permute-start | bytes 577544 | tf_op jit(solution)/shard_map/ppermute | solution.py:672
  6.6 6.1 %collective-permute-start.2 = (f32[200,128]{1,0:T(8,128)S(1)}, f32[200,128]{1,0:T(8,128)S(1)}, u32[]{:S(2)}, u32[]{:S(2)}) collective-permute-start(f32[200,128]{1,0:T(8,128)S(1)} %get-tuple-element.19), channel_id=1, source_target_pairs={{0,4},{4,0},{1,5},{5,1},{2,6},{6,2},{3,7},{7,3},{8,12},{12,8},{9,1... | collective-permute-start | bytes 307208 | tf_op jit(solution)/shard_map/ppermute | solution.py:674
  8.2 3.6 %collective-permute-start.3 = (f32[56,128]{1,0:T(8,128)S(1)}, f32[56,128]{1,0:T(8,128)S(1)}, u32[]{:S(2)}, u32[]{:S(2)}) collective-permute-start(f32[56,128]{1,0:T(8,128)S(1)} %get-tuple-element.20), channel_id=1, source_target_pairs={{0,12},{4,8},{8,4},{12,0},{16,28},{20,24},{24,20},{28,16},{1,13},{... | collective-permute-start | bytes 86024 | tf_op jit(solution)/shard_map/ppermute | solution.py:648
  8.2 4.6 %collective-permute-start.4 = (f32[56,128]{1,0:T(8,128)S(1)}, f32[56,128]{1,0:T(8,128)S(1)}, u32[]{:S(2)}, u32[]{:S(2)}) collective-permute-start(f32[56,128]{1,0:T(8,128)S(1)} %get-tuple-element.21), channel_id=1, source_target_pairs={{0,28},{4,24},{8,20},{12,16},{16,12},{20,8},{24,4},{28,0},{1,29},{... | collective-permute-start | bytes 86024 | tf_op jit(solution)/shard_map/ppermute | solution.py:648
  13.9 8.7 %collective-permute-start.5 = (f32[120,128]{1,0:T(8,128)S(1)}, f32[120,128]{1,0:T(8,128)S(1)}, u32[]{:S(2)}, u32[]{:S(2)}) collective-permute-start(f32[120,128]{1,0:T(8,128)S(1)} %get-tuple-element.23.zown_ref), channel_id=1, source_target_pairs={{0,1},{1,0},{2,3},{3,2},{4,5},{5,4},{6,7},{7,6},{8,9},{9,8},{10,11... | collective-permute-start | bytes 184328 | tf_op jit(solution)/shard_map/ppermute | solution.py:697
  15.6 7.1 %collective-permute-start.6 = (f32[120,128]{1,0:T(8,128)S(1)}, f32[120,128]{1,0:T(8,128)S(1)}, u32[]{:S(2)}, u32[]{:S(2)}) collective-permute-start(f32[120,128]{1,0:T(8,128)S(1)} %get-tuple-element.23.zown_ref), channel_id=1, source_target_pairs={{0,3},{1,2},{2,1},{3,0},{4,7},{5,6},{6,5},{7,4},{8,11},{9,10},{10,... | collective-permute-start | bytes 184328 | tf_op jit(solution)/shard_map/ppermute | solution.py:696
  18.1 4.6 %collective-permute-start.7 = (f32[24,128]{1,0:T(8,128)S(1)}, f32[24,128]{1,0:T(8,128)S(1)}, u32[]{:S(2)}, u32[]{:S(2)}) collective-permute-start(f32[24,128]{1,0:T(8,128)S(1)} %get-tuple-element.26), channel_id=1, source_target_pairs={{0,2},{1,3},{2,0},{3,1},{4,6},{5,7},{6,4},{7,5},{8,10},{9,11},{10,... | collective-permute-start | bytes 36872 | tf_op jit(solution)/shard_map/ppermute | solution.py:699
  22.7 5.1 %collective-permute-start.8 = (f32[8,128]{1,0:T(8,128)S(1)}, f32[8,128]{1,0:T(8,128)S(1)}, u32[]{:S(2)}, u32[]{:S(2)}) collective-permute-start(f32[8,128]{1,0:T(8,128)S(1)} %slice.25), channel_id=1, source_target_pairs={{0,8},{8,0},{16,24},{24,16},{1,9},{9,1},{17,25},{25,17},{2,10},{10... | collective-permute-start | bytes 12296 | tf_op jit(solution)/shard_map/ppermute | solution.py:701

commit v3 on v2

--- a/solution.py
+++ b/solution.py
@@ -419,7 +419,7 @@
             cx, cy, cz = VEL[q] if q < 19 else (0, 0, 0)
             for p in range(nx + 2):
                 plane = p + 1 + cx
-                start = 16 * k + 2 * p
+                start = 32 * (k // 2) + 4 * p + 2 * (k % 2)
                 mask = pair == start // 2
                 for t in range(tiles + 1):
                     if t < tiles:
@@ -451,30 +451,136 @@
         zmsg_ref[row + 8 * k : row + 8 * k + 8, :] = drag
 
 
-def levels_kernel(
+def pack_state_kernel(states_ref, ub_ref, f0_ref, f1_ref):
+    nx, ny, nz = ub_ref.shape[1:]
+    lane = lax.broadcasted_iota(jnp.int32, (8, nz), 1)
+    slot = lane // 4
+
+    def tile(t, carry):
+        rows = pl.ds(pl.multiple_of(t * 8, 8), 8)
+        for i in range(20):
+            for out_ref, level, first in ((f0_ref, 0, 0), (f1_ref, 1, 1)):
+                if i == 19 and level == 1:
+                    continue
+                acc = jnp.zeros((8, nz), jnp.float32)
+                for x in range(nx):
+                    value = (
+                        states_ref[level, i, x, rows, :]
+                        if i < 19
+                        else ub_ref[3, x, rows, :]
+                    )
+                    p = x + first
+                    acc = jnp.where(slot == p, pltpu.roll(value, 4 * p + 2, 1), acc)
+                out_ref[i, rows, :] = acc
+        return carry
+
+    lax.fori_loop(0, ny // 8, tile, 0)
+
+
+def turn(value, shift):
+    nz = value.shape[1]
+    return pltpu.roll(value, shift % nz, 1) if shift % nz else value
+
+
+def z_shifted(value, cz):
+    return turn(value, -cz) if cz else value
+
+
+def inner_kernel(states_ref, read_ref, out_ref, grad1_ref, grad_ref, pack_ref, mid):
+    nx, ny, nz = grad_ref.shape
+    tiles = ny // 8
+    lane = lax.broadcasted_iota(jnp.int32, (8, nz), 1)
+    slot = lane // 4
+
+    def first_level(p, t):
+        rows = pl.ds(pl.multiple_of(t * 8, 8), 8)
+        got = [z_shifted(read_ref[i, p, rows, :], VEL[i][2]) for i in range(19)]
+        ub = [read_ref[19 + k, p, rows, :] for k in range(4)]
+        out, kept = adjoint_cell(got, ub[:3], ub[3], 1.0)
+        for i in range(19):
+            mid[i, p, pl.ds(pl.multiple_of(t * 8 + 8, 8), 8), :] = out[i]
+        return out, kept, ub[:3]
+
+    def inside(n, carry):
+        x = n // tiles
+        t = n % tiles
+        out, kept, u = first_level(x + 1, t)
+        rows = pl.ds(pl.multiple_of(t * 8, 8), 8)
+        f0, fs, fd, fm, _ = state_of(states_ref, (1, x, rows))
+        grad1_ref[x, rows, :] = gradient_cell(kept, f0, fs, fd, fm, u)
+        return carry
+
+    lax.fori_loop(0, nx * tiles, inside, 0)
+
+    def halo(n, carry):
+        faces = 2 * (tiles + 1)
+        p = jnp.where(n < faces, (nx + 1) * (n // (tiles + 1)), n - faces + 1)
+        t = jnp.where(n < faces, n % (tiles + 1), tiles)
+        out, _, _ = first_level(p, t)
+
+        @pl.when(t == tiles)
+        def _():
+            for i in range(19):
+                mid[i, p, 0:8, :] = out[i]
+
+        return carry
+
+    lax.fori_loop(0, 2 * (tiles + 1) + nx, halo, 0)
+
+    def second_level(x, carry):
+        for t in range(tiles):
+            rows = slice(t * 8, t * 8 + 8)
+            got = []
+            for i in range(19):
+                cx, cy, cz = VEL[i]
+                low = 8 + 8 * t + cy
+                value = z_shifted(mid[i, x + 1 + cx, low : low + 8, :], cz)
+                got.append(value)
+                pack_ref[i, rows, :] = jnp.where(
+                    slot == x, pltpu.roll(value, 4 * x + 2, 1), pack_ref[i, rows, :]
+                )
+            f0, fs, fd, fm, u = state_of(states_ref, (0, x, rows))
+            b = read_ref[22, x + 1, rows, :]
+            out, kept = adjoint_cell(got, u, b, 1.0)
+            for i in range(19):
+                out_ref[i, x, rows, :] = out[i]
+            grad_ref[x, rows, :] = grad1_ref[x, rows, :] + gradient_cell(
+                kept, f0, fs, fd, fm, u
+            )
+        return carry
+
+    lax.fori_loop(0, nx, second_level, 0)
+
+
+def edge_kernel(
     par_ref,
-    states_ref,
     mask_ref,
-    read_ref,
     zown_ref,
     za_ref,
     zb_ref,
+    pack_ref,
+    f0_ref,
+    f1_ref,
+    inner_ref,
+    grad1_ref,
+    inner_grad_ref,
     out_ref,
     grad_ref,
-    lo_ref,
-    hi_ref,
-    slab_ref,
-    mid,
+    first_ref,
+    second_ref,
     zmid,
+    zout,
 ):
     nx, ny, nz = mask_ref.shape
     tiles = ny // 8
     height = (tiles + 1) * 8
     even = par_ref[2] == 0
     lane = lax.broadcasted_iota(jnp.int32, (8, nz), 1)
-    side = lane % 2
-    first_lane = lane == 0
-    last_lane = lane == nz - 1
+    even_lane = lane % 2 == 0
+    low_pair = lane % 4 < 2
+
+    def swapped(value):
+        return jnp.where(even_lane, turn(value, -1), turn(value, 1))
 
     for g in range(4):
         for t in range(tiles + 1):
@@ -483,122 +589,80 @@
             vb = zb_ref[rows]
             high = jnp.where(even, va, vb)
             low = jnp.where(even, vb, va)
-            lo_ref[rows] = low
-            hi_ref[rows] = high
             own = zown_ref[rows]
-            slab_ref[rows] = jnp.where(
-                side == 0, own if g == 1 else low, own if g == 0 else high
-            )
-
-    def rolled(value, shift):
-        return pltpu.roll(value, lax.rem(shift + 2 * nz, nz), 1)
-
-    def z_slab(t, carry):
-        row = pl.multiple_of(t * 8, 8)
+            if g == 0:
+                head, tail = own, low
+            elif g == 1:
+                head, tail = high, own
+            else:
+                head, tail = jnp.where(even_lane, own, high), jnp.where(even_lane, low, own)
+            head = swapped(head)
+            tail = swapped(tail)
+            first_ref[rows] = jnp.where(low_pair, head, turn(tail, 2))
+            second_ref[rows] = jnp.where(low_pair, turn(head, -2), tail)
+
+    slab_grad = []
+    for t in range(tiles + 1):
         got = []
         for q in range(NSLOT):
             g, k = ZSLOT[q]
-            tile = slab_ref[pl.ds(pl.multiple_of(g * height + row, 8), 8), :]
-            got.append(tile if k == 0 else pltpu.roll(tile, nz - 16 * k, 1))
+            row = g * height + t * 8
+            ref = second_ref if k % 2 else first_ref
+            got.append(turn(ref[row : row + 8, :], -32 * (k // 2)))
         out, kept = adjoint_cell(got[:19], got[19:22], got[22], 1.0)
-        for n, i in enumerate(ZGROUPS[0] + ZGROUPS[1]):
-            if_last = t == tiles
-
-            zmid[n, pl.ds(pl.multiple_of(row + 8, 8), 8), :] = out[i]
-
-            @pl.when(if_last)
-            def _():
-                zmid[n, 0:8, :] = out[i]
-
-        return carry
-
-    lax.fori_loop(0, tiles + 1, z_slab, 0)
-
-    def first_reads(p, t):
-        rows = pl.ds(pl.multiple_of(t * 8, 8), 8)
+        for i in range(19):
+            zmid[i, 8 * t + 8 : 8 * t + 16, :] = out[i]
+            if t == tiles:
+                zmid[i, 0:8, :] = out[i]
+        if t < tiles:
+            f = [f1_ref[i, 8 * t : 8 * t + 8, :] for i in range(19)]
+            fs, fd = pairs_of(f)
+            fm = moments(f[0], fs, fd)
+            grad = gradient_cell(kept, f[0], fs, fd, fm, got[19:22])
+            slab_grad.append(turn(grad, -4))
+
+    at = lane % 4
+    for t in range(tiles):
+        rows = slice(8 * t, 8 * t + 8)
         got = []
         for i in range(19):
-            value = read_ref[i, p, rows, :]
-            cz = VEL[i][2]
-            if cz:
-                g, k = ZSLOT[i]
-                zrows = pl.ds(pl.multiple_of(g * height + t * 8, 8), 8)
-                value = pltpu.roll(value, 1 if cz < 0 else nz - 1, 1)
-                if cz < 0:
-                    edge = rolled(lo_ref[zrows, :], -(16 * k + 2 * p + 1))
-                    value = jnp.where(first_lane, edge, value)
-                else:
-                    edge = rolled(hi_ref[zrows, :], nz - 1 - 16 * k - 2 * p)
-                    value = jnp.where(last_lane, edge, value)
+            cx, cy, cz = VEL[i]
+            value = pack_ref[i, rows, :]
+            edge = zmid[i, 8 + 8 * t + cy : 16 + 8 * t + cy, :]
+            back = -4 * (1 + cx)
+            if cz == 0:
+                value = jnp.where((at == 1) | (at == 2), turn(edge, back), value)
+            else:
+                near_lane = 2 if cz < 0 else 0
+                value = jnp.where(at == near_lane, turn(edge, back - 1), value)
+                value = jnp.where(at == near_lane + 1, turn(edge, back + 1), value)
             got.append(value)
-        ub = [read_ref[19 + k, p, rows, :] for k in range(4)]
-        return got, ub[:3], ub[3]
-
-    def store_mid(out, p, t):
+        f = [f0_ref[i, rows, :] for i in range(19)]
+        fs, fd = pairs_of(f)
+        fm = moments(f[0], fs, fd)
+        inverse = 1.0 / fm["total"]
+        u = [one * inverse for one in fm["one"]]
+        out, kept = adjoint_cell(got, u, f0_ref[19, rows, :], 1.0)
         for i in range(19):
-            mid[i, p, pl.ds(pl.multiple_of(t * 8 + 8, 8), 8), :] = out[i]
-
-    def inner(n, carry):
-        x = n // tiles
-        t = n % tiles
-        got, u, b = first_reads(x + 1, t)
-        out, kept = adjoint_cell(got, u, b, 1.0)
-        store_mid(out, x + 1, t)
-        rows = pl.ds(pl.multiple_of(t * 8, 8), 8)
-        f0, fs, fd, fm, _ = state_of(states_ref, (1, x, rows))
-        grad_ref[x, rows, :] = gradient_cell(kept, f0, fs, fd, fm, u)
-        return carry
-
-    lax.fori_loop(0, nx * tiles, inner, 0)
-
-    def outer(n, carry):
-        faces = 2 * (tiles + 1)
-        p = jnp.where(n < faces, (nx + 1) * (n // (tiles + 1)), n - faces + 1)
-        t = jnp.where(n < faces, n % (tiles + 1), tiles)
-        got, u, b = first_reads(p, t)
-        out, kept = adjoint_cell(got, u, b, 1.0)
-        store_mid(out, p, t)
-
-        @pl.when(t == tiles)
-        def _():
+            zout[i, rows, :] = out[i]
+        zout[19, rows, :] = gradient_cell(kept, f[0], fs, fd, fm, u)
+        zout[20, rows, :] = slab_grad[t]
+
+    outer = (lane < 2) | (lane >= nz - 2)
+    ends = (lane < 1) | (lane >= nz - 1)
+    for x in range(nx):
+        for t in range(tiles):
+            rows = slice(8 * t, 8 * t + 8)
             for i in range(19):
-                mid[i, p, 0:8, :] = out[i]
-
-        return carry
-
-    lax.fori_loop(0, 2 * (tiles + 1) + nx, outer, 0)
-
-    edge_pops = ZGROUPS[0] + ZGROUPS[1]
-
-    def second(x, carry):
-        for t in range(tiles):
-            rows = slice(t * 8, t * 8 + 8)
-            got = []
-            for i in range(19):
-                cx, cy, cz = VEL[i]
-                low = 8 + 8 * t + cy
-                value = mid[i, x + 1 + cx, low : low + 8, :]
-                if cz:
-                    value = pltpu.roll(value, 1 if cz < 0 else nz - 1, 1)
-                    edge = zmid[edge_pops.index(i), low : low + 8, :]
-                    at = 2 * (x + 1 + cx)
-                    if cz < 0:
-                        value = jnp.where(first_lane, rolled(edge, -at), value)
-                    else:
-                        value = jnp.where(
-                            last_lane, rolled(edge, nz - 2 - at), value
-                        )
-                got.append(value)
-            f0, fs, fd, fm, u = state_of(states_ref, (0, x, rows))
-            b = read_ref[22, x + 1, rows, :]
-            out, kept = adjoint_cell(got, u, b, 1.0)
-            for i in range(19):
-                out_ref[i, x, rows, :] = out[i]
-            grad = grad_ref[x, rows, :] + gradient_cell(kept, f0, fs, fd, fm, u)
+                out_ref[i, x, rows, :] = jnp.where(
+                    outer, turn(zout[i, rows, :], -2 - 4 * x), inner_ref[i, x, rows, :]
+                )
+            level1 = jnp.where(
+                ends, turn(zout[20, rows, :], -2 - 4 * x), grad1_ref[x, rows, :]
+            )
+            edge = turn(zout[19, rows, :], -2 - 4 * x) + level1
+            grad = jnp.where(outer, edge, inner_grad_ref[x, rows, :])
             grad_ref[x, rows, :] = jnp.where(mask_ref[x, rows, :] == 0, grad, 0.0)
-        return carry
-
-    lax.fori_loop(0, nx, second, 0)
 
 
 def swaps(count):
@@ -622,7 +686,7 @@
     return pl.pallas_call(
         kernel,
         out_shape=[jax.ShapeDtypeStruct(s, jnp.float32) for s in shapes],
-        in_specs=[SMEM] + [space] * (len(inputs) - 1),
+        in_specs=[SMEM if x.dtype == jnp.int32 and x.ndim == 1 else space for x in inputs],
         out_specs=[VMEM] * len(shapes),
         scratch_shapes=list(scratch),
         compiler_params=PARAMS,
@@ -687,6 +751,11 @@
         ya = both(ya, CORNER, lambda m, pairs: diagonal(m, x_first, pairs))
     xa = lax.ppermute(xa, "gx", x_first)
 
+    f0, f1 = call(
+        pack_state_kernel, (primal_states, ub), [(20, ny, nz), (19, ny, nz)]
+    )
+    drag, f1 = lax.optimization_barrier((drag, f1))
+
     read, zmsg, drags = call(
         pack_z_kernel,
         (parity, adjoint_last, ub, xa, xb, y, ya, yb, drag),
@@ -695,8 +764,16 @@
     )
     zb = lax.ppermute(zmsg, "gz", z_second)
     za = lax.ppermute(zmsg, "gz", z_first)
+    inner, grad1, inner_grad, pack = call(
+        inner_kernel,
+        (primal_states, read),
+        [(19, nx, ny, nz), (nx, ny, nz), (nx, ny, nz), (19, ny, nz)],
+        [pltpu.VMEM((19, nx + 2, height + 8, nz), f32)],
+        micros=4,
+    )
     if (gx, gy, gz) == (4, 2, 4):
         across = lax.ppermute(drags, "gz", [(i, i ^ 2) for i in range(gz)])
+        drags, grad1 = lax.optimization_barrier((drags, grad1))
         drags = (drags + across) + (za[4 * height :] + zb[4 * height :])
         fourth = lax.ppermute(drags[16:], "gx", x_first)
         drag = jnp.sum(drags[:8] + drags[8:16] + drags[16:] + fourth)
@@ -704,17 +781,15 @@
         drag = lax.psum(jnp.sum(drag), AXES)
 
     first, gradient = call(
-        levels_kernel,
-        (parity, primal_states, solid_mask, read, zmsg, za, zb),
+        edge_kernel,
+        (parity, solid_mask, zmsg, za, zb, pack, f0, f1, inner, grad1, inner_grad),
         [(19, nx, ny, nz), (nx, ny, nz)],
         [
             pltpu.VMEM((4 * height, nz), f32),
             pltpu.VMEM((4 * height, nz), f32),
-            pltpu.VMEM((4 * height, nz), f32),
-            pltpu.VMEM((19, nx + 2, height + 8, nz), f32),
-            pltpu.VMEM((10, height + 8, nz), f32),
+            pltpu.VMEM((19, height + 8, nz), f32),
+            pltpu.VMEM((21, ny, nz), f32),
         ],
-        micros=4,
     )
     return (first, gradient, drag / (nx * ny * nz * gx * gy * gz))
 

time: 30.3 us -> 27.1 us (0.89)
  waiting for transfers between devices: 7.34 us -> 3.19 us
  Pallas kernels: 8.87 us -> 9.52 us
    ppermute x1, waiting for transfers between devices: 4.49 us -> 0.81 us  [body(): across = lax.ppermute(drags, 'gz', [(i, i ^ 2) for i in range(gz)])]
    ppermute x1, starting transfers between devices: 1.64 us -> 0.01 us  [body(): za = lax.ppermute(zmsg, 'gz', z_first)]
    ppermute x1, starting transfers between devices: 2.47 us -> 3.67 us  [body(): zb = lax.ppermute(zmsg, 'gz', z_second)]
    ppermute x1, starting transfers between devices: 0.12 us -> 0.78 us  [body(): across = lax.ppermute(drags, 'gz', [(i, i ^ 2) for i in range(gz)])]
    pallas_call x4 -> x6, Pallas kernels: 8.87 us -> 9.52 us  [call(): pl.pallas_call(kernel, out_shape=[jax.ShapeDtypeStruct(s, jnp.float32) fo...]
    ppermute x2, waiting for transfers between devices: 2.84 us -> 2.36 us  [diagonal(): return lax.ppermute(message, ('gx', 'gy'), pairs)]
  transfers between devices with their start and end apart: 9 -> 9, of which waited for: 3 -> 3; matrix products, arithmetic and copies ran while one was open for 0% -> 0% of each run, Pallas kernels for 19% -> 23%
where the time goes in v3:
time: 27.1 us; the launch traced here: 26.9 us
  starting transfers between devices  11 us (41%)
  Pallas kernels  9.52 us (35%)
  waiting for transfers between devices  3.19 us (12%)
  between operations  2.52 us (9%)
  other arithmetic  0.68 us (3%)
    pallas_call x6, Pallas kernels, call(): pl.pallas_call(kernel, out_shape=[jax.ShapeDtypeStruct(s, jnp.float32) fo...  9.52 us
    ppermute x1, starting transfers between devices, body(): zb = lax.ppermute(zmsg, 'gz', z_second)  3.67 us
    ppermute x1, starting transfers between devices, body(): xb = lax.ppermute(xb, 'gx', x_second)  2.61 us
    ppermute x2, waiting for transfers between devices, diagonal(): return lax.ppermute(message, ('gx', 'gy'), pairs)  2.36 us
    ppermute x2, starting transfers between devices, diagonal(): return lax.ppermute(message, ('gx', 'gy'), pairs)  1.72 us
    ppermute x1, starting transfers between devices, body(): y = lax.ppermute(y, 'gy', y_first)  1.58 us
    ppermute x1, waiting for transfers between devices, body(): across = lax.ppermute(drags, 'gz', [(i, i ^ 2) for i in range(gz)])  0.81 us
    ppermute x1, starting transfers between devices, body(): across = lax.ppermute(drags, 'gz', [(i, i ^ 2) for i in range(gz)])  0.78 us
  transfers between devices with their start and end apart: 9, of which 3 were waited for; matrix products, arithmetic and copies ran while one was open for 0% of the time, Pallas kernels for 23%

profile of v3, /device:TPU:0, one launch (start us, length us, event | category | flops | bytes accessed | tf_op | source)
XLA Modules:
  0.0 26.9 jit_solution(10489982342706140758)
XLA Ops:
  0.6 0.0 copy-start.1
  0.6 0.0 copy-start
  0.7 0.1 pad_add_fusion.par_ref
  0.7 2.0 %shard_map.67 = (f32[376,128]{1,0:T(8,128)S(1)}, f32[376,128]{1,0:T(8,128)S(1)}, f32[4,4,16,128]{3,2,1,0:T(8,128)S(1)}, f32[8,128]{1,0:T(8,128)S(1)}) custom-call(s32[3]{0:T(128)S(1)} %pad_add_fusion.par_ref, f32[2,19,4,16,128]{4,3,2,1,0:T(8,128)} %states_ref.3, f32[19,4,16,128]{3,2,1,0:T(8,128)} %adj_ref.3, f32[4,16,128]{2,1,0:T(8,128)} %por_hbm.1, ...), custom_call_target="tpu_custom_call" | custom-call | bytes 3600000 | tf_op jit(solution)/shard_map/pallas_call | solution.py:686
  2.8 0.5 %collective-permute-start = (f32[376,128]{1,0:T(8,128)S(1)}, f32[376,128]{1,0:T(8,128)S(1)}, u32[]{:S(2)}, u32[]{:S(2)}) collective-permute-start(f32[376,128]{1,0:T(8,128)S(1)} %get-tuple-element.26), channel_id=1, source_target_pairs={{0,8},{8,0},{16,24},{24,16},{1,9},{9,1},{17,25},{25,17},{2,10},{10... | collective-permute-start | bytes 577544 | tf_op jit(solution)/shard_map/ppermute | solution.py:752
  3.3 2.6 %collective-permute-start.1 = (f32[376,128]{1,0:T(8,128)S(1)}, f32[376,128]{1,0:T(8,128)S(1)}, u32[]{:S(2)}, u32[]{:S(2)}) collective-permute-start(f32[376,128]{1,0:T(8,128)S(1)} %get-tuple-element.27), channel_id=1, source_target_pairs={{0,24},{8,16},{16,8},{24,0},{1,25},{9,17},{17,9},{25,1},{2,26},{10... | collective-permute-start | bytes 577544 | tf_op jit(solution)/shard_map/ppermute | solution.py:736
  5.9 0.7 %shard_map.68 = (f32[200,128]{1,0:T(8,128)S(1)}, f32[56,128]{1,0:T(8,128)S(1)}, f32[56,128]{1,0:T(8,128)S(1)}) custom-call(s32[3]{0:T(128)S(1)} %pad_add_fusion.par_ref, f32[19,4,16,128]{3,2,1,0:T(8,128)S(1)} %copy-done.1, f32[4,4,16,128]{3,2,1,0:T(8,128)S(1)} %get-tuple-element.25.ub_ref, f32[8,128]{1,0:T(8,128)S(1)} %get-tuple-element.33.drag_ref.own_ref), custom_call_target="tpu_custom_call" | custom-call | bytes 14400000 | tf_op jit(solution)/shard_map/pallas_call | solution.py:686
  6.6 1.6 %collective-permute-start.2 = (f32[200,128]{1,0:T(8,128)S(1)}, f32[200,128]{1,0:T(8,128)S(1)}, u32[]{:S(2)}, u32[]{:S(2)}) collective-permute-start(f32[200,128]{1,0:T(8,128)S(1)} %get-tuple-element.29), channel_id=1, source_target_pairs={{0,4},{4,0},{1,5},{5,1},{2,6},{6,2},{3,7},{7,3},{8,12},{12,8},{9,1... | collective-permute-start | bytes 307208 | tf_op jit(solution)/shard_map/ppermute | solution.py:738
  8.2 0.0 collective-permute-start.3
  8.2 1.7 %collective-permute-start.4 = (f32[56,128]{1,0:T(8,128)S(1)}, f32[56,128]{1,0:T(8,128)S(1)}, u32[]{:S(2)}, u32[]{:S(2)}) collective-permute-start(f32[56,128]{1,0:T(8,128)S(1)} %get-tuple-element.31), channel_id=1, source_target_pairs={{0,28},{4,24},{8,20},{12,16},{16,12},{20,8},{24,4},{28,0},{1,29},{... | collective-permute-start | bytes 86024 | tf_op jit(solution)/shard_map/ppermute | solution.py:712
  9.9 0.5 %shard_map.69 = (f32[20,16,128]{2,1,0:T(8,128)S(1)}, f32[19,16,128]{2,1,0:T(8,128)S(1)}) custom-call(f32[2,19,4,16,128]{4,3,2,1,0:T(8,128)S(1)} %copy-done, f32[4,4,16,128]{3,2,1,0:T(8,128)S(1)} %get-tuple-element.25.ub_ref), custom_call_target="tpu_custom_call" | custom-call | bytes 3600000 | tf_op jit(solution)/shard_map/pallas_call | solution.py:686
  10.4 1.4 %collective-permute-done.3.ya_ref = f32[56,128]{1,0:T(8,128)S(1)} collective-permute-done((f32[56,128]{1,0:T(8,128)S(1)}, f32[56,128]{1,0:T(8,128)S(1)}, u32[]{:S(2)}, u32[]{:S(2)}) %collective-permute-start.3) | collective-permute-done | bytes 28704 | tf_op jit(solution)/shard_map/ppermute | solution.py:712
  11.8 1.0 %collective-permute-done.4.yb_ref = f32[56,128]{1,0:T(8,128)S(1)} collective-permute-done((f32[56,128]{1,0:T(8,128)S(1)}, f32[56,128]{1,0:T(8,128)S(1)}, u32[]{:S(2)}, u32[]{:S(2)}) %collective-permute-start.4) | collective-permute-done | bytes 28704 | tf_op jit(solution)/shard_map/ppermute | solution.py:712
  12.8 0.0 collective-permute-done.2.y_ref
  12.8 0.0 collective-permute-done.xa_ref
  12.8 1.2 %shard_map.70 = (f32[23,6,24,128]{3,2,1,0:T(8,128)S(1)}, f32[120,128]{1,0:T(8,128)S(1)}, f32[24,128]{1,0:T(8,128)S(1)}) custom-call(s32[3]{0:T(128)S(1)} %pad_add_fusion.par_ref, f32[19,4,16,128]{3,2,1,0:T(8,128)S(1)} %copy-done.1, f32[4,4,16,128]{3,2,1,0:T(8,128)S(1)} %get-tuple-element.25.ub_ref, f32[376,128]{1,0:T(8,128)S(1)} %collective-permute-done.xa_ref, ...), custom_call_target="tpu_custom_call" | custom-call | bytes 3600000 | tf_op jit(solution)/shard_map/pallas_call | solution.py:686
  14.0 0.0 copy-start.2
  14.0 3.7 %collective-permute-start.6 = (f32[120,128]{1,0:T(8,128)S(1)}, f32[120,128]{1,0:T(8,128)S(1)}, u32[]{:S(2)}, u32[]{:S(2)}) collective-permute-start(f32[120,128]{1,0:T(8,128)S(1)} %get-tuple-element.34.zown_ref), channel_id=1, source_target_pairs={{0,3},{1,2},{2,1},{3,0},{4,7},{5,6},{6,5},{7,4},{8,11},{9,10},{10,... | collective-permute-start | bytes 184328 | tf_op jit(solution)/shard_map/ppermute | solution.py:765
  17.6 0.8 %collective-permute-start.7 = (f32[24,128]{1,0:T(8,128)S(1)}, f32[24,128]{1,0:T(8,128)S(1)}, u32[]{:S(2)}, u32[]{:S(2)}) collective-permute-start(f32[24,128]{1,0:T(8,128)S(1)} %get-tuple-element.46), channel_id=1, source_target_pairs={{0,2},{1,3},{2,0},{3,1},{4,6},{5,7},{6,4},{7,5},{8,10},{9,11},{10,... | collective-permute-start | bytes 36872 | tf_op jit(solution)/shard_map/ppermute | solution.py:775
  18.4 3.0 %shard_map.71 = (f32[19,4,16,128]{3,2,1,0:T(8,128)S(1)}, f32[4,16,128]{2,1,0:T(8,128)S(1)}, f32[4,16,128]{2,1,0:T(8,128)S(1)}, f32[19,16,128]{2,1,0:T(8,128)S(1)}) custom-call(f32[2,19,4,16,128]{4,3,2,1,0:T(8,128)S(1)} %copy-done, f32[23,6,24,128]{3,2,1,0:T(8,128)S(1)} %get-tuple-element.35.read_ref), custom_call_target="tpu_custom_call" | custom-call | bytes 14400000 | tf_op jit(solution)/shard_map/pallas_call | solution.py:686
  21.4 0.8 %collective-permute-done.7 = f32[24,128]{1,0:T(8,128)S(1)} collective-permute-done((f32[24,128]{1,0:T(8,128)S(1)}, f32[24,128]{1,0:T(8,128)S(1)}, u32[]{:S(2)}, u32[]{:S(2)}) %collective-permute-start.7) | collective-permute-done | bytes 12320 | tf_op jit(solution)/shard_map/ppermute | solution.py:775
  22.3 0.1 collective-permute-start.8
  22.3 2.2 %shard_map.72 = (f32[19,4,16,128]{3,2,1,0:T(8,128)}, f32[4,16,128]{2,1,0:T(8,128)}) custom-call(s32[3]{0:T(128)S(1)} %pad_add_fusion.par_ref, s32[4,16,128]{2,1,0:T(8,128)S(1)} %copy-done.2, f32[120,128]{1,0:T(8,128)S(1)} %get-tuple-element.34.zown_ref, f32[120,128]{1,0:T(8,128)S(1)} %collective-permute-done.5.za_ref, ...), custom_call_target="tpu_custom_call" | custom-call | bytes 3600000 | tf_op jit(solution)/shard_map/pallas_call | solution.py:686
  24.5 0.6 %fusion.3 = f32[]{:T(128)} fusion(f32[8,128]{1,0:T(8,128)S(1)} %collective-permute-done.8, f32[24,128]{1,0:T(8,128)S(1)} %fusion), kind=kLoop, calls=%fused_computation.5 | loop fusion | flops 4095 | bytes 16388 | tf_op jit(solution)/shard_map/reduce_sum | solution.py:779
  (10 shorter events, 0.0 us)
Async XLA Ops:
  0.6 5.3 %copy-start.1 = (f32[19,4,16,128]{3,2,1,0:T(8,128)S(1)}, f32[19,4,16,128]{3,2,1,0:T(8,128)}, u32[]{:S(2)}) copy-start(f32[19,4,16,128]{3,2,1,0:T(8,128)} %adj_ref.3) | copy-start | bytes 1867780
  0.6 9.3 %copy-start = (f32[2,19,4,16,128]{4,3,2,1,0:T(8,128)S(1)}, f32[2,19,4,16,128]{4,3,2,1,0:T(8,128)}, u32[]{:S(2)}) copy-start(f32[2,19,4,16,128]{4,3,2,1,0:T(8,128)} %states_ref.3) | copy-start | bytes 3735556
  2.8 10.0 %collective-permute-start = (f32[376,128]{1,0:T(8,128)S(1)}, f32[376,128]{1,0:T(8,128)S(1)}, u32[]{:S(2)}, u32[]{:S(2)}) collective-permute-start(f32[376,128]{1,0:T(8,128)S(1)} %get-tuple-element.26), channel_id=1, source_target_pairs={{0,8},{8,0},{16,24},{24,16},{1,9},{9,1},{17,25},{25,17},{2,10},{10... | collective-permute-start | bytes 577544 | tf_op jit(solution)/shard_map/ppermute | solution.py:752
  3.3 9.5 %collective-permute-start.1 = (f32[376,128]{1,0:T(8,128)S(1)}, f32[376,128]{1,0:T(8,128)S(1)}, u32[]{:S(2)}, u32[]{:S(2)}) collective-permute-start(f32[376,128]{1,0:T(8,128)S(1)} %get-tuple-element.27), channel_id=1, source_target_pairs={{0,24},{8,16},{16,8},{24,0},{1,25},{9,17},{17,9},{25,1},{2,26},{10... | collective-permute-start | bytes 577544 | tf_op jit(solution)/shard_map/ppermute | solution.py:736
  6.6 6.1 %collective-permute-start.2 = (f32[200,128]{1,0:T(8,128)S(1)}, f32[200,128]{1,0:T(8,128)S(1)}, u32[]{:S(2)}, u32[]{:S(2)}) collective-permute-start(f32[200,128]{1,0:T(8,128)S(1)} %get-tuple-element.29), channel_id=1, source_target_pairs={{0,4},{4,0},{1,5},{5,1},{2,6},{6,2},{3,7},{7,3},{8,12},{12,8},{9,1... | collective-permute-start | bytes 307208 | tf_op jit(solution)/shard_map/ppermute | solution.py:738
  8.2 3.6 %collective-permute-start.3 = (f32[56,128]{1,0:T(8,128)S(1)}, f32[56,128]{1,0:T(8,128)S(1)}, u32[]{:S(2)}, u32[]{:S(2)}) collective-permute-start(f32[56,128]{1,0:T(8,128)S(1)} %get-tuple-element.30), channel_id=1, source_target_pairs={{0,12},{4,8},{8,4},{12,0},{16,28},{20,24},{24,20},{28,16},{1,13},{... | collective-permute-start | bytes 86024 | tf_op jit(solution)/shard_map/ppermute | solution.py:712
  8.2 4.6 %collective-permute-start.4 = (f32[56,128]{1,0:T(8,128)S(1)}, f32[56,128]{1,0:T(8,128)S(1)}, u32[]{:S(2)}, u32[]{:S(2)}) collective-permute-start(f32[56,128]{1,0:T(8,128)S(1)} %get-tuple-element.31), channel_id=1, source_target_pairs={{0,28},{4,24},{8,20},{12,16},{16,12},{20,8},{24,4},{28,0},{1,29},{... | collective-permute-start | bytes 86024 | tf_op jit(solution)/shard_map/ppermute | solution.py:712
  14.0 8.4 %copy-start.2 = (s32[4,16,128]{2,1,0:T(8,128)S(1)}, s32[4,16,128]{2,1,0:T(8,128)}, u32[]{:S(2)}) copy-start(s32[4,16,128]{2,1,0:T(8,128)} %mask_ref.1) | copy-start | bytes 98308
  14.0 8.3 %collective-permute-start.6 = (f32[120,128]{1,0:T(8,128)S(1)}, f32[120,128]{1,0:T(8,128)S(1)}, u32[]{:S(2)}, u32[]{:S(2)}) collective-permute-start(f32[120,128]{1,0:T(8,128)S(1)} %get-tuple-element.34.zown_ref), channel_id=1, source_target_pairs={{0,3},{1,2},{2,1},{3,0},{4,7},{5,6},{6,5},{7,4},{8,11},{9,10},{10,... | collective-permute-start | bytes 184328 | tf_op jit(solution)/shard_map/ppermute | solution.py:765
  17.6 4.6 %collective-permute-start.5 = (f32[120,128]{1,0:T(8,128)S(1)}, f32[120,128]{1,0:T(8,128)S(1)}, u32[]{:S(2)}, u32[]{:S(2)}) collective-permute-start(f32[120,128]{1,0:T(8,128)S(1)} %get-tuple-element.34.zown_ref), channel_id=1, source_target_pairs={{0,1},{1,0},{2,3},{3,2},{4,5},{5,4},{6,7},{7,6},{8,9},{9,8},{10,11... | collective-permute-start | bytes 184328 | tf_op jit(solution)/shard_map/ppermute | solution.py:766
  17.6 4.6 %collective-permute-start.7 = (f32[24,128]{1,0:T(8,128)S(1)}, f32[24,128]{1,0:T(8,128)S(1)}, u32[]{:S(2)}, u32[]{:S(2)}) collective-permute-start(f32[24,128]{1,0:T(8,128)S(1)} %get-tuple-element.46), channel_id=1, source_target_pairs={{0,2},{1,3},{2,0},{3,1},{4,6},{5,7},{6,4},{7,5},{8,10},{9,11},{10,... | collective-permute-start | bytes 36872 | tf_op jit(solution)/shard_map/ppermute | solution.py:775
  22.3 2.2 %collective-permute-start.8 = (f32[8,128]{1,0:T(8,128)S(1)}, f32[8,128]{1,0:T(8,128)S(1)}, u32[]{:S(2)}, u32[]{:S(2)}) collective-permute-start(f32[8,128]{1,0:T(8,128)S(1)} %slice.25), channel_id=1, source_target_pairs={{0,8},{8,0},{16,24},{24,16},{1,9},{9,1},{17,25},{25,17},{2,10},{10... | collective-permute-start | bytes 12296 | tf_op jit(solution)/shard_map/ppermute | solution.py:778

commit v4 on v3

--- a/solution.py
+++ b/solution.py
@@ -44,6 +44,7 @@
 
 NSLOT = 23
 CORNER = 24
+EDGE_ROWS = 8
 
 
 def y_rows(nx):
@@ -229,6 +230,7 @@
     mask_hbm,
     a_ref,
     b_ref,
+    cols_ref,
     ub_ref,
     drag_ref,
     states_ref,
@@ -243,39 +245,64 @@
         pltpu.make_async_copy(src, dst, sems.at[k])
         for k, (src, dst) in enumerate(
             (
+                (adj_hbm, adj_ref),
                 (states_hbm.at[1], states_ref.at[1]),
                 (por_hbm, por_ref),
                 (mask_hbm, mask_ref),
                 (states_hbm.at[0, 1:3], states_ref.at[0, 1:3]),
                 (states_hbm.at[0, 7:15], states_ref.at[0, 7:15]),
-                (adj_hbm, adj_ref),
             )
         )
     ]
     for copy in copies:
         copy.start()
-    for copy in copies[:5]:
+    copies[0].wait()
+
+    pair = lax.broadcasted_iota(jnp.int32, (8, nz), 1) // 2
+
+    def columns(acc, g, t, wanted):
+        for k, q in enumerate(ZGROUPS[g]):
+            if q not in wanted:
+                continue
+            cz = VEL[q][2] if q < 19 else 0
+            for x in range(nx):
+                start = 32 * (k // 2) + 4 * (x + 2) + 2 * (k % 2)
+                value = cell_rows(adj_ref, ub_ref, q, x, slice(8 * t, 8 * t + 8))
+                acc = jnp.where(pair == start // 2, turn(value, start + 1 - cz), acc)
+        row = g * ny + 8 * t
+        cols_ref[row : row + 8] = acc
+        a_ref[NSLOT * ny + row : NSLOT * ny + row + 8] = acc
+
+    for g in range(4):
+        for t in range(tiles):
+            columns(jnp.zeros((8, nz), jnp.float32), g, t, range(19))
+    for copy in copies[1:]:
         copy.wait()
 
-    def cells(n, carry):
-        x = n // tiles
-        rows = pl.ds(pl.multiple_of((n % tiles) * 8, 8), 8)
-        blocking = jnp.where(mask_ref[x, rows, :] == 0, por_ref[x, rows, :], 1.0)
-        f0, s, d, m, u = state_of(states_ref, (1, x, rows))
-        flux = m["one"][0]
-        for a, b in PAIRS:
-            if VEL[a][0]:
-                flux = flux + (states_ref[0, a, x, rows, :] - states_ref[0, b, x, rows, :])
-        for k in range(3):
-            ub_ref[k, x, rows, :] = u[k]
-        ub_ref[3, x, rows, :] = blocking
-        return carry + blocking * flux
-
-    drag = lax.fori_loop(0, nx * tiles, cells, jnp.zeros((8, nz), jnp.float32))
+    def cells(x, carry):
+        for t in range(tiles):
+            rows = slice(8 * t, 8 * t + 8)
+            blocking = jnp.where(mask_ref[x, rows, :] == 0, por_ref[x, rows, :], 1.0)
+            f0, s, d, m, u = state_of(states_ref, (1, x, rows))
+            flux = m["one"][0]
+            for a, b in PAIRS:
+                if VEL[a][0]:
+                    flux = flux + (
+                        states_ref[0, a, x, rows, :] - states_ref[0, b, x, rows, :]
+                    )
+            for k in range(3):
+                ub_ref[k, x, rows, :] = u[k]
+            ub_ref[3, x, rows, :] = blocking
+            carry = carry + blocking * flux
+        return carry
+
+    drag = lax.fori_loop(0, nx, cells, jnp.zeros((8, nz), jnp.float32))
     drag_ref[...] = drag
-    a_ref[NSLOT * ny :] = drag
-    b_ref[NSLOT * ny :] = drag
-    copies[5].wait()
+    for t in range(tiles):
+        row = 3 * ny + 8 * t
+        columns(cols_ref[row : row + 8], 3, t, UB)
+    cols_ref[4 * ny :] = drag
+    a_ref[(NSLOT + 4) * ny :] = drag
 
     def fill_x(out_ref, sign):
         for names, offset, x in (
@@ -297,8 +324,21 @@
             fill_x(b_ref, -sa)
 
 
-def pack_y_kernel(par_ref, adj_ref, ub_ref, drag_ref, y_ref, ya_ref, yb_ref):
+def pack_y_kernel(par_ref, adj_ref, ub_ref, cols_ref, y_ref, ya_ref, yb_ref):
     nx, ny, nz = adj_ref.shape[1:]
+    y_block = y_rows(nx) + EDGE_ROWS
+    corner_block = CORNER + EDGE_ROWS
+
+    def fill_edges(place, sign):
+        for g in range(4):
+            for d in range(2):
+                y = d if sign > 0 else ny - 1 - d
+                line = cols_ref[g * ny + y : g * ny + y + 1]
+                row = place * y_block + y_rows(nx) + 2 * g + d
+                y_ref[row : row + 1] = line
+                row = place * corner_block + CORNER + 2 * g + d
+                ya_ref[row : row + 1] = line
+                yb_ref[row : row + 1] = line
 
     def fill_y(place, sign):
         for names, offset, y in (
@@ -307,7 +347,7 @@
         ):
             for k, q in enumerate(names):
                 for x in range(nx):
-                    row = place * y_rows(nx) + (k + offset) * nx + x
+                    row = place * y_block + (k + offset) * nx + x
                     y_ref[row : row + 1] = cell_rows(
                         adj_ref, ub_ref, q, x, slice(y, y + 1)
                     )
@@ -317,17 +357,16 @@
         for k, (q, dx, dy) in enumerate(names):
             x = dx if sx > 0 else nx - 1 - dx
             y = dy if sy > 0 else ny - 1 - dy
-            row = place * CORNER + k
+            row = place * corner_block + k
             out_ref[row : row + 1] = cell_rows(adj_ref, ub_ref, q, x, slice(y, y + 1))
-        row = place * CORNER + len(names)
-        out_ref[row : (place + 1) * CORNER] = jnp.zeros(
-            ((place + 1) * CORNER - row, nz), jnp.float32
-        )
-
-    drag = drag_ref[...]
-    y_ref[2 * y_rows(nx) :] = drag
-    ya_ref[2 * CORNER :] = drag
-    yb_ref[2 * CORNER :] = drag
+        row = place * corner_block + len(names)
+        last = place * corner_block + CORNER
+        out_ref[row:last] = jnp.zeros((last - row, nz), jnp.float32)
+
+    drag = cols_ref[4 * ny :]
+    y_ref[2 * y_block :] = drag
+    ya_ref[2 * corner_block :] = drag
+    yb_ref[2 * corner_block :] = drag
     for py in (0, 1):
 
         @pl.when(par_ref[1] == py)
@@ -335,6 +374,8 @@
             s0 = 1 if py else -1
             fill_y(0, s0)
             fill_y(1, -s0)
+            fill_edges(0, s0)
+            fill_edges(1, -s0)
 
     for px in (0, 1):
         for py in (0, 1):
@@ -350,6 +391,122 @@
 
 def pack_z_kernel(
     par_ref,
+    cols_ref,
+    xa_ref,
+    xc_ref,
+    y_ref,
+    ya_ref,
+    yb_ref,
+    zown_ref,
+    za_ref,
+    zb_ref,
+    drag_ref,
+    ext,
+):
+    ny = (cols_ref.shape[0] - 8) // 4
+    nz = cols_ref.shape[1]
+    tiles = ny // 8
+    base = 16
+    even_x = par_ref[0] == 0
+    even_y = par_ref[1] == 0
+    lane = lax.broadcasted_iota(jnp.int32, (8, nz), 1)
+    sub = lax.broadcasted_iota(jnp.int32, (8, nz), 0)
+    plane = (lane % 32) // 4
+    slot = 2 * (lane // 32) + (lane % 4) // 2
+
+    def along_x(own, va, vb):
+        low = turn(jnp.where(even_x, vb, va), -16)
+        high = turn(jnp.where(even_x, va, vb), 16)
+        return jnp.where(plane < 2, low, jnp.where(plane > 5, high, own))
+
+    offset = xa_ref.shape[0] - 8 - 4 * ny
+    for g in range(4):
+        for t in range(tiles):
+            row = g * ny + 8 * t
+            ext[g, base + 8 * t : base + 8 * t + 8, :] = along_x(
+                cols_ref[row : row + 8],
+                xa_ref[offset + row : offset + row + 8],
+                xc_ref[row : row + 8],
+            )
+    y_block = (y_ref.shape[0] - 8) // 2
+    corner_block = CORNER + EDGE_ROWS
+
+    def edges(ref, block, place):
+        return ref[(place + 1) * block - EDGE_ROWS : (place + 1) * block]
+
+    first, second = [
+        along_x(
+            edges(y_ref, y_block, place),
+            edges(ya_ref, corner_block, place),
+            edges(yb_ref, corner_block, place),
+        )
+        for place in range(2)
+    ]
+    high = jnp.where(even_y, first, second)
+    low = jnp.where(even_y, second, first)
+    for g in range(4):
+        for d in range(2):
+            row = 2 * g + d
+            ext[g, base + ny + d : base + ny + d + 1, :] = high[row : row + 1]
+            ext[g, base - 1 - d : base - d, :] = low[row : row + 1]
+
+    packed = []
+    for g, group in enumerate(ZGROUPS):
+        moves = {}
+        for k, q in enumerate(group):
+            cx, cy, _ = VEL[q] if q < 19 else (0, 0, 0)
+            moves.setdefault((cx, cy), []).append(k)
+        acc = [jnp.zeros((8, nz), jnp.float32) for t in range(tiles + 1)]
+        for (cx, cy), slots in moves.items():
+            mask = slot == slots[0]
+            for k in slots[1:]:
+                mask = mask | (slot == k)
+            for t in range(tiles + 1):
+                if t < tiles:
+                    row = base + 8 * t + cy
+                    value = ext[g, row : row + 8, :]
+                else:
+                    above = base + ny + cy
+                    below = base - 8 + cy
+                    value = jnp.where(
+                        sub < 4, ext[g, above : above + 8, :], ext[g, below : below + 8, :]
+                    )
+                acc[t] = jnp.where(mask, turn(value, -4 * cx), acc[t])
+        packed.append(acc)
+        for t in range(tiles + 1):
+            row = (g * (tiles + 1) + t) * 8
+            zown_ref[row : row + 8, :] = acc[t]
+    up_first = par_ref[2] == 0
+    even_lane = lane % 2 == 0
+    for t in range(tiles + 1):
+        two, three = packed[2][t], packed[3][t]
+        up = (packed[0][t], jnp.where(even_lane, two, pltpu.roll(three, 1, 1)))
+        down = (packed[1][t], jnp.where(even_lane, pltpu.roll(two, nz - 1, 1), three))
+        for g in range(2):
+            row = (g * (tiles + 1) + t) * 8
+            za_ref[row : row + 8, :] = jnp.where(up_first, up[g], down[g])
+            zb_ref[row : row + 8, :] = jnp.where(up_first, down[g], up[g])
+    drag = cols_ref[4 * ny :] + y_ref[2 * y_block :]
+    for x_ref, c_ref in ((xa_ref, ya_ref), (xc_ref, yb_ref)):
+        drag = drag + (x_ref[x_ref.shape[0] - 8 :] + c_ref[2 * corner_block :])
+    drag_ref[...] = drag
+
+
+OUT_GROUPS = ((0, 7), (7, 13), (13, 17), (17, 19))
+
+
+def turn(value, shift):
+    nz = value.shape[1]
+    return pltpu.roll(value, shift % nz, 1) if shift % nz else value
+
+
+def z_shifted(value, cz):
+    return turn(value, -cz) if cz else value
+
+
+def inner_kernel(
+    par_ref,
+    states_ref,
     adj_ref,
     ub_ref,
     xa_ref,
@@ -357,13 +514,20 @@
     y_ref,
     ya_ref,
     yb_ref,
-    own_ref,
-    read_ref,
-    zmsg_ref,
-    drag_ref,
+    out_ref,
+    grad1_ref,
+    grad_ref,
+    pack_ref,
+    f0_ref,
+    f1_ref,
     ext,
+    mid,
 ):
-    nx, ny, nz = adj_ref.shape[1:]
+    nx, ny, nz = grad_ref.shape
+    tiles = ny // 8
+    lane = lax.broadcasted_iota(jnp.int32, (8, nz), 1)
+    slot = lane // 4
+    sub = lax.broadcasted_iota(jnp.int32, (8, nz), 0)
     even_x = par_ref[0] == 0
     even_y = par_ref[1] == 0
     base = 16
@@ -383,9 +547,8 @@
                 ext[q, planes[sign][depth], base : base + ny, :] = jnp.where(
                     even_x, first[rows], second[rows]
                 )
-        block = y_rows(nx)
+        block = y_rows(nx) + EDGE_ROWS
         first, second = (0, block) if sign > 0 else (block, 0)
-        per = 8 // nx if nx < 8 else 1
         for names, depth, offset in ((near(1, sign), 0, 0), (far(1, sign), 1, 18)):
             line = lines[sign][depth]
             for k, q in enumerate(names):
@@ -399,7 +562,8 @@
                     ext[q, x + 2, line : line + 1, :] = got[x : x + 1]
         for sx in (1, -1):
             xs = (ya_ref, yb_ref) if sx > 0 else (yb_ref, ya_ref)
-            ys = (0, CORNER) if sign > 0 else (CORNER, 0)
+            block = CORNER + EDGE_ROWS
+            ys = (0, block) if sign > 0 else (block, 0)
             low, high = [
                 jnp.where(even_x, xs[0][r : r + CORNER], xs[1][r : r + CORNER])
                 for r in ys
@@ -409,57 +573,80 @@
                 line = lines[sign][dy]
                 ext[q, planes[sx][dx], line : line + 1, :] = got[k : k + 1]
 
-    lane = lax.broadcasted_iota(jnp.int32, (8, nz), 1)
-    sub = lax.broadcasted_iota(jnp.int32, (8, nz), 0)
-    pair = lane // 2
-    tiles = ny // 8
-    for g, group in enumerate(ZGROUPS):
-        acc = [jnp.zeros((8, nz), jnp.float32) for t in range(tiles + 1)]
-        for k, q in enumerate(group):
-            cx, cy, cz = VEL[q] if q < 19 else (0, 0, 0)
-            for p in range(nx + 2):
-                plane = p + 1 + cx
-                start = 32 * (k // 2) + 4 * p + 2 * (k % 2)
-                mask = pair == start // 2
-                for t in range(tiles + 1):
-                    if t < tiles:
-                        low = base + 8 * t + cy
-                        value = ext[q, plane, low : low + 8, :]
-                    else:
-                        high = base + ny + cy
-                        low = base - 8 + cy
-                        value = jnp.where(
-                            sub < 4,
-                            ext[q, plane, high : high + 8, :],
-                            ext[q, plane, low : low + 8, :],
-                        )
-                    read_ref[q, p, 8 * t : 8 * t + 8, :] = value
-                    shift = start + (2 if cz < 0 else 1 if cz == 0 else 0)
-                    moved = pltpu.roll(value, shift % nz, 1)
-                    acc[t] = jnp.where(mask, moved, acc[t])
-        for t in range(tiles + 1):
-            row = (g * (tiles + 1) + t) * 8
-            zmsg_ref[row : row + 8, :] = acc[t]
-    drags = [
-        own_ref[...] + y_ref[2 * y_rows(nx) :],
-        xa_ref[NSLOT * ny :] + ya_ref[2 * CORNER :],
-        xb_ref[NSLOT * ny :] + yb_ref[2 * CORNER :],
-    ]
-    row = 4 * (tiles + 1) * 8
-    for k, drag in enumerate(drags):
-        drag_ref[8 * k : 8 * k + 8, :] = drag
-        zmsg_ref[row + 8 * k : row + 8 * k + 8, :] = drag
-
-
-def pack_state_kernel(states_ref, ub_ref, f0_ref, f1_ref):
-    nx, ny, nz = ub_ref.shape[1:]
-    lane = lax.broadcasted_iota(jnp.int32, (8, nz), 1)
-    slot = lane // 4
+    def near_cells(q, plane, t, cy):
+        if t < tiles:
+            row = base + 8 * t + cy
+            return ext[q, plane, row : row + 8, :]
+        above = base + ny + cy
+        below = base - 8 + cy
+        return jnp.where(
+            sub < 4, ext[q, plane, above : above + 8, :], ext[q, plane, below : below + 8, :]
+        )
+
+    def first_level(p, t, kinds):
+        got = []
+        for i in range(19):
+            cx, cy, cz = VEL[i]
+            got.append(z_shifted(near_cells(i, p + 1 + cx, t, cy), cz))
+        ub = [near_cells(19 + k, p + 1, t, 0) for k in range(4)]
+        out, kept = adjoint_cell(got, ub[:3], ub[3], 1.0)
+        for i in kinds:
+            if t < tiles:
+                mid[i, p, t * 8 + 8 : t * 8 + 16, :] = out[i]
+            elif VEL[i][1] > 0:
+                mid[i, p, t * 8 + 8 : t * 8 + 16, :] = out[i]
+            elif VEL[i][1] < 0:
+                mid[i, p, 0:8, :] = out[i]
+        return kept, ub[:3]
+
+    def inside(x, carry):
+        for t in range(tiles):
+            kept, u = first_level(x + 1, t, range(19))
+            rows = slice(t * 8, t * 8 + 8)
+            f0, fs, fd, fm, _ = state_of(states_ref, (1, x, rows))
+            grad1_ref[x, rows, :] = gradient_cell(kept, f0, fs, fd, fm, u)
+        return carry
+
+    lax.fori_loop(0, nx, inside, 0)
+    for t in range(tiles):
+        first_level(0, t, far(0, -1))
+        first_level(nx + 1, t, far(0, 1))
+
+    def rim(n, carry):
+        for p in (2 * n, 2 * n + 1):
+            first_level(p, tiles, far(1, -1) + far(1, 1))
+        return carry
+
+    lax.fori_loop(0, (nx + 2) // 2, rim, 0)
+
+    def second_level(x, carry):
+        for t in range(tiles):
+            rows = slice(t * 8, t * 8 + 8)
+            got = []
+            for i in range(19):
+                cx, cy, cz = VEL[i]
+                low = 8 + 8 * t + cy
+                value = z_shifted(mid[i, x + 1 + cx, low : low + 8, :], cz)
+                got.append(value)
+                pack_ref[i, rows, :] = jnp.where(
+                    slot == x, pltpu.roll(value, 4 * x + 2, 1), pack_ref[i, rows, :]
+                )
+            f0, fs, fd, fm, u = state_of(states_ref, (0, x, rows))
+            b = ub_ref[3, x, rows, :]
+            out, kept = adjoint_cell(got, u, b, 1.0)
+            for i in range(19):
+                out_ref[i, x, rows, :] = out[i]
+            grad_ref[x, rows, :] = grad1_ref[x, rows, :] + gradient_cell(
+                kept, f0, fs, fd, fm, u
+            )
+        return carry
+
+    lax.fori_loop(0, nx, second_level, 0)
 
     def tile(t, carry):
         rows = pl.ds(pl.multiple_of(t * 8, 8), 8)
         for i in range(20):
-            for out_ref, level, first in ((f0_ref, 0, 0), (f1_ref, 1, 1)):
+            for out_ref, level, first in ((f0_ref, 0, 0), (f1_ref, 1, 2)):
                 if i == 19 and level == 1:
                     continue
                 acc = jnp.zeros((8, nz), jnp.float32)
@@ -477,81 +664,6 @@
     lax.fori_loop(0, ny // 8, tile, 0)
 
 
-def turn(value, shift):
-    nz = value.shape[1]
-    return pltpu.roll(value, shift % nz, 1) if shift % nz else value
-
-
-def z_shifted(value, cz):
-    return turn(value, -cz) if cz else value
-
-
-def inner_kernel(states_ref, read_ref, out_ref, grad1_ref, grad_ref, pack_ref, mid):
-    nx, ny, nz = grad_ref.shape
-    tiles = ny // 8
-    lane = lax.broadcasted_iota(jnp.int32, (8, nz), 1)
-    slot = lane // 4
-
-    def first_level(p, t):
-        rows = pl.ds(pl.multiple_of(t * 8, 8), 8)
-        got = [z_shifted(read_ref[i, p, rows, :], VEL[i][2]) for i in range(19)]
-        ub = [read_ref[19 + k, p, rows, :] for k in range(4)]
-        out, kept = adjoint_cell(got, ub[:3], ub[3], 1.0)
-        for i in range(19):
-            mid[i, p, pl.ds(pl.multiple_of(t * 8 + 8, 8), 8), :] = out[i]
-        return out, kept, ub[:3]
-
-    def inside(n, carry):
-        x = n // tiles
-        t = n % tiles
-        out, kept, u = first_level(x + 1, t)
-        rows = pl.ds(pl.multiple_of(t * 8, 8), 8)
-        f0, fs, fd, fm, _ = state_of(states_ref, (1, x, rows))
-        grad1_ref[x, rows, :] = gradient_cell(kept, f0, fs, fd, fm, u)
-        return carry
-
-    lax.fori_loop(0, nx * tiles, inside, 0)
-
-    def halo(n, carry):
-        faces = 2 * (tiles + 1)
-        p = jnp.where(n < faces, (nx + 1) * (n // (tiles + 1)), n - faces + 1)
-        t = jnp.where(n < faces, n % (tiles + 1), tiles)
-        out, _, _ = first_level(p, t)
-
-        @pl.when(t == tiles)
-        def _():
-            for i in range(19):
-                mid[i, p, 0:8, :] = out[i]
-
-        return carry
-
-    lax.fori_loop(0, 2 * (tiles + 1) + nx, halo, 0)
-
-    def second_level(x, carry):
-        for t in range(tiles):
-            rows = slice(t * 8, t * 8 + 8)
-            got = []
-            for i in range(19):
-                cx, cy, cz = VEL[i]
-                low = 8 + 8 * t + cy
-                value = z_shifted(mid[i, x + 1 + cx, low : low + 8, :], cz)
-                got.append(value)
-                pack_ref[i, rows, :] = jnp.where(
-                    slot == x, pltpu.roll(value, 4 * x + 2, 1), pack_ref[i, rows, :]
-                )
-            f0, fs, fd, fm, u = state_of(states_ref, (0, x, rows))
-            b = read_ref[22, x + 1, rows, :]
-            out, kept = adjoint_cell(got, u, b, 1.0)
-            for i in range(19):
-                out_ref[i, x, rows, :] = out[i]
-            grad_ref[x, rows, :] = grad1_ref[x, rows, :] + gradient_cell(
-                kept, f0, fs, fd, fm, u
-            )
-        return carry
-
-    lax.fori_loop(0, nx, second_level, 0)
-
-
 def edge_kernel(
     par_ref,
     mask_ref,
@@ -564,12 +676,16 @@
     inner_ref,
     grad1_ref,
     inner_grad_ref,
-    out_ref,
-    grad_ref,
+    out_hbm,
+    grad_hbm,
+    tail_ref,
     first_ref,
     second_ref,
     zmid,
     zout,
+    out_ref,
+    grad_ref,
+    sems,
 ):
     nx, ny, nz = mask_ref.shape
     tiles = ny // 8
@@ -579,23 +695,34 @@
     even_lane = lane % 2 == 0
     low_pair = lane % 4 < 2
 
+    last = slice(2 * height, 2 * height + 8)
+    tail_ref[...] = za_ref[last] + zb_ref[last]
+
     def swapped(value):
         return jnp.where(even_lane, turn(value, -1), turn(value, 1))
 
-    for g in range(4):
-        for t in range(tiles + 1):
-            rows = slice((g * (tiles + 1) + t) * 8, (g * (tiles + 1) + t) * 8 + 8)
-            va = za_ref[rows]
-            vb = zb_ref[rows]
-            high = jnp.where(even, va, vb)
-            low = jnp.where(even, vb, va)
+    for t in range(tiles + 1):
+        received = []
+        for g in range(2):
+            row = (g * (tiles + 1) + t) * 8
+            va = za_ref[row : row + 8, :]
+            vb = zb_ref[row : row + 8, :]
+            received.append((jnp.where(even, va, vb), jnp.where(even, vb, va)))
+        (high0, low0), (high1, low1) = received
+        for g in range(4):
+            row = (g * (tiles + 1) + t) * 8
+            rows = slice(row, row + 8)
             own = zown_ref[rows]
             if g == 0:
-                head, tail = own, low
+                head, tail = own, low0
             elif g == 1:
-                head, tail = high, own
+                head, tail = high0, own
+            elif g == 2:
+                head = jnp.where(even_lane, own, turn(high1, 1))
+                tail = jnp.where(even_lane, low1, own)
             else:
-                head, tail = jnp.where(even_lane, own, high), jnp.where(even_lane, low, own)
+                head = jnp.where(even_lane, own, high1)
+                tail = jnp.where(even_lane, turn(low1, -1), own)
             head = swapped(head)
             tail = swapped(tail)
             first_ref[rows] = jnp.where(low_pair, head, turn(tail, 2))
@@ -619,7 +746,7 @@
             fs, fd = pairs_of(f)
             fm = moments(f[0], fs, fd)
             grad = gradient_cell(kept, f[0], fs, fd, fm, got[19:22])
-            slab_grad.append(turn(grad, -4))
+            slab_grad.append(turn(grad, -8))
 
     at = lane % 4
     for t in range(tiles):
@@ -629,7 +756,7 @@
             cx, cy, cz = VEL[i]
             value = pack_ref[i, rows, :]
             edge = zmid[i, 8 + 8 * t + cy : 16 + 8 * t + cy, :]
-            back = -4 * (1 + cx)
+            back = -4 * (2 + cx)
             if cz == 0:
                 value = jnp.where((at == 1) | (at == 2), turn(edge, back), value)
             else:
@@ -648,21 +775,45 @@
         zout[19, rows, :] = gradient_cell(kept, f[0], fs, fd, fm, u)
         zout[20, rows, :] = slab_grad[t]
 
+    def out_copy(k):
+        part = slice(*OUT_GROUPS[k])
+        return pltpu.make_async_copy(out_ref.at[part], out_hbm.at[part], sems.at[k])
+
     outer = (lane < 2) | (lane >= nz - 2)
     ends = (lane < 1) | (lane >= nz - 1)
     for x in range(nx):
         for t in range(tiles):
             rows = slice(8 * t, 8 * t + 8)
-            for i in range(19):
-                out_ref[i, x, rows, :] = jnp.where(
-                    outer, turn(zout[i, rows, :], -2 - 4 * x), inner_ref[i, x, rows, :]
-                )
             level1 = jnp.where(
                 ends, turn(zout[20, rows, :], -2 - 4 * x), grad1_ref[x, rows, :]
             )
             edge = turn(zout[19, rows, :], -2 - 4 * x) + level1
             grad = jnp.where(outer, edge, inner_grad_ref[x, rows, :])
             grad_ref[x, rows, :] = jnp.where(mask_ref[x, rows, :] == 0, grad, 0.0)
+    grad_copy = pltpu.make_async_copy(grad_ref, grad_hbm, sems.at[len(OUT_GROUPS)])
+    grad_copy.start()
+    for k, group in enumerate(OUT_GROUPS):
+        for i in range(*group):
+            for x in range(nx):
+                for t in range(tiles):
+                    rows = slice(8 * t, 8 * t + 8)
+                    out_ref[i, x, rows, :] = jnp.where(
+                        outer,
+                        turn(zout[i, rows, :], -2 - 4 * x),
+                        inner_ref[i, x, rows, :],
+                    )
+        out_copy(k).start()
+    grad_copy.wait()
+    for k in range(len(OUT_GROUPS)):
+        out_copy(k).wait()
+
+
+def drag_kernel(whole_cells, *refs):
+    total = refs[0][...]
+    for ref in refs[1:-1]:
+        total = total + ref[...]
+    summed = jnp.sum(jnp.sum(total, axis=1, keepdims=True), axis=0, keepdims=True)
+    refs[-1][...] = summed / whole_cells
 
 
 def swaps(count):
@@ -678,7 +829,7 @@
 PARAMS = pltpu.CompilerParams(vmem_limit_bytes=48 * 2**20)
 
 
-def call(kernel, inputs, shapes, scratch=(), space=VMEM, micros=1):
+def call(kernel, inputs, shapes, scratch=(), space=VMEM, micros=1, outs=None):
     if space is HBM:
         inputs = inputs[:1] + tuple(
             pltpu.with_memory_space_constraint(x, pltpu.HBM) for x in inputs[1:]
@@ -687,7 +838,7 @@
         kernel,
         out_shape=[jax.ShapeDtypeStruct(s, jnp.float32) for s in shapes],
         in_specs=[SMEM if x.dtype == jnp.int32 and x.ndim == 1 else space for x in inputs],
-        out_specs=[VMEM] * len(shapes),
+        out_specs=outs or [VMEM] * len(shapes),
         scratch_shapes=list(scratch),
         compiler_params=PARAMS,
         cost_estimate=pl.CostEstimate(
@@ -711,13 +862,21 @@
         pairs = [(a * gy + c, b * gy + d) for a, b in x_pairs for c, d in y_pairs]
         return lax.ppermute(message, ("gx", "gy"), pairs)
 
-    rows_x = NSLOT * ny + 8
-    rows_y = 2 * y_rows(nx) + 8
-    rows_c = 2 * CORNER + 8
-    xa, xb, ub, drag = call(
+    rows_x = NSLOT * ny
+    rows_y = 2 * (y_rows(nx) + EDGE_ROWS) + 8
+    rows_c = 2 * (CORNER + EDGE_ROWS) + 8
+    rows_z = 2 * height + 8
+    rides = (gx, gy, gz) == (4, 2, 4)
+    xa, xb, cols, ub, drag = call(
         pack_x_kernel,
         (parity, primal_states, adjoint_last, porosity, solid_mask),
-        [(rows_x, nz), (rows_x, nz), (4, nx, ny, nz), (8, nz)],
+        [
+            (rows_x + 4 * ny + 8, nz),
+            (rows_x, nz),
+            (4 * ny + 8, nz),
+            (4, nx, ny, nz),
+            (8, nz),
+        ],
         [
             pltpu.VMEM((2, 19, nx, ny, nz), f32),
             pltpu.VMEM((19, nx, ny, nz), f32),
@@ -729,11 +888,12 @@
     )
     y, ya, yb = call(
         pack_y_kernel,
-        (parity, adjoint_last, ub, drag),
+        (parity, adjoint_last, ub, cols),
         [(rows_y, nz), (rows_c, nz), (rows_c, nz)],
         micros=4,
     )
-    xb = lax.ppermute(xb, "gx", x_second)
+    xc = lax.ppermute(cols, "gx", x_second)
+    xa = lax.ppermute(xa, "gx", x_first)
     if gy == 2:
         y = lax.ppermute(y, "gy", y_first)
         yb = diagonal(yb, x_second, y_first)
@@ -746,52 +906,70 @@
                 [send(parts[0], y_first), send(parts[1], y_second), parts[2]]
             )
 
-        y = both(y, y_rows(nx), lambda m, pairs: lax.ppermute(m, "gy", pairs))
-        yb = both(yb, CORNER, lambda m, pairs: diagonal(m, x_second, pairs))
-        ya = both(ya, CORNER, lambda m, pairs: diagonal(m, x_first, pairs))
-    xa = lax.ppermute(xa, "gx", x_first)
-
-    f0, f1 = call(
-        pack_state_kernel, (primal_states, ub), [(20, ny, nz), (19, ny, nz)]
-    )
-    drag, f1 = lax.optimization_barrier((drag, f1))
-
-    read, zmsg, drags = call(
+        block = y_rows(nx) + EDGE_ROWS
+        y = both(y, block, lambda m, pairs: lax.ppermute(m, "gy", pairs))
+        block = CORNER + EDGE_ROWS
+        yb = both(yb, block, lambda m, pairs: diagonal(m, x_second, pairs))
+        ya = both(ya, block, lambda m, pairs: diagonal(m, x_first, pairs))
+    xb, xa = lax.optimization_barrier((xb, xa))
+    xb = lax.ppermute(xb, "gx", x_second)
+
+    zown, za, zb, drag_xy = call(
         pack_z_kernel,
-        (parity, adjoint_last, ub, xa, xb, y, ya, yb, drag),
-        [(NSLOT, nx + 2, height, nz), (4 * height + 24, nz), (24, nz)],
-        [pltpu.VMEM((NSLOT, nx + 4, ny + 32, nz), f32)],
-    )
-    zb = lax.ppermute(zmsg, "gz", z_second)
-    za = lax.ppermute(zmsg, "gz", z_first)
-    inner, grad1, inner_grad, pack = call(
+        (parity, cols, xa, xc, y, ya, yb),
+        [(4 * height, nz), (rows_z, nz), (rows_z, nz), (8, nz)],
+        [pltpu.VMEM((4, ny + 32, nz), f32)],
+    )
+    if rides:
+        second = xc[4 * ny :] + yb[rows_c - 8 :]
+        drag_xy = drag_xy + lax.ppermute(second, "gx", x_first)
+        za = za.at[2 * height :].set(drag_xy)
+        zb = zb.at[2 * height :].set(drag_xy)
+    zb = lax.ppermute(zb, "gz", z_second)
+    za = lax.ppermute(za, "gz", z_first)
+    inner, grad1, inner_grad, pack, f0, f1 = call(
         inner_kernel,
-        (primal_states, read),
-        [(19, nx, ny, nz), (nx, ny, nz), (nx, ny, nz), (19, ny, nz)],
-        [pltpu.VMEM((19, nx + 2, height + 8, nz), f32)],
+        (parity, primal_states, adjoint_last, ub, xa, xb, y, ya, yb),
+        [
+            (19, nx, ny, nz),
+            (nx, ny, nz),
+            (nx, ny, nz),
+            (19, ny, nz),
+            (20, ny, nz),
+            (19, ny, nz),
+        ],
+        [
+            pltpu.VMEM((NSLOT, nx + 4, ny + 32, nz), f32),
+            pltpu.VMEM((19, nx + 2, height + 8, nz), f32),
+        ],
         micros=4,
     )
-    if (gx, gy, gz) == (4, 2, 4):
-        across = lax.ppermute(drags, "gz", [(i, i ^ 2) for i in range(gz)])
-        drags, grad1 = lax.optimization_barrier((drags, grad1))
-        drags = (drags + across) + (za[4 * height :] + zb[4 * height :])
-        fourth = lax.ppermute(drags[16:], "gx", x_first)
-        drag = jnp.sum(drags[:8] + drags[8:16] + drags[16:] + fourth)
+    if rides:
+        zhalf = lax.ppermute(drag_xy, "gz", [(i, i ^ 2) for i in range(gz)])
+        drags = (drag_xy, zhalf)
     else:
-        drag = lax.psum(jnp.sum(drag), AXES)
-
-    first, gradient = call(
+        drags = (lax.psum(drag, AXES),)
+
+    first, gradient, tails = call(
         edge_kernel,
-        (parity, solid_mask, zmsg, za, zb, pack, f0, f1, inner, grad1, inner_grad),
-        [(19, nx, ny, nz), (nx, ny, nz)],
+        (parity, solid_mask, zown, za, zb, pack, f0, f1, inner, grad1, inner_grad),
+        [(19, nx, ny, nz), (nx, ny, nz), (8, nz)],
         [
             pltpu.VMEM((4 * height, nz), f32),
             pltpu.VMEM((4 * height, nz), f32),
             pltpu.VMEM((19, height + 8, nz), f32),
             pltpu.VMEM((21, ny, nz), f32),
+            pltpu.VMEM((19, nx, ny, nz), f32),
+            pltpu.VMEM((nx, ny, nz), f32),
+            pltpu.SemaphoreType.DMA((len(OUT_GROUPS) + 1,)),
         ],
-    )
-    return (first, gradient, drag / (nx * ny * nz * gx * gy * gz))
+        outs=[HBM, HBM, VMEM],
+    )
+    if rides:
+        drags += (tails,)
+    whole_cells = float(nx * ny * nz * gx * gy * gz)
+    (drag,) = call(functools.partial(drag_kernel, whole_cells), drags, [(1, 1)])
+    return (first, gradient, drag.reshape(()))
 
 
 def solution(mesh):

time: 27.1 us -> 24.8 us (0.915)
  waiting for transfers between devices: 3.19 us -> 0.96 us
  between operations: 2.52 us -> 0.75 us
  starting transfers between devices: 11 us -> 12.7 us
  other arithmetic: 0.68 us -> 0.08 us
  Pallas kernels: 9.52 us -> 10.1 us
    ppermute x2, starting transfers between devices: 1.72 us -> 4.63 us  [diagonal(): return lax.ppermute(message, ('gx', 'gy'), pairs)]
    ppermute x2, waiting for transfers between devices: 2.36 us -> 0.01 us  [diagonal(): return lax.ppermute(message, ('gx', 'gy'), pairs)]
    ppermute x1, starting transfers between devices: 1.58 us -> 0.01 us  [body(): y = lax.ppermute(y, 'gy', y_first)]
    ppermute x4 -> x5, starting transfers between devices: 4.52 us -> 5.69 us  [the longest x1 2.47 us: body(): zb = lax.ppermute(zb, 'gz', z_second)]
    ppermute x1, starting transfers between devices: 2.61 us -> 1.47 us  [body(): xb = lax.ppermute(xb, 'gx', x_second)]
    pallas_call x6, Pallas kernels: 9.52 us -> 10.1 us  [call(): pl.pallas_call(kernel, out_shape=[jax.ShapeDtypeStruct(s, jnp.float32) fo...]
    reduce_sum x1 -> x0, other arithmetic: 0.6 us -> none  [body(): drag = jnp.sum(drags[:8] + drags[8:16] + drags[16:] + fourth)]
    ppermute x1, waiting for transfers between devices: 0.01 us -> 0.5 us  [body(): y = lax.ppermute(y, 'gy', y_first)]
  transfers between devices with their start and end apart: 9 -> 10, of which waited for: 3 -> 2; matrix products, arithmetic and copies ran while one was open for 0% -> 0% of each run, Pallas kernels for 23% -> 25%
where the time goes in v4:
time: 24.8 us; the launch traced here: 24.7 us
  starting transfers between devices  12.7 us (51%)
  Pallas kernels  10.1 us (41%)
  waiting for transfers between devices  0.96 us (4%)
  between operations  0.75 us (3%)
    pallas_call x6, Pallas kernels, call(): pl.pallas_call(kernel, out_shape=[jax.ShapeDtypeStruct(s, jnp.float32) fo...  10.1 us
    ppermute x2, starting transfers between devices, diagonal(): return lax.ppermute(message, ('gx', 'gy'), pairs)  4.63 us
    ppermute x1, starting transfers between devices, body(): zb = lax.ppermute(zb, 'gz', z_second)  2.47 us
    ppermute x1, starting transfers between devices, body(): za = lax.ppermute(za, 'gz', z_first)  1.64 us
    ppermute x1, starting transfers between devices, body(): xb = lax.ppermute(xb, 'gx', x_second)  1.47 us
    ppermute x1, starting transfers between devices, body(): xa = lax.ppermute(xa, 'gx', x_first)  0.93 us
    ppermute x1, starting transfers between devices, body(): xc = lax.ppermute(cols, 'gx', x_second)  0.8 us
    ppermute x1, starting transfers between devices, body(): drag_xy = drag_xy + lax.ppermute(second, 'gx', x_first)  0.66 us
  transfers between devices with their start and end apart: 10, of which 2 were waited for; matrix products, arithmetic and copies ran while one was open for 0% of the time, Pallas kernels for 25%

profile of v4, /device:TPU:0, one launch (start us, length us, event | category | flops | bytes accessed | tf_op | source)
XLA Modules:
  0.0 24.7 jit_solution(9089001539004385806)
XLA Ops:
  0.6 0.0 copy-start
  0.6 0.1 pad_add_fusion.par_ref
  0.7 2.8 %shard_map.67 = (f32[440,128]{1,0:T(8,128)S(1)}, f32[368,128]{1,0:T(8,128)S(1)}, f32[72,128]{1,0:T(8,128)S(1)}, f32[4,4,16,128]{3,2,1,0:T(8,128)S(1)}, f32[8,128]{1,0:T(8,128)}) custom-call(s32[3]{0:T(128)S(1)} %pad_add_fusion.par_ref, f32[2,19,4,16,128]{4,3,2,1,0:T(8,128)} %states_ref.1, f32[19,4,16,128]{3,2,1,0:T(8,128)} %adj_ref.3, ...), custom_call_target="tpu_custom_call" | custom-call | bytes 3600000 | tf_op jit(solution)/shard_map/pallas_call | solution.py:837
  3.5 0.7 %shard_map.68 = (f32[216,128]{1,0:T(8,128)S(1)}, f32[72,128]{1,0:T(8,128)S(1)}, f32[72,128]{1,0:T(8,128)S(1)}) custom-call(s32[3]{0:T(128)S(1)} %pad_add_fusion.par_ref, f32[19,4,16,128]{3,2,1,0:T(8,128)S(1)} %copy-done, f32[4,4,16,128]{3,2,1,0:T(8,128)S(1)} %get-tuple-element.53.ub_ref, f32[72,128]{1,0:T(8,128)S(1)} %get-tuple-element.49.cols_ref), custom_call_target="tpu_custom_call" | custom-call | bytes 14400000 | tf_op jit(solution)/shard_map/pallas_call | solution.py:837
  4.2 3.4 %collective-permute-start.4 = (f32[72,128]{1,0:T(8,128)S(1)}, f32[72,128]{1,0:T(8,128)S(1)}, u32[]{:S(2)}, u32[]{:S(2)}) collective-permute-start(f32[72,128]{1,0:T(8,128)S(1)} %get-tuple-element.56), channel_id=1, source_target_pairs={{0,28},{4,24},{8,20},{12,16},{16,12},{20,8},{24,4},{28,0},{1,29},{... | collective-permute-start | bytes 110600 | tf_op jit(solution)/shard_map/ppermute | solution.py:863
  7.6 0.8 %collective-permute-start.1 = (f32[72,128]{1,0:T(8,128)S(1)}, f32[72,128]{1,0:T(8,128)S(1)}, u32[]{:S(2)}, u32[]{:S(2)}) collective-permute-start(f32[72,128]{1,0:T(8,128)S(1)} %get-tuple-element.49.cols_ref), channel_id=1, source_target_pairs={{0,24},{8,16},{16,8},{24,0},{1,25},{9,17},{17,9},{25,1},{2,26},{10... | collective-permute-start | bytes 110600 | tf_op jit(solution)/shard_map/ppermute | solution.py:895
  8.4 1.2 %collective-permute-start.3 = (f32[72,128]{1,0:T(8,128)S(1)}, f32[72,128]{1,0:T(8,128)S(1)}, u32[]{:S(2)}, u32[]{:S(2)}) collective-permute-start(f32[72,128]{1,0:T(8,128)S(1)} %get-tuple-element.55), channel_id=1, source_target_pairs={{0,12},{4,8},{8,4},{12,0},{16,28},{20,24},{24,20},{28,16},{1,13},{... | collective-permute-start | bytes 110600 | tf_op jit(solution)/shard_map/ppermute | solution.py:863
  9.7 0.9 %collective-permute-start = (f32[440,128]{1,0:T(8,128)S(1)}, f32[440,128]{1,0:T(8,128)S(1)}, u32[]{:S(2)}, u32[]{:S(2)}) collective-permute-start(f32[440,128]{1,0:T(8,128)S(1)} %get-tuple-element.51), channel_id=1, source_target_pairs={{0,8},{8,0},{16,24},{24,16},{1,9},{9,1},{17,25},{25,17},{2,10},{10... | collective-permute-start | bytes 675848 | tf_op jit(solution)/shard_map/ppermute | solution.py:896
  10.6 0.0 collective-permute-done.4.yb_ref
  10.6 0.4 %collective-permute-done.1.xc_ref = f32[72,128]{1,0:T(8,128)S(1)} collective-permute-done((f32[72,128]{1,0:T(8,128)S(1)}, f32[72,128]{1,0:T(8,128)S(1)}, u32[]{:S(2)}, u32[]{:S(2)}) %collective-permute-start.1) | collective-permute-done | bytes 36896 | tf_op jit(solution)/shard_map/ppermute | solution.py:895
  11.0 0.7 %collective-permute-start.5 = (f32[8,128]{1,0:T(8,128)S(1)}, f32[8,128]{1,0:T(8,128)S(1)}, u32[]{:S(2)}, u32[]{:S(2)}) collective-permute-start(f32[8,128]{1,0:T(8,128)S(1)} %slice_add_fusion), channel_id=1, source_target_pairs={{0,8},{8,0},{16,24},{24,16},{1,9},{9,1},{17,25},{25,17},{2,10},{10... | collective-permute-start | bytes 12296 | tf_op jit(solution)/shard_map/ppermute | solution.py:925
  11.7 0.0 collective-permute-done.xa_ref
  11.7 1.5 %collective-permute-start.8 = (f32[368,128]{1,0:T(8,128)S(1)}, f32[368,128]{1,0:T(8,128)S(1)}, u32[]{:S(2)}, u32[]{:S(2)}) collective-permute-start(f32[368,128]{1,0:T(8,128)S(1)} %get-tuple-element.61), channel_id=1, source_target_pairs={{0,24},{8,16},{16,8},{24,0},{1,25},{9,17},{17,9},{25,1},{2,26},{10... | collective-permute-start | bytes 565256 | tf_op jit(solution)/shard_map/ppermute | solution.py:915
  13.2 0.5 %collective-permute-done.2.y_ref = f32[216,128]{1,0:T(8,128)S(1)} collective-permute-done((f32[216,128]{1,0:T(8,128)S(1)}, f32[216,128]{1,0:T(8,128)S(1)}, u32[]{:S(2)}, u32[]{:S(2)}) %collective-permute-start.2) | collective-permute-done | bytes 110624 | tf_op jit(solution)/shard_map/ppermute | solution.py:898
  13.7 0.8 %shard_map.69 = (f32[96,128]{1,0:T(8,128)S(1)}, f32[56,128]{1,0:T(8,128)S(1)}, f32[56,128]{1,0:T(8,128)S(1)}, f32[8,128]{1,0:T(8,128)S(1)}) custom-call(s32[3]{0:T(128)S(1)} %pad_add_fusion.par_ref, f32[72,128]{1,0:T(8,128)S(1)} %get-tuple-element.49.cols_ref, f32[440,128]{1,0:T(8,128)S(1)} %collective-permute-done.xa_ref, ...), custom_call_target="tpu_custom_call" | custom-call | bytes 3600000 | tf_op jit(solution)/shard_map/pallas_call | solution.py:837
  14.4 0.0 collective-permute-done.5
  14.5 1.6 %collective-permute-start.6 = (f32[56,128]{1,0:T(8,128)S(1)}, f32[56,128]{1,0:T(8,128)S(1)}, u32[]{:S(2)}, u32[]{:S(2)}) collective-permute-start(f32[56,128]{1,0:T(8,128)S(1)} %constant_dynamic-update-slice_fusion.1), channel_id=1, source_target_pairs={{0,1},{1,0},{2,3},{3,2},{4,5},{5,4},{6,7},{7,6},{8,9},{9,8},{10,11... | collective-permute-start | bytes 86024 | tf_op jit(solution)/shard_map/ppermute | solution.py:929
  16.1 2.5 %collective-permute-start.7 = (f32[56,128]{1,0:T(8,128)S(1)}, f32[56,128]{1,0:T(8,128)S(1)}, u32[]{:S(2)}, u32[]{:S(2)}) collective-permute-start(f32[56,128]{1,0:T(8,128)S(1)} %get-tuple-element.71), channel_id=1, source_target_pairs={{0,3},{1,2},{2,1},{3,0},{4,7},{5,6},{6,5},{7,4},{8,11},{9,10},{10,... | collective-permute-start | bytes 86024 | tf_op jit(solution)/shard_map/ppermute | solution.py:928
  18.6 0.1 collective-permute-start.9
  18.7 3.1 %shard_map.70 = (f32[19,4,16,128]{3,2,1,0:T(8,128)S(1)}, f32[4,16,128]{2,1,0:T(8,128)S(1)}, f32[4,16,128]{2,1,0:T(8,128)S(1)}, f32[19,16,128]{2,1,0:T(8,128)S(1)...) custom-call(s32[3]{0:T(128)S(1)} %pad_add_fusion.par_ref, f32[2,19,4,16,128]{4,3,2,1,0:T(8,128)S(1)} %copy-done.1, ...), custom_call_target="tpu_custom_call" | custom-call | bytes 14400000 | tf_op jit(solution)/shard_map/pallas_call | solution.py:837
  21.8 0.0 collective-permute-done.6.za_ref
  21.9 2.2 %shard_map.71 = (f32[19,4,16,128]{3,2,1,0:T(8,128)}, f32[4,16,128]{2,1,0:T(8,128)}, f32[8,128]{1,0:T(8,128)S(1)}) custom-call(s32[3]{0:T(128)S(1)} %pad_add_fusion.par_ref, s32[4,16,128]{2,1,0:T(8,128)S(1)} %copy-done.2, f32[96,128]{1,0:T(8,128)S(1)} %get-tuple-element.57.zown_ref, f32[56,128]{1,0:T(8,128)S(1)} %collective-permute-done.6.za_ref, ...), custom_call_target="tpu_custom_call" | custom-call | bytes 3600000 | tf_op jit(solution)/shard_map/pallas_call | solution.py:837
  24.0 0.0 collective-permute-done.9.refs_1_
  24.1 0.6 %shard_map.72 = f32[1,1]{1,0:T(1,128)} custom-call(f32[8,128]{1,0:T(8,128)S(1)} %get-tuple-element.72.refs_0_, f32[8,128]{1,0:T(8,128)S(1)} %collective-permute-done.9.refs_1_, f32[8,128]{1,0:T(8,128)S(1)} %get-tuple-element.70.refs_2_), custom_call_target="tpu_custom_call" | custom-call | bytes 3600000 | tf_op jit(solution)/shard_map/pallas_call | solution.py:837
  (12 shorter events, 0.0 us)
Async XLA Ops:
  0.6 2.9 %copy-start = (f32[19,4,16,128]{3,2,1,0:T(8,128)S(1)}, f32[19,4,16,128]{3,2,1,0:T(8,128)}, u32[]{:S(2)}) copy-start(f32[19,4,16,128]{3,2,1,0:T(8,128)} %adj_ref.3) | copy-start | bytes 1867780
  0.7 18.0 %copy-start.1 = (f32[2,19,4,16,128]{4,3,2,1,0:T(8,128)S(1)}, f32[2,19,4,16,128]{4,3,2,1,0:T(8,128)}, u32[]{:S(2)}) copy-start(f32[2,19,4,16,128]{4,3,2,1,0:T(8,128)} %states_ref.1) | copy-start | bytes 3735556
  4.2 6.4 %collective-permute-start.4 = (f32[72,128]{1,0:T(8,128)S(1)}, f32[72,128]{1,0:T(8,128)S(1)}, u32[]{:S(2)}, u32[]{:S(2)}) collective-permute-start(f32[72,128]{1,0:T(8,128)S(1)} %get-tuple-element.56), channel_id=1, source_target_pairs={{0,28},{4,24},{8,20},{12,16},{16,12},{20,8},{24,4},{28,0},{1,29},{... | collective-permute-start | bytes 110600 | tf_op jit(solution)/shard_map/ppermute | solution.py:863
  7.6 3.4 %collective-permute-start.1 = (f32[72,128]{1,0:T(8,128)S(1)}, f32[72,128]{1,0:T(8,128)S(1)}, u32[]{:S(2)}, u32[]{:S(2)}) collective-permute-start(f32[72,128]{1,0:T(8,128)S(1)} %get-tuple-element.49.cols_ref), channel_id=1, source_target_pairs={{0,24},{8,16},{16,8},{24,0},{1,25},{9,17},{17,9},{25,1},{2,26},{10... | collective-permute-start | bytes 110600 | tf_op jit(solution)/shard_map/ppermute | solution.py:895
  8.4 5.2 %collective-permute-start.2 = (f32[216,128]{1,0:T(8,128)S(1)}, f32[216,128]{1,0:T(8,128)S(1)}, u32[]{:S(2)}, u32[]{:S(2)}) collective-permute-start(f32[216,128]{1,0:T(8,128)S(1)} %get-tuple-element.54), channel_id=1, source_target_pairs={{0,4},{4,0},{1,5},{5,1},{2,6},{6,2},{3,7},{7,3},{8,12},{12,8},{9,1... | collective-permute-start | bytes 331784 | tf_op jit(solution)/shard_map/ppermute | solution.py:898
  8.4 4.7 %collective-permute-start.3 = (f32[72,128]{1,0:T(8,128)S(1)}, f32[72,128]{1,0:T(8,128)S(1)}, u32[]{:S(2)}, u32[]{:S(2)}) collective-permute-start(f32[72,128]{1,0:T(8,128)S(1)} %get-tuple-element.55), channel_id=1, source_target_pairs={{0,12},{4,8},{8,4},{12,0},{16,28},{20,24},{24,20},{28,16},{1,13},{... | collective-permute-start | bytes 110600 | tf_op jit(solution)/shard_map/ppermute | solution.py:863
  9.7 2.0 %collective-permute-start = (f32[440,128]{1,0:T(8,128)S(1)}, f32[440,128]{1,0:T(8,128)S(1)}, u32[]{:S(2)}, u32[]{:S(2)}) collective-permute-start(f32[440,128]{1,0:T(8,128)S(1)} %get-tuple-element.51), channel_id=1, source_target_pairs={{0,8},{8,0},{16,24},{24,16},{1,9},{9,1},{17,25},{25,17},{2,10},{10... | collective-permute-start | bytes 675848 | tf_op jit(solution)/shard_map/ppermute | solution.py:896
  11.0 3.4 %collective-permute-start.5 = (f32[8,128]{1,0:T(8,128)S(1)}, f32[8,128]{1,0:T(8,128)S(1)}, u32[]{:S(2)}, u32[]{:S(2)}) collective-permute-start(f32[8,128]{1,0:T(8,128)S(1)} %slice_add_fusion), channel_id=1, source_target_pairs={{0,8},{8,0},{16,24},{24,16},{1,9},{9,1},{17,25},{25,17},{2,10},{10... | collective-permute-start | bytes 12296 | tf_op jit(solution)/shard_map/ppermute | solution.py:925
  11.7 7.0 %collective-permute-start.8 = (f32[368,128]{1,0:T(8,128)S(1)}, f32[368,128]{1,0:T(8,128)S(1)}, u32[]{:S(2)}, u32[]{:S(2)}) collective-permute-start(f32[368,128]{1,0:T(8,128)S(1)} %get-tuple-element.61), channel_id=1, source_target_pairs={{0,24},{8,16},{16,8},{24,0},{1,25},{9,17},{17,9},{25,1},{2,26},{10... | collective-permute-start | bytes 565256 | tf_op jit(solution)/shard_map/ppermute | solution.py:915
  14.5 7.4 %collective-permute-start.6 = (f32[56,128]{1,0:T(8,128)S(1)}, f32[56,128]{1,0:T(8,128)S(1)}, u32[]{:S(2)}, u32[]{:S(2)}) collective-permute-start(f32[56,128]{1,0:T(8,128)S(1)} %constant_dynamic-update-slice_fusion.1), channel_id=1, source_target_pairs={{0,1},{1,0},{2,3},{3,2},{4,5},{5,4},{6,7},{7,6},{8,9},{9,8},{10,11... | collective-permute-start | bytes 86024 | tf_op jit(solution)/shard_map/ppermute | solution.py:929
  16.1 5.7 %copy-start.2 = (s32[4,16,128]{2,1,0:T(8,128)S(1)}, s32[4,16,128]{2,1,0:T(8,128)}, u32[]{:S(2)}) copy-start(s32[4,16,128]{2,1,0:T(8,128)} %mask_ref.1) | copy-start | bytes 98308
  16.1 5.7 %collective-permute-start.7 = (f32[56,128]{1,0:T(8,128)S(1)}, f32[56,128]{1,0:T(8,128)S(1)}, u32[]{:S(2)}, u32[]{:S(2)}) collective-permute-start(f32[56,128]{1,0:T(8,128)S(1)} %get-tuple-element.71), channel_id=1, source_target_pairs={{0,3},{1,2},{2,1},{3,0},{4,7},{5,6},{6,5},{7,4},{8,11},{9,10},{10,... | collective-permute-start | bytes 86024 | tf_op jit(solution)/shard_map/ppermute | solution.py:928
  18.6 5.5 %collective-permute-start.9 = (f32[8,128]{1,0:T(8,128)S(1)}, f32[8,128]{1,0:T(8,128)S(1)}, u32[]{:S(2)}, u32[]{:S(2)}) collective-permute-start(f32[8,128]{1,0:T(8,128)S(1)} %get-tuple-element.72.refs_0_), channel_id=1, source_target_pairs={{0,2},{1,3},{2,0},{3,1},{4,6},{5,7},{6,4},{7,5},{8,10},{9,11},{10,... | collective-permute-start | bytes 12296 | tf_op jit(solution)/shard_map/ppermute | solution.py:948

commit v5 on v4

--- a/solution.py
+++ b/solution.py
@@ -230,7 +230,6 @@
     mask_hbm,
     a_ref,
     b_ref,
-    cols_ref,
     ub_ref,
     drag_ref,
     states_ref,
@@ -245,38 +244,18 @@
         pltpu.make_async_copy(src, dst, sems.at[k])
         for k, (src, dst) in enumerate(
             (
-                (adj_hbm, adj_ref),
                 (states_hbm.at[1], states_ref.at[1]),
                 (por_hbm, por_ref),
                 (mask_hbm, mask_ref),
                 (states_hbm.at[0, 1:3], states_ref.at[0, 1:3]),
                 (states_hbm.at[0, 7:15], states_ref.at[0, 7:15]),
+                (adj_hbm, adj_ref),
             )
         )
     ]
     for copy in copies:
         copy.start()
-    copies[0].wait()
-
-    pair = lax.broadcasted_iota(jnp.int32, (8, nz), 1) // 2
-
-    def columns(acc, g, t, wanted):
-        for k, q in enumerate(ZGROUPS[g]):
-            if q not in wanted:
-                continue
-            cz = VEL[q][2] if q < 19 else 0
-            for x in range(nx):
-                start = 32 * (k // 2) + 4 * (x + 2) + 2 * (k % 2)
-                value = cell_rows(adj_ref, ub_ref, q, x, slice(8 * t, 8 * t + 8))
-                acc = jnp.where(pair == start // 2, turn(value, start + 1 - cz), acc)
-        row = g * ny + 8 * t
-        cols_ref[row : row + 8] = acc
-        a_ref[NSLOT * ny + row : NSLOT * ny + row + 8] = acc
-
-    for g in range(4):
-        for t in range(tiles):
-            columns(jnp.zeros((8, nz), jnp.float32), g, t, range(19))
-    for copy in copies[1:]:
+    for copy in copies[:5]:
         copy.wait()
 
     def cells(x, carry):
@@ -298,11 +277,9 @@
 
     drag = lax.fori_loop(0, nx, cells, jnp.zeros((8, nz), jnp.float32))
     drag_ref[...] = drag
-    for t in range(tiles):
-        row = 3 * ny + 8 * t
-        columns(cols_ref[row : row + 8], 3, t, UB)
-    cols_ref[4 * ny :] = drag
-    a_ref[(NSLOT + 4) * ny :] = drag
+    a_ref[NSLOT * ny :] = drag
+    b_ref[NSLOT * ny :] = drag
+    copies[5].wait()
 
     def fill_x(out_ref, sign):
         for names, offset, x in (
@@ -324,8 +301,26 @@
             fill_x(b_ref, -sa)
 
 
-def pack_y_kernel(par_ref, adj_ref, ub_ref, cols_ref, y_ref, ya_ref, yb_ref):
+def column_pair(acc, value, pair, q, k, plane):
+    start = 32 * (k // 2) + 4 * plane + 2 * (k % 2)
+    cz = VEL[q][2] if q < 19 else 0
+    return jnp.where(pair == start // 2, turn(value, start + 1 - cz), acc)
+
+
+def pack_y_kernel(
+    par_ref, adj_ref, ub_ref, drag_ref, cols_ref, y_ref, ya_ref, yb_ref
+):
     nx, ny, nz = adj_ref.shape[1:]
+    pair = lax.broadcasted_iota(jnp.int32, (8, nz), 1) // 2
+    for g, group in enumerate(ZGROUPS):
+        for t in range(ny // 8):
+            acc = jnp.zeros((8, nz), jnp.float32)
+            for k, q in enumerate(group):
+                for x in range(nx):
+                    value = cell_rows(adj_ref, ub_ref, q, x, slice(8 * t, 8 * t + 8))
+                    acc = column_pair(acc, value, pair, q, k, x + 2)
+            row = g * ny + 8 * t
+            cols_ref[row : row + 8] = acc
     y_block = y_rows(nx) + EDGE_ROWS
     corner_block = CORNER + EDGE_ROWS
 
@@ -363,7 +358,8 @@
         last = place * corner_block + CORNER
         out_ref[row:last] = jnp.zeros((last - row, nz), jnp.float32)
 
-    drag = cols_ref[4 * ny :]
+    drag = drag_ref[...]
+    cols_ref[4 * ny :] = drag
     y_ref[2 * y_block :] = drag
     ya_ref[2 * corner_block :] = drag
     yb_ref[2 * corner_block :] = drag
@@ -419,15 +415,38 @@
         high = turn(jnp.where(even_x, va, vb), 16)
         return jnp.where(plane < 2, low, jnp.where(plane > 5, high, own))
 
-    offset = xa_ref.shape[0] - 8 - 4 * ny
-    for g in range(4):
-        for t in range(tiles):
-            row = g * ny + 8 * t
-            ext[g, base + 8 * t : base + 8 * t + 8, :] = along_x(
-                cols_ref[row : row + 8],
-                xa_ref[offset + row : offset + row + 8],
-                xc_ref[row : row + 8],
-            )
+    pair = lane // 2
+
+    def fill_main(sign):
+        halo = {}
+        for names, offset, p in (
+            (near(0, sign), 0, 6 if sign > 0 else 1),
+            (far(0, sign), 18, 7 if sign > 0 else 0),
+        ):
+            for k, q in enumerate(names):
+                halo.setdefault(q, []).append((k + offset, p))
+        for g, group in enumerate(ZGROUPS):
+            for t in range(tiles):
+                rows = slice(g * ny + 8 * t, g * ny + 8 * t + 8)
+                acc = jnp.where(
+                    plane < 2 if sign > 0 else plane > 5,
+                    turn(xc_ref[rows], -16 * sign),
+                    cols_ref[rows],
+                )
+                for k, q in enumerate(group):
+                    for at, p in halo.get(q, ()):
+                        row = at * ny + 8 * t
+                        acc = column_pair(acc, xa_ref[row : row + 8], pair, q, k, p)
+                ext[g, base + 8 * t : base + 8 * t + 8, :] = acc
+
+    @pl.when(par_ref[0] == 0)
+    def _():
+        fill_main(1)
+
+    @pl.when(par_ref[0] == 1)
+    def _():
+        fill_main(-1)
+
     y_block = (y_ref.shape[0] - 8) // 2
     corner_block = CORNER + EDGE_ROWS
 
@@ -862,21 +881,15 @@
         pairs = [(a * gy + c, b * gy + d) for a, b in x_pairs for c, d in y_pairs]
         return lax.ppermute(message, ("gx", "gy"), pairs)
 
-    rows_x = NSLOT * ny
+    rows_x = NSLOT * ny + 8
     rows_y = 2 * (y_rows(nx) + EDGE_ROWS) + 8
     rows_c = 2 * (CORNER + EDGE_ROWS) + 8
     rows_z = 2 * height + 8
     rides = (gx, gy, gz) == (4, 2, 4)
-    xa, xb, cols, ub, drag = call(
+    xa, xb, ub, drag = call(
         pack_x_kernel,
         (parity, primal_states, adjoint_last, porosity, solid_mask),
-        [
-            (rows_x + 4 * ny + 8, nz),
-            (rows_x, nz),
-            (4 * ny + 8, nz),
-            (4, nx, ny, nz),
-            (8, nz),
-        ],
+        [(rows_x, nz), (rows_x, nz), (4, nx, ny, nz), (8, nz)],
         [
             pltpu.VMEM((2, 19, nx, ny, nz), f32),
             pltpu.VMEM((19, nx, ny, nz), f32),
@@ -886,10 +899,10 @@
         ],
         HBM,
     )
-    y, ya, yb = call(
+    cols, y, ya, yb = call(
         pack_y_kernel,
-        (parity, adjoint_last, ub, cols),
-        [(rows_y, nz), (rows_c, nz), (rows_c, nz)],
+        (parity, adjoint_last, ub, drag),
+        [(4 * ny + 8, nz), (rows_y, nz), (rows_c, nz), (rows_c, nz)],
         micros=4,
     )
     xc = lax.ppermute(cols, "gx", x_second)
@@ -911,7 +924,7 @@
         block = CORNER + EDGE_ROWS
         yb = both(yb, block, lambda m, pairs: diagonal(m, x_second, pairs))
         ya = both(ya, block, lambda m, pairs: diagonal(m, x_first, pairs))
-    xb, xa = lax.optimization_barrier((xb, xa))
+    xb, yb = lax.optimization_barrier((xb, yb))
     xb = lax.ppermute(xb, "gx", x_second)
 
     zown, za, zb, drag_xy = call(

time: 24.8 us -> 24.4 us (0.984)
  Pallas kernels: 10.1 us -> 9.69 us
  waiting for transfers between devices: 0.96 us -> 1.24 us
    pallas_call x6, Pallas kernels: 10.1 us -> 9.69 us  [call(): pl.pallas_call(kernel, out_shape=[jax.ShapeDtypeStruct(s, jnp.float32) fo...]
    ppermute x1, starting transfers between devices: 1.47 us -> 1.17 us  [body(): xb = lax.ppermute(xb, 'gx', x_second)]
  transfers between devices with their start and end apart: 10 -> 10, of which waited for: 2 -> 3; matrix products, arithmetic and copies ran while one was open for 0% -> 0% of each run, Pallas kernels for 25% -> 25%
where the time goes in v5:
time: 24.4 us; the launch traced here: 24.2 us
  starting transfers between devices  12.5 us (51%)
  Pallas kernels  9.69 us (40%)
  waiting for transfers between devices  1.24 us (5%)
  between operations  0.75 us (3%)
    pallas_call x6, Pallas kernels, call(): pl.pallas_call(kernel, out_shape=[jax.ShapeDtypeStruct(s, jnp.float32) fo...  9.69 us
    ppermute x2, starting transfers between devices, diagonal(): return lax.ppermute(message, ('gx', 'gy'), pairs)  4.64 us
    ppermute x1, starting transfers between devices, body(): zb = lax.ppermute(zb, 'gz', z_second)  2.47 us
    ppermute x1, starting transfers between devices, body(): za = lax.ppermute(za, 'gz', z_first)  1.64 us
    ppermute x1, starting transfers between devices, body(): xb = lax.ppermute(xb, 'gx', x_second)  1.17 us
    ppermute x1, starting transfers between devices, body(): xa = lax.ppermute(xa, 'gx', x_first)  0.93 us
    ppermute x1, starting transfers between devices, body(): xc = lax.ppermute(cols, 'gx', x_second)  0.82 us
    ppermute x1, waiting for transfers between devices, body(): y = lax.ppermute(y, 'gy', y_first)  0.72 us
  transfers between devices with their start and end apart: 10, of which 3 were waited for; matrix products, arithmetic and copies ran while one was open for 0% of the time, Pallas kernels for 25%

profile of v5, /device:TPU:0, one launch (start us, length us, event | category | flops | bytes accessed | tf_op | source)
XLA Modules:
  0.0 24.2 jit_solution(11644563296073568427)
XLA Ops:
  0.6 0.0 copy-start
  0.6 0.1 pad_add_fusion.par_ref
  0.7 2.0 %shard_map.67 = (f32[376,128]{1,0:T(8,128)S(1)}, f32[376,128]{1,0:T(8,128)S(1)}, f32[4,4,16,128]{3,2,1,0:T(8,128)S(1)}, f32[8,128]{1,0:T(8,128)S(1)}) custom-call(s32[3]{0:T(128)S(1)} %pad_add_fusion.par_ref, f32[2,19,4,16,128]{4,3,2,1,0:T(8,128)} %states_ref.1, f32[19,4,16,128]{3,2,1,0:T(8,128)} %adj_ref.3, f32[4,16,128]{2,1,0:T(8,128)} %por_hbm.1, ...), custom_call_target="tpu_custom_call" | custom-call | bytes 3600000 | tf_op jit(solution)/shard_map/pallas_call | solution.py:856
  2.8 0.9 %shard_map.68 = (f32[72,128]{1,0:T(8,128)S(1)}, f32[216,128]{1,0:T(8,128)S(1)}, f32[72,128]{1,0:T(8,128)S(1)}, f32[72,128]{1,0:T(8,128)S(1)}) custom-call(s32[3]{0:T(128)S(1)} %pad_add_fusion.par_ref, f32[19,4,16,128]{3,2,1,0:T(8,128)S(1)} %copy-done, f32[4,4,16,128]{3,2,1,0:T(8,128)S(1)} %get-tuple-element.50.ub_ref, f32[8,128]{1,0:T(8,128)S(1)} %get-tuple-element.51.drag_ref), custom_call_target="tpu_custom_call" | custom-call | bytes 14400000 | tf_op jit(solution)/shard_map/pallas_call | solution.py:856
  3.7 3.4 %collective-permute-start.4 = (f32[72,128]{1,0:T(8,128)S(1)}, f32[72,128]{1,0:T(8,128)S(1)}, u32[]{:S(2)}, u32[]{:S(2)}) collective-permute-start(f32[72,128]{1,0:T(8,128)S(1)} %get-tuple-element.57), channel_id=1, source_target_pairs={{0,28},{4,24},{8,20},{12,16},{16,12},{20,8},{24,4},{28,0},{1,29},{... | collective-permute-start | bytes 110600 | tf_op jit(solution)/shard_map/ppermute | solution.py:882
  7.1 0.8 %collective-permute-start.1 = (f32[72,128]{1,0:T(8,128)S(1)}, f32[72,128]{1,0:T(8,128)S(1)}, u32[]{:S(2)}, u32[]{:S(2)}) collective-permute-start(f32[72,128]{1,0:T(8,128)S(1)} %get-tuple-element.52.cols_ref), channel_id=1, source_target_pairs={{0,24},{8,16},{16,8},{24,0},{1,25},{9,17},{17,9},{25,1},{2,26},{10... | collective-permute-start | bytes 110600 | tf_op jit(solution)/shard_map/ppermute | solution.py:908
  7.9 0.0 collective-permute-start.2
  7.9 1.2 %collective-permute-start.3 = (f32[72,128]{1,0:T(8,128)S(1)}, f32[72,128]{1,0:T(8,128)S(1)}, u32[]{:S(2)}, u32[]{:S(2)}) collective-permute-start(f32[72,128]{1,0:T(8,128)S(1)} %get-tuple-element.55), channel_id=1, source_target_pairs={{0,12},{4,8},{8,4},{12,0},{16,28},{20,24},{24,20},{28,16},{1,13},{... | collective-permute-start | bytes 110600 | tf_op jit(solution)/shard_map/ppermute | solution.py:882
  9.1 0.9 %collective-permute-start = (f32[376,128]{1,0:T(8,128)S(1)}, f32[376,128]{1,0:T(8,128)S(1)}, u32[]{:S(2)}, u32[]{:S(2)}) collective-permute-start(f32[376,128]{1,0:T(8,128)S(1)} %get-tuple-element.53), channel_id=1, source_target_pairs={{0,8},{8,0},{16,24},{24,16},{1,9},{9,1},{17,25},{25,17},{2,10},{10... | collective-permute-start | bytes 577544 | tf_op jit(solution)/shard_map/ppermute | solution.py:909
  10.1 0.4 %collective-permute-done.1.xc_ref = f32[72,128]{1,0:T(8,128)S(1)} collective-permute-done((f32[72,128]{1,0:T(8,128)S(1)}, f32[72,128]{1,0:T(8,128)S(1)}, u32[]{:S(2)}, u32[]{:S(2)}) %collective-permute-start.1) | collective-permute-done | bytes 36896 | tf_op jit(solution)/shard_map/ppermute | solution.py:908
  10.5 0.7 %collective-permute-start.5 = (f32[8,128]{1,0:T(8,128)S(1)}, f32[8,128]{1,0:T(8,128)S(1)}, u32[]{:S(2)}, u32[]{:S(2)}) collective-permute-start(f32[8,128]{1,0:T(8,128)S(1)} %slice_add_fusion), channel_id=1, source_target_pairs={{0,8},{8,0},{16,24},{24,16},{1,9},{9,1},{17,25},{25,17},{2,10},{10... | collective-permute-start | bytes 12296 | tf_op jit(solution)/shard_map/ppermute | solution.py:938
  11.2 1.2 %collective-permute-start.8 = (f32[376,128]{1,0:T(8,128)S(1)}, f32[376,128]{1,0:T(8,128)S(1)}, u32[]{:S(2)}, u32[]{:S(2)}) collective-permute-start(f32[376,128]{1,0:T(8,128)S(1)} %get-tuple-element.63), channel_id=1, source_target_pairs={{0,24},{8,16},{16,8},{24,0},{1,25},{9,17},{17,9},{25,1},{2,26},{10... | collective-permute-start | bytes 577544 | tf_op jit(solution)/shard_map/ppermute | solution.py:928
  12.3 0.1 collective-permute-done.3.ya_ref
  12.4 0.7 %collective-permute-done.2.y_ref = f32[216,128]{1,0:T(8,128)S(1)} collective-permute-done((f32[216,128]{1,0:T(8,128)S(1)}, f32[216,128]{1,0:T(8,128)S(1)}, u32[]{:S(2)}, u32[]{:S(2)}) %collective-permute-start.2) | collective-permute-done | bytes 110624 | tf_op jit(solution)/shard_map/ppermute | solution.py:911
  13.2 0.0 collective-permute-done.xa_ref
  13.2 0.9 %shard_map.69 = (f32[96,128]{1,0:T(8,128)S(1)}, f32[56,128]{1,0:T(8,128)S(1)}, f32[56,128]{1,0:T(8,128)S(1)}, f32[8,128]{1,0:T(8,128)S(1)}) custom-call(s32[3]{0:T(128)S(1)} %pad_add_fusion.par_ref, f32[72,128]{1,0:T(8,128)S(1)} %get-tuple-element.52.cols_ref, f32[376,128]{1,0:T(8,128)S(1)} %collective-permute-done.xa_ref, ...), custom_call_target="tpu_custom_call" | custom-call | bytes 3600000 | tf_op jit(solution)/shard_map/pallas_call | solution.py:856
  14.1 0.0 collective-permute-done.5
  14.1 1.6 %collective-permute-start.6 = (f32[56,128]{1,0:T(8,128)S(1)}, f32[56,128]{1,0:T(8,128)S(1)}, u32[]{:S(2)}, u32[]{:S(2)}) collective-permute-start(f32[56,128]{1,0:T(8,128)S(1)} %constant_dynamic-update-slice_fusion.1), channel_id=1, source_target_pairs={{0,1},{1,0},{2,3},{3,2},{4,5},{5,4},{6,7},{7,6},{8,9},{9,8},{10,11... | collective-permute-start | bytes 86024 | tf_op jit(solution)/shard_map/ppermute | solution.py:942
  15.7 2.5 %collective-permute-start.7 = (f32[56,128]{1,0:T(8,128)S(1)}, f32[56,128]{1,0:T(8,128)S(1)}, u32[]{:S(2)}, u32[]{:S(2)}) collective-permute-start(f32[56,128]{1,0:T(8,128)S(1)} %get-tuple-element.73), channel_id=1, source_target_pairs={{0,3},{1,2},{2,1},{3,0},{4,7},{5,6},{6,5},{7,4},{8,11},{9,10},{10,... | collective-permute-start | bytes 86024 | tf_op jit(solution)/shard_map/ppermute | solution.py:941
  18.2 0.1 collective-permute-start.9
  18.3 3.1 %shard_map.70 = (f32[19,4,16,128]{3,2,1,0:T(8,128)S(1)}, f32[4,16,128]{2,1,0:T(8,128)S(1)}, f32[4,16,128]{2,1,0:T(8,128)S(1)}, f32[19,16,128]{2,1,0:T(8,128)S(1)...) custom-call(s32[3]{0:T(128)S(1)} %pad_add_fusion.par_ref, f32[2,19,4,16,128]{4,3,2,1,0:T(8,128)S(1)} %copy-done.1, ...), custom_call_target="tpu_custom_call" | custom-call | bytes 14400000 | tf_op jit(solution)/shard_map/pallas_call | solution.py:856
  21.4 0.0 collective-permute-done.6.za_ref
  21.5 2.2 %shard_map.71 = (f32[19,4,16,128]{3,2,1,0:T(8,128)}, f32[4,16,128]{2,1,0:T(8,128)}, f32[8,128]{1,0:T(8,128)S(1)}) custom-call(s32[3]{0:T(128)S(1)} %pad_add_fusion.par_ref, s32[4,16,128]{2,1,0:T(8,128)S(1)} %copy-done.2, f32[96,128]{1,0:T(8,128)S(1)} %get-tuple-element.59.zown_ref, f32[56,128]{1,0:T(8,128)S(1)} %collective-permute-done.6.za_ref, ...), custom_call_target="tpu_custom_call" | custom-call | bytes 3600000 | tf_op jit(solution)/shard_map/pallas_call | solution.py:856
  23.7 0.6 %shard_map.72 = f32[1,1]{1,0:T(1,128)} custom-call(f32[8,128]{1,0:T(8,128)S(1)} %get-tuple-element.74.refs_0_, f32[8,128]{1,0:T(8,128)S(1)} %collective-permute-done.9.refs_1_, f32[8,128]{1,0:T(8,128)S(1)} %get-tuple-element.72.refs_2_), custom_call_target="tpu_custom_call" | custom-call | bytes 3600000 | tf_op jit(solution)/shard_map/pallas_call | solution.py:856
  (12 shorter events, 0.0 us)
Async XLA Ops:
  0.6 2.1 %copy-start = (f32[19,4,16,128]{3,2,1,0:T(8,128)S(1)}, f32[19,4,16,128]{3,2,1,0:T(8,128)}, u32[]{:S(2)}) copy-start(f32[19,4,16,128]{3,2,1,0:T(8,128)} %adj_ref.3) | copy-start | bytes 1867780
  0.7 17.6 %copy-start.1 = (f32[2,19,4,16,128]{4,3,2,1,0:T(8,128)S(1)}, f32[2,19,4,16,128]{4,3,2,1,0:T(8,128)}, u32[]{:S(2)}) copy-start(f32[2,19,4,16,128]{4,3,2,1,0:T(8,128)} %states_ref.1) | copy-start | bytes 3735556
  3.7 6.4 %collective-permute-start.4 = (f32[72,128]{1,0:T(8,128)S(1)}, f32[72,128]{1,0:T(8,128)S(1)}, u32[]{:S(2)}, u32[]{:S(2)}) collective-permute-start(f32[72,128]{1,0:T(8,128)S(1)} %get-tuple-element.57), channel_id=1, source_target_pairs={{0,28},{4,24},{8,20},{12,16},{16,12},{20,8},{24,4},{28,0},{1,29},{... | collective-permute-start | bytes 110600 | tf_op jit(solution)/shard_map/ppermute | solution.py:882
  7.1 3.4 %collective-permute-start.1 = (f32[72,128]{1,0:T(8,128)S(1)}, f32[72,128]{1,0:T(8,128)S(1)}, u32[]{:S(2)}, u32[]{:S(2)}) collective-permute-start(f32[72,128]{1,0:T(8,128)S(1)} %get-tuple-element.52.cols_ref), channel_id=1, source_target_pairs={{0,24},{8,16},{16,8},{24,0},{1,25},{9,17},{17,9},{25,1},{2,26},{10... | collective-permute-start | bytes 110600 | tf_op jit(solution)/shard_map/ppermute | solution.py:908
  7.9 5.2 %collective-permute-start.2 = (f32[216,128]{1,0:T(8,128)S(1)}, f32[216,128]{1,0:T(8,128)S(1)}, u32[]{:S(2)}, u32[]{:S(2)}) collective-permute-start(f32[216,128]{1,0:T(8,128)S(1)} %get-tuple-element.54), channel_id=1, source_target_pairs={{0,4},{4,0},{1,5},{5,1},{2,6},{6,2},{3,7},{7,3},{8,12},{12,8},{9,1... | collective-permute-start | bytes 331784 | tf_op jit(solution)/shard_map/ppermute | solution.py:911
  7.9 4.5 %collective-permute-start.3 = (f32[72,128]{1,0:T(8,128)S(1)}, f32[72,128]{1,0:T(8,128)S(1)}, u32[]{:S(2)}, u32[]{:S(2)}) collective-permute-start(f32[72,128]{1,0:T(8,128)S(1)} %get-tuple-element.55), channel_id=1, source_target_pairs={{0,12},{4,8},{8,4},{12,0},{16,28},{20,24},{24,20},{28,16},{1,13},{... | collective-permute-start | bytes 110600 | tf_op jit(solution)/shard_map/ppermute | solution.py:882
  9.1 4.0 %collective-permute-start = (f32[376,128]{1,0:T(8,128)S(1)}, f32[376,128]{1,0:T(8,128)S(1)}, u32[]{:S(2)}, u32[]{:S(2)}) collective-permute-start(f32[376,128]{1,0:T(8,128)S(1)} %get-tuple-element.53), channel_id=1, source_target_pairs={{0,8},{8,0},{16,24},{24,16},{1,9},{9,1},{17,25},{25,17},{2,10},{10... | collective-permute-start | bytes 577544 | tf_op jit(solution)/shard_map/ppermute | solution.py:909
  10.5 3.6 %collective-permute-start.5 = (f32[8,128]{1,0:T(8,128)S(1)}, f32[8,128]{1,0:T(8,128)S(1)}, u32[]{:S(2)}, u32[]{:S(2)}) collective-permute-start(f32[8,128]{1,0:T(8,128)S(1)} %slice_add_fusion), channel_id=1, source_target_pairs={{0,8},{8,0},{16,24},{24,16},{1,9},{9,1},{17,25},{25,17},{2,10},{10... | collective-permute-start | bytes 12296 | tf_op jit(solution)/shard_map/ppermute | solution.py:938
  11.2 7.1 %collective-permute-start.8 = (f32[376,128]{1,0:T(8,128)S(1)}, f32[376,128]{1,0:T(8,128)S(1)}, u32[]{:S(2)}, u32[]{:S(2)}) collective-permute-start(f32[376,128]{1,0:T(8,128)S(1)} %get-tuple-element.63), channel_id=1, source_target_pairs={{0,24},{8,16},{16,8},{24,0},{1,25},{9,17},{17,9},{25,1},{2,26},{10... | collective-permute-start | bytes 577544 | tf_op jit(solution)/shard_map/ppermute | solution.py:928
  14.1 7.4 %collective-permute-start.6 = (f32[56,128]{1,0:T(8,128)S(1)}, f32[56,128]{1,0:T(8,128)S(1)}, u32[]{:S(2)}, u32[]{:S(2)}) collective-permute-start(f32[56,128]{1,0:T(8,128)S(1)} %constant_dynamic-update-slice_fusion.1), channel_id=1, source_target_pairs={{0,1},{1,0},{2,3},{3,2},{4,5},{5,4},{6,7},{7,6},{8,9},{9,8},{10,11... | collective-permute-start | bytes 86024 | tf_op jit(solution)/shard_map/ppermute | solution.py:942
  15.7 5.7 %copy-start.2 = (s32[4,16,128]{2,1,0:T(8,128)S(1)}, s32[4,16,128]{2,1,0:T(8,128)}, u32[]{:S(2)}) copy-start(s32[4,16,128]{2,1,0:T(8,128)} %mask_ref.1) | copy-start | bytes 98308
  15.7 5.7 %collective-permute-start.7 = (f32[56,128]{1,0:T(8,128)S(1)}, f32[56,128]{1,0:T(8,128)S(1)}, u32[]{:S(2)}, u32[]{:S(2)}) collective-permute-start(f32[56,128]{1,0:T(8,128)S(1)} %get-tuple-element.73), channel_id=1, source_target_pairs={{0,3},{1,2},{2,1},{3,0},{4,7},{5,6},{6,5},{7,4},{8,11},{9,10},{10,... | collective-permute-start | bytes 86024 | tf_op jit(solution)/shard_map/ppermute | solution.py:941
  18.2 5.4 %collective-permute-start.9 = (f32[8,128]{1,0:T(8,128)S(1)}, f32[8,128]{1,0:T(8,128)S(1)}, u32[]{:S(2)}, u32[]{:S(2)}) collective-permute-start(f32[8,128]{1,0:T(8,128)S(1)} %get-tuple-element.74.refs_0_), channel_id=1, source_target_pairs={{0,2},{1,3},{2,0},{3,1},{4,6},{5,7},{6,4},{7,5},{8,10},{9,11},{10,... | collective-permute-start | bytes 12296 | tf_op jit(solution)/shard_map/ppermute | solution.py:961

commit v6 on v5

--- a/solution.py
+++ b/solution.py
@@ -218,12 +218,15 @@
     return rows
 
 
+def parity(axis):
+    return lax.axis_index(axis) % 2
+
+
 def cell_rows(adj_ref, ub_ref, q, x, rows):
     return adj_ref[q, x, rows, :] if q < 19 else ub_ref[q - 19, x, rows, :]
 
 
 def pack_x_kernel(
-    par_ref,
     states_hbm,
     adj_hbm,
     por_hbm,
@@ -294,7 +297,7 @@
 
     for px in (0, 1):
 
-        @pl.when(par_ref[0] == px)
+        @pl.when(parity("gx") == px)
         def _():
             sa = 1 if px else -1
             fill_x(a_ref, sa)
@@ -308,7 +311,7 @@
 
 
 def pack_y_kernel(
-    par_ref, adj_ref, ub_ref, drag_ref, cols_ref, y_ref, ya_ref, yb_ref
+    adj_ref, ub_ref, drag_ref, cols_ref, y_ref, ya_ref, yb_ref
 ):
     nx, ny, nz = adj_ref.shape[1:]
     pair = lax.broadcasted_iota(jnp.int32, (8, nz), 1) // 2
@@ -365,7 +368,7 @@
     yb_ref[2 * corner_block :] = drag
     for py in (0, 1):
 
-        @pl.when(par_ref[1] == py)
+        @pl.when(parity("gy") == py)
         def _():
             s0 = 1 if py else -1
             fill_y(0, s0)
@@ -376,7 +379,7 @@
     for px in (0, 1):
         for py in (0, 1):
 
-            @pl.when((par_ref[0] == px) & (par_ref[1] == py))
+            @pl.when((parity("gx") == px) & (parity("gy") == py))
             def _():
                 sa = 1 if px else -1
                 s0 = 1 if py else -1
@@ -386,7 +389,6 @@
 
 
 def pack_z_kernel(
-    par_ref,
     cols_ref,
     xa_ref,
     xc_ref,
@@ -403,8 +405,8 @@
     nz = cols_ref.shape[1]
     tiles = ny // 8
     base = 16
-    even_x = par_ref[0] == 0
-    even_y = par_ref[1] == 0
+    even_x = parity("gx") == 0
+    even_y = parity("gy") == 0
     lane = lax.broadcasted_iota(jnp.int32, (8, nz), 1)
     sub = lax.broadcasted_iota(jnp.int32, (8, nz), 0)
     plane = (lane % 32) // 4
@@ -439,11 +441,11 @@
                         acc = column_pair(acc, xa_ref[row : row + 8], pair, q, k, p)
                 ext[g, base + 8 * t : base + 8 * t + 8, :] = acc
 
-    @pl.when(par_ref[0] == 0)
+    @pl.when(parity("gx") == 0)
     def _():
         fill_main(1)
 
-    @pl.when(par_ref[0] == 1)
+    @pl.when(parity("gx") == 1)
     def _():
         fill_main(-1)
 
@@ -495,7 +497,7 @@
         for t in range(tiles + 1):
             row = (g * (tiles + 1) + t) * 8
             zown_ref[row : row + 8, :] = acc[t]
-    up_first = par_ref[2] == 0
+    up_first = parity("gz") == 0
     even_lane = lane % 2 == 0
     for t in range(tiles + 1):
         two, three = packed[2][t], packed[3][t]
@@ -524,7 +526,6 @@
 
 
 def inner_kernel(
-    par_ref,
     states_ref,
     adj_ref,
     ub_ref,
@@ -547,8 +548,8 @@
     lane = lax.broadcasted_iota(jnp.int32, (8, nz), 1)
     slot = lane // 4
     sub = lax.broadcasted_iota(jnp.int32, (8, nz), 0)
-    even_x = par_ref[0] == 0
-    even_y = par_ref[1] == 0
+    even_x = parity("gx") == 0
+    even_y = parity("gy") == 0
     base = 16
 
     for q in range(NSLOT):
@@ -684,7 +685,6 @@
 
 
 def edge_kernel(
-    par_ref,
     mask_ref,
     zown_ref,
     za_ref,
@@ -709,7 +709,7 @@
     nx, ny, nz = mask_ref.shape
     tiles = ny // 8
     height = (tiles + 1) * 8
-    even = par_ref[2] == 0
+    even = parity("gz") == 0
     lane = lax.broadcasted_iota(jnp.int32, (8, nz), 1)
     even_lane = lane % 2 == 0
     low_pair = lane % 4 < 2
@@ -843,20 +843,17 @@
 
 
 VMEM = pl.BlockSpec(memory_space=pltpu.VMEM)
-SMEM = pl.BlockSpec(memory_space=pltpu.SMEM)
 HBM = pl.BlockSpec(memory_space=pltpu.HBM)
 PARAMS = pltpu.CompilerParams(vmem_limit_bytes=48 * 2**20)
 
 
 def call(kernel, inputs, shapes, scratch=(), space=VMEM, micros=1, outs=None):
     if space is HBM:
-        inputs = inputs[:1] + tuple(
-            pltpu.with_memory_space_constraint(x, pltpu.HBM) for x in inputs[1:]
-        )
+        inputs = [pltpu.with_memory_space_constraint(x, pltpu.HBM) for x in inputs]
     return pl.pallas_call(
         kernel,
         out_shape=[jax.ShapeDtypeStruct(s, jnp.float32) for s in shapes],
-        in_specs=[SMEM if x.dtype == jnp.int32 and x.ndim == 1 else space for x in inputs],
+        in_specs=[space] * len(inputs),
         out_specs=outs or [VMEM] * len(shapes),
         scratch_shapes=list(scratch),
         compiler_params=PARAMS,
@@ -872,7 +869,6 @@
     x_first, x_second = swaps(gx)
     y_first, y_second = swaps(gy)
     z_first, z_second = swaps(gz)
-    parity = jnp.stack([lax.axis_index(axis) & 1 for axis in AXES]).astype(jnp.int32)
     tiles = ny // 8
     height = (tiles + 1) * 8
     f32 = jnp.float32
@@ -888,7 +884,7 @@
     rides = (gx, gy, gz) == (4, 2, 4)
     xa, xb, ub, drag = call(
         pack_x_kernel,
-        (parity, primal_states, adjoint_last, porosity, solid_mask),
+        (primal_states, adjoint_last, porosity, solid_mask),
         [(rows_x, nz), (rows_x, nz), (4, nx, ny, nz), (8, nz)],
         [
             pltpu.VMEM((2, 19, nx, ny, nz), f32),
@@ -901,7 +897,7 @@
     )
     cols, y, ya, yb = call(
         pack_y_kernel,
-        (parity, adjoint_last, ub, drag),
+        (adjoint_last, ub, drag),
         [(4 * ny + 8, nz), (rows_y, nz), (rows_c, nz), (rows_c, nz)],
         micros=4,
     )
@@ -929,7 +925,7 @@
 
     zown, za, zb, drag_xy = call(
         pack_z_kernel,
-        (parity, cols, xa, xc, y, ya, yb),
+        (cols, xa, xc, y, ya, yb),
         [(4 * height, nz), (rows_z, nz), (rows_z, nz), (8, nz)],
         [pltpu.VMEM((4, ny + 32, nz), f32)],
     )
@@ -942,7 +938,7 @@
     za = lax.ppermute(za, "gz", z_first)
     inner, grad1, inner_grad, pack, f0, f1 = call(
         inner_kernel,
-        (parity, primal_states, adjoint_last, ub, xa, xb, y, ya, yb),
+        (primal_states, adjoint_last, ub, xa, xb, y, ya, yb),
         [
             (19, nx, ny, nz),
             (nx, ny, nz),
@@ -965,7 +961,7 @@
 
     first, gradient, tails = call(
         edge_kernel,
-        (parity, solid_mask, zown, za, zb, pack, f0, f1, inner, grad1, inner_grad),
+        (solid_mask, zown, za, zb, pack, f0, f1, inner, grad1, inner_grad),
         [(19, nx, ny, nz), (nx, ny, nz), (8, nz)],
         [
             pltpu.VMEM((4 * height, nz), f32),

time: 24.4 us -> 22.3 us (0.914)
  Pallas kernels: 9.69 us -> 7.13 us
  waiting for transfers between devices: 1.24 us -> 1.71 us
    pallas_call x6, Pallas kernels: 9.69 us -> 7.13 us  [call(): pl.pallas_call(kernel, out_shape=[jax.ShapeDtypeStruct(s, jnp.float32) fo...]
    ppermute x1, waiting for transfers between devices: 0.01 us -> 0.32 us  [body(): xb = lax.ppermute(xb, 'gx', x_second)]
  transfers between devices with their start and end apart: 10 -> 10, of which waited for: 3 -> 5; matrix products, arithmetic and copies ran while one was open for 0% -> 0% of each run, Pallas kernels for 25% -> 21%
where the time goes in v6:
time: 22.3 us; the launch traced here: 22.1 us
  starting transfers between devices  12.5 us (56%)
  Pallas kernels  7.13 us (32%)
  waiting for transfers between devices  1.71 us (8%)
  between operations  0.73 us (3%)
    pallas_call x6, Pallas kernels, call(): pl.pallas_call(kernel, out_shape=[jax.ShapeDtypeStruct(s, jnp.float32) fo...  7.13 us
    ppermute x2, starting transfers between devices, diagonal(): return lax.ppermute(message, ('gx', 'gy'), pairs)  4.64 us
    ppermute x1, starting transfers between devices, body(): zb = lax.ppermute(zb, 'gz', z_second)  2.47 us
    ppermute x1, starting transfers between devices, body(): za = lax.ppermute(za, 'gz', z_first)  1.64 us
    ppermute x1, starting transfers between devices, body(): xb = lax.ppermute(xb, 'gx', x_second)  1.17 us
    ppermute x1, starting transfers between devices, body(): xa = lax.ppermute(xa, 'gx', x_first)  0.93 us
    ppermute x1, starting transfers between devices, body(): xc = lax.ppermute(cols, 'gx', x_second)  0.82 us
    ppermute x1, waiting for transfers between devices, body(): y = lax.ppermute(y, 'gy', y_first)  0.72 us
  transfers between devices with their start and end apart: 10, of which 5 were waited for; matrix products, arithmetic and copies ran while one was open for 0% of the time, Pallas kernels for 21%

profile of v6, /device:TPU:0, one launch (start us, length us, event | category | flops | bytes accessed | tf_op | source)
XLA Modules:
  0.0 22.1 jit_solution(10274496902127479854)
XLA Ops:
  0.7 1.6 %shard_map.67 = (f32[376,128]{1,0:T(8,128)S(1)}, f32[376,128]{1,0:T(8,128)S(1)}, f32[4,4,16,128]{3,2,1,0:T(8,128)S(1)}, f32[8,128]{1,0:T(8,128)S(1)}) custom-call(f32[2,19,4,16,128]{4,3,2,1,0:T(8,128)} %states_ref.1, f32[19,4,16,128]{3,2,1,0:T(8,128)} %adj_ref.3, f32[4,16,128]{2,1,0:T(8,128)} %por_hbm.1, s32[4,16,128]{2,1,0:T(8,128)} %mask_ref.1), custom_call_target="tpu_custom_call" | custom-call | bytes 3600000 | tf_op jit(solution)/shard_map/pallas_call | solution.py:853
  2.3 0.1 copy-done
  2.3 0.4 %shard_map.68 = (f32[72,128]{1,0:T(8,128)S(1)}, f32[216,128]{1,0:T(8,128)S(1)}, f32[72,128]{1,0:T(8,128)S(1)}, f32[72,128]{1,0:T(8,128)S(1)}) custom-call(f32[19,4,16,128]{3,2,1,0:T(8,128)S(1)} %copy-done, f32[4,4,16,128]{3,2,1,0:T(8,128)S(1)} %get-tuple-element.50.ub_ref, f32[8,128]{1,0:T(8,128)S(1)} %get-tuple-element.51.drag_ref), custom_call_target="tpu_custom_call" | custom-call | bytes 14400000 | tf_op jit(solution)/shard_map/pallas_call | solution.py:853
  2.7 3.4 %collective-permute-start.4 = (f32[72,128]{1,0:T(8,128)S(1)}, f32[72,128]{1,0:T(8,128)S(1)}, u32[]{:S(2)}, u32[]{:S(2)}) collective-permute-start(f32[72,128]{1,0:T(8,128)S(1)} %get-tuple-element.57), channel_id=1, source_target_pairs={{0,28},{4,24},{8,20},{12,16},{16,12},{20,8},{24,4},{28,0},{1,29},{... | collective-permute-start | bytes 110600 | tf_op jit(solution)/shard_map/ppermute | solution.py:878
  6.1 0.8 %collective-permute-start.1 = (f32[72,128]{1,0:T(8,128)S(1)}, f32[72,128]{1,0:T(8,128)S(1)}, u32[]{:S(2)}, u32[]{:S(2)}) collective-permute-start(f32[72,128]{1,0:T(8,128)S(1)} %get-tuple-element.52.cols_ref), channel_id=1, source_target_pairs={{0,24},{8,16},{16,8},{24,0},{1,25},{9,17},{17,9},{25,1},{2,26},{10... | collective-permute-start | bytes 110600 | tf_op jit(solution)/shard_map/ppermute | solution.py:904
  6.9 1.2 %collective-permute-start.3 = (f32[72,128]{1,0:T(8,128)S(1)}, f32[72,128]{1,0:T(8,128)S(1)}, u32[]{:S(2)}, u32[]{:S(2)}) collective-permute-start(f32[72,128]{1,0:T(8,128)S(1)} %get-tuple-element.55), channel_id=1, source_target_pairs={{0,12},{4,8},{8,4},{12,0},{16,28},{20,24},{24,20},{28,16},{1,13},{... | collective-permute-start | bytes 110600 | tf_op jit(solution)/shard_map/ppermute | solution.py:878
  8.2 0.9 %collective-permute-start = (f32[376,128]{1,0:T(8,128)S(1)}, f32[376,128]{1,0:T(8,128)S(1)}, u32[]{:S(2)}, u32[]{:S(2)}) collective-permute-start(f32[376,128]{1,0:T(8,128)S(1)} %get-tuple-element.53), channel_id=1, source_target_pairs={{0,8},{8,0},{16,24},{24,16},{1,9},{9,1},{17,25},{25,17},{2,10},{10... | collective-permute-start | bytes 577544 | tf_op jit(solution)/shard_map/ppermute | solution.py:905
  9.1 0.0 collective-permute-done.4.yb_ref
  9.1 0.4 %collective-permute-done.1.xc_ref = f32[72,128]{1,0:T(8,128)S(1)} collective-permute-done((f32[72,128]{1,0:T(8,128)S(1)}, f32[72,128]{1,0:T(8,128)S(1)}, u32[]{:S(2)}, u32[]{:S(2)}) %collective-permute-start.1) | collective-permute-done | bytes 36896 | tf_op jit(solution)/shard_map/ppermute | solution.py:904
  9.5 0.7 %collective-permute-start.5 = (f32[8,128]{1,0:T(8,128)S(1)}, f32[8,128]{1,0:T(8,128)S(1)}, u32[]{:S(2)}, u32[]{:S(2)}) collective-permute-start(f32[8,128]{1,0:T(8,128)S(1)} %slice_add_fusion), channel_id=1, source_target_pairs={{0,8},{8,0},{16,24},{24,16},{1,9},{9,1},{17,25},{25,17},{2,10},{10... | collective-permute-start | bytes 12296 | tf_op jit(solution)/shard_map/ppermute | solution.py:934
  10.2 1.2 %collective-permute-start.8 = (f32[376,128]{1,0:T(8,128)S(1)}, f32[376,128]{1,0:T(8,128)S(1)}, u32[]{:S(2)}, u32[]{:S(2)}) collective-permute-start(f32[376,128]{1,0:T(8,128)S(1)} %get-tuple-element.63), channel_id=1, source_target_pairs={{0,24},{8,16},{16,8},{24,0},{1,25},{9,17},{17,9},{25,1},{2,26},{10... | collective-permute-start | bytes 577544 | tf_op jit(solution)/shard_map/ppermute | solution.py:924
  11.4 0.1 collective-permute-done.3.ya_ref
  11.4 0.7 %collective-permute-done.2.y_ref = f32[216,128]{1,0:T(8,128)S(1)} collective-permute-done((f32[216,128]{1,0:T(8,128)S(1)}, f32[216,128]{1,0:T(8,128)S(1)}, u32[]{:S(2)}, u32[]{:S(2)}) %collective-permute-start.2) | collective-permute-done | bytes 110624 | tf_op jit(solution)/shard_map/ppermute | solution.py:907
  12.2 0.4 %shard_map.69 = (f32[96,128]{1,0:T(8,128)S(1)}, f32[56,128]{1,0:T(8,128)S(1)}, f32[56,128]{1,0:T(8,128)S(1)}, f32[8,128]{1,0:T(8,128)S(1)}) custom-call(f32[72,128]{1,0:T(8,128)S(1)} %get-tuple-element.52.cols_ref, f32[376,128]{1,0:T(8,128)S(1)} %collective-permute-done.xa_ref, f32[72,128]{1,0:T(8,128)S(1)} %collective-permute-done.1.xc_ref, ...), custom_call_target="tpu_custom_call" | custom-call | bytes 3600000 | tf_op jit(solution)/shard_map/pallas_call | solution.py:853
  12.5 0.0 collective-permute-done.5
  12.6 1.6 %collective-permute-start.6 = (f32[56,128]{1,0:T(8,128)S(1)}, f32[56,128]{1,0:T(8,128)S(1)}, u32[]{:S(2)}, u32[]{:S(2)}) collective-permute-start(f32[56,128]{1,0:T(8,128)S(1)} %constant_dynamic-update-slice_fusion.1), channel_id=1, source_target_pairs={{0,1},{1,0},{2,3},{3,2},{4,5},{5,4},{6,7},{7,6},{8,9},{9,8},{10,11... | collective-permute-start | bytes 86024 | tf_op jit(solution)/shard_map/ppermute | solution.py:938
  14.2 2.5 %collective-permute-start.7 = (f32[56,128]{1,0:T(8,128)S(1)}, f32[56,128]{1,0:T(8,128)S(1)}, u32[]{:S(2)}, u32[]{:S(2)}) collective-permute-start(f32[56,128]{1,0:T(8,128)S(1)} %get-tuple-element.73), channel_id=1, source_target_pairs={{0,3},{1,2},{2,1},{3,0},{4,7},{5,6},{6,5},{7,4},{8,11},{9,10},{10,... | collective-permute-start | bytes 86024 | tf_op jit(solution)/shard_map/ppermute | solution.py:937
  16.7 0.1 collective-permute-start.9
  16.8 0.3 %collective-permute-done.8.xb_ref = f32[376,128]{1,0:T(8,128)S(1)} collective-permute-done((f32[376,128]{1,0:T(8,128)S(1)}, f32[376,128]{1,0:T(8,128)S(1)}, u32[]{:S(2)}, u32[]{:S(2)}) %collective-permute-start.8) | collective-permute-done | bytes 192544 | tf_op jit(solution)/shard_map/ppermute | solution.py:924
  17.1 2.6 %shard_map.70 = (f32[19,4,16,128]{3,2,1,0:T(8,128)S(1)}, f32[4,16,128]{2,1,0:T(8,128)S(1)}, f32[4,16,128]{2,1,0:T(8,128)S(1)}, f32[19,16,128]{2,1,0:T(8,128)S(1)...) custom-call(f32[2,19,4,16,128]{4,3,2,1,0:T(8,128)S(1)} %copy-done.1, f32[19,4,16,128]{3,2,1,0:T(8,128)S(1)} %copy-done, ...), custom_call_target="tpu_custom_call" | custom-call | bytes 14400000 | tf_op jit(solution)/shard_map/pallas_call | solution.py:853
  19.7 0.0 collective-permute-done.6.za_ref
  19.7 0.1 collective-permute-done.7.zb_ref
  19.9 1.6 %shard_map.71 = (f32[19,4,16,128]{3,2,1,0:T(8,128)}, f32[4,16,128]{2,1,0:T(8,128)}, f32[8,128]{1,0:T(8,128)S(1)}) custom-call(s32[4,16,128]{2,1,0:T(8,128)S(1)} %copy-done.2, f32[96,128]{1,0:T(8,128)S(1)} %get-tuple-element.59.zown_ref, f32[56,128]{1,0:T(8,128)S(1)} %collective-permute-done.6.za_ref, f32[56,128]{1,0:T(8,128)S(1)} %collective-permute-done.7.zb_ref, ...), custom_call_target="tpu_custom_call" | custom-call | bytes 3600000 | tf_op jit(solution)/shard_map/pallas_call | solution.py:853
  21.5 0.6 %shard_map.72 = f32[1,1]{1,0:T(1,128)} custom-call(f32[8,128]{1,0:T(8,128)S(1)} %get-tuple-element.74.refs_0_, f32[8,128]{1,0:T(8,128)S(1)} %collective-permute-done.9.refs_1_, f32[8,128]{1,0:T(8,128)S(1)} %get-tuple-element.72.refs_2_), custom_call_target="tpu_custom_call" | custom-call | bytes 3600000 | tf_op jit(solution)/shard_map/pallas_call | solution.py:853
  (11 shorter events, 0.0 us)
Async XLA Ops:
  0.6 16.5 %copy-start.1 = (f32[2,19,4,16,128]{4,3,2,1,0:T(8,128)S(1)}, f32[2,19,4,16,128]{4,3,2,1,0:T(8,128)}, u32[]{:S(2)}) copy-start(f32[2,19,4,16,128]{4,3,2,1,0:T(8,128)} %states_ref.1) | copy-start | bytes 3735556
  0.6 1.7 %copy-start = (f32[19,4,16,128]{3,2,1,0:T(8,128)S(1)}, f32[19,4,16,128]{3,2,1,0:T(8,128)}, u32[]{:S(2)}) copy-start(f32[19,4,16,128]{3,2,1,0:T(8,128)} %adj_ref.3) | copy-start | bytes 1867780
  2.7 6.4 %collective-permute-start.4 = (f32[72,128]{1,0:T(8,128)S(1)}, f32[72,128]{1,0:T(8,128)S(1)}, u32[]{:S(2)}, u32[]{:S(2)}) collective-permute-start(f32[72,128]{1,0:T(8,128)S(1)} %get-tuple-element.57), channel_id=1, source_target_pairs={{0,28},{4,24},{8,20},{12,16},{16,12},{20,8},{24,4},{28,0},{1,29},{... | collective-permute-start | bytes 110600 | tf_op jit(solution)/shard_map/ppermute | solution.py:878
  6.1 3.4 %collective-permute-start.1 = (f32[72,128]{1,0:T(8,128)S(1)}, f32[72,128]{1,0:T(8,128)S(1)}, u32[]{:S(2)}, u32[]{:S(2)}) collective-permute-start(f32[72,128]{1,0:T(8,128)S(1)} %get-tuple-element.52.cols_ref), channel_id=1, source_target_pairs={{0,24},{8,16},{16,8},{24,0},{1,25},{9,17},{17,9},{25,1},{2,26},{10... | collective-permute-start | bytes 110600 | tf_op jit(solution)/shard_map/ppermute | solution.py:904
  6.9 5.2 %collective-permute-start.2 = (f32[216,128]{1,0:T(8,128)S(1)}, f32[216,128]{1,0:T(8,128)S(1)}, u32[]{:S(2)}, u32[]{:S(2)}) collective-permute-start(f32[216,128]{1,0:T(8,128)S(1)} %get-tuple-element.54), channel_id=1, source_target_pairs={{0,4},{4,0},{1,5},{5,1},{2,6},{6,2},{3,7},{7,3},{8,12},{12,8},{9,1... | collective-permute-start | bytes 331784 | tf_op jit(solution)/shard_map/ppermute | solution.py:907
  6.9 4.5 %collective-permute-start.3 = (f32[72,128]{1,0:T(8,128)S(1)}, f32[72,128]{1,0:T(8,128)S(1)}, u32[]{:S(2)}, u32[]{:S(2)}) collective-permute-start(f32[72,128]{1,0:T(8,128)S(1)} %get-tuple-element.55), channel_id=1, source_target_pairs={{0,12},{4,8},{8,4},{12,0},{16,28},{20,24},{24,20},{28,16},{1,13},{... | collective-permute-start | bytes 110600 | tf_op jit(solution)/shard_map/ppermute | solution.py:878
  8.2 4.0 %collective-permute-start = (f32[376,128]{1,0:T(8,128)S(1)}, f32[376,128]{1,0:T(8,128)S(1)}, u32[]{:S(2)}, u32[]{:S(2)}) collective-permute-start(f32[376,128]{1,0:T(8,128)S(1)} %get-tuple-element.53), channel_id=1, source_target_pairs={{0,8},{8,0},{16,24},{24,16},{1,9},{9,1},{17,25},{25,17},{2,10},{10... | collective-permute-start | bytes 577544 | tf_op jit(solution)/shard_map/ppermute | solution.py:905
  9.5 3.0 %collective-permute-start.5 = (f32[8,128]{1,0:T(8,128)S(1)}, f32[8,128]{1,0:T(8,128)S(1)}, u32[]{:S(2)}, u32[]{:S(2)}) collective-permute-start(f32[8,128]{1,0:T(8,128)S(1)} %slice_add_fusion), channel_id=1, source_target_pairs={{0,8},{8,0},{16,24},{24,16},{1,9},{9,1},{17,25},{25,17},{2,10},{10... | collective-permute-start | bytes 12296 | tf_op jit(solution)/shard_map/ppermute | solution.py:934
  10.2 6.9 %collective-permute-start.8 = (f32[376,128]{1,0:T(8,128)S(1)}, f32[376,128]{1,0:T(8,128)S(1)}, u32[]{:S(2)}, u32[]{:S(2)}) collective-permute-start(f32[376,128]{1,0:T(8,128)S(1)} %get-tuple-element.63), channel_id=1, source_target_pairs={{0,24},{8,16},{16,8},{24,0},{1,25},{9,17},{17,9},{25,1},{2,26},{10... | collective-permute-start | bytes 577544 | tf_op jit(solution)/shard_map/ppermute | solution.py:924
  12.6 7.2 %collective-permute-start.6 = (f32[56,128]{1,0:T(8,128)S(1)}, f32[56,128]{1,0:T(8,128)S(1)}, u32[]{:S(2)}, u32[]{:S(2)}) collective-permute-start(f32[56,128]{1,0:T(8,128)S(1)} %constant_dynamic-update-slice_fusion.1), channel_id=1, source_target_pairs={{0,1},{1,0},{2,3},{3,2},{4,5},{5,4},{6,7},{7,6},{8,9},{9,8},{10,11... | collective-permute-start | bytes 86024 | tf_op jit(solution)/shard_map/ppermute | solution.py:938
  14.2 5.7 %copy-start.2 = (s32[4,16,128]{2,1,0:T(8,128)S(1)}, s32[4,16,128]{2,1,0:T(8,128)}, u32[]{:S(2)}) copy-start(s32[4,16,128]{2,1,0:T(8,128)} %mask_ref.1) | copy-start | bytes 98308
  14.2 5.7 %collective-permute-start.7 = (f32[56,128]{1,0:T(8,128)S(1)}, f32[56,128]{1,0:T(8,128)S(1)}, u32[]{:S(2)}, u32[]{:S(2)}) collective-permute-start(f32[56,128]{1,0:T(8,128)S(1)} %get-tuple-element.73), channel_id=1, source_target_pairs={{0,3},{1,2},{2,1},{3,0},{4,7},{5,6},{6,5},{7,4},{8,11},{9,10},{10,... | collective-permute-start | bytes 86024 | tf_op jit(solution)/shard_map/ppermute | solution.py:937
  16.7 4.8 %collective-permute-start.9 = (f32[8,128]{1,0:T(8,128)S(1)}, f32[8,128]{1,0:T(8,128)S(1)}, u32[]{:S(2)}, u32[]{:S(2)}) collective-permute-start(f32[8,128]{1,0:T(8,128)S(1)} %get-tuple-element.74.refs_0_), channel_id=1, source_target_pairs={{0,2},{1,3},{2,0},{3,1},{4,6},{5,7},{6,4},{7,5},{8,10},{9,11},{10,... | collective-permute-start | bytes 12296 | tf_op jit(solution)/shard_map/ppermute | solution.py:957

commit v7 on v6

--- a/solution.py
+++ b/solution.py
@@ -226,17 +226,13 @@
     return adj_ref[q, x, rows, :] if q < 19 else ub_ref[q - 19, x, rows, :]
 
 
-def pack_x_kernel(
+def state_kernel(
     states_hbm,
-    adj_hbm,
     por_hbm,
     mask_hbm,
-    a_ref,
-    b_ref,
     ub_ref,
     drag_ref,
     states_ref,
-    adj_ref,
     por_ref,
     mask_ref,
     sems,
@@ -252,13 +248,12 @@
                 (mask_hbm, mask_ref),
                 (states_hbm.at[0, 1:3], states_ref.at[0, 1:3]),
                 (states_hbm.at[0, 7:15], states_ref.at[0, 7:15]),
-                (adj_hbm, adj_ref),
             )
         )
     ]
     for copy in copies:
         copy.start()
-    for copy in copies[:5]:
+    for copy in copies[:3]:
         copy.wait()
 
     def cells(x, carry):
@@ -266,23 +261,37 @@
             rows = slice(8 * t, 8 * t + 8)
             blocking = jnp.where(mask_ref[x, rows, :] == 0, por_ref[x, rows, :], 1.0)
             f0, s, d, m, u = state_of(states_ref, (1, x, rows))
-            flux = m["one"][0]
+            for k in range(3):
+                ub_ref[k, x, rows, :] = u[k]
+            ub_ref[3, x, rows, :] = blocking
+            carry = carry + blocking * m["one"][0]
+        return carry
+
+    drag = lax.fori_loop(0, nx, cells, jnp.zeros((8, nz), jnp.float32))
+    for copy in copies[3:]:
+        copy.wait()
+
+    def flux_cells(x, carry):
+        for t in range(tiles):
+            rows = slice(8 * t, 8 * t + 8)
+            flux = 0.0
             for a, b in PAIRS:
                 if VEL[a][0]:
                     flux = flux + (
                         states_ref[0, a, x, rows, :] - states_ref[0, b, x, rows, :]
                     )
-            for k in range(3):
-                ub_ref[k, x, rows, :] = u[k]
-            ub_ref[3, x, rows, :] = blocking
-            carry = carry + blocking * flux
+            carry = carry + ub_ref[3, x, rows, :] * flux
         return carry
 
-    drag = lax.fori_loop(0, nx, cells, jnp.zeros((8, nz), jnp.float32))
+    drag = lax.fori_loop(0, nx, flux_cells, drag)
     drag_ref[...] = drag
+
+
+def pack_x_kernel(adj_ref, ub_ref, drag_ref, a_ref, b_ref):
+    nx, ny = adj_ref.shape[1:3]
+    drag = drag_ref[...]
     a_ref[NSLOT * ny :] = drag
     b_ref[NSLOT * ny :] = drag
-    copies[5].wait()
 
     def fill_x(out_ref, sign):
         for names, offset, x in (
@@ -882,16 +891,15 @@
     rows_c = 2 * (CORNER + EDGE_ROWS) + 8
     rows_z = 2 * height + 8
     rides = (gx, gy, gz) == (4, 2, 4)
-    xa, xb, ub, drag = call(
-        pack_x_kernel,
-        (primal_states, adjoint_last, porosity, solid_mask),
-        [(rows_x, nz), (rows_x, nz), (4, nx, ny, nz), (8, nz)],
+    ub, drag = call(
+        state_kernel,
+        (primal_states, porosity, solid_mask),
+        [(4, nx, ny, nz), (8, nz)],
         [
             pltpu.VMEM((2, 19, nx, ny, nz), f32),
-            pltpu.VMEM((19, nx, ny, nz), f32),
             pltpu.VMEM((nx, ny, nz), f32),
             pltpu.VMEM((nx, ny, nz), jnp.int32),
-            pltpu.SemaphoreType.DMA((6,)),
+            pltpu.SemaphoreType.DMA((5,)),
         ],
         HBM,
     )
@@ -900,6 +908,9 @@
         (adjoint_last, ub, drag),
         [(4 * ny + 8, nz), (rows_y, nz), (rows_c, nz), (rows_c, nz)],
         micros=4,
+    )
+    xa, xb = call(
+        pack_x_kernel, (adjoint_last, ub, drag), [(rows_x, nz), (rows_x, nz)]
     )
     xc = lax.ppermute(cols, "gx", x_second)
     xa = lax.ppermute(xa, "gx", x_first)

time: 22.3 us -> 22 us (0.987)
  Pallas kernels: 7.13 us -> 6.9 us
    pallas_call x6 -> x7, Pallas kernels: 7.13 us -> 6.9 us  [call(): pl.pallas_call(kernel, out_shape=[jax.ShapeDtypeStruct(s, jnp.float32) fo...]
where the time goes in v7:
time: 22 us; the launch traced here: 21.8 us
  starting transfers between devices  12.5 us (57%)
  Pallas kernels  6.9 us (31%)
  waiting for transfers between devices  1.62 us (7%)
  between operations  0.74 us (3%)
    pallas_call x7, Pallas kernels, call(): pl.pallas_call(kernel, out_shape=[jax.ShapeDtypeStruct(s, jnp.float32) fo...  6.9 us
    ppermute x2, starting transfers between devices, diagonal(): return lax.ppermute(message, ('gx', 'gy'), pairs)  4.64 us
    ppermute x1, starting transfers between devices, body(): zb = lax.ppermute(zb, 'gz', z_second)  2.47 us
    ppermute x1, starting transfers between devices, body(): za = lax.ppermute(za, 'gz', z_first)  1.64 us
    ppermute x1, starting transfers between devices, body(): xb = lax.ppermute(xb, 'gx', x_second)  1.17 us
    ppermute x1, starting transfers between devices, body(): xa = lax.ppermute(xa, 'gx', x_first)  0.99 us
    ppermute x1, starting transfers between devices, body(): xc = lax.ppermute(cols, 'gx', x_second)  0.82 us
    ppermute x1, waiting for transfers between devices, body(): y = lax.ppermute(y, 'gy', y_first)  0.72 us
  transfers between devices with their start and end apart: 10, of which 5 were waited for; matrix products, arithmetic and copies ran while one was open for 0% of the time, Pallas kernels for 21%

profile of v7, /device:TPU:0, one launch (start us, length us, event | category | flops | bytes accessed | tf_op | source)
XLA Modules:
  0.0 21.8 jit_solution(10745188156121623508)
XLA Ops:
  0.6 1.3 %shard_map.67 = (f32[4,4,16,128]{3,2,1,0:T(8,128)S(1)}, f32[8,128]{1,0:T(8,128)S(1)}) custom-call(f32[2,19,4,16,128]{4,3,2,1,0:T(8,128)} %states_ref.1, f32[4,16,128]{2,1,0:T(8,128)} %por_hbm.1, s32[4,16,128]{2,1,0:T(8,128)} %mask_ref.1), custom_call_target="tpu_custom_call" | custom-call | bytes 3600000 | tf_op jit(solution)/shard_map/pallas_call | solution.py:862
  2.0 0.0 copy-start.1
  2.0 0.0 copy-done
  2.0 0.4 %shard_map.68 = (f32[72,128]{1,0:T(8,128)S(1)}, f32[216,128]{1,0:T(8,128)S(1)}, f32[72,128]{1,0:T(8,128)S(1)}, f32[72,128]{1,0:T(8,128)S(1)}) custom-call(f32[19,4,16,128]{3,2,1,0:T(8,128)S(1)} %copy-done, f32[4,4,16,128]{3,2,1,0:T(8,128)S(1)} %get-tuple-element.50.ub_ref, f32[8,128]{1,0:T(8,128)S(1)} %get-tuple-element.51.drag_ref), custom_call_target="tpu_custom_call" | custom-call | bytes 14400000 | tf_op jit(solution)/shard_map/pallas_call | solution.py:862
  2.4 3.4 %collective-permute-start.4 = (f32[72,128]{1,0:T(8,128)S(1)}, f32[72,128]{1,0:T(8,128)S(1)}, u32[]{:S(2)}, u32[]{:S(2)}) collective-permute-start(f32[72,128]{1,0:T(8,128)S(1)} %get-tuple-element.57), channel_id=1, source_target_pairs={{0,28},{4,24},{8,20},{12,16},{16,12},{20,8},{24,4},{28,0},{1,29},{... | collective-permute-start | bytes 110600 | tf_op jit(solution)/shard_map/ppermute | solution.py:887
  5.8 0.8 %collective-permute-start.1 = (f32[72,128]{1,0:T(8,128)S(1)}, f32[72,128]{1,0:T(8,128)S(1)}, u32[]{:S(2)}, u32[]{:S(2)}) collective-permute-start(f32[72,128]{1,0:T(8,128)S(1)} %get-tuple-element.52.cols_ref), channel_id=1, source_target_pairs={{0,24},{8,16},{16,8},{24,0},{1,25},{9,17},{17,9},{25,1},{2,26},{10... | collective-permute-start | bytes 110600 | tf_op jit(solution)/shard_map/ppermute | solution.py:915
  6.6 0.0 collective-permute-start.2
  6.6 1.2 %collective-permute-start.3 = (f32[72,128]{1,0:T(8,128)S(1)}, f32[72,128]{1,0:T(8,128)S(1)}, u32[]{:S(2)}, u32[]{:S(2)}) collective-permute-start(f32[72,128]{1,0:T(8,128)S(1)} %get-tuple-element.55), channel_id=1, source_target_pairs={{0,12},{4,8},{8,4},{12,0},{16,28},{20,24},{24,20},{28,16},{1,13},{... | collective-permute-start | bytes 110600 | tf_op jit(solution)/shard_map/ppermute | solution.py:887
  7.9 1.0 %collective-permute-start = (f32[376,128]{1,0:T(8,128)S(1)}, f32[376,128]{1,0:T(8,128)S(1)}, u32[]{:S(2)}, u32[]{:S(2)}) collective-permute-start(f32[376,128]{1,0:T(8,128)S(1)} %get-tuple-element.53), channel_id=1, source_target_pairs={{0,8},{8,0},{16,24},{24,16},{1,9},{9,1},{17,25},{25,17},{2,10},{10... | collective-permute-start | bytes 577544 | tf_op jit(solution)/shard_map/ppermute | solution.py:916
  8.9 0.0 collective-permute-done.4.yb_ref
  8.9 0.3 %collective-permute-done.1.xc_ref = f32[72,128]{1,0:T(8,128)S(1)} collective-permute-done((f32[72,128]{1,0:T(8,128)S(1)}, f32[72,128]{1,0:T(8,128)S(1)}, u32[]{:S(2)}, u32[]{:S(2)}) %collective-permute-start.1) | collective-permute-done | bytes 36896 | tf_op jit(solution)/shard_map/ppermute | solution.py:915
  9.2 0.7 %collective-permute-start.5 = (f32[8,128]{1,0:T(8,128)S(1)}, f32[8,128]{1,0:T(8,128)S(1)}, u32[]{:S(2)}, u32[]{:S(2)}) collective-permute-start(f32[8,128]{1,0:T(8,128)S(1)} %slice_add_fusion), channel_id=1, source_target_pairs={{0,8},{8,0},{16,24},{24,16},{1,9},{9,1},{17,25},{25,17},{2,10},{10... | collective-permute-start | bytes 12296 | tf_op jit(solution)/shard_map/ppermute | solution.py:945
  9.9 1.2 %collective-permute-start.8 = (f32[376,128]{1,0:T(8,128)S(1)}, f32[376,128]{1,0:T(8,128)S(1)}, u32[]{:S(2)}, u32[]{:S(2)}) collective-permute-start(f32[376,128]{1,0:T(8,128)S(1)} %get-tuple-element.63), channel_id=1, source_target_pairs={{0,24},{8,16},{16,8},{24,0},{1,25},{9,17},{17,9},{25,1},{2,26},{10... | collective-permute-start | bytes 577544 | tf_op jit(solution)/shard_map/ppermute | solution.py:935
  11.1 0.1 collective-permute-done.3.ya_ref
  11.1 0.7 %collective-permute-done.2.y_ref = f32[216,128]{1,0:T(8,128)S(1)} collective-permute-done((f32[216,128]{1,0:T(8,128)S(1)}, f32[216,128]{1,0:T(8,128)S(1)}, u32[]{:S(2)}, u32[]{:S(2)}) %collective-permute-start.2) | collective-permute-done | bytes 110624 | tf_op jit(solution)/shard_map/ppermute | solution.py:918
  11.9 0.4 %shard_map.70 = (f32[96,128]{1,0:T(8,128)S(1)}, f32[56,128]{1,0:T(8,128)S(1)}, f32[56,128]{1,0:T(8,128)S(1)}, f32[8,128]{1,0:T(8,128)S(1)}) custom-call(f32[72,128]{1,0:T(8,128)S(1)} %get-tuple-element.52.cols_ref, f32[376,128]{1,0:T(8,128)S(1)} %collective-permute-done.xa_ref, f32[72,128]{1,0:T(8,128)S(1)} %collective-permute-done.1.xc_ref, ...), custom_call_target="tpu_custom_call" | custom-call | bytes 3600000 | tf_op jit(solution)/shard_map/pallas_call | solution.py:862
  12.3 1.6 %collective-permute-start.6 = (f32[56,128]{1,0:T(8,128)S(1)}, f32[56,128]{1,0:T(8,128)S(1)}, u32[]{:S(2)}, u32[]{:S(2)}) collective-permute-start(f32[56,128]{1,0:T(8,128)S(1)} %constant_dynamic-update-slice_fusion.1), channel_id=1, source_target_pairs={{0,1},{1,0},{2,3},{3,2},{4,5},{5,4},{6,7},{7,6},{8,9},{9,8},{10,11... | collective-permute-start | bytes 86024 | tf_op jit(solution)/shard_map/ppermute | solution.py:949
  13.9 2.5 %collective-permute-start.7 = (f32[56,128]{1,0:T(8,128)S(1)}, f32[56,128]{1,0:T(8,128)S(1)}, u32[]{:S(2)}, u32[]{:S(2)}) collective-permute-start(f32[56,128]{1,0:T(8,128)S(1)} %get-tuple-element.73), channel_id=1, source_target_pairs={{0,3},{1,2},{2,1},{3,0},{4,7},{5,6},{6,5},{7,4},{8,11},{9,10},{10,... | collective-permute-start | bytes 86024 | tf_op jit(solution)/shard_map/ppermute | solution.py:948
  16.4 0.1 collective-permute-start.9
  16.5 0.3 %collective-permute-done.8.xb_ref = f32[376,128]{1,0:T(8,128)S(1)} collective-permute-done((f32[376,128]{1,0:T(8,128)S(1)}, f32[376,128]{1,0:T(8,128)S(1)}, u32[]{:S(2)}, u32[]{:S(2)}) %collective-permute-start.8) | collective-permute-done | bytes 192544 | tf_op jit(solution)/shard_map/ppermute | solution.py:935
  16.8 2.6 %shard_map.71 = (f32[19,4,16,128]{3,2,1,0:T(8,128)S(1)}, f32[4,16,128]{2,1,0:T(8,128)S(1)}, f32[4,16,128]{2,1,0:T(8,128)S(1)}, f32[19,16,128]{2,1,0:T(8,128)S(1)...) custom-call(f32[2,19,4,16,128]{4,3,2,1,0:T(8,128)S(1)} %copy-done.1, f32[19,4,16,128]{3,2,1,0:T(8,128)S(1)} %copy-done, ...), custom_call_target="tpu_custom_call" | custom-call | bytes 14400000 | tf_op jit(solution)/shard_map/pallas_call | solution.py:862
  19.4 0.2 collective-permute-done.7.zb_ref
  19.6 1.6 %shard_map.72 = (f32[19,4,16,128]{3,2,1,0:T(8,128)}, f32[4,16,128]{2,1,0:T(8,128)}, f32[8,128]{1,0:T(8,128)S(1)}) custom-call(s32[4,16,128]{2,1,0:T(8,128)S(1)} %copy-done.2, f32[96,128]{1,0:T(8,128)S(1)} %get-tuple-element.59.zown_ref, f32[56,128]{1,0:T(8,128)S(1)} %collective-permute-done.6.za_ref, f32[56,128]{1,0:T(8,128)S(1)} %collective-permute-done.7.zb_ref, ...), custom_call_target="tpu_custom_call" | custom-call | bytes 3600000 | tf_op jit(solution)/shard_map/pallas_call | solution.py:862
  21.2 0.6 %shard_map.73 = f32[1,1]{1,0:T(1,128)} custom-call(f32[8,128]{1,0:T(8,128)S(1)} %get-tuple-element.74.refs_0_, f32[8,128]{1,0:T(8,128)S(1)} %collective-permute-done.9.refs_1_, f32[8,128]{1,0:T(8,128)S(1)} %get-tuple-element.72.refs_2_), custom_call_target="tpu_custom_call" | custom-call | bytes 3600000 | tf_op jit(solution)/shard_map/pallas_call | solution.py:862
  (12 shorter events, 0.1 us)
Async XLA Ops:
  0.6 1.4 %copy-start = (f32[19,4,16,128]{3,2,1,0:T(8,128)S(1)}, f32[19,4,16,128]{3,2,1,0:T(8,128)}, u32[]{:S(2)}) copy-start(f32[19,4,16,128]{3,2,1,0:T(8,128)} %adj_ref.5) | copy-start | bytes 1867780
  2.0 14.8 %copy-start.1 = (f32[2,19,4,16,128]{4,3,2,1,0:T(8,128)S(1)}, f32[2,19,4,16,128]{4,3,2,1,0:T(8,128)}, u32[]{:S(2)}) copy-start(f32[2,19,4,16,128]{4,3,2,1,0:T(8,128)} %states_ref.1) | copy-start | bytes 3735556
  2.4 6.5 %collective-permute-start.4 = (f32[72,128]{1,0:T(8,128)S(1)}, f32[72,128]{1,0:T(8,128)S(1)}, u32[]{:S(2)}, u32[]{:S(2)}) collective-permute-start(f32[72,128]{1,0:T(8,128)S(1)} %get-tuple-element.57), channel_id=1, source_target_pairs={{0,28},{4,24},{8,20},{12,16},{16,12},{20,8},{24,4},{28,0},{1,29},{... | collective-permute-start | bytes 110600 | tf_op jit(solution)/shard_map/ppermute | solution.py:887
  5.8 3.4 %collective-permute-start.1 = (f32[72,128]{1,0:T(8,128)S(1)}, f32[72,128]{1,0:T(8,128)S(1)}, u32[]{:S(2)}, u32[]{:S(2)}) collective-permute-start(f32[72,128]{1,0:T(8,128)S(1)} %get-tuple-element.52.cols_ref), channel_id=1, source_target_pairs={{0,24},{8,16},{16,8},{24,0},{1,25},{9,17},{17,9},{25,1},{2,26},{10... | collective-permute-start | bytes 110600 | tf_op jit(solution)/shard_map/ppermute | solution.py:915
  6.6 5.2 %collective-permute-start.2 = (f32[216,128]{1,0:T(8,128)S(1)}, f32[216,128]{1,0:T(8,128)S(1)}, u32[]{:S(2)}, u32[]{:S(2)}) collective-permute-start(f32[216,128]{1,0:T(8,128)S(1)} %get-tuple-element.54), channel_id=1, source_target_pairs={{0,4},{4,0},{1,5},{5,1},{2,6},{6,2},{3,7},{7,3},{8,12},{12,8},{9,1... | collective-permute-start | bytes 331784 | tf_op jit(solution)/shard_map/ppermute | solution.py:918
  6.6 4.5 %collective-permute-start.3 = (f32[72,128]{1,0:T(8,128)S(1)}, f32[72,128]{1,0:T(8,128)S(1)}, u32[]{:S(2)}, u32[]{:S(2)}) collective-permute-start(f32[72,128]{1,0:T(8,128)S(1)} %get-tuple-element.55), channel_id=1, source_target_pairs={{0,12},{4,8},{8,4},{12,0},{16,28},{20,24},{24,20},{28,16},{1,13},{... | collective-permute-start | bytes 110600 | tf_op jit(solution)/shard_map/ppermute | solution.py:887
  7.9 4.0 %collective-permute-start = (f32[376,128]{1,0:T(8,128)S(1)}, f32[376,128]{1,0:T(8,128)S(1)}, u32[]{:S(2)}, u32[]{:S(2)}) collective-permute-start(f32[376,128]{1,0:T(8,128)S(1)} %get-tuple-element.53), channel_id=1, source_target_pairs={{0,8},{8,0},{16,24},{24,16},{1,9},{9,1},{17,25},{25,17},{2,10},{10... | collective-permute-start | bytes 577544 | tf_op jit(solution)/shard_map/ppermute | solution.py:916
  9.2 3.0 %collective-permute-start.5 = (f32[8,128]{1,0:T(8,128)S(1)}, f32[8,128]{1,0:T(8,128)S(1)}, u32[]{:S(2)}, u32[]{:S(2)}) collective-permute-start(f32[8,128]{1,0:T(8,128)S(1)} %slice_add_fusion), channel_id=1, source_target_pairs={{0,8},{8,0},{16,24},{24,16},{1,9},{9,1},{17,25},{25,17},{2,10},{10... | collective-permute-start | bytes 12296 | tf_op jit(solution)/shard_map/ppermute | solution.py:945
  9.9 6.9 %collective-permute-start.8 = (f32[376,128]{1,0:T(8,128)S(1)}, f32[376,128]{1,0:T(8,128)S(1)}, u32[]{:S(2)}, u32[]{:S(2)}) collective-permute-start(f32[376,128]{1,0:T(8,128)S(1)} %get-tuple-element.63), channel_id=1, source_target_pairs={{0,24},{8,16},{16,8},{24,0},{1,25},{9,17},{17,9},{25,1},{2,26},{10... | collective-permute-start | bytes 577544 | tf_op jit(solution)/shard_map/ppermute | solution.py:935
  12.3 7.2 %collective-permute-start.6 = (f32[56,128]{1,0:T(8,128)S(1)}, f32[56,128]{1,0:T(8,128)S(1)}, u32[]{:S(2)}, u32[]{:S(2)}) collective-permute-start(f32[56,128]{1,0:T(8,128)S(1)} %constant_dynamic-update-slice_fusion.1), channel_id=1, source_target_pairs={{0,1},{1,0},{2,3},{3,2},{4,5},{5,4},{6,7},{7,6},{8,9},{9,8},{10,11... | collective-permute-start | bytes 86024 | tf_op jit(solution)/shard_map/ppermute | solution.py:949
  13.9 5.7 %copy-start.2 = (s32[4,16,128]{2,1,0:T(8,128)S(1)}, s32[4,16,128]{2,1,0:T(8,128)}, u32[]{:S(2)}) copy-start(s32[4,16,128]{2,1,0:T(8,128)} %mask_ref.1) | copy-start | bytes 98308
  13.9 5.7 %collective-permute-start.7 = (f32[56,128]{1,0:T(8,128)S(1)}, f32[56,128]{1,0:T(8,128)S(1)}, u32[]{:S(2)}, u32[]{:S(2)}) collective-permute-start(f32[56,128]{1,0:T(8,128)S(1)} %get-tuple-element.73), channel_id=1, source_target_pairs={{0,3},{1,2},{2,1},{3,0},{4,7},{5,6},{6,5},{7,4},{8,11},{9,10},{10,... | collective-permute-start | bytes 86024 | tf_op jit(solution)/shard_map/ppermute | solution.py:948
  16.4 4.8 %collective-permute-start.9 = (f32[8,128]{1,0:T(8,128)S(1)}, f32[8,128]{1,0:T(8,128)S(1)}, u32[]{:S(2)}, u32[]{:S(2)}) collective-permute-start(f32[8,128]{1,0:T(8,128)S(1)} %get-tuple-element.74.refs_0_), channel_id=1, source_target_pairs={{0,2},{1,3},{2,0},{3,1},{4,6},{5,7},{6,4},{7,5},{8,10},{9,11},{10,... | collective-permute-start | bytes 12296 | tf_op jit(solution)/shard_map/ppermute | solution.py:968

commit v8 on v7

--- a/solution.py
+++ b/solution.py
@@ -287,13 +287,11 @@
     drag_ref[...] = drag
 
 
-def pack_x_kernel(adj_ref, ub_ref, drag_ref, a_ref, b_ref):
+def pack_x_kernel(adj_ref, ub_ref, drag_ref, out_ref):
     nx, ny = adj_ref.shape[1:3]
-    drag = drag_ref[...]
-    a_ref[NSLOT * ny :] = drag
-    b_ref[NSLOT * ny :] = drag
-
-    def fill_x(out_ref, sign):
+    out_ref[NSLOT * ny :] = drag_ref[...]
+
+    def fill(sign):
         for names, offset, x in (
             (near(0, sign), 0, 0 if sign > 0 else nx - 1),
             (far(0, sign), 18, 1 if sign > 0 else nx - 2),
@@ -304,13 +302,60 @@
                     adj_ref, ub_ref, q, x, slice(0, ny)
                 )
 
-    for px in (0, 1):
-
-        @pl.when(parity("gx") == px)
-        def _():
-            sa = 1 if px else -1
-            fill_x(a_ref, sa)
-            fill_x(b_ref, -sa)
+    pl.when(parity("gx") == 0)(functools.partial(fill, -1))
+    pl.when(parity("gx") == 1)(functools.partial(fill, 1))
+
+
+def edge_entries(sign):
+    rows = []
+    for side in (1, -1):
+        rows += [(i, 0, side) for i in far(1, side) if VEL[i][0] == 0]
+        rows += [(i, 1, side) for i in far(1, side) if VEL[i][0] == sign]
+    return rows
+
+
+def pack_partial_kernel(adj_ref, ub_ref, out_ref):
+    nx, ny, nz = adj_ref.shape[1:]
+    tiles = ny // 8
+    sub = lax.broadcasted_iota(jnp.int32, (8, nz), 0)
+
+    def fill(sign):
+        here, inside = (0, 1) if sign > 0 else (nx - 1, nx - 2)
+        names = far(0, sign)
+        for t in range(tiles):
+            rows = slice(8 * t, 8 * t + 8)
+            got = []
+            for i in range(19):
+                cx, cy, cz = VEL[i]
+                if cx * sign < 0:
+                    got.append(jnp.zeros((8, nz), jnp.float32))
+                    continue
+                x = inside if cx else here
+                if t == 0 and cy < 0:
+                    value = pltpu.roll(adj_ref[i, x, rows, :], 1, 0)
+                    value = jnp.where(sub == 0, 0.0, value)
+                elif t == tiles - 1 and cy > 0:
+                    value = pltpu.roll(adj_ref[i, x, rows, :], 7, 0)
+                    value = jnp.where(sub == 7, 0.0, value)
+                else:
+                    value = adj_ref[i, x, 8 * t + cy : 8 * t + 8 + cy, :]
+                got.append(z_shifted(value, cz))
+            u = [ub_ref[k, here, rows, :] for k in range(3)]
+            out, _ = adjoint_cell(got, u, ub_ref[3, here, rows, :], 0.0)
+            for k, i in enumerate(names):
+                out_ref[k * ny + 8 * t : k * ny + 8 * t + 8] = out[i]
+        for k, q in enumerate(names + UB):
+            k += 5
+            out_ref[k * ny : (k + 1) * ny] = cell_rows(
+                adj_ref, ub_ref, q, here, slice(0, ny)
+            )
+        for k, (i, depth, side) in enumerate(edge_entries(sign)):
+            y = 0 if side > 0 else ny - 1
+            row = 14 * ny + k
+            out_ref[row : row + 1] = adj_ref[i, inside if depth else here, y : y + 1, :]
+
+    pl.when(parity("gx") == 0)(functools.partial(fill, 1))
+    pl.when(parity("gx") == 1)(functools.partial(fill, -1))
 
 
 def column_pair(acc, value, pair, q, k, plane):
@@ -516,9 +561,8 @@
             row = (g * (tiles + 1) + t) * 8
             za_ref[row : row + 8, :] = jnp.where(up_first, up[g], down[g])
             zb_ref[row : row + 8, :] = jnp.where(up_first, down[g], up[g])
-    drag = cols_ref[4 * ny :] + y_ref[2 * y_block :]
-    for x_ref, c_ref in ((xa_ref, ya_ref), (xc_ref, yb_ref)):
-        drag = drag + (x_ref[x_ref.shape[0] - 8 :] + c_ref[2 * corner_block :])
+    drag = (cols_ref[4 * ny :] + y_ref[2 * y_block :]) + xa_ref[xa_ref.shape[0] - 8 :]
+    drag = drag + (xc_ref[4 * ny :] + yb_ref[2 * corner_block :])
     drag_ref[...] = drag
 
 
@@ -568,14 +612,39 @@
             )
     planes = {1: (nx + 2, nx + 3), -1: (1, 0)}
     lines = {1: (base + ny, base + ny + 1), -1: (base - 1, base - 2)}
-    for sign in (1, -1):
-        first, second = (xa_ref, xb_ref) if sign > 0 else (xb_ref, xa_ref)
+
+    def fill_whole(sign):
         for names, depth, offset in ((near(0, sign), 0, 0), (far(0, sign), 1, 18)):
             for k, q in enumerate(names):
                 rows = slice((k + offset) * ny, (k + offset + 1) * ny)
-                ext[q, planes[sign][depth], base : base + ny, :] = jnp.where(
-                    even_x, first[rows], second[rows]
-                )
+                ext[q, planes[sign][depth], base : base + ny, :] = xa_ref[rows]
+
+    def fill_partial(sign):
+        one, two = planes[sign]
+        for k, q in enumerate(far(0, sign) + UB):
+            ext[q, one, base : base + ny, :] = xb_ref[(5 + k) * ny : (6 + k) * ny]
+        nothing = jnp.zeros((ny, nz), jnp.float32)
+        for q in range(19):
+            if VEL[q][0] == 0:
+                ext[q, one, base : base + ny, :] = nothing
+            elif VEL[q][0] == sign:
+                ext[q, two, base : base + ny, :] = nothing
+        for k, (q, depth, side) in enumerate(edge_entries(sign)):
+            line = base if side > 0 else base + ny - 1
+            row = 14 * ny + k
+            ext[q, planes[sign][depth], line : line + 1, :] = xb_ref[row : row + 1]
+
+    @pl.when(parity("gx") == 0)
+    def _():
+        fill_whole(1)
+        fill_partial(-1)
+
+    @pl.when(parity("gx") == 1)
+    def _():
+        fill_whole(-1)
+        fill_partial(1)
+
+    for sign in (1, -1):
         block = y_rows(nx) + EDGE_ROWS
         first, second = (0, block) if sign > 0 else (block, 0)
         for names, depth, offset in ((near(1, sign), 0, 0), (far(1, sign), 1, 18)):
@@ -612,13 +681,17 @@
             sub < 4, ext[q, plane, above : above + 8, :], ext[q, plane, below : below + 8, :]
         )
 
-    def first_level(p, t, kinds):
+    def first_level(p, t, kinds, partial=None):
         got = []
         for i in range(19):
             cx, cy, cz = VEL[i]
             got.append(z_shifted(near_cells(i, p + 1 + cx, t, cy), cz))
         ub = [near_cells(19 + k, p + 1, t, 0) for k in range(4)]
         out, kept = adjoint_cell(got, ub[:3], ub[3], 1.0)
+        if partial is not None:
+            for k, i in enumerate(kinds):
+                row = k * ny + 8 * t
+                out[i] = out[i] + jnp.where(partial, xb_ref[row : row + 8], 0.0)
         for i in kinds:
             if t < tiles:
                 mid[i, p, t * 8 + 8 : t * 8 + 16, :] = out[i]
@@ -638,8 +711,8 @@
 
     lax.fori_loop(0, nx, inside, 0)
     for t in range(tiles):
-        first_level(0, t, far(0, -1))
-        first_level(nx + 1, t, far(0, 1))
+        first_level(0, t, far(0, -1), even_x)
+        first_level(nx + 1, t, far(0, 1), jnp.logical_not(even_x))
 
     def rim(n, carry):
         for p in (2 * n, 2 * n + 1):
@@ -909,9 +982,8 @@
         [(4 * ny + 8, nz), (rows_y, nz), (rows_c, nz), (rows_c, nz)],
         micros=4,
     )
-    xa, xb = call(
-        pack_x_kernel, (adjoint_last, ub, drag), [(rows_x, nz), (rows_x, nz)]
-    )
+    (xa,) = call(pack_x_kernel, (adjoint_last, ub, drag), [(rows_x, nz)])
+    (xb,) = call(pack_partial_kernel, (adjoint_last, ub), [(14 * ny + 8, nz)])
     xc = lax.ppermute(cols, "gx", x_second)
     xa = lax.ppermute(xa, "gx", x_first)
     if gy == 2:
@@ -941,7 +1013,7 @@
         [pltpu.VMEM((4, ny + 32, nz), f32)],
     )
     if rides:
-        second = xc[4 * ny :] + yb[rows_c - 8 :]
+        second = xc[4 * ny :] + yb[rows_c - 8 :] + y[rows_y - 8 :]
         drag_xy = drag_xy + lax.ppermute(second, "gx", x_first)
         za = za.at[2 * height :].set(drag_xy)
         zb = zb.at[2 * height :].set(drag_xy)

time: 22 us -> 21.8 us (level)
    ppermute x1, starting transfers between devices: 0.01 us -> 3.07 us  [body(): y = lax.ppermute(y, 'gy', y_first)]
    ppermute x2, starting transfers between devices: 4.64 us -> 1.97 us  [diagonal(): return lax.ppermute(message, ('gx', 'gy'), pairs)]
    ppermute x2, waiting for transfers between devices: 0.08 us -> 0.88 us  [diagonal(): return lax.ppermute(message, ('gx', 'gy'), pairs)]
    ppermute x1, waiting for transfers between devices: 0.72 us -> 0.01 us  [body(): y = lax.ppermute(y, 'gy', y_first)]
    ppermute x1, waiting for transfers between devices: 0.15 us -> 0.52 us  [body(): zb = lax.ppermute(zb, 'gz', z_second)]
    ppermute x1, waiting for transfers between devices: 0.33 us -> 0.01 us  [body(): xc = lax.ppermute(cols, 'gx', x_second)]
    ppermute x1, waiting for transfers between devices: 0.32 us -> 0.01 us  [body(): xb = lax.ppermute(xb, 'gx', x_second)]
    ppermute x1, starting transfers between devices: 0.99 us -> 0.71 us  [body(): xa = lax.ppermute(xa, 'gx', x_first)]
  transfers between devices with their start and end apart: 10 -> 10, of which waited for: 5 -> 2; matrix products, arithmetic and copies ran while one was open for 0% -> 0% of each run, Pallas kernels for 21% -> 22%
where the time goes in v8:
time: 21.8 us; the launch traced here: 21.6 us
  starting transfers between devices  12.4 us (57%)
  Pallas kernels  7.03 us (32%)
  waiting for transfers between devices  1.43 us (7%)
  between operations  0.74 us (3%)
    pallas_call x8, Pallas kernels, call(): pl.pallas_call(kernel, out_shape=[jax.ShapeDtypeStruct(s, jnp.float32) fo...  7.03 us
    ppermute x1, starting transfers between devices, body(): y = lax.ppermute(y, 'gy', y_first)  3.07 us
    ppermute x1, starting transfers between devices, body(): zb = lax.ppermute(zb, 'gz', z_second)  2.47 us
    ppermute x2, starting transfers between devices, diagonal(): return lax.ppermute(message, ('gx', 'gy'), pairs)  1.97 us
    ppermute x1, starting transfers between devices, body(): za = lax.ppermute(za, 'gz', z_first)  1.64 us
    ppermute x1, starting transfers between devices, body(): xb = lax.ppermute(xb, 'gx', x_second)  1.09 us
    ppermute x2, waiting for transfers between devices, diagonal(): return lax.ppermute(message, ('gx', 'gy'), pairs)  0.88 us
    ppermute x1, starting transfers between devices, body(): xa = lax.ppermute(xa, 'gx', x_first)  0.71 us
  transfers between devices with their start and end apart: 10, of which 2 were waited for; matrix products, arithmetic and copies ran while one was open for 0% of the time, Pallas kernels for 22%

profile of v8, /device:TPU:0, one launch (start us, length us, event | category | flops | bytes accessed | tf_op | source)
XLA Modules:
  0.0 21.6 jit_solution(12961808242107457890)
XLA Ops:
  0.6 1.3 %shard_map.67 = (f32[4,4,16,128]{3,2,1,0:T(8,128)S(1)}, f32[8,128]{1,0:T(8,128)S(1)}) custom-call(f32[2,19,4,16,128]{4,3,2,1,0:T(8,128)} %states_ref.1, f32[4,16,128]{2,1,0:T(8,128)} %por_hbm.1, s32[4,16,128]{2,1,0:T(8,128)} %mask_ref.1), custom_call_target="tpu_custom_call" | custom-call | bytes 3600000 | tf_op jit(solution)/shard_map/pallas_call | solution.py:935
  2.0 0.0 copy-done
  2.0 0.4 %shard_map.68 = (f32[72,128]{1,0:T(8,128)S(1)}, f32[216,128]{1,0:T(8,128)S(1)}, f32[72,128]{1,0:T(8,128)S(1)}, f32[72,128]{1,0:T(8,128)S(1)}) custom-call(f32[19,4,16,128]{3,2,1,0:T(8,128)S(1)} %copy-done, f32[4,4,16,128]{3,2,1,0:T(8,128)S(1)} %get-tuple-element.48.ub_ref, f32[8,128]{1,0:T(8,128)S(1)} %get-tuple-element.49.drag_ref), custom_call_target="tpu_custom_call" | custom-call | bytes 14400000 | tf_op jit(solution)/shard_map/pallas_call | solution.py:935
  2.4 0.0 copy-start.1
  2.4 3.1 %collective-permute-start.2 = (f32[216,128]{1,0:T(8,128)S(1)}, f32[216,128]{1,0:T(8,128)S(1)}, u32[]{:S(2)}, u32[]{:S(2)}) collective-permute-start(f32[216,128]{1,0:T(8,128)S(1)} %get-tuple-element.51), channel_id=1, source_target_pairs={{0,4},{4,0},{1,5},{5,1},{2,6},{6,2},{3,7},{7,3},{8,12},{12,8},{9,1... | collective-permute-start | bytes 331784 | tf_op jit(solution)/shard_map/ppermute | solution.py:990
  5.5 0.6 %collective-permute-start.4 = (f32[72,128]{1,0:T(8,128)S(1)}, f32[72,128]{1,0:T(8,128)S(1)}, u32[]{:S(2)}, u32[]{:S(2)}) collective-permute-start(f32[72,128]{1,0:T(8,128)S(1)} %get-tuple-element.53), channel_id=1, source_target_pairs={{0,28},{4,24},{8,20},{12,16},{16,12},{20,8},{24,4},{28,0},{1,29},{... | collective-permute-start | bytes 110600 | tf_op jit(solution)/shard_map/ppermute | solution.py:960
  6.0 0.7 %collective-permute-start.1 = (f32[72,128]{1,0:T(8,128)S(1)}, f32[72,128]{1,0:T(8,128)S(1)}, u32[]{:S(2)}, u32[]{:S(2)}) collective-permute-start(f32[72,128]{1,0:T(8,128)S(1)} %get-tuple-element.50.cols_ref), channel_id=1, source_target_pairs={{0,24},{8,16},{16,8},{24,0},{1,25},{9,17},{17,9},{25,1},{2,26},{10... | collective-permute-start | bytes 110600 | tf_op jit(solution)/shard_map/ppermute | solution.py:987
  6.7 1.4 %collective-permute-start.3 = (f32[72,128]{1,0:T(8,128)S(1)}, f32[72,128]{1,0:T(8,128)S(1)}, u32[]{:S(2)}, u32[]{:S(2)}) collective-permute-start(f32[72,128]{1,0:T(8,128)S(1)} %get-tuple-element.52), channel_id=1, source_target_pairs={{0,12},{4,8},{8,4},{12,0},{16,28},{20,24},{24,20},{28,16},{1,13},{... | collective-permute-start | bytes 110600 | tf_op jit(solution)/shard_map/ppermute | solution.py:960
  8.2 0.7 %collective-permute-start = (f32[376,128]{1,0:T(8,128)S(1)}, f32[376,128]{1,0:T(8,128)S(1)}, u32[]{:S(2)}, u32[]{:S(2)}) collective-permute-start(f32[376,128]{1,0:T(8,128)S(1)} %shard_map.69), channel_id=1, source_target_pairs={{0,8},{8,0},{16,24},{24,16},{1,9},{9,1},{17,25},{25,17},{2,10},{10... | collective-permute-start | bytes 577544 | tf_op jit(solution)/shard_map/ppermute | solution.py:988
  8.9 0.1 shard_map.70
  9.0 0.9 %collective-permute-done.4.yb_ref = f32[72,128]{1,0:T(8,128)S(1)} collective-permute-done((f32[72,128]{1,0:T(8,128)S(1)}, f32[72,128]{1,0:T(8,128)S(1)}, u32[]{:S(2)}, u32[]{:S(2)}) %collective-permute-start.4) | collective-permute-done | bytes 36896 | tf_op jit(solution)/shard_map/ppermute | solution.py:960
  9.9 0.0 collective-permute-done.1.xc_ref
  9.9 0.0 collective-permute-done.2.y_ref
  9.9 0.6 %collective-permute-start.5 = (f32[8,128]{1,0:T(8,128)S(1)}, f32[8,128]{1,0:T(8,128)S(1)}, u32[]{:S(2)}, u32[]{:S(2)}) collective-permute-start(f32[8,128]{1,0:T(8,128)S(1)} %slice_add_fusion), channel_id=1, source_target_pairs={{0,8},{8,0},{16,24},{24,16},{1,9},{9,1},{17,25},{25,17},{2,10},{10... | collective-permute-start | bytes 12296 | tf_op jit(solution)/shard_map/ppermute | solution.py:1017
  10.5 1.1 %collective-permute-start.8 = (f32[232,128]{1,0:T(8,128)S(1)}, f32[232,128]{1,0:T(8,128)S(1)}, u32[]{:S(2)}, u32[]{:S(2)}) collective-permute-start(f32[232,128]{1,0:T(8,128)S(1)} %shard_map.70), channel_id=1, source_target_pairs={{0,24},{8,16},{16,8},{24,0},{1,25},{9,17},{17,9},{25,1},{2,26},{10... | collective-permute-start | bytes 356360 | tf_op jit(solution)/shard_map/ppermute | solution.py:1007
  11.6 0.4 %shard_map.71 = (f32[96,128]{1,0:T(8,128)S(1)}, f32[56,128]{1,0:T(8,128)S(1)}, f32[56,128]{1,0:T(8,128)S(1)}, f32[8,128]{1,0:T(8,128)S(1)}) custom-call(f32[72,128]{1,0:T(8,128)S(1)} %get-tuple-element.50.cols_ref, f32[376,128]{1,0:T(8,128)S(1)} %collective-permute-done.xa_ref, f32[72,128]{1,0:T(8,128)S(1)} %collective-permute-done.1.xc_ref, ...), custom_call_target="tpu_custom_call" | custom-call | bytes 3600000 | tf_op jit(solution)/shard_map/pallas_call | solution.py:935
  12.0 1.6 %collective-permute-start.6 = (f32[56,128]{1,0:T(8,128)S(1)}, f32[56,128]{1,0:T(8,128)S(1)}, u32[]{:S(2)}, u32[]{:S(2)}) collective-permute-start(f32[56,128]{1,0:T(8,128)S(1)} %constant_dynamic-update-slice_fusion.1), channel_id=1, source_target_pairs={{0,1},{1,0},{2,3},{3,2},{4,5},{5,4},{6,7},{7,6},{8,9},{9,8},{10,11... | collective-permute-start | bytes 86024 | tf_op jit(solution)/shard_map/ppermute | solution.py:1021
  13.6 2.5 %collective-permute-start.7 = (f32[56,128]{1,0:T(8,128)S(1)}, f32[56,128]{1,0:T(8,128)S(1)}, u32[]{:S(2)}, u32[]{:S(2)}) collective-permute-start(f32[56,128]{1,0:T(8,128)S(1)} %get-tuple-element.69), channel_id=1, source_target_pairs={{0,3},{1,2},{2,1},{3,0},{4,7},{5,6},{6,5},{7,4},{8,11},{9,10},{10,... | collective-permute-start | bytes 86024 | tf_op jit(solution)/shard_map/ppermute | solution.py:1020
  16.1 0.1 collective-permute-start.9
  16.2 2.6 %shard_map.72 = (f32[19,4,16,128]{3,2,1,0:T(8,128)S(1)}, f32[4,16,128]{2,1,0:T(8,128)S(1)}, f32[4,16,128]{2,1,0:T(8,128)S(1)}, f32[19,16,128]{2,1,0:T(8,128)S(1)...) custom-call(f32[2,19,4,16,128]{4,3,2,1,0:T(8,128)S(1)} %copy-done.1, f32[19,4,16,128]{3,2,1,0:T(8,128)S(1)} %copy-done, ...), custom_call_target="tpu_custom_call" | custom-call | bytes 14400000 | tf_op jit(solution)/shard_map/pallas_call | solution.py:935
  18.8 0.0 collective-permute-done.6.za_ref
  18.8 0.5 %collective-permute-done.7.zb_ref = f32[56,128]{1,0:T(8,128)S(1)} collective-permute-done((f32[56,128]{1,0:T(8,128)S(1)}, f32[56,128]{1,0:T(8,128)S(1)}, u32[]{:S(2)}, u32[]{:S(2)}) %collective-permute-start.7) | collective-permute-done | bytes 28704 | tf_op jit(solution)/shard_map/ppermute | solution.py:1020
  19.4 1.6 %shard_map.73 = (f32[19,4,16,128]{3,2,1,0:T(8,128)}, f32[4,16,128]{2,1,0:T(8,128)}, f32[8,128]{1,0:T(8,128)S(1)}) custom-call(s32[4,16,128]{2,1,0:T(8,128)S(1)} %copy-done.2, f32[96,128]{1,0:T(8,128)S(1)} %get-tuple-element.55.zown_ref, f32[56,128]{1,0:T(8,128)S(1)} %collective-permute-done.6.za_ref, f32[56,128]{1,0:T(8,128)S(1)} %collective-permute-done.7.zb_ref, ...), custom_call_target="tpu_custom_call" | custom-call | bytes 3600000 | tf_op jit(solution)/shard_map/pallas_call | solution.py:935
  21.0 0.6 %shard_map.74 = f32[1,1]{1,0:T(1,128)} custom-call(f32[8,128]{1,0:T(8,128)S(1)} %get-tuple-element.70.refs_0_, f32[8,128]{1,0:T(8,128)S(1)} %collective-permute-done.9.refs_1_, f32[8,128]{1,0:T(8,128)S(1)} %get-tuple-element.68.refs_2_), custom_call_target="tpu_custom_call" | custom-call | bytes 3600000 | tf_op jit(solution)/shard_map/pallas_call | solution.py:935
  (13 shorter events, 0.0 us)
Async XLA Ops:
  0.6 1.4 %copy-start = (f32[19,4,16,128]{3,2,1,0:T(8,128)S(1)}, f32[19,4,16,128]{3,2,1,0:T(8,128)}, u32[]{:S(2)}) copy-start(f32[19,4,16,128]{3,2,1,0:T(8,128)} %adj_ref.7) | copy-start | bytes 1867780
  2.4 13.8 %copy-start.1 = (f32[2,19,4,16,128]{4,3,2,1,0:T(8,128)S(1)}, f32[2,19,4,16,128]{4,3,2,1,0:T(8,128)}, u32[]{:S(2)}) copy-start(f32[2,19,4,16,128]{4,3,2,1,0:T(8,128)} %states_ref.1) | copy-start | bytes 3735556
  2.4 7.5 %collective-permute-start.2 = (f32[216,128]{1,0:T(8,128)S(1)}, f32[216,128]{1,0:T(8,128)S(1)}, u32[]{:S(2)}, u32[]{:S(2)}) collective-permute-start(f32[216,128]{1,0:T(8,128)S(1)} %get-tuple-element.51), channel_id=1, source_target_pairs={{0,4},{4,0},{1,5},{5,1},{2,6},{6,2},{3,7},{7,3},{8,12},{12,8},{9,1... | collective-permute-start | bytes 331784 | tf_op jit(solution)/shard_map/ppermute | solution.py:990
  5.5 4.4 %collective-permute-start.4 = (f32[72,128]{1,0:T(8,128)S(1)}, f32[72,128]{1,0:T(8,128)S(1)}, u32[]{:S(2)}, u32[]{:S(2)}) collective-permute-start(f32[72,128]{1,0:T(8,128)S(1)} %get-tuple-element.53), channel_id=1, source_target_pairs={{0,28},{4,24},{8,20},{12,16},{16,12},{20,8},{24,4},{28,0},{1,29},{... | collective-permute-start | bytes 110600 | tf_op jit(solution)/shard_map/ppermute | solution.py:960
  6.0 3.9 %collective-permute-start.1 = (f32[72,128]{1,0:T(8,128)S(1)}, f32[72,128]{1,0:T(8,128)S(1)}, u32[]{:S(2)}, u32[]{:S(2)}) collective-permute-start(f32[72,128]{1,0:T(8,128)S(1)} %get-tuple-element.50.cols_ref), channel_id=1, source_target_pairs={{0,24},{8,16},{16,8},{24,0},{1,25},{9,17},{17,9},{25,1},{2,26},{10... | collective-permute-start | bytes 110600 | tf_op jit(solution)/shard_map/ppermute | solution.py:987
  6.7 4.9 %collective-permute-start.3 = (f32[72,128]{1,0:T(8,128)S(1)}, f32[72,128]{1,0:T(8,128)S(1)}, u32[]{:S(2)}, u32[]{:S(2)}) collective-permute-start(f32[72,128]{1,0:T(8,128)S(1)} %get-tuple-element.52), channel_id=1, source_target_pairs={{0,12},{4,8},{8,4},{12,0},{16,28},{20,24},{24,20},{28,16},{1,13},{... | collective-permute-start | bytes 110600 | tf_op jit(solution)/shard_map/ppermute | solution.py:960
  8.2 3.4 %collective-permute-start = (f32[376,128]{1,0:T(8,128)S(1)}, f32[376,128]{1,0:T(8,128)S(1)}, u32[]{:S(2)}, u32[]{:S(2)}) collective-permute-start(f32[376,128]{1,0:T(8,128)S(1)} %shard_map.69), channel_id=1, source_target_pairs={{0,8},{8,0},{16,24},{24,16},{1,9},{9,1},{17,25},{25,17},{2,10},{10... | collective-permute-start | bytes 577544 | tf_op jit(solution)/shard_map/ppermute | solution.py:988
  9.9 2.0 %collective-permute-start.5 = (f32[8,128]{1,0:T(8,128)S(1)}, f32[8,128]{1,0:T(8,128)S(1)}, u32[]{:S(2)}, u32[]{:S(2)}) collective-permute-start(f32[8,128]{1,0:T(8,128)S(1)} %slice_add_fusion), channel_id=1, source_target_pairs={{0,8},{8,0},{16,24},{24,16},{1,9},{9,1},{17,25},{25,17},{2,10},{10... | collective-permute-start | bytes 12296 | tf_op jit(solution)/shard_map/ppermute | solution.py:1017
  10.5 5.7 %collective-permute-start.8 = (f32[232,128]{1,0:T(8,128)S(1)}, f32[232,128]{1,0:T(8,128)S(1)}, u32[]{:S(2)}, u32[]{:S(2)}) collective-permute-start(f32[232,128]{1,0:T(8,128)S(1)} %shard_map.70), channel_id=1, source_target_pairs={{0,24},{8,16},{16,8},{24,0},{1,25},{9,17},{17,9},{25,1},{2,26},{10... | collective-permute-start | bytes 356360 | tf_op jit(solution)/shard_map/ppermute | solution.py:1007
  12.0 6.8 %collective-permute-start.6 = (f32[56,128]{1,0:T(8,128)S(1)}, f32[56,128]{1,0:T(8,128)S(1)}, u32[]{:S(2)}, u32[]{:S(2)}) collective-permute-start(f32[56,128]{1,0:T(8,128)S(1)} %constant_dynamic-update-slice_fusion.1), channel_id=1, source_target_pairs={{0,1},{1,0},{2,3},{3,2},{4,5},{5,4},{6,7},{7,6},{8,9},{9,8},{10,11... | collective-permute-start | bytes 86024 | tf_op jit(solution)/shard_map/ppermute | solution.py:1021
  13.6 5.7 %copy-start.2 = (s32[4,16,128]{2,1,0:T(8,128)S(1)}, s32[4,16,128]{2,1,0:T(8,128)}, u32[]{:S(2)}) copy-start(s32[4,16,128]{2,1,0:T(8,128)} %mask_ref.1) | copy-start | bytes 98308
  13.6 5.7 %collective-permute-start.7 = (f32[56,128]{1,0:T(8,128)S(1)}, f32[56,128]{1,0:T(8,128)S(1)}, u32[]{:S(2)}, u32[]{:S(2)}) collective-permute-start(f32[56,128]{1,0:T(8,128)S(1)} %get-tuple-element.69), channel_id=1, source_target_pairs={{0,3},{1,2},{2,1},{3,0},{4,7},{5,6},{6,5},{7,4},{8,11},{9,10},{10,... | collective-permute-start | bytes 86024 | tf_op jit(solution)/shard_map/ppermute | solution.py:1020
  16.1 4.9 %collective-permute-start.9 = (f32[8,128]{1,0:T(8,128)S(1)}, f32[8,128]{1,0:T(8,128)S(1)}, u32[]{:S(2)}, u32[]{:S(2)}) collective-permute-start(f32[8,128]{1,0:T(8,128)S(1)} %get-tuple-element.70.refs_0_), channel_id=1, source_target_pairs={{0,2},{1,3},{2,0},{3,1},{4,6},{5,7},{6,4},{7,5},{8,10},{9,11},{10,... | collective-permute-start | bytes 12296 | tf_op jit(solution)/shard_map/ppermute | solution.py:1040

commit v9 on v8

--- a/solution.py
+++ b/solution.py
@@ -48,7 +48,7 @@
 
 
 def y_rows(nx):
-    return -(-NSLOT * nx // 8) * 8
+    return 14 * nx + 8
 
 
 ZGROUPS = (
@@ -304,6 +304,15 @@
 
     pl.when(parity("gx") == 0)(functools.partial(fill, -1))
     pl.when(parity("gx") == 1)(functools.partial(fill, 1))
+
+
+def y_edge_entries(sign, nx):
+    rows = []
+    for side in (1, -1):
+        x = 0 if side > 0 else nx - 1
+        rows += [(i, 0, x) for i in far(0, side) if VEL[i][1] == 0]
+        rows += [(i, 1, x) for i in far(0, side) if VEL[i][1] == sign]
+    return rows
 
 
 def edge_entries(sign):
@@ -365,7 +374,7 @@
 
 
 def pack_y_kernel(
-    adj_ref, ub_ref, drag_ref, cols_ref, y_ref, ya_ref, yb_ref
+    adj_ref, ub_ref, drag_ref, cols_ref, y_ref, ya_ref, yb_ref, read_ref
 ):
     nx, ny, nz = adj_ref.shape[1:]
     pair = lax.broadcasted_iota(jnp.int32, (8, nz), 1) // 2
@@ -392,17 +401,45 @@
                 ya_ref[row : row + 1] = line
                 yb_ref[row : row + 1] = line
 
+    faces = ((1, 0, 1), (-1, ny - 1, ny - 2))
+    for i in range(19):
+        cx, cy, _ = VEL[i]
+        read_ref[i] = jnp.zeros((2 * nx, nz), jnp.float32)
+        for n, (sign, here, inside) in enumerate(faces):
+            for x in range(max(0, -cx), min(nx, nx - cx)):
+                if cy * sign >= 0:
+                    y = inside if cy else here
+                    read_ref[i, n * nx + x : n * nx + x + 1, :] = adj_ref[
+                        i, x + cx, y : y + 1, :
+                    ]
+    for k in range(4):
+        for n, (sign, here, inside) in enumerate(faces):
+            for x in range(nx):
+                read_ref[19 + k, n * nx + x : n * nx + x + 1, :] = ub_ref[
+                    k, x, here : here + 1, :
+                ]
+    got = [z_shifted(read_ref[i], VEL[i][2]) for i in range(19)]
+    sums, _ = adjoint_cell(
+        got, [read_ref[19 + k] for k in range(3)], read_ref[22], 0.0
+    )
+
     def fill_y(place, sign):
-        for names, offset, y in (
-            (near(1, sign), 0, 0 if sign > 0 else ny - 1),
-            (far(1, sign), 18, 1 if sign > 0 else ny - 2),
-        ):
-            for k, q in enumerate(names):
-                for x in range(nx):
-                    row = place * y_block + (k + offset) * nx + x
-                    y_ref[row : row + 1] = cell_rows(
-                        adj_ref, ub_ref, q, x, slice(y, y + 1)
-                    )
+        n = 0 if sign > 0 else 1
+        _, here, inside = faces[n]
+        first = place * y_block
+        for k, i in enumerate(far(1, sign)):
+            row = first + k * nx
+            y_ref[row : row + nx] = sums[i][n * nx : (n + 1) * nx]
+        for k, q in enumerate(far(1, sign) + UB):
+            for x in range(nx):
+                row = first + (5 + k) * nx + x
+                y_ref[row : row + 1] = cell_rows(
+                    adj_ref, ub_ref, q, x, slice(here, here + 1)
+                )
+        for k, (i, depth, x) in enumerate(y_edge_entries(sign, nx)):
+            y = inside if depth else here
+            row = first + 14 * nx + k
+            y_ref[row : row + 1] = adj_ref[i, x, y : y + 1, :]
 
     def fill_corner(out_ref, place, sx, sy):
         names = corner_rows(sx, sy)
@@ -566,9 +603,6 @@
     drag_ref[...] = drag
 
 
-OUT_GROUPS = ((0, 7), (7, 13), (13, 17), (17, 19))
-
-
 def turn(value, shift):
     nz = value.shape[1]
     return pltpu.roll(value, shift % nz, 1) if shift % nz else value
@@ -644,20 +678,32 @@
         fill_whole(-1)
         fill_partial(1)
 
+    sums = {}
     for sign in (1, -1):
         block = y_rows(nx) + EDGE_ROWS
         first, second = (0, block) if sign > 0 else (block, 0)
-        for names, depth, offset in ((near(1, sign), 0, 0), (far(1, sign), 1, 18)):
+        one, two = lines[sign]
+        nothing = jnp.zeros((1, nz), jnp.float32)
+        for q in range(19):
+            for x in range(nx):
+                if VEL[q][1] == 0:
+                    ext[q, x + 2, one : one + 1, :] = nothing
+                elif VEL[q][1] == sign:
+                    ext[q, x + 2, two : two + 1, :] = nothing
+        got = jnp.where(
+            even_y,
+            y_ref[first : first + y_rows(nx)],
+            y_ref[second : second + y_rows(nx)],
+        )
+        sums[sign] = got
+        for k, q in enumerate(far(1, sign) + UB):
+            for x in range(nx):
+                row = (5 + k) * nx + x
+                ext[q, x + 2, one : one + 1, :] = got[row : row + 1]
+        for k, (q, depth, x) in enumerate(y_edge_entries(sign, nx)):
             line = lines[sign][depth]
-            for k, q in enumerate(names):
-                row = (k + offset) * nx
-                got = jnp.where(
-                    even_y,
-                    y_ref[first + row : first + row + nx],
-                    y_ref[second + row : second + row + nx],
-                )
-                for x in range(nx):
-                    ext[q, x + 2, line : line + 1, :] = got[x : x + 1]
+            row = 14 * nx + k
+            ext[q, x + 2, line : line + 1, :] = got[row : row + 1]
         for sx in (1, -1):
             xs = (ya_ref, yb_ref) if sx > 0 else (yb_ref, ya_ref)
             block = CORNER + EDGE_ROWS
@@ -688,6 +734,12 @@
             got.append(z_shifted(near_cells(i, p + 1 + cx, t, cy), cz))
         ub = [near_cells(19 + k, p + 1, t, 0) for k in range(4)]
         out, kept = adjoint_cell(got, ub[:3], ub[3], 1.0)
+        if t == tiles and 1 <= p <= nx:
+            for sign, row in ((1, 0), (-1, 7)):
+                for k, i in enumerate(far(1, sign)):
+                    line = k * nx + p - 1
+                    term = sums[sign][line : line + 1]
+                    out[i] = out[i] + jnp.where(sub == row, term, 0.0)
         if partial is not None:
             for k, i in enumerate(kinds):
                 row = k * ny + 8 * t
@@ -714,12 +766,8 @@
         first_level(0, t, far(0, -1), even_x)
         first_level(nx + 1, t, far(0, 1), jnp.logical_not(even_x))
 
-    def rim(n, carry):
-        for p in (2 * n, 2 * n + 1):
-            first_level(p, tiles, far(1, -1) + far(1, 1))
-        return carry
-
-    lax.fori_loop(0, (nx + 2) // 2, rim, 0)
+    for p in range(nx + 2):
+        first_level(p, tiles, far(1, -1) + far(1, 1))
 
     def second_level(x, carry):
         for t in range(tiles):
@@ -777,16 +825,13 @@
     inner_ref,
     grad1_ref,
     inner_grad_ref,
-    out_hbm,
-    grad_hbm,
+    out_ref,
+    grad_ref,
     tail_ref,
     first_ref,
     second_ref,
     zmid,
     zout,
-    out_ref,
-    grad_ref,
-    sems,
 ):
     nx, ny, nz = mask_ref.shape
     tiles = ny // 8
@@ -876,10 +921,6 @@
         zout[19, rows, :] = gradient_cell(kept, f[0], fs, fd, fm, u)
         zout[20, rows, :] = slab_grad[t]
 
-    def out_copy(k):
-        part = slice(*OUT_GROUPS[k])
-        return pltpu.make_async_copy(out_ref.at[part], out_hbm.at[part], sems.at[k])
-
     outer = (lane < 2) | (lane >= nz - 2)
     ends = (lane < 1) | (lane >= nz - 1)
     for x in range(nx):
@@ -891,30 +932,32 @@
             edge = turn(zout[19, rows, :], -2 - 4 * x) + level1
             grad = jnp.where(outer, edge, inner_grad_ref[x, rows, :])
             grad_ref[x, rows, :] = jnp.where(mask_ref[x, rows, :] == 0, grad, 0.0)
-    grad_copy = pltpu.make_async_copy(grad_ref, grad_hbm, sems.at[len(OUT_GROUPS)])
-    grad_copy.start()
-    for k, group in enumerate(OUT_GROUPS):
-        for i in range(*group):
-            for x in range(nx):
-                for t in range(tiles):
-                    rows = slice(8 * t, 8 * t + 8)
-                    out_ref[i, x, rows, :] = jnp.where(
-                        outer,
-                        turn(zout[i, rows, :], -2 - 4 * x),
-                        inner_ref[i, x, rows, :],
-                    )
-        out_copy(k).start()
-    grad_copy.wait()
-    for k in range(len(OUT_GROUPS)):
-        out_copy(k).wait()
-
-
-def drag_kernel(whole_cells, *refs):
-    total = refs[0][...]
-    for ref in refs[1:-1]:
+    for i in range(19):
+        for x in range(nx):
+            for t in range(tiles):
+                rows = slice(8 * t, 8 * t + 8)
+                out_ref[i, x, rows, :] = jnp.where(
+                    outer, turn(zout[i, rows, :], -2 - 4 * x), inner_ref[i, x, rows, :]
+                )
+
+
+def finish_kernel(whole_cells, out_ref, grad_ref, *refs):
+    tiles, (out_hbm, grad_hbm, drag_hbm, drag_ref, sems) = refs[:-5], refs[-5:]
+    copies = [
+        pltpu.make_async_copy(out_ref, out_hbm, sems.at[0]),
+        pltpu.make_async_copy(grad_ref, grad_hbm, sems.at[1]),
+        pltpu.make_async_copy(drag_ref, drag_hbm, sems.at[2]),
+    ]
+    for copy in copies[:2]:
+        copy.start()
+    total = tiles[0][...]
+    for ref in tiles[1:]:
         total = total + ref[...]
     summed = jnp.sum(jnp.sum(total, axis=1, keepdims=True), axis=0, keepdims=True)
-    refs[-1][...] = summed / whole_cells
+    drag_ref[...] = summed / whole_cells
+    copies[2].start()
+    for copy in copies:
+        copy.wait()
 
 
 def swaps(count):
@@ -929,7 +972,7 @@
 PARAMS = pltpu.CompilerParams(vmem_limit_bytes=48 * 2**20)
 
 
-def call(kernel, inputs, shapes, scratch=(), space=VMEM, micros=1, outs=None):
+def call(kernel, inputs, shapes, scratch=(), space=VMEM, micros=0.05, outs=None):
     if space is HBM:
         inputs = [pltpu.with_memory_space_constraint(x, pltpu.HBM) for x in inputs]
     return pl.pallas_call(
@@ -980,6 +1023,7 @@
         pack_y_kernel,
         (adjoint_last, ub, drag),
         [(4 * ny + 8, nz), (rows_y, nz), (rows_c, nz), (rows_c, nz)],
+        [pltpu.VMEM((NSLOT, 2 * nx, nz), f32)],
         micros=4,
     )
     (xa,) = call(pack_x_kernel, (adjoint_last, ub, drag), [(rows_x, nz)])
@@ -1003,7 +1047,7 @@
         block = CORNER + EDGE_ROWS
         yb = both(yb, block, lambda m, pairs: diagonal(m, x_second, pairs))
         ya = both(ya, block, lambda m, pairs: diagonal(m, x_first, pairs))
-    xb, yb = lax.optimization_barrier((xb, yb))
+    xb, y = lax.optimization_barrier((xb, y))
     xb = lax.ppermute(xb, "gx", x_second)
 
     zown, za, zb, drag_xy = call(
@@ -1051,16 +1095,18 @@
             pltpu.VMEM((4 * height, nz), f32),
             pltpu.VMEM((19, height + 8, nz), f32),
             pltpu.VMEM((21, ny, nz), f32),
-            pltpu.VMEM((19, nx, ny, nz), f32),
-            pltpu.VMEM((nx, ny, nz), f32),
-            pltpu.SemaphoreType.DMA((len(OUT_GROUPS) + 1,)),
         ],
-        outs=[HBM, HBM, VMEM],
     )
     if rides:
         drags += (tails,)
     whole_cells = float(nx * ny * nz * gx * gy * gz)
-    (drag,) = call(functools.partial(drag_kernel, whole_cells), drags, [(1, 1)])
+    first, gradient, drag = call(
+        functools.partial(finish_kernel, whole_cells),
+        (first, gradient) + drags,
+        [(19, nx, ny, nz), (nx, ny, nz), (1, 1)],
+        [pltpu.VMEM((1, 1), f32), pltpu.SemaphoreType.DMA((3,))],
+        outs=[HBM, HBM, HBM],
+    )
     return (first, gradient, drag.reshape(()))
 
 

time: 21.8 us -> 21.5 us (0.986)
  Pallas kernels: 7.03 us -> 6.34 us
  waiting for transfers between devices: 1.43 us -> 1.97 us
    pallas_call x8, Pallas kernels: 7.03 us -> 6.34 us  [call(): pl.pallas_call(kernel, out_shape=[jax.ShapeDtypeStruct(s, jnp.float32) fo...]
    ppermute x1, waiting for transfers between devices: 0.01 us -> 0.37 us  [body(): zhalf = lax.ppermute(drag_xy, 'gz', [(i, i ^ 2) for i in range(gz)])]
  transfers between devices with their start and end apart: 10 -> 10, of which waited for: 2 -> 3; matrix products, arithmetic and copies ran while one was open for 0% -> 0% of each run, Pallas kernels for 22% -> 18%
where the time goes in v9:
time: 21.5 us; the launch traced here: 21.4 us
  starting transfers between devices  12.3 us (57%)
  Pallas kernels  6.34 us (29%)
  waiting for transfers between devices  1.97 us (9%)
  between operations  0.75 us (3%)
    pallas_call x8, Pallas kernels, call(): pl.pallas_call(kernel, out_shape=[jax.ShapeDtypeStruct(s, jnp.float32) fo...  6.34 us
    ppermute x1, starting transfers between devices, body(): y = lax.ppermute(y, 'gy', y_first)  3.05 us
    ppermute x1, starting transfers between devices, body(): zb = lax.ppermute(zb, 'gz', z_second)  2.47 us
    ppermute x2, starting transfers between devices, diagonal(): return lax.ppermute(message, ('gx', 'gy'), pairs)  1.99 us
    ppermute x1, starting transfers between devices, body(): za = lax.ppermute(za, 'gz', z_first)  1.64 us
    ppermute x1, starting transfers between devices, body(): xb = lax.ppermute(xb, 'gx', x_second)  1.01 us
    ppermute x2, waiting for transfers between devices, diagonal(): return lax.ppermute(message, ('gx', 'gy'), pairs)  0.87 us
    ppermute x1, waiting for transfers between devices, body(): zb = lax.ppermute(zb, 'gz', z_second)  0.71 us
  transfers between devices with their start and end apart: 10, of which 3 were waited for; matrix products, arithmetic and copies ran while one was open for 0% of the time, Pallas kernels for 18%

profile of v9, /device:TPU:0, one launch (start us, length us, event | category | flops | bytes accessed | tf_op | source)
XLA Modules:
  0.0 21.4 jit_solution(8067057298701947244)
XLA Ops:
  0.6 1.3 %shard_map.67 = (f32[4,4,16,128]{3,2,1,0:T(8,128)S(1)}, f32[8,128]{1,0:T(8,128)S(1)}) custom-call(f32[2,19,4,16,128]{4,3,2,1,0:T(8,128)} %states_ref.1, f32[4,16,128]{2,1,0:T(8,128)} %por_hbm.1, s32[4,16,128]{2,1,0:T(8,128)} %mask_ref.1), custom_call_target="tpu_custom_call" | custom-call | bytes 180000 | tf_op jit(solution)/shard_map/pallas_call | solution.py:978
  2.0 0.0 copy-done
  2.0 0.4 %shard_map.68 = (f32[72,128]{1,0:T(8,128)S(1)}, f32[152,128]{1,0:T(8,128)S(1)}, f32[72,128]{1,0:T(8,128)S(1)}, f32[72,128]{1,0:T(8,128)S(1)}) custom-call(f32[19,4,16,128]{3,2,1,0:T(8,128)S(1)} %copy-done, f32[4,4,16,128]{3,2,1,0:T(8,128)S(1)} %get-tuple-element.51.ub_ref, f32[8,128]{1,0:T(8,128)S(1)} %get-tuple-element.52.drag_ref), custom_call_target="tpu_custom_call" | custom-call | bytes 14400000 | tf_op jit(solution)/shard_map/pallas_call | solution.py:978
  2.4 0.0 copy-start.1
  2.4 3.0 %collective-permute-start.2 = (f32[152,128]{1,0:T(8,128)S(1)}, f32[152,128]{1,0:T(8,128)S(1)}, u32[]{:S(2)}, u32[]{:S(2)}) collective-permute-start(f32[152,128]{1,0:T(8,128)S(1)} %get-tuple-element.54), channel_id=1, source_target_pairs={{0,4},{4,0},{1,5},{5,1},{2,6},{6,2},{3,7},{7,3},{8,12},{12,8},{9,1... | collective-permute-start | bytes 233480 | tf_op jit(solution)/shard_map/ppermute | solution.py:1034
  5.5 0.6 %collective-permute-start.4 = (f32[72,128]{1,0:T(8,128)S(1)}, f32[72,128]{1,0:T(8,128)S(1)}, u32[]{:S(2)}, u32[]{:S(2)}) collective-permute-start(f32[72,128]{1,0:T(8,128)S(1)} %get-tuple-element.57), channel_id=1, source_target_pairs={{0,28},{4,24},{8,20},{12,16},{16,12},{20,8},{24,4},{28,0},{1,29},{... | collective-permute-start | bytes 110600 | tf_op jit(solution)/shard_map/ppermute | solution.py:1003
  6.0 0.7 %collective-permute-start.1 = (f32[72,128]{1,0:T(8,128)S(1)}, f32[72,128]{1,0:T(8,128)S(1)}, u32[]{:S(2)}, u32[]{:S(2)}) collective-permute-start(f32[72,128]{1,0:T(8,128)S(1)} %get-tuple-element.53.cols_ref), channel_id=1, source_target_pairs={{0,24},{8,16},{16,8},{24,0},{1,25},{9,17},{17,9},{25,1},{2,26},{10... | collective-permute-start | bytes 110600 | tf_op jit(solution)/shard_map/ppermute | solution.py:1031
  6.7 1.4 %collective-permute-start.3 = (f32[72,128]{1,0:T(8,128)S(1)}, f32[72,128]{1,0:T(8,128)S(1)}, u32[]{:S(2)}, u32[]{:S(2)}) collective-permute-start(f32[72,128]{1,0:T(8,128)S(1)} %get-tuple-element.56), channel_id=1, source_target_pairs={{0,12},{4,8},{8,4},{12,0},{16,28},{20,24},{24,20},{28,16},{1,13},{... | collective-permute-start | bytes 110600 | tf_op jit(solution)/shard_map/ppermute | solution.py:1003
  8.2 0.7 %collective-permute-start = (f32[376,128]{1,0:T(8,128)S(1)}, f32[376,128]{1,0:T(8,128)S(1)}, u32[]{:S(2)}, u32[]{:S(2)}) collective-permute-start(f32[376,128]{1,0:T(8,128)S(1)} %shard_map.69), channel_id=1, source_target_pairs={{0,8},{8,0},{16,24},{24,16},{1,9},{9,1},{17,25},{25,17},{2,10},{10... | collective-permute-start | bytes 577544 | tf_op jit(solution)/shard_map/ppermute | solution.py:1032
  8.9 0.1 shard_map.70
  9.0 0.0 collective-permute-done.2.y_ref
  9.0 0.9 %collective-permute-done.4.yb_ref = f32[72,128]{1,0:T(8,128)S(1)} collective-permute-done((f32[72,128]{1,0:T(8,128)S(1)}, f32[72,128]{1,0:T(8,128)S(1)}, u32[]{:S(2)}, u32[]{:S(2)}) %collective-permute-start.4) | collective-permute-done | bytes 36896 | tf_op jit(solution)/shard_map/ppermute | solution.py:1003
  9.9 0.6 %collective-permute-start.5 = (f32[8,128]{1,0:T(8,128)S(1)}, f32[8,128]{1,0:T(8,128)S(1)}, u32[]{:S(2)}, u32[]{:S(2)}) collective-permute-start(f32[8,128]{1,0:T(8,128)S(1)} %fusion), channel_id=1, source_target_pairs={{0,8},{8,0},{16,24},{24,16},{1,9},{9,1},{17,25},{25,17},{2,10},{10... | collective-permute-start | bytes 12296 | tf_op jit(solution)/shard_map/ppermute | solution.py:1061
  10.5 1.0 %collective-permute-start.8 = (f32[232,128]{1,0:T(8,128)S(1)}, f32[232,128]{1,0:T(8,128)S(1)}, u32[]{:S(2)}, u32[]{:S(2)}) collective-permute-start(f32[232,128]{1,0:T(8,128)S(1)} %shard_map.70), channel_id=1, source_target_pairs={{0,24},{8,16},{16,8},{24,0},{1,25},{9,17},{17,9},{25,1},{2,26},{10... | collective-permute-start | bytes 356360 | tf_op jit(solution)/shard_map/ppermute | solution.py:1051
  11.5 0.4 %shard_map.71 = (f32[96,128]{1,0:T(8,128)S(1)}, f32[56,128]{1,0:T(8,128)S(1)}, f32[56,128]{1,0:T(8,128)S(1)}, f32[8,128]{1,0:T(8,128)S(1)}) custom-call(f32[72,128]{1,0:T(8,128)S(1)} %get-tuple-element.53.cols_ref, f32[376,128]{1,0:T(8,128)S(1)} %collective-permute-done.xa_ref, f32[72,128]{1,0:T(8,128)S(1)} %collective-permute-done.1.xc_ref, ...), custom_call_target="tpu_custom_call" | custom-call | bytes 180000 | tf_op jit(solution)/shard_map/pallas_call | solution.py:978
  11.9 0.0 copy-start.2
  11.9 1.6 %collective-permute-start.6 = (f32[56,128]{1,0:T(8,128)S(1)}, f32[56,128]{1,0:T(8,128)S(1)}, u32[]{:S(2)}, u32[]{:S(2)}) collective-permute-start(f32[56,128]{1,0:T(8,128)S(1)} %constant_dynamic-update-slice_fusion.1), channel_id=1, source_target_pairs={{0,1},{1,0},{2,3},{3,2},{4,5},{5,4},{6,7},{7,6},{8,9},{9,8},{10,11... | collective-permute-start | bytes 86024 | tf_op jit(solution)/shard_map/ppermute | solution.py:1065
  13.5 2.5 %collective-permute-start.7 = (f32[56,128]{1,0:T(8,128)S(1)}, f32[56,128]{1,0:T(8,128)S(1)}, u32[]{:S(2)}, u32[]{:S(2)}) collective-permute-start(f32[56,128]{1,0:T(8,128)S(1)} %get-tuple-element.75), channel_id=1, source_target_pairs={{0,3},{1,2},{2,1},{3,0},{4,7},{5,6},{6,5},{7,4},{8,11},{9,10},{10,... | collective-permute-start | bytes 86024 | tf_op jit(solution)/shard_map/ppermute | solution.py:1064
  16.0 0.1 collective-permute-start.9
  16.1 2.4 %shard_map.72 = (f32[19,4,16,128]{3,2,1,0:T(8,128)S(1)}, f32[4,16,128]{2,1,0:T(8,128)S(1)}, f32[4,16,128]{2,1,0:T(8,128)S(1)}, f32[19,16,128]{2,1,0:T(8,128)S(1)...) custom-call(f32[2,19,4,16,128]{4,3,2,1,0:T(8,128)S(1)} %copy-done.1, f32[19,4,16,128]{3,2,1,0:T(8,128)S(1)} %copy-done, ...), custom_call_target="tpu_custom_call" | custom-call | bytes 14400000 | tf_op jit(solution)/shard_map/pallas_call | solution.py:978
  18.6 0.7 %collective-permute-done.7.zb_ref = f32[56,128]{1,0:T(8,128)S(1)} collective-permute-done((f32[56,128]{1,0:T(8,128)S(1)}, f32[56,128]{1,0:T(8,128)S(1)}, u32[]{:S(2)}, u32[]{:S(2)}) %collective-permute-start.7) | collective-permute-done | bytes 28704 | tf_op jit(solution)/shard_map/ppermute | solution.py:1064
  19.3 0.9 %shard_map.73 = (f32[19,4,16,128]{3,2,1,0:T(8,128)S(1)}, f32[4,16,128]{2,1,0:T(8,128)S(1)}, f32[8,128]{1,0:T(8,128)S(1)}) custom-call(s32[4,16,128]{2,1,0:T(8,128)S(1)} %copy-done.2, f32[96,128]{1,0:T(8,128)S(1)} %get-tuple-element.58.zown_ref, f32[56,128]{1,0:T(8,128)S(1)} %collective-permute-done.6.za_ref, f32[56,128]{1,0:T(8,128)S(1)} %collective-permute-done.7.zb_ref, ...), custom_call_target="tpu_custom_call" | custom-call | bytes 180000 | tf_op jit(solution)/shard_map/pallas_call | solution.py:978
  20.1 0.4 %collective-permute-done.9.refs_1_ = f32[8,128]{1,0:T(8,128)S(1)} collective-permute-done((f32[8,128]{1,0:T(8,128)S(1)}, f32[8,128]{1,0:T(8,128)S(1)}, u32[]{:S(2)}, u32[]{:S(2)}) %collective-permute-start.9) | collective-permute-done | bytes 4128 | tf_op jit(solution)/shard_map/ppermute | solution.py:1084
  20.5 0.9 %shard_map.74 = (f32[19,4,16,128]{3,2,1,0:T(8,128)}, f32[4,16,128]{2,1,0:T(8,128)}, f32[1,1]{1,0:T(1,128)}) custom-call(f32[19,4,16,128]{3,2,1,0:T(8,128)S(1)} %get-tuple-element.69.out_ref, f32[4,16,128]{2,1,0:T(8,128)S(1)} %get-tuple-element.70.grad_ref, f32[8,128]{1,0:T(8,128)S(1)} %get-tuple-element.76.refs_0_, ...), custom_call_target="tpu_custom_call" | custom-call | bytes 180000 | tf_op jit(solution)/shard_map/pallas_call | solution.py:978
  (13 shorter events, 0.0 us)
Async XLA Ops:
  0.6 1.4 %copy-start = (f32[19,4,16,128]{3,2,1,0:T(8,128)S(1)}, f32[19,4,16,128]{3,2,1,0:T(8,128)}, u32[]{:S(2)}) copy-start(f32[19,4,16,128]{3,2,1,0:T(8,128)} %adj_ref.7) | copy-start | bytes 1867780
  2.4 13.7 %copy-start.1 = (f32[2,19,4,16,128]{4,3,2,1,0:T(8,128)S(1)}, f32[2,19,4,16,128]{4,3,2,1,0:T(8,128)}, u32[]{:S(2)}) copy-start(f32[2,19,4,16,128]{4,3,2,1,0:T(8,128)} %states_ref.1) | copy-start | bytes 3735556
  2.4 6.6 %collective-permute-start.2 = (f32[152,128]{1,0:T(8,128)S(1)}, f32[152,128]{1,0:T(8,128)S(1)}, u32[]{:S(2)}, u32[]{:S(2)}) collective-permute-start(f32[152,128]{1,0:T(8,128)S(1)} %get-tuple-element.54), channel_id=1, source_target_pairs={{0,4},{4,0},{1,5},{5,1},{2,6},{6,2},{3,7},{7,3},{8,12},{12,8},{9,1... | collective-permute-start | bytes 233480 | tf_op jit(solution)/shard_map/ppermute | solution.py:1034
  5.5 4.4 %collective-permute-start.4 = (f32[72,128]{1,0:T(8,128)S(1)}, f32[72,128]{1,0:T(8,128)S(1)}, u32[]{:S(2)}, u32[]{:S(2)}) collective-permute-start(f32[72,128]{1,0:T(8,128)S(1)} %get-tuple-element.57), channel_id=1, source_target_pairs={{0,28},{4,24},{8,20},{12,16},{16,12},{20,8},{24,4},{28,0},{1,29},{... | collective-permute-start | bytes 110600 | tf_op jit(solution)/shard_map/ppermute | solution.py:1003
  6.0 3.9 %collective-permute-start.1 = (f32[72,128]{1,0:T(8,128)S(1)}, f32[72,128]{1,0:T(8,128)S(1)}, u32[]{:S(2)}, u32[]{:S(2)}) collective-permute-start(f32[72,128]{1,0:T(8,128)S(1)} %get-tuple-element.53.cols_ref), channel_id=1, source_target_pairs={{0,24},{8,16},{16,8},{24,0},{1,25},{9,17},{17,9},{25,1},{2,26},{10... | collective-permute-start | bytes 110600 | tf_op jit(solution)/shard_map/ppermute | solution.py:1031
  6.7 4.8 %collective-permute-start.3 = (f32[72,128]{1,0:T(8,128)S(1)}, f32[72,128]{1,0:T(8,128)S(1)}, u32[]{:S(2)}, u32[]{:S(2)}) collective-permute-start(f32[72,128]{1,0:T(8,128)S(1)} %get-tuple-element.56), channel_id=1, source_target_pairs={{0,12},{4,8},{8,4},{12,0},{16,28},{20,24},{24,20},{28,16},{1,13},{... | collective-permute-start | bytes 110600 | tf_op jit(solution)/shard_map/ppermute | solution.py:1003
  8.2 3.3 %collective-permute-start = (f32[376,128]{1,0:T(8,128)S(1)}, f32[376,128]{1,0:T(8,128)S(1)}, u32[]{:S(2)}, u32[]{:S(2)}) collective-permute-start(f32[376,128]{1,0:T(8,128)S(1)} %shard_map.69), channel_id=1, source_target_pairs={{0,8},{8,0},{16,24},{24,16},{1,9},{9,1},{17,25},{25,17},{2,10},{10... | collective-permute-start | bytes 577544 | tf_op jit(solution)/shard_map/ppermute | solution.py:1032
  9.9 2.0 %collective-permute-start.5 = (f32[8,128]{1,0:T(8,128)S(1)}, f32[8,128]{1,0:T(8,128)S(1)}, u32[]{:S(2)}, u32[]{:S(2)}) collective-permute-start(f32[8,128]{1,0:T(8,128)S(1)} %fusion), channel_id=1, source_target_pairs={{0,8},{8,0},{16,24},{24,16},{1,9},{9,1},{17,25},{25,17},{2,10},{10... | collective-permute-start | bytes 12296 | tf_op jit(solution)/shard_map/ppermute | solution.py:1061
  10.5 5.7 %collective-permute-start.8 = (f32[232,128]{1,0:T(8,128)S(1)}, f32[232,128]{1,0:T(8,128)S(1)}, u32[]{:S(2)}, u32[]{:S(2)}) collective-permute-start(f32[232,128]{1,0:T(8,128)S(1)} %shard_map.70), channel_id=1, source_target_pairs={{0,24},{8,16},{16,8},{24,0},{1,25},{9,17},{17,9},{25,1},{2,26},{10... | collective-permute-start | bytes 356360 | tf_op jit(solution)/shard_map/ppermute | solution.py:1051
  11.9 7.4 %copy-start.2 = (s32[4,16,128]{2,1,0:T(8,128)S(1)}, s32[4,16,128]{2,1,0:T(8,128)}, u32[]{:S(2)}) copy-start(s32[4,16,128]{2,1,0:T(8,128)} %mask_ref.1) | copy-start | bytes 98308
  11.9 6.7 %collective-permute-start.6 = (f32[56,128]{1,0:T(8,128)S(1)}, f32[56,128]{1,0:T(8,128)S(1)}, u32[]{:S(2)}, u32[]{:S(2)}) collective-permute-start(f32[56,128]{1,0:T(8,128)S(1)} %constant_dynamic-update-slice_fusion.1), channel_id=1, source_target_pairs={{0,1},{1,0},{2,3},{3,2},{4,5},{5,4},{6,7},{7,6},{8,9},{9,8},{10,11... | collective-permute-start | bytes 86024 | tf_op jit(solution)/shard_map/ppermute | solution.py:1065
  13.5 5.7 %collective-permute-start.7 = (f32[56,128]{1,0:T(8,128)S(1)}, f32[56,128]{1,0:T(8,128)S(1)}, u32[]{:S(2)}, u32[]{:S(2)}) collective-permute-start(f32[56,128]{1,0:T(8,128)S(1)} %get-tuple-element.75), channel_id=1, source_target_pairs={{0,3},{1,2},{2,1},{3,0},{4,7},{5,6},{6,5},{7,4},{8,11},{9,10},{10,... | collective-permute-start | bytes 86024 | tf_op jit(solution)/shard_map/ppermute | solution.py:1064
  16.0 4.5 %collective-permute-start.9 = (f32[8,128]{1,0:T(8,128)S(1)}, f32[8,128]{1,0:T(8,128)S(1)}, u32[]{:S(2)}, u32[]{:S(2)}) collective-permute-start(f32[8,128]{1,0:T(8,128)S(1)} %get-tuple-element.76.refs_0_), channel_id=1, source_target_pairs={{0,2},{1,3},{2,0},{3,1},{4,6},{5,7},{6,4},{7,5},{8,10},{9,11},{10,... | collective-permute-start | bytes 12296 | tf_op jit(solution)/shard_map/ppermute | solution.py:1084

commit v10 on v9

--- a/solution.py
+++ b/solution.py
@@ -594,12 +594,26 @@
         two, three = packed[2][t], packed[3][t]
         up = (packed[0][t], jnp.where(even_lane, two, pltpu.roll(three, 1, 1)))
         down = (packed[1][t], jnp.where(even_lane, pltpu.roll(two, nz - 1, 1), three))
-        for g in range(2):
-            row = (g * (tiles + 1) + t) * 8
+        if t == tiles:
+            up, down = [
+                (
+                    jnp.where(
+                        (sub == 0) | (sub == 7),
+                        side[0],
+                        jnp.where(
+                            sub < 4, pltpu.roll(side[1], 1, 0), pltpu.roll(side[1], 7, 0)
+                        ),
+                    ),
+                )
+                for side in (up, down)
+            ]
+        for g in range(len(up)):
+            row = (g * tiles + t) * 8 if t < tiles else 2 * tiles * 8
             za_ref[row : row + 8, :] = jnp.where(up_first, up[g], down[g])
             zb_ref[row : row + 8, :] = jnp.where(up_first, down[g], up[g])
-    drag = (cols_ref[4 * ny :] + y_ref[2 * y_block :]) + xa_ref[xa_ref.shape[0] - 8 :]
-    drag = drag + (xc_ref[4 * ny :] + yb_ref[2 * corner_block :])
+    drag = cols_ref[4 * ny :] + y_ref[2 * y_block :]
+    for x_ref, c_ref in ((xa_ref, ya_ref), (xc_ref, yb_ref)):
+        drag = drag + (x_ref[x_ref.shape[0] - 8 :] + c_ref[2 * corner_block :])
     drag_ref[...] = drag
 
 
@@ -838,10 +852,11 @@
     height = (tiles + 1) * 8
     even = parity("gz") == 0
     lane = lax.broadcasted_iota(jnp.int32, (8, nz), 1)
+    sub = lax.broadcasted_iota(jnp.int32, (8, nz), 0)
     even_lane = lane % 2 == 0
     low_pair = lane % 4 < 2
 
-    last = slice(2 * height, 2 * height + 8)
+    last = slice(2 * ny + 3, 2 * ny + 4)
     tail_ref[...] = za_ref[last] + zb_ref[last]
 
     def swapped(value):
@@ -850,9 +865,14 @@
     for t in range(tiles + 1):
         received = []
         for g in range(2):
-            row = (g * (tiles + 1) + t) * 8
+            row = (g * tiles + t) * 8 if t < tiles else 2 * ny
             va = za_ref[row : row + 8, :]
             vb = zb_ref[row : row + 8, :]
+            if t == tiles and g:
+                va, vb = [
+                    jnp.where(sub < 4, pltpu.roll(v, 7, 0), pltpu.roll(v, 1, 0))
+                    for v in (va, vb)
+                ]
             received.append((jnp.where(even, va, vb), jnp.where(even, vb, va)))
         (high0, low0), (high1, low1) = received
         for g in range(4):
@@ -950,11 +970,10 @@
     ]
     for copy in copies[:2]:
         copy.start()
-    total = tiles[0][...]
-    for ref in tiles[1:]:
-        total = total + ref[...]
-    summed = jnp.sum(jnp.sum(total, axis=1, keepdims=True), axis=0, keepdims=True)
-    drag_ref[...] = summed / whole_cells
+    total = 0.0
+    for ref in tiles:
+        total = total + jnp.sum(ref[...], axis=0, keepdims=True)
+    drag_ref[...] = jnp.sum(total, axis=1, keepdims=True) / whole_cells
     copies[2].start()
     for copy in copies:
         copy.wait()
@@ -1005,7 +1024,7 @@
     rows_x = NSLOT * ny + 8
     rows_y = 2 * (y_rows(nx) + EDGE_ROWS) + 8
     rows_c = 2 * (CORNER + EDGE_ROWS) + 8
-    rows_z = 2 * height + 8
+    rows_z = 2 * ny + 8
     rides = (gx, gy, gz) == (4, 2, 4)
     ub, drag = call(
         state_kernel,
@@ -1047,7 +1066,7 @@
         block = CORNER + EDGE_ROWS
         yb = both(yb, block, lambda m, pairs: diagonal(m, x_second, pairs))
         ya = both(ya, block, lambda m, pairs: diagonal(m, x_first, pairs))
-    xb, y = lax.optimization_barrier((xb, y))
+    xb, yb = lax.optimization_barrier((xb, yb))
     xb = lax.ppermute(xb, "gx", x_second)
 
     zown, za, zb, drag_xy = call(
@@ -1057,10 +1076,11 @@
         [pltpu.VMEM((4, ny + 32, nz), f32)],
     )
     if rides:
-        second = xc[4 * ny :] + yb[rows_c - 8 :] + y[rows_y - 8 :]
+        second = xc[4 * ny :] + yb[rows_c - 8 :]
         drag_xy = drag_xy + lax.ppermute(second, "gx", x_first)
-        za = za.at[2 * height :].set(drag_xy)
-        zb = zb.at[2 * height :].set(drag_xy)
+        drag_xy = jnp.sum(drag_xy, axis=0, keepdims=True)
+        za = za.at[2 * ny + 3 : 2 * ny + 4].set(drag_xy)
+        zb = zb.at[2 * ny + 3 : 2 * ny + 4].set(drag_xy)
     zb = lax.ppermute(zb, "gz", z_second)
     za = lax.ppermute(za, "gz", z_first)
     inner, grad1, inner_grad, pack, f0, f1 = call(
@@ -1089,7 +1109,7 @@
     first, gradient, tails = call(
         edge_kernel,
         (solid_mask, zown, za, zb, pack, f0, f1, inner, grad1, inner_grad),
-        [(19, nx, ny, nz), (nx, ny, nz), (8, nz)],
+        [(19, nx, ny, nz), (nx, ny, nz), (1, nz)],
         [
             pltpu.VMEM((4 * height, nz), f32),
             pltpu.VMEM((4 * height, nz), f32),

time: 21.5 us -> 21.2 us (0.986)
  waiting for transfers between devices: 1.97 us -> 1.09 us
  starting transfers between devices: 12.3 us -> 12.8 us
    ppermute x1, starting transfers between devices: 3.05 us -> 0.01 us  [body(): y = lax.ppermute(y, 'gy', y_first)]
    ppermute x2, starting transfers between devices: 1.99 us -> 4.63 us  [diagonal(): return lax.ppermute(message, ('gx', 'gy'), pairs)]
    ppermute x1, starting transfers between devices: 1.64 us -> 0.06 us  [body(): za = lax.ppermute(za, 'gz', z_first)]
    ppermute x1, starting transfers between devices: 2.47 us -> 3.85 us  [body(): zb = lax.ppermute(zb, 'gz', z_second)]
    ppermute x2, waiting for transfers between devices: 0.87 us -> 0.01 us  [diagonal(): return lax.ppermute(message, ('gx', 'gy'), pairs)]
    ppermute x1, waiting for transfers between devices: 0.01 us -> 0.77 us  [body(): za = lax.ppermute(za, 'gz', z_first)]
    ppermute x1, waiting for transfers between devices: 0.71 us -> 0.01 us  [body(): zb = lax.ppermute(zb, 'gz', z_second)]
    ppermute x1, starting transfers between devices: 0.12 us -> 0.59 us  [body(): zhalf = lax.ppermute(drag_xy, 'gz', [(i, i ^ 2) for i in range(gz)])]
where the time goes in v10:
time: 21.2 us; the launch traced here: 21.1 us
  starting transfers between devices  12.8 us (60%)
  Pallas kernels  6.32 us (30%)
  waiting for transfers between devices  1.09 us (5%)
  between operations  0.76 us (4%)
    pallas_call x8, Pallas kernels, call(): pl.pallas_call(kernel, out_shape=[jax.ShapeDtypeStruct(s, jnp.float32) fo...  6.32 us
    ppermute x2, starting transfers between devices, diagonal(): return lax.ppermute(message, ('gx', 'gy'), pairs)  4.63 us
    ppermute x1, starting transfers between devices, body(): zb = lax.ppermute(zb, 'gz', z_second)  3.85 us
    ppermute x1, starting transfers between devices, body(): xa = lax.ppermute(xa, 'gx', x_first)  0.99 us
    ppermute x1, starting transfers between devices, body(): drag_xy = drag_xy + lax.ppermute(second, 'gx', x_first)  0.97 us
    ppermute x1, starting transfers between devices, body(): xb = lax.ppermute(xb, 'gx', x_second)  0.87 us
    ppermute x1, starting transfers between devices, body(): xc = lax.ppermute(cols, 'gx', x_second)  0.82 us
    ppermute x1, waiting for transfers between devices, body(): za = lax.ppermute(za, 'gz', z_first)  0.77 us
  transfers between devices with their start and end apart: 10, of which 3 were waited for; matrix products, arithmetic and copies ran while one was open for 0% of the time, Pallas kernels for 18%

profile of v10, /device:TPU:0, one launch (start us, length us, event | category | flops | bytes accessed | tf_op | source)
XLA Modules:
  0.0 21.1 jit_solution(10967582830238180608)
XLA Ops:
  0.6 1.3 %shard_map.67 = (f32[4,4,16,128]{3,2,1,0:T(8,128)S(1)}, f32[8,128]{1,0:T(8,128)S(1)}) custom-call(f32[2,19,4,16,128]{4,3,2,1,0:T(8,128)} %states_ref.1, f32[4,16,128]{2,1,0:T(8,128)} %por_hbm.1, s32[4,16,128]{2,1,0:T(8,128)} %mask_ref.1), custom_call_target="tpu_custom_call" | custom-call | bytes 180000 | tf_op jit(solution)/shard_map/pallas_call | solution.py:997
  2.0 0.0 copy-done
  2.0 0.4 %shard_map.68 = (f32[72,128]{1,0:T(8,128)S(1)}, f32[152,128]{1,0:T(8,128)S(1)}, f32[72,128]{1,0:T(8,128)S(1)}, f32[72,128]{1,0:T(8,128)S(1)}) custom-call(f32[19,4,16,128]{3,2,1,0:T(8,128)S(1)} %copy-done, f32[4,4,16,128]{3,2,1,0:T(8,128)S(1)} %get-tuple-element.51.ub_ref, f32[8,128]{1,0:T(8,128)S(1)} %get-tuple-element.52.drag_ref), custom_call_target="tpu_custom_call" | custom-call | bytes 14400000 | tf_op jit(solution)/shard_map/pallas_call | solution.py:997
  2.4 0.0 copy-start.1
  2.4 3.4 %collective-permute-start.4 = (f32[72,128]{1,0:T(8,128)S(1)}, f32[72,128]{1,0:T(8,128)S(1)}, u32[]{:S(2)}, u32[]{:S(2)}) collective-permute-start(f32[72,128]{1,0:T(8,128)S(1)} %get-tuple-element.56), channel_id=1, source_target_pairs={{0,28},{4,24},{8,20},{12,16},{16,12},{20,8},{24,4},{28,0},{1,29},{... | collective-permute-start | bytes 110600 | tf_op jit(solution)/shard_map/ppermute | solution.py:1022
  5.8 0.8 %collective-permute-start.1 = (f32[72,128]{1,0:T(8,128)S(1)}, f32[72,128]{1,0:T(8,128)S(1)}, u32[]{:S(2)}, u32[]{:S(2)}) collective-permute-start(f32[72,128]{1,0:T(8,128)S(1)} %get-tuple-element.53.cols_ref), channel_id=1, source_target_pairs={{0,24},{8,16},{16,8},{24,0},{1,25},{9,17},{17,9},{25,1},{2,26},{10... | collective-permute-start | bytes 110600 | tf_op jit(solution)/shard_map/ppermute | solution.py:1050
  6.6 0.0 collective-permute-start.2
  6.6 1.2 %collective-permute-start.3 = (f32[72,128]{1,0:T(8,128)S(1)}, f32[72,128]{1,0:T(8,128)S(1)}, u32[]{:S(2)}, u32[]{:S(2)}) collective-permute-start(f32[72,128]{1,0:T(8,128)S(1)} %get-tuple-element.55), channel_id=1, source_target_pairs={{0,12},{4,8},{8,4},{12,0},{16,28},{20,24},{24,20},{28,16},{1,13},{... | collective-permute-start | bytes 110600 | tf_op jit(solution)/shard_map/ppermute | solution.py:1022
  7.9 1.0 %collective-permute-start = (f32[376,128]{1,0:T(8,128)S(1)}, f32[376,128]{1,0:T(8,128)S(1)}, u32[]{:S(2)}, u32[]{:S(2)}) collective-permute-start(f32[376,128]{1,0:T(8,128)S(1)} %shard_map.69), channel_id=1, source_target_pairs={{0,8},{8,0},{16,24},{24,16},{1,9},{9,1},{17,25},{25,17},{2,10},{10... | collective-permute-start | bytes 577544 | tf_op jit(solution)/shard_map/ppermute | solution.py:1051
  8.9 0.1 shard_map.70
  9.0 0.2 collective-permute-done.1.xc_ref
  9.2 1.0 %collective-permute-start.5 = (f32[8,128]{1,0:T(8,128)S(1)}, f32[8,128]{1,0:T(8,128)S(1)}, u32[]{:S(2)}, u32[]{:S(2)}) collective-permute-start(f32[8,128]{1,0:T(8,128)S(1)} %slice_add_fusion), channel_id=1, source_target_pairs={{0,8},{8,0},{16,24},{24,16},{1,9},{9,1},{17,25},{25,17},{2,10},{10... | collective-permute-start | bytes 12296 | tf_op jit(solution)/shard_map/ppermute | solution.py:1080
  10.2 0.9 %collective-permute-start.8 = (f32[232,128]{1,0:T(8,128)S(1)}, f32[232,128]{1,0:T(8,128)S(1)}, u32[]{:S(2)}, u32[]{:S(2)}) collective-permute-start(f32[232,128]{1,0:T(8,128)S(1)} %shard_map.70), channel_id=1, source_target_pairs={{0,24},{8,16},{16,8},{24,0},{1,25},{9,17},{17,9},{25,1},{2,26},{10... | collective-permute-start | bytes 356360 | tf_op jit(solution)/shard_map/ppermute | solution.py:1070
  11.1 0.1 collective-permute-done.2.y_ref
  11.2 0.0 collective-permute-done.xa_ref
  11.2 0.4 %shard_map.71 = (f32[96,128]{1,0:T(8,128)S(1)}, f32[40,128]{1,0:T(8,128)S(1)}, f32[40,128]{1,0:T(8,128)S(1)}, f32[8,128]{1,0:T(8,128)S(1)}) custom-call(f32[72,128]{1,0:T(8,128)S(1)} %get-tuple-element.53.cols_ref, f32[376,128]{1,0:T(8,128)S(1)} %collective-permute-done.xa_ref, f32[72,128]{1,0:T(8,128)S(1)} %collective-permute-done.1.xc_ref, ...), custom_call_target="tpu_custom_call" | custom-call | bytes 180000 | tf_op jit(solution)/shard_map/pallas_call | solution.py:997
  11.5 0.0 copy-start.2
  11.6 3.9 %collective-permute-start.7 = (f32[40,128]{1,0:T(8,128)S(1)}, f32[40,128]{1,0:T(8,128)S(1)}, u32[]{:S(2)}, u32[]{:S(2)}) collective-permute-start(f32[40,128]{1,0:T(8,128)S(1)} %scatter.9), channel_id=1, source_target_pairs={{0,3},{1,2},{2,1},{3,0},{4,7},{5,6},{6,5},{7,4},{8,11},{9,10},{10,... | collective-permute-start | bytes 61448 | tf_op jit(solution)/shard_map/ppermute | solution.py:1084
  15.5 0.1 collective-permute-start.6
  15.6 0.6 %collective-permute-start.9 = (f32[1,128]{1,0:T(1,128)S(1)}, f32[1,128]{1,0:T(1,128)S(1)}, u32[]{:S(2)}, u32[]{:S(2)}) collective-permute-start(f32[1,128]{1,0:T(1,128)S(1)} %bitcast.4), channel_id=1, source_target_pairs={{0,2},{1,3},{2,0},{3,1},{4,6},{5,7},{6,4},{7,5},{8,10},{9,11},{10,... | collective-permute-start | bytes 1544 | tf_op jit(solution)/shard_map/ppermute | solution.py:1104
  16.2 2.4 %shard_map.72 = (f32[19,4,16,128]{3,2,1,0:T(8,128)S(1)}, f32[4,16,128]{2,1,0:T(8,128)S(1)}, f32[4,16,128]{2,1,0:T(8,128)S(1)}, f32[19,16,128]{2,1,0:T(8,128)S(1)...) custom-call(f32[2,19,4,16,128]{4,3,2,1,0:T(8,128)S(1)} %copy-done.1, f32[19,4,16,128]{3,2,1,0:T(8,128)S(1)} %copy-done, ...), custom_call_target="tpu_custom_call" | custom-call | bytes 14400000 | tf_op jit(solution)/shard_map/pallas_call | solution.py:997
  18.6 0.8 %collective-permute-done.6.za_ref = f32[40,128]{1,0:T(8,128)S(1)} collective-permute-done((f32[40,128]{1,0:T(8,128)S(1)}, f32[40,128]{1,0:T(8,128)S(1)}, u32[]{:S(2)}, u32[]{:S(2)}) %collective-permute-start.6) | collective-permute-done | bytes 20512 | tf_op jit(solution)/shard_map/ppermute | solution.py:1085
  19.3 0.9 %shard_map.73 = (f32[19,4,16,128]{3,2,1,0:T(8,128)S(1)}, f32[4,16,128]{2,1,0:T(8,128)S(1)}, f32[1,128]{1,0:T(1,128)S(1)}) custom-call(s32[4,16,128]{2,1,0:T(8,128)S(1)} %copy-done.2, f32[96,128]{1,0:T(8,128)S(1)} %get-tuple-element.58.zown_ref, f32[40,128]{1,0:T(8,128)S(1)} %collective-permute-done.6.za_ref, f32[40,128]{1,0:T(8,128)S(1)} %collective-permute-done.7.zb_ref, ...), custom_call_target="tpu_custom_call" | custom-call | bytes 180000 | tf_op jit(solution)/shard_map/pallas_call | solution.py:997
  20.2 0.9 %shard_map.74 = (f32[19,4,16,128]{3,2,1,0:T(8,128)}, f32[4,16,128]{2,1,0:T(8,128)}, f32[1,1]{1,0:T(1,128)}) custom-call(f32[19,4,16,128]{3,2,1,0:T(8,128)S(1)} %get-tuple-element.69.out_ref, f32[4,16,128]{2,1,0:T(8,128)S(1)} %get-tuple-element.70.grad_ref, f32[1,128]{1,0:T(1,128)S(1)} %bitcast.5, f32[1,128]{1,0:T(1,128)S(1)} %collective-permute-done.9.refs_1_, ...), custom_call_target="tpu_custom_call" | custom-call | bytes 180000 | tf_op jit(solution)/shard_map/pallas_call | solution.py:997
  (14 shorter events, 0.1 us)
Async XLA Ops:
  0.6 1.4 %copy-start = (f32[19,4,16,128]{3,2,1,0:T(8,128)S(1)}, f32[19,4,16,128]{3,2,1,0:T(8,128)}, u32[]{:S(2)}) copy-start(f32[19,4,16,128]{3,2,1,0:T(8,128)} %adj_ref.7) | copy-start | bytes 1867780
  2.4 13.8 %copy-start.1 = (f32[2,19,4,16,128]{4,3,2,1,0:T(8,128)S(1)}, f32[2,19,4,16,128]{4,3,2,1,0:T(8,128)}, u32[]{:S(2)}) copy-start(f32[2,19,4,16,128]{4,3,2,1,0:T(8,128)} %states_ref.1) | copy-start | bytes 3735556
  2.4 6.6 %collective-permute-start.4 = (f32[72,128]{1,0:T(8,128)S(1)}, f32[72,128]{1,0:T(8,128)S(1)}, u32[]{:S(2)}, u32[]{:S(2)}) collective-permute-start(f32[72,128]{1,0:T(8,128)S(1)} %get-tuple-element.56), channel_id=1, source_target_pairs={{0,28},{4,24},{8,20},{12,16},{16,12},{20,8},{24,4},{28,0},{1,29},{... | collective-permute-start | bytes 110600 | tf_op jit(solution)/shard_map/ppermute | solution.py:1022
  5.8 3.4 %collective-permute-start.1 = (f32[72,128]{1,0:T(8,128)S(1)}, f32[72,128]{1,0:T(8,128)S(1)}, u32[]{:S(2)}, u32[]{:S(2)}) collective-permute-start(f32[72,128]{1,0:T(8,128)S(1)} %get-tuple-element.53.cols_ref), channel_id=1, source_target_pairs={{0,24},{8,16},{16,8},{24,0},{1,25},{9,17},{17,9},{25,1},{2,26},{10... | collective-permute-start | bytes 110600 | tf_op jit(solution)/shard_map/ppermute | solution.py:1050
  6.6 4.5 %collective-permute-start.2 = (f32[152,128]{1,0:T(8,128)S(1)}, f32[152,128]{1,0:T(8,128)S(1)}, u32[]{:S(2)}, u32[]{:S(2)}) collective-permute-start(f32[152,128]{1,0:T(8,128)S(1)} %get-tuple-element.54), channel_id=1, source_target_pairs={{0,4},{4,0},{1,5},{5,1},{2,6},{6,2},{3,7},{7,3},{8,12},{12,8},{9,1... | collective-permute-start | bytes 233480 | tf_op jit(solution)/shard_map/ppermute | solution.py:1053
  6.6 4.4 %collective-permute-start.3 = (f32[72,128]{1,0:T(8,128)S(1)}, f32[72,128]{1,0:T(8,128)S(1)}, u32[]{:S(2)}, u32[]{:S(2)}) collective-permute-start(f32[72,128]{1,0:T(8,128)S(1)} %get-tuple-element.55), channel_id=1, source_target_pairs={{0,12},{4,8},{8,4},{12,0},{16,28},{20,24},{24,20},{28,16},{1,13},{... | collective-permute-start | bytes 110600 | tf_op jit(solution)/shard_map/ppermute | solution.py:1022
  7.9 3.3 %collective-permute-start = (f32[376,128]{1,0:T(8,128)S(1)}, f32[376,128]{1,0:T(8,128)S(1)}, u32[]{:S(2)}, u32[]{:S(2)}) collective-permute-start(f32[376,128]{1,0:T(8,128)S(1)} %shard_map.69), channel_id=1, source_target_pairs={{0,8},{8,0},{16,24},{24,16},{1,9},{9,1},{17,25},{25,17},{2,10},{10... | collective-permute-start | bytes 577544 | tf_op jit(solution)/shard_map/ppermute | solution.py:1051
  9.2 2.3 %collective-permute-start.5 = (f32[8,128]{1,0:T(8,128)S(1)}, f32[8,128]{1,0:T(8,128)S(1)}, u32[]{:S(2)}, u32[]{:S(2)}) collective-permute-start(f32[8,128]{1,0:T(8,128)S(1)} %slice_add_fusion), channel_id=1, source_target_pairs={{0,8},{8,0},{16,24},{24,16},{1,9},{9,1},{17,25},{25,17},{2,10},{10... | collective-permute-start | bytes 12296 | tf_op jit(solution)/shard_map/ppermute | solution.py:1080
  10.2 6.0 %collective-permute-start.8 = (f32[232,128]{1,0:T(8,128)S(1)}, f32[232,128]{1,0:T(8,128)S(1)}, u32[]{:S(2)}, u32[]{:S(2)}) collective-permute-start(f32[232,128]{1,0:T(8,128)S(1)} %shard_map.70), channel_id=1, source_target_pairs={{0,24},{8,16},{16,8},{24,0},{1,25},{9,17},{17,9},{25,1},{2,26},{10... | collective-permute-start | bytes 356360 | tf_op jit(solution)/shard_map/ppermute | solution.py:1070
  11.5 7.8 %copy-start.2 = (s32[4,16,128]{2,1,0:T(8,128)S(1)}, s32[4,16,128]{2,1,0:T(8,128)}, u32[]{:S(2)}) copy-start(s32[4,16,128]{2,1,0:T(8,128)} %mask_ref.1) | copy-start | bytes 98308
  11.6 6.9 %collective-permute-start.7 = (f32[40,128]{1,0:T(8,128)S(1)}, f32[40,128]{1,0:T(8,128)S(1)}, u32[]{:S(2)}, u32[]{:S(2)}) collective-permute-start(f32[40,128]{1,0:T(8,128)S(1)} %scatter.9), channel_id=1, source_target_pairs={{0,3},{1,2},{2,1},{3,0},{4,7},{5,6},{6,5},{7,4},{8,11},{9,10},{10,... | collective-permute-start | bytes 61448 | tf_op jit(solution)/shard_map/ppermute | solution.py:1084
  15.5 3.8 %collective-permute-start.6 = (f32[40,128]{1,0:T(8,128)S(1)}, f32[40,128]{1,0:T(8,128)S(1)}, u32[]{:S(2)}, u32[]{:S(2)}) collective-permute-start(f32[40,128]{1,0:T(8,128)S(1)} %scatter.6), channel_id=1, source_target_pairs={{0,1},{1,0},{2,3},{3,2},{4,5},{5,4},{6,7},{7,6},{8,9},{9,8},{10,11... | collective-permute-start | bytes 61448 | tf_op jit(solution)/shard_map/ppermute | solution.py:1085
  15.6 4.6 %collective-permute-start.9 = (f32[1,128]{1,0:T(1,128)S(1)}, f32[1,128]{1,0:T(1,128)S(1)}, u32[]{:S(2)}, u32[]{:S(2)}) collective-permute-start(f32[1,128]{1,0:T(1,128)S(1)} %bitcast.4), channel_id=1, source_target_pairs={{0,2},{1,3},{2,0},{3,1},{4,6},{5,7},{6,4},{7,5},{8,10},{9,11},{10,... | collective-permute-start | bytes 1544 | tf_op jit(solution)/shard_map/ppermute | solution.py:1104

commit v11 on v10

--- a/solution.py
+++ b/solution.py
@@ -43,7 +43,8 @@
 
 
 NSLOT = 23
-CORNER = 24
+CORNER = 16
+DRAG_ROW = 14
 EDGE_ROWS = 8
 
 
@@ -210,12 +211,21 @@
 
 
 def corner_rows(sx, sy):
-    rows = []
-    for dx, dy in ((0, 0), (1, 0), (0, 1), (1, 1)):
-        for i in near(0, sx) if dx == 0 else far(0, sx):
-            if i in (near(1, sy) if dy == 0 else far(1, sy)):
-                rows.append((i, dx, dy))
-    return rows
+    both = [i for i in far(0, sx) if VEL[i][1] == sy]
+    along_y = [i for i in far(1, sy) if VEL[i][0] == 0]
+    along_x = [i for i in far(0, sx) if VEL[i][1] == 0]
+    rows = [(i, 0, 0) for i in both + along_y + along_x]
+    return rows + [(i, 1, 0) for i in both] + [(i, 0, 1) for i in both]
+
+
+def corner_zeros(sx, sy):
+    rows = [(i, 0, 0) for i in range(19) if VEL[i][0] == 0 and VEL[i][1] == 0]
+    rows += [(i, 1, 0) for i in far(0, sx) if VEL[i][1] == 0]
+    rows += [(i, 0, 1) for i in far(1, sy) if VEL[i][0] == 0]
+    return rows + [(i, 1, 1) for i in far(0, sx) if VEL[i][1] == sy]
+
+
+CORNERS = ((1, 1), (1, -1), (-1, 1), (-1, -1))
 
 
 def parity(axis):
@@ -441,22 +451,41 @@
             row = first + 14 * nx + k
             y_ref[row : row + 1] = adj_ref[i, x, y : y + 1, :]
 
+    for i in range(19):
+        read_ref[i] = jnp.zeros((2 * nx, nz), jnp.float32)
+    for n, (sx, sy) in enumerate(CORNERS):
+        xs = (0, 1) if sx > 0 else (nx - 1, nx - 2)
+        ys = (0, 1) if sy > 0 else (ny - 1, ny - 2)
+        for i, dx, dy in corner_zeros(sx, sy):
+            read_ref[i, n : n + 1, :] = adj_ref[i, xs[dx], ys[dy] : ys[dy] + 1, :]
+        for k in range(4):
+            read_ref[19 + k, n : n + 1, :] = ub_ref[k, xs[0], ys[0] : ys[0] + 1, :]
+    got = [z_shifted(read_ref[i], VEL[i][2]) for i in range(19)]
+    corner_sums, _ = adjoint_cell(
+        got, [read_ref[19 + k] for k in range(3)], read_ref[22], 0.0
+    )
+    line = jnp.sum(drag_ref[...], axis=0, keepdims=True)
+
     def fill_corner(out_ref, place, sx, sy):
-        names = corner_rows(sx, sy)
-        for k, (q, dx, dy) in enumerate(names):
-            x = dx if sx > 0 else nx - 1 - dx
-            y = dy if sy > 0 else ny - 1 - dy
-            row = place * corner_block + k
-            out_ref[row : row + 1] = cell_rows(adj_ref, ub_ref, q, x, slice(y, y + 1))
-        row = place * corner_block + len(names)
-        last = place * corner_block + CORNER
-        out_ref[row:last] = jnp.zeros((last - row, nz), jnp.float32)
+        xs = (0, 1) if sx > 0 else (nx - 1, nx - 2)
+        ys = (0, 1) if sy > 0 else (ny - 1, ny - 2)
+        n = CORNERS.index((sx, sy))
+        first = place * corner_block
+        rows = corner_rows(sx, sy)
+        out_ref[first : first + 1] = corner_sums[rows[0][0]][n : n + 1]
+        for k in range(4):
+            out_ref[first + 1 + k : first + 2 + k] = ub_ref[
+                k, xs[0], ys[0] : ys[0] + 1, :
+            ]
+        for k, (i, dx, dy) in enumerate(rows):
+            row = first + 5 + k
+            out_ref[row : row + 1] = adj_ref[i, xs[dx], ys[dy] : ys[dy] + 1, :]
+        out_ref[first + DRAG_ROW : first + DRAG_ROW + 1] = line
+        out_ref[first + DRAG_ROW + 1 : first + CORNER] = jnp.zeros((1, nz), jnp.float32)
 
     drag = drag_ref[...]
     cols_ref[4 * ny :] = drag
     y_ref[2 * y_block :] = drag
-    ya_ref[2 * corner_block :] = drag
-    yb_ref[2 * corner_block :] = drag
     for py in (0, 1):
 
         @pl.when(parity("gy") == py)
@@ -611,10 +640,14 @@
             row = (g * tiles + t) * 8 if t < tiles else 2 * tiles * 8
             za_ref[row : row + 8, :] = jnp.where(up_first, up[g], down[g])
             zb_ref[row : row + 8, :] = jnp.where(up_first, down[g], up[g])
-    drag = cols_ref[4 * ny :] + y_ref[2 * y_block :]
-    for x_ref, c_ref in ((xa_ref, ya_ref), (xc_ref, yb_ref)):
-        drag = drag + (x_ref[x_ref.shape[0] - 8 :] + c_ref[2 * corner_block :])
-    drag_ref[...] = drag
+    drag = (cols_ref[4 * ny :] + y_ref[2 * y_block :]) + (
+        xa_ref[xa_ref.shape[0] - 8 :] + xc_ref[4 * ny :]
+    )
+    row = slice(DRAG_ROW, DRAG_ROW + 1)
+    drag_ref[...] = jnp.sum(drag, axis=0, keepdims=True) + (ya_ref[row] + yb_ref[row])
+
+
+OUT_GROUPS = ((0, 5), (5, 10), (10, 15), (15, 19))
 
 
 def turn(value, shift):
@@ -693,6 +726,7 @@
         fill_partial(1)
 
     sums = {}
+    corner_sums = {}
     for sign in (1, -1):
         block = y_rows(nx) + EDGE_ROWS
         first, second = (0, block) if sign > 0 else (block, 0)
@@ -727,9 +761,16 @@
                 for r in ys
             ]
             got = jnp.where(even_y, low, high)
+            corner_sums[sx, sign] = got[0:1]
+            for k in range(4):
+                line = lines[sign][0]
+                ext[19 + k, planes[sx][0], line : line + 1, :] = got[1 + k : 2 + k]
+            for q, dx, dy in corner_zeros(sx, sign):
+                line = lines[sign][dy]
+                ext[q, planes[sx][dx], line : line + 1, :] = nothing
             for k, (q, dx, dy) in enumerate(corner_rows(sx, sign)):
                 line = lines[sign][dy]
-                ext[q, planes[sx][dx], line : line + 1, :] = got[k : k + 1]
+                ext[q, planes[sx][dx], line : line + 1, :] = got[5 + k : 6 + k]
 
     def near_cells(q, plane, t, cy):
         if t < tiles:
@@ -754,6 +795,11 @@
                     line = k * nx + p - 1
                     term = sums[sign][line : line + 1]
                     out[i] = out[i] + jnp.where(sub == row, term, 0.0)
+        elif t == tiles:
+            sx = -1 if p == 0 else 1
+            for sign, row in ((1, 0), (-1, 7)):
+                i = corner_rows(sx, sign)[0][0]
+                out[i] = out[i] + jnp.where(sub == row, corner_sums[sx, sign], 0.0)
         if partial is not None:
             for k, i in enumerate(kinds):
                 row = k * ny + 8 * t
@@ -829,25 +875,17 @@
 
 
 def edge_kernel(
-    mask_ref,
     zown_ref,
     za_ref,
     zb_ref,
     pack_ref,
     f0_ref,
     f1_ref,
-    inner_ref,
-    grad1_ref,
-    inner_grad_ref,
-    out_ref,
-    grad_ref,
+    zout,
     tail_ref,
-    first_ref,
-    second_ref,
     zmid,
-    zout,
 ):
-    nx, ny, nz = mask_ref.shape
+    ny, nz = pack_ref.shape[1:]
     tiles = ny // 8
     height = (tiles + 1) * 8
     even = parity("gz") == 0
@@ -862,6 +900,7 @@
     def swapped(value):
         return jnp.where(even_lane, turn(value, -1), turn(value, 1))
 
+    slab_grad = []
     for t in range(tiles + 1):
         received = []
         for g in range(2):
@@ -875,10 +914,10 @@
                 ]
             received.append((jnp.where(even, va, vb), jnp.where(even, vb, va)))
         (high0, low0), (high1, low1) = received
+        pairs = []
         for g in range(4):
             row = (g * (tiles + 1) + t) * 8
-            rows = slice(row, row + 8)
-            own = zown_ref[rows]
+            own = zown_ref[row : row + 8]
             if g == 0:
                 head, tail = own, low0
             elif g == 1:
@@ -891,21 +930,21 @@
                 tail = jnp.where(even_lane, turn(low1, -1), own)
             head = swapped(head)
             tail = swapped(tail)
-            first_ref[rows] = jnp.where(low_pair, head, turn(tail, 2))
-            second_ref[rows] = jnp.where(low_pair, turn(head, -2), tail)
-
-    slab_grad = []
-    for t in range(tiles + 1):
+            pairs.append(
+                (
+                    jnp.where(low_pair, head, turn(tail, 2)),
+                    jnp.where(low_pair, turn(head, -2), tail),
+                )
+            )
         got = []
         for q in range(NSLOT):
             g, k = ZSLOT[q]
-            row = g * height + t * 8
-            ref = second_ref if k % 2 else first_ref
-            got.append(turn(ref[row : row + 8, :], -32 * (k // 2)))
+            got.append(turn(pairs[g][k % 2], -32 * (k // 2)))
         out, kept = adjoint_cell(got[:19], got[19:22], got[22], 1.0)
         for i in range(19):
-            zmid[i, 8 * t + 8 : 8 * t + 16, :] = out[i]
-            if t == tiles:
+            if t < tiles or VEL[i][1] > 0:
+                zmid[i, 8 * t + 8 : 8 * t + 16, :] = out[i]
+            elif VEL[i][1] < 0:
                 zmid[i, 0:8, :] = out[i]
         if t < tiles:
             f = [f1_ref[i, 8 * t : 8 * t + 8, :] for i in range(19)]
@@ -941,8 +980,35 @@
         zout[19, rows, :] = gradient_cell(kept, f[0], fs, fd, fm, u)
         zout[20, rows, :] = slab_grad[t]
 
+
+def finish_kernel(whole_cells, mask_ref, zout, inner_ref, grad1_ref, inner_grad_ref, *refs):
+    tiles_of_drag, (out_hbm, grad_hbm, drag_hbm, out_ref, grad_ref, drag_ref, sems) = (
+        refs[:-7],
+        refs[-7:],
+    )
+    nx, ny, nz = mask_ref.shape
+    tiles = ny // 8
+    lane = lax.broadcasted_iota(jnp.int32, (8, nz), 1)
     outer = (lane < 2) | (lane >= nz - 2)
     ends = (lane < 1) | (lane >= nz - 1)
+    copies = []
+
+    def send(src, dst):
+        copy = pltpu.make_async_copy(src, dst, sems.at[len(copies)])
+        copy.start()
+        copies.append(copy)
+
+    for low, high in OUT_GROUPS:
+        for i in range(low, high):
+            for x in range(nx):
+                for t in range(tiles):
+                    rows = slice(8 * t, 8 * t + 8)
+                    out_ref[i, x, rows, :] = jnp.where(
+                        outer,
+                        turn(zout[i, rows, :], -2 - 4 * x),
+                        inner_ref[i, x, rows, :],
+                    )
+        send(out_ref.at[low:high], out_hbm.at[low:high])
     for x in range(nx):
         for t in range(tiles):
             rows = slice(8 * t, 8 * t + 8)
@@ -952,29 +1018,12 @@
             edge = turn(zout[19, rows, :], -2 - 4 * x) + level1
             grad = jnp.where(outer, edge, inner_grad_ref[x, rows, :])
             grad_ref[x, rows, :] = jnp.where(mask_ref[x, rows, :] == 0, grad, 0.0)
-    for i in range(19):
-        for x in range(nx):
-            for t in range(tiles):
-                rows = slice(8 * t, 8 * t + 8)
-                out_ref[i, x, rows, :] = jnp.where(
-                    outer, turn(zout[i, rows, :], -2 - 4 * x), inner_ref[i, x, rows, :]
-                )
-
-
-def finish_kernel(whole_cells, out_ref, grad_ref, *refs):
-    tiles, (out_hbm, grad_hbm, drag_hbm, drag_ref, sems) = refs[:-5], refs[-5:]
-    copies = [
-        pltpu.make_async_copy(out_ref, out_hbm, sems.at[0]),
-        pltpu.make_async_copy(grad_ref, grad_hbm, sems.at[1]),
-        pltpu.make_async_copy(drag_ref, drag_hbm, sems.at[2]),
-    ]
-    for copy in copies[:2]:
-        copy.start()
+    send(grad_ref, grad_hbm)
     total = 0.0
-    for ref in tiles:
+    for ref in tiles_of_drag:
         total = total + jnp.sum(ref[...], axis=0, keepdims=True)
     drag_ref[...] = jnp.sum(total, axis=1, keepdims=True) / whole_cells
-    copies[2].start()
+    send(drag_ref, drag_hbm)
     for copy in copies:
         copy.wait()
 
@@ -1023,7 +1072,7 @@
 
     rows_x = NSLOT * ny + 8
     rows_y = 2 * (y_rows(nx) + EDGE_ROWS) + 8
-    rows_c = 2 * (CORNER + EDGE_ROWS) + 8
+    rows_c = 2 * (CORNER + EDGE_ROWS)
     rows_z = 2 * ny + 8
     rides = (gx, gy, gz) == (4, 2, 4)
     ub, drag = call(
@@ -1066,19 +1115,19 @@
         block = CORNER + EDGE_ROWS
         yb = both(yb, block, lambda m, pairs: diagonal(m, x_second, pairs))
         ya = both(ya, block, lambda m, pairs: diagonal(m, x_first, pairs))
-    xb, yb = lax.optimization_barrier((xb, yb))
+    xb, xc = lax.optimization_barrier((xb, xc))
     xb = lax.ppermute(xb, "gx", x_second)
 
     zown, za, zb, drag_xy = call(
         pack_z_kernel,
         (cols, xa, xc, y, ya, yb),
-        [(4 * height, nz), (rows_z, nz), (rows_z, nz), (8, nz)],
+        [(4 * height, nz), (rows_z, nz), (rows_z, nz), (1, nz)],
         [pltpu.VMEM((4, ny + 32, nz), f32)],
     )
     if rides:
-        second = xc[4 * ny :] + yb[rows_c - 8 :]
+        second = jnp.sum(xc[4 * ny :], axis=0, keepdims=True)
+        second = second + yb[DRAG_ROW : DRAG_ROW + 1]
         drag_xy = drag_xy + lax.ppermute(second, "gx", x_first)
-        drag_xy = jnp.sum(drag_xy, axis=0, keepdims=True)
         za = za.at[2 * ny + 3 : 2 * ny + 4].set(drag_xy)
         zb = zb.at[2 * ny + 3 : 2 * ny + 4].set(drag_xy)
     zb = lax.ppermute(zb, "gz", z_second)
@@ -1106,25 +1155,25 @@
     else:
         drags = (lax.psum(drag, AXES),)
 
-    first, gradient, tails = call(
+    zout, tails = call(
         edge_kernel,
-        (solid_mask, zown, za, zb, pack, f0, f1, inner, grad1, inner_grad),
-        [(19, nx, ny, nz), (nx, ny, nz), (1, nz)],
-        [
-            pltpu.VMEM((4 * height, nz), f32),
-            pltpu.VMEM((4 * height, nz), f32),
-            pltpu.VMEM((19, height + 8, nz), f32),
-            pltpu.VMEM((21, ny, nz), f32),
-        ],
+        (zown, za, zb, pack, f0, f1),
+        [(21, ny, nz), (1, nz)],
+        [pltpu.VMEM((19, height + 8, nz), f32)],
     )
     if rides:
         drags += (tails,)
     whole_cells = float(nx * ny * nz * gx * gy * gz)
     first, gradient, drag = call(
         functools.partial(finish_kernel, whole_cells),
-        (first, gradient) + drags,
+        (solid_mask, zout, inner, grad1, inner_grad) + drags,
         [(19, nx, ny, nz), (nx, ny, nz), (1, 1)],
-        [pltpu.VMEM((1, 1), f32), pltpu.SemaphoreType.DMA((3,))],
+        [
+            pltpu.VMEM((19, nx, ny, nz), f32),
+            pltpu.VMEM((nx, ny, nz), f32),
+            pltpu.VMEM((1, 1), f32),
+            pltpu.SemaphoreType.DMA((len(OUT_GROUPS) + 2,)),
+        ],
         outs=[HBM, HBM, HBM],
     )
     return (first, gradient, drag.reshape(()))

time: 21.2 us -> 21.2 us (level)
  waiting for transfers between devices: 1.09 us -> 1.39 us
    ppermute x1, starting transfers between devices: 0.82 us -> 2.44 us  [body(): xc = lax.ppermute(cols, 'gx', x_second)]
    ppermute x2, starting transfers between devices: 4.63 us -> 3.06 us  [diagonal(): return lax.ppermute(message, ('gx', 'gy'), pairs)]
    ppermute x1, starting transfers between devices: 0.97 us -> 0.48 us  [body(): drag_xy = drag_xy + lax.ppermute(second, 'gx', x_first)]
    ppermute x1, waiting for transfers between devices: 0.1 us -> 0.5 us  [body(): y = lax.ppermute(y, 'gy', y_first)]
    ppermute x1, starting transfers between devices: 0.87 us -> 1.19 us  [body(): xb = lax.ppermute(xb, 'gx', x_second)]
  transfers between devices with their start and end apart: 10 -> 10, of which waited for: 3 -> 4; matrix products, arithmetic and copies ran while one was open for 0% -> 0% of each run, Pallas kernels for 18% -> 17%
where the time goes in v11:
time: 21.2 us; the launch traced here: 21.1 us
  starting transfers between devices  12.6 us (59%)
  Pallas kernels  6.2 us (29%)
  waiting for transfers between devices  1.39 us (7%)
  between operations  0.75 us (4%)
    pallas_call x8, Pallas kernels, call(): pl.pallas_call(kernel, out_shape=[jax.ShapeDtypeStruct(s, jnp.float32) fo...  6.2 us
    ppermute x1, starting transfers between devices, body(): zb = lax.ppermute(zb, 'gz', z_second)  3.67 us
    ppermute x2, starting transfers between devices, diagonal(): return lax.ppermute(message, ('gx', 'gy'), pairs)  3.06 us
    ppermute x1, starting transfers between devices, body(): xc = lax.ppermute(cols, 'gx', x_second)  2.44 us
    ppermute x1, starting transfers between devices, body(): xb = lax.ppermute(xb, 'gx', x_second)  1.19 us
    ppermute x1, starting transfers between devices, body(): xa = lax.ppermute(xa, 'gx', x_first)  0.91 us
    ppermute x1, starting transfers between devices, body(): zhalf = lax.ppermute(drag_xy, 'gz', [(i, i ^ 2) for i in range(gz)])  0.77 us
    ppermute x1, waiting for transfers between devices, body(): za = lax.ppermute(za, 'gz', z_first)  0.59 us
  transfers between devices with their start and end apart: 10, of which 4 were waited for; matrix products, arithmetic and copies ran while one was open for 0% of the time, Pallas kernels for 17%

profile of v11, /device:TPU:0, one launch (start us, length us, event | category | flops | bytes accessed | tf_op | source)
XLA Modules:
  0.0 21.1 jit_solution(1444112294620076503)
XLA Ops:
  0.6 1.3 %shard_map.67 = (f32[4,4,16,128]{3,2,1,0:T(8,128)S(1)}, f32[8,128]{1,0:T(8,128)S(1)}) custom-call(f32[2,19,4,16,128]{4,3,2,1,0:T(8,128)} %states_ref.1, f32[4,16,128]{2,1,0:T(8,128)} %por_hbm.1, s32[4,16,128]{2,1,0:T(8,128)} %mask_ref.1), custom_call_target="tpu_custom_call" | custom-call | bytes 180000 | tf_op jit(solution)/shard_map/pallas_call | solution.py:1046
  2.0 0.0 copy-done
  2.0 0.4 %shard_map.68 = (f32[72,128]{1,0:T(8,128)S(1)}, f32[152,128]{1,0:T(8,128)S(1)}, f32[48,128]{1,0:T(8,128)S(1)}, f32[48,128]{1,0:T(8,128)S(1)}) custom-call(f32[19,4,16,128]{3,2,1,0:T(8,128)S(1)} %copy-done, f32[4,4,16,128]{3,2,1,0:T(8,128)S(1)} %get-tuple-element.50.ub_ref, f32[8,128]{1,0:T(8,128)S(1)} %get-tuple-element.51.drag_ref), custom_call_target="tpu_custom_call" | custom-call | bytes 14400000 | tf_op jit(solution)/shard_map/pallas_call | solution.py:1046
  2.4 0.0 copy-start.1
  2.4 2.4 %collective-permute-start.1 = (f32[72,128]{1,0:T(8,128)S(1)}, f32[72,128]{1,0:T(8,128)S(1)}, u32[]{:S(2)}, u32[]{:S(2)}) collective-permute-start(f32[72,128]{1,0:T(8,128)S(1)} %get-tuple-element.52.cols_ref), channel_id=1, source_target_pairs={{0,24},{8,16},{16,8},{24,0},{1,25},{9,17},{17,9},{25,1},{2,26},{10... | collective-permute-start | bytes 110600 | tf_op jit(solution)/shard_map/ppermute | solution.py:1099
  4.9 1.8 %collective-permute-start.4 = (f32[48,128]{1,0:T(8,128)S(1)}, f32[48,128]{1,0:T(8,128)S(1)}, u32[]{:S(2)}, u32[]{:S(2)}) collective-permute-start(f32[48,128]{1,0:T(8,128)S(1)} %get-tuple-element.56), channel_id=1, source_target_pairs={{0,28},{4,24},{8,20},{12,16},{16,12},{20,8},{24,4},{28,0},{1,29},{... | collective-permute-start | bytes 73736 | tf_op jit(solution)/shard_map/ppermute | solution.py:1071
  6.6 0.0 collective-permute-start.2
  6.6 1.3 %collective-permute-start.3 = (f32[48,128]{1,0:T(8,128)S(1)}, f32[48,128]{1,0:T(8,128)S(1)}, u32[]{:S(2)}, u32[]{:S(2)}) collective-permute-start(f32[48,128]{1,0:T(8,128)S(1)} %get-tuple-element.55), channel_id=1, source_target_pairs={{0,12},{4,8},{8,4},{12,0},{16,28},{20,24},{24,20},{28,16},{1,13},{... | collective-permute-start | bytes 73736 | tf_op jit(solution)/shard_map/ppermute | solution.py:1071
  8.0 0.9 %collective-permute-start = (f32[376,128]{1,0:T(8,128)S(1)}, f32[376,128]{1,0:T(8,128)S(1)}, u32[]{:S(2)}, u32[]{:S(2)}) collective-permute-start(f32[376,128]{1,0:T(8,128)S(1)} %shard_map.69), channel_id=1, source_target_pairs={{0,8},{8,0},{16,24},{24,16},{1,9},{9,1},{17,25},{25,17},{2,10},{10... | collective-permute-start | bytes 577544 | tf_op jit(solution)/shard_map/ppermute | solution.py:1100
  8.9 0.1 shard_map.70
  9.0 0.0 collective-permute-done.1.xc_ref
  9.0 1.2 %collective-permute-start.8 = (f32[232,128]{1,0:T(8,128)S(1)}, f32[232,128]{1,0:T(8,128)S(1)}, u32[]{:S(2)}, u32[]{:S(2)}) collective-permute-start(f32[232,128]{1,0:T(8,128)S(1)} %shard_map.70), channel_id=1, source_target_pairs={{0,24},{8,16},{16,8},{24,0},{1,25},{9,17},{17,9},{25,1},{2,26},{10... | collective-permute-start | bytes 356360 | tf_op jit(solution)/shard_map/ppermute | solution.py:1119
  10.2 0.5 %collective-permute-start.5 = (f32[1,128]{1,0:T(1,128)S(1)}, f32[1,128]{1,0:T(1,128)S(1)}, u32[]{:S(2)}, u32[]{:S(2)}) collective-permute-start(f32[1,128]{1,0:T(1,128)S(1)} %slice_add_fusion), channel_id=1, source_target_pairs={{0,8},{8,0},{16,24},{24,16},{1,9},{9,1},{17,25},{25,17},{2,10},{10... | collective-permute-start | bytes 1544 | tf_op jit(solution)/shard_map/ppermute | solution.py:1130
  10.7 0.2 collective-permute-done.3.ya_ref
  10.9 0.5 %collective-permute-done.2.y_ref = f32[152,128]{1,0:T(8,128)S(1)} collective-permute-done((f32[152,128]{1,0:T(8,128)S(1)}, f32[152,128]{1,0:T(8,128)S(1)}, u32[]{:S(2)}, u32[]{:S(2)}) %collective-permute-start.2) | collective-permute-done | bytes 77856 | tf_op jit(solution)/shard_map/ppermute | solution.py:1102
  11.4 0.4 %shard_map.71 = (f32[96,128]{1,0:T(8,128)S(1)}, f32[40,128]{1,0:T(8,128)S(1)}, f32[40,128]{1,0:T(8,128)S(1)}, f32[1,128]{1,0:T(1,128)S(1)}) custom-call(f32[72,128]{1,0:T(8,128)S(1)} %get-tuple-element.52.cols_ref, f32[376,128]{1,0:T(8,128)S(1)} %collective-permute-done.xa_ref, f32[72,128]{1,0:T(8,128)S(1)} %collective-permute-done.1.xc_ref, ...), custom_call_target="tpu_custom_call" | custom-call | bytes 180000 | tf_op jit(solution)/shard_map/pallas_call | solution.py:1046
  11.8 3.7 %collective-permute-start.7 = (f32[40,128]{1,0:T(8,128)S(1)}, f32[40,128]{1,0:T(8,128)S(1)}, u32[]{:S(2)}, u32[]{:S(2)}) collective-permute-start(f32[40,128]{1,0:T(8,128)S(1)} %scatter.9), channel_id=1, source_target_pairs={{0,3},{1,2},{2,1},{3,0},{4,7},{5,6},{6,5},{7,4},{8,11},{9,10},{10,... | collective-permute-start | bytes 61448 | tf_op jit(solution)/shard_map/ppermute | solution.py:1133
  15.5 0.1 collective-permute-start.6
  15.6 0.8 %collective-permute-start.9 = (f32[1,128]{1,0:T(1,128)S(1)}, f32[1,128]{1,0:T(1,128)S(1)}, u32[]{:S(2)}, u32[]{:S(2)}) collective-permute-start(f32[1,128]{1,0:T(1,128)S(1)} %add.11.refs_0_), channel_id=1, source_target_pairs={{0,2},{1,3},{2,0},{3,1},{4,6},{5,7},{6,4},{7,5},{8,10},{9,11},{10,... | collective-permute-start | bytes 1544 | tf_op jit(solution)/shard_map/ppermute | solution.py:1153
  16.4 2.4 %shard_map.72 = (f32[19,4,16,128]{3,2,1,0:T(8,128)S(1)}, f32[4,16,128]{2,1,0:T(8,128)S(1)}, f32[4,16,128]{2,1,0:T(8,128)S(1)}, f32[19,16,128]{2,1,0:T(8,128)S(1)...) custom-call(f32[2,19,4,16,128]{4,3,2,1,0:T(8,128)S(1)} %copy-done.1, f32[19,4,16,128]{3,2,1,0:T(8,128)S(1)} %copy-done, ...), custom_call_target="tpu_custom_call" | custom-call | bytes 14400000 | tf_op jit(solution)/shard_map/pallas_call | solution.py:1046
  18.8 0.6 %collective-permute-done.6.za_ref = f32[40,128]{1,0:T(8,128)S(1)} collective-permute-done((f32[40,128]{1,0:T(8,128)S(1)}, f32[40,128]{1,0:T(8,128)S(1)}, u32[]{:S(2)}, u32[]{:S(2)}) %collective-permute-start.6) | collective-permute-done | bytes 20512 | tf_op jit(solution)/shard_map/ppermute | solution.py:1134
  19.4 0.6 %shard_map.73 = (f32[21,16,128]{2,1,0:T(8,128)S(1)}, f32[1,128]{1,0:T(1,128)S(1)}) custom-call(f32[96,128]{1,0:T(8,128)S(1)} %get-tuple-element.57.zown_ref, f32[40,128]{1,0:T(8,128)S(1)} %collective-permute-done.6.za_ref, f32[40,128]{1,0:T(8,128)S(1)} %collective-permute-done.7.zb_ref, f32[19,16,128]{2,1,0:T(8,128)S(1)} %get-tuple-element.62.pack_ref, ...), custom_call_target="tpu_custom_call" | custom-call | bytes 180000 | tf_op jit(solution)/shard_map/pallas_call | solution.py:1046
  20.0 0.1 collective-permute-done.9.refs_1_
  20.1 1.0 %shard_map.74 = (f32[19,4,16,128]{3,2,1,0:T(8,128)}, f32[4,16,128]{2,1,0:T(8,128)}, f32[1,1]{1,0:T(1,128)}) custom-call(s32[4,16,128]{2,1,0:T(8,128)S(1)} %copy-done.2, f32[21,16,128]{2,1,0:T(8,128)S(1)} %get-tuple-element.65.zout, f32[19,4,16,128]{3,2,1,0:T(8,128)S(1)} %get-tuple-element.66.inner_ref, f32[4,16,128]{2,1,0:T(8,128)S(1)} %get-tuple-element.67.grad1_ref, ...), custom_call_target="tpu_custom_call" | custom-call | bytes 180000 | tf_op jit(solution)/shard_map/pallas_call | solution.py:1046
  (15 shorter events, 0.1 us)
Async XLA Ops:
  0.6 1.4 %copy-start = (f32[19,4,16,128]{3,2,1,0:T(8,128)S(1)}, f32[19,4,16,128]{3,2,1,0:T(8,128)}, u32[]{:S(2)}) copy-start(f32[19,4,16,128]{3,2,1,0:T(8,128)} %adj_ref.7) | copy-start | bytes 1867780
  2.4 14.0 %copy-start.1 = (f32[2,19,4,16,128]{4,3,2,1,0:T(8,128)S(1)}, f32[2,19,4,16,128]{4,3,2,1,0:T(8,128)}, u32[]{:S(2)}) copy-start(f32[2,19,4,16,128]{4,3,2,1,0:T(8,128)} %states_ref.1) | copy-start | bytes 3735556
  2.4 6.6 %collective-permute-start.1 = (f32[72,128]{1,0:T(8,128)S(1)}, f32[72,128]{1,0:T(8,128)S(1)}, u32[]{:S(2)}, u32[]{:S(2)}) collective-permute-start(f32[72,128]{1,0:T(8,128)S(1)} %get-tuple-element.52.cols_ref), channel_id=1, source_target_pairs={{0,24},{8,16},{16,8},{24,0},{1,25},{9,17},{17,9},{25,1},{2,26},{10... | collective-permute-start | bytes 110600 | tf_op jit(solution)/shard_map/ppermute | solution.py:1099
  4.9 5.4 %collective-permute-start.4 = (f32[48,128]{1,0:T(8,128)S(1)}, f32[48,128]{1,0:T(8,128)S(1)}, u32[]{:S(2)}, u32[]{:S(2)}) collective-permute-start(f32[48,128]{1,0:T(8,128)S(1)} %get-tuple-element.56), channel_id=1, source_target_pairs={{0,28},{4,24},{8,20},{12,16},{16,12},{20,8},{24,4},{28,0},{1,29},{... | collective-permute-start | bytes 73736 | tf_op jit(solution)/shard_map/ppermute | solution.py:1071
  6.6 4.7 %collective-permute-start.2 = (f32[152,128]{1,0:T(8,128)S(1)}, f32[152,128]{1,0:T(8,128)S(1)}, u32[]{:S(2)}, u32[]{:S(2)}) collective-permute-start(f32[152,128]{1,0:T(8,128)S(1)} %get-tuple-element.54), channel_id=1, source_target_pairs={{0,4},{4,0},{1,5},{5,1},{2,6},{6,2},{3,7},{7,3},{8,12},{12,8},{9,1... | collective-permute-start | bytes 233480 | tf_op jit(solution)/shard_map/ppermute | solution.py:1102
  6.6 4.2 %collective-permute-start.3 = (f32[48,128]{1,0:T(8,128)S(1)}, f32[48,128]{1,0:T(8,128)S(1)}, u32[]{:S(2)}, u32[]{:S(2)}) collective-permute-start(f32[48,128]{1,0:T(8,128)S(1)} %get-tuple-element.55), channel_id=1, source_target_pairs={{0,12},{4,8},{8,4},{12,0},{16,28},{20,24},{24,20},{28,16},{1,13},{... | collective-permute-start | bytes 73736 | tf_op jit(solution)/shard_map/ppermute | solution.py:1071
  8.0 3.4 %collective-permute-start = (f32[376,128]{1,0:T(8,128)S(1)}, f32[376,128]{1,0:T(8,128)S(1)}, u32[]{:S(2)}, u32[]{:S(2)}) collective-permute-start(f32[376,128]{1,0:T(8,128)S(1)} %shard_map.69), channel_id=1, source_target_pairs={{0,8},{8,0},{16,24},{24,16},{1,9},{9,1},{17,25},{25,17},{2,10},{10... | collective-permute-start | bytes 577544 | tf_op jit(solution)/shard_map/ppermute | solution.py:1100
  9.0 7.3 %collective-permute-start.8 = (f32[232,128]{1,0:T(8,128)S(1)}, f32[232,128]{1,0:T(8,128)S(1)}, u32[]{:S(2)}, u32[]{:S(2)}) collective-permute-start(f32[232,128]{1,0:T(8,128)S(1)} %shard_map.70), channel_id=1, source_target_pairs={{0,24},{8,16},{16,8},{24,0},{1,25},{9,17},{17,9},{25,1},{2,26},{10... | collective-permute-start | bytes 356360 | tf_op jit(solution)/shard_map/ppermute | solution.py:1119
  10.2 1.5 %collective-permute-start.5 = (f32[1,128]{1,0:T(1,128)S(1)}, f32[1,128]{1,0:T(1,128)S(1)}, u32[]{:S(2)}, u32[]{:S(2)}) collective-permute-start(f32[1,128]{1,0:T(1,128)S(1)} %slice_add_fusion), channel_id=1, source_target_pairs={{0,8},{8,0},{16,24},{24,16},{1,9},{9,1},{17,25},{25,17},{2,10},{10... | collective-permute-start | bytes 1544 | tf_op jit(solution)/shard_map/ppermute | solution.py:1130
  11.8 6.9 %collective-permute-start.7 = (f32[40,128]{1,0:T(8,128)S(1)}, f32[40,128]{1,0:T(8,128)S(1)}, u32[]{:S(2)}, u32[]{:S(2)}) collective-permute-start(f32[40,128]{1,0:T(8,128)S(1)} %scatter.9), channel_id=1, source_target_pairs={{0,3},{1,2},{2,1},{3,0},{4,7},{5,6},{6,5},{7,4},{8,11},{9,10},{10,... | collective-permute-start | bytes 61448 | tf_op jit(solution)/shard_map/ppermute | solution.py:1133
  15.5 4.6 %copy-start.2 = (s32[4,16,128]{2,1,0:T(8,128)S(1)}, s32[4,16,128]{2,1,0:T(8,128)}, u32[]{:S(2)}) copy-start(s32[4,16,128]{2,1,0:T(8,128)} %mask_ref.1) | copy-start | bytes 98308
  15.5 3.8 %collective-permute-start.6 = (f32[40,128]{1,0:T(8,128)S(1)}, f32[40,128]{1,0:T(8,128)S(1)}, u32[]{:S(2)}, u32[]{:S(2)}) collective-permute-start(f32[40,128]{1,0:T(8,128)S(1)} %scatter.6), channel_id=1, source_target_pairs={{0,1},{1,0},{2,3},{3,2},{4,5},{5,4},{6,7},{7,6},{8,9},{9,8},{10,11... | collective-permute-start | bytes 61448 | tf_op jit(solution)/shard_map/ppermute | solution.py:1134
  15.6 4.5 %collective-permute-start.9 = (f32[1,128]{1,0:T(1,128)S(1)}, f32[1,128]{1,0:T(1,128)S(1)}, u32[]{:S(2)}, u32[]{:S(2)}) collective-permute-start(f32[1,128]{1,0:T(1,128)S(1)} %add.11.refs_0_), channel_id=1, source_target_pairs={{0,2},{1,3},{2,0},{3,1},{4,6},{5,7},{6,4},{7,5},{8,10},{9,11},{10,... | collective-permute-start | bytes 1544 | tf_op jit(solution)/shard_map/ppermute | solution.py:1153

commit v12 on v11

--- a/solution.py
+++ b/solution.py
@@ -508,7 +508,47 @@
                     fill_corner(out_ref, 1, sx, -s0)
 
 
+def pack_columns_kernel(cols_ref, xa_ref, xc_ref, out_ref):
+    ny = (cols_ref.shape[0] - 8) // 4
+    nz = cols_ref.shape[1]
+    tiles = ny // 8
+    lane = lax.broadcasted_iota(jnp.int32, (8, nz), 1)
+    plane = (lane % 32) // 4
+    pair = lane // 2
+
+    def fill_main(sign):
+        halo = {}
+        for names, offset, p in (
+            (near(0, sign), 0, 6 if sign > 0 else 1),
+            (far(0, sign), 18, 7 if sign > 0 else 0),
+        ):
+            for k, q in enumerate(names):
+                halo.setdefault(q, []).append((k + offset, p))
+        for g, group in enumerate(ZGROUPS):
+            for t in range(tiles):
+                rows = slice(g * ny + 8 * t, g * ny + 8 * t + 8)
+                acc = jnp.where(
+                    plane < 2 if sign > 0 else plane > 5,
+                    turn(xc_ref[rows], -16 * sign),
+                    cols_ref[rows],
+                )
+                for k, q in enumerate(group):
+                    for at, p in halo.get(q, ()):
+                        row = at * ny + 8 * t
+                        acc = column_pair(acc, xa_ref[row : row + 8], pair, q, k, p)
+                    out_ref[rows] = acc
+
+    @pl.when(parity("gx") == 0)
+    def _():
+        fill_main(1)
+
+    @pl.when(parity("gx") == 1)
+    def _():
+        fill_main(-1)
+
+
 def pack_z_kernel(
+    main_ref,
     cols_ref,
     xa_ref,
     xc_ref,
@@ -537,37 +577,10 @@
         high = turn(jnp.where(even_x, va, vb), 16)
         return jnp.where(plane < 2, low, jnp.where(plane > 5, high, own))
 
-    pair = lane // 2
-
-    def fill_main(sign):
-        halo = {}
-        for names, offset, p in (
-            (near(0, sign), 0, 6 if sign > 0 else 1),
-            (far(0, sign), 18, 7 if sign > 0 else 0),
-        ):
-            for k, q in enumerate(names):
-                halo.setdefault(q, []).append((k + offset, p))
-        for g, group in enumerate(ZGROUPS):
-            for t in range(tiles):
-                rows = slice(g * ny + 8 * t, g * ny + 8 * t + 8)
-                acc = jnp.where(
-                    plane < 2 if sign > 0 else plane > 5,
-                    turn(xc_ref[rows], -16 * sign),
-                    cols_ref[rows],
-                )
-                for k, q in enumerate(group):
-                    for at, p in halo.get(q, ()):
-                        row = at * ny + 8 * t
-                        acc = column_pair(acc, xa_ref[row : row + 8], pair, q, k, p)
-                ext[g, base + 8 * t : base + 8 * t + 8, :] = acc
-
-    @pl.when(parity("gx") == 0)
-    def _():
-        fill_main(1)
-
-    @pl.when(parity("gx") == 1)
-    def _():
-        fill_main(-1)
+    for g in range(4):
+        for t in range(tiles):
+            row = g * ny + 8 * t
+            ext[g, base + 8 * t : base + 8 * t + 8, :] = main_ref[row : row + 8]
 
     y_block = (y_ref.shape[0] - 8) // 2
     corner_block = CORNER + EDGE_ROWS
@@ -1115,12 +1128,13 @@
         block = CORNER + EDGE_ROWS
         yb = both(yb, block, lambda m, pairs: diagonal(m, x_second, pairs))
         ya = both(ya, block, lambda m, pairs: diagonal(m, x_first, pairs))
-    xb, xc = lax.optimization_barrier((xb, xc))
+    xb, yb = lax.optimization_barrier((xb, yb))
     xb = lax.ppermute(xb, "gx", x_second)
 
+    (columns,) = call(pack_columns_kernel, (cols, xa, xc), [(4 * ny, nz)])
     zown, za, zb, drag_xy = call(
         pack_z_kernel,
-        (cols, xa, xc, y, ya, yb),
+        (columns, cols, xa, xc, y, ya, yb),
         [(4 * height, nz), (rows_z, nz), (rows_z, nz), (1, nz)],
         [pltpu.VMEM((4, ny + 32, nz), f32)],
     )

time: 21.2 us -> 21.1 us (level)
  waiting for transfers between devices: 1.39 us -> 1.16 us
    pallas_call x8 -> x9, Pallas kernels: 6.2 us -> 6.2 us  [call(): pl.pallas_call(kernel, out_shape=[jax.ShapeDtypeStruct(s, jnp.float32) fo...]
where the time goes in v12:
time: 21.1 us; the launch traced here: 21 us
  starting transfers between devices  12.8 us (61%)
  Pallas kernels  6.2 us (29%)
  waiting for transfers between devices  1.16 us (5%)
  between operations  0.74 us (4%)
    pallas_call x9, Pallas kernels, call(): pl.pallas_call(kernel, out_shape=[jax.ShapeDtypeStruct(s, jnp.float32) fo...  6.2 us
    ppermute x1, starting transfers between devices, body(): zb = lax.ppermute(zb, 'gz', z_second)  3.66 us
    ppermute x2, starting transfers between devices, diagonal(): return lax.ppermute(message, ('gx', 'gy'), pairs)  3.06 us
    ppermute x1, starting transfers between devices, body(): xc = lax.ppermute(cols, 'gx', x_second)  2.44 us
    ppermute x1, starting transfers between devices, body(): xb = lax.ppermute(xb, 'gx', x_second)  1.38 us
    ppermute x1, starting transfers between devices, body(): xa = lax.ppermute(xa, 'gx', x_first)  0.91 us
    ppermute x1, starting transfers between devices, body(): zhalf = lax.ppermute(drag_xy, 'gz', [(i, i ^ 2) for i in range(gz)])  0.77 us
    ppermute x1, waiting for transfers between devices, body(): za = lax.ppermute(za, 'gz', z_first)  0.59 us
  transfers between devices with their start and end apart: 10, of which 4 were waited for; matrix products, arithmetic and copies ran while one was open for 0% of the time, Pallas kernels for 17%

profile of v12, /device:TPU:0, one launch (start us, length us, event | category | flops | bytes accessed | tf_op | source)
XLA Modules:
  0.0 21.0 jit_solution(6712724443845877476)
XLA Ops:
  0.6 1.3 %shard_map.67 = (f32[4,4,16,128]{3,2,1,0:T(8,128)S(1)}, f32[8,128]{1,0:T(8,128)S(1)}) custom-call(f32[2,19,4,16,128]{4,3,2,1,0:T(8,128)} %states_ref.1, f32[4,16,128]{2,1,0:T(8,128)} %por_hbm.1, s32[4,16,128]{2,1,0:T(8,128)} %mask_ref.1), custom_call_target="tpu_custom_call" | custom-call | bytes 180000 | tf_op jit(solution)/shard_map/pallas_call | solution.py:1059
  2.0 0.0 copy-done
  2.0 0.4 %shard_map.68 = (f32[72,128]{1,0:T(8,128)S(1)}, f32[152,128]{1,0:T(8,128)S(1)}, f32[48,128]{1,0:T(8,128)S(1)}, f32[48,128]{1,0:T(8,128)S(1)}) custom-call(f32[19,4,16,128]{3,2,1,0:T(8,128)S(1)} %copy-done, f32[4,4,16,128]{3,2,1,0:T(8,128)S(1)} %get-tuple-element.50.ub_ref, f32[8,128]{1,0:T(8,128)S(1)} %get-tuple-element.51.drag_ref), custom_call_target="tpu_custom_call" | custom-call | bytes 14400000 | tf_op jit(solution)/shard_map/pallas_call | solution.py:1059
  2.4 2.4 %collective-permute-start.1 = (f32[72,128]{1,0:T(8,128)S(1)}, f32[72,128]{1,0:T(8,128)S(1)}, u32[]{:S(2)}, u32[]{:S(2)}) collective-permute-start(f32[72,128]{1,0:T(8,128)S(1)} %get-tuple-element.52.cols_ref), channel_id=1, source_target_pairs={{0,24},{8,16},{16,8},{24,0},{1,25},{9,17},{17,9},{25,1},{2,26},{10... | collective-permute-start | bytes 110600 | tf_op jit(solution)/shard_map/ppermute | solution.py:1112
  4.9 1.8 %collective-permute-start.4 = (f32[48,128]{1,0:T(8,128)S(1)}, f32[48,128]{1,0:T(8,128)S(1)}, u32[]{:S(2)}, u32[]{:S(2)}) collective-permute-start(f32[48,128]{1,0:T(8,128)S(1)} %get-tuple-element.55), channel_id=1, source_target_pairs={{0,28},{4,24},{8,20},{12,16},{16,12},{20,8},{24,4},{28,0},{1,29},{... | collective-permute-start | bytes 73736 | tf_op jit(solution)/shard_map/ppermute | solution.py:1084
  6.6 1.3 %collective-permute-start.3 = (f32[48,128]{1,0:T(8,128)S(1)}, f32[48,128]{1,0:T(8,128)S(1)}, u32[]{:S(2)}, u32[]{:S(2)}) collective-permute-start(f32[48,128]{1,0:T(8,128)S(1)} %get-tuple-element.54), channel_id=1, source_target_pairs={{0,12},{4,8},{8,4},{12,0},{16,28},{20,24},{24,20},{28,16},{1,13},{... | collective-permute-start | bytes 73736 | tf_op jit(solution)/shard_map/ppermute | solution.py:1084
  7.9 0.9 %collective-permute-start = (f32[376,128]{1,0:T(8,128)S(1)}, f32[376,128]{1,0:T(8,128)S(1)}, u32[]{:S(2)}, u32[]{:S(2)}) collective-permute-start(f32[376,128]{1,0:T(8,128)S(1)} %shard_map.69), channel_id=1, source_target_pairs={{0,8},{8,0},{16,24},{24,16},{1,9},{9,1},{17,25},{25,17},{2,10},{10... | collective-permute-start | bytes 577544 | tf_op jit(solution)/shard_map/ppermute | solution.py:1113
  8.9 0.1 shard_map.71
  9.0 0.0 collective-permute-done.4.yb_ref
  9.0 1.4 %collective-permute-start.8 = (f32[232,128]{1,0:T(8,128)S(1)}, f32[232,128]{1,0:T(8,128)S(1)}, u32[]{:S(2)}, u32[]{:S(2)}) collective-permute-start(f32[232,128]{1,0:T(8,128)S(1)} %shard_map.71), channel_id=1, source_target_pairs={{0,24},{8,16},{16,8},{24,0},{1,25},{9,17},{17,9},{25,1},{2,26},{10... | collective-permute-start | bytes 356360 | tf_op jit(solution)/shard_map/ppermute | solution.py:1132
  10.4 0.5 %collective-permute-start.5 = (f32[1,128]{1,0:T(1,128)S(1)}, f32[1,128]{1,0:T(1,128)S(1)}, u32[]{:S(2)}, u32[]{:S(2)}) collective-permute-start(f32[1,128]{1,0:T(1,128)S(1)} %bitcast_add_fusion), channel_id=1, source_target_pairs={{0,8},{8,0},{16,24},{24,16},{1,9},{9,1},{17,25},{25,17},{2,10},{10... | collective-permute-start | bytes 1544 | tf_op jit(solution)/shard_map/ppermute | solution.py:1144
  10.9 0.0 collective-permute-done.xa_ref
  10.9 0.1 shard_map.70.main_ref
  11.0 0.3 %collective-permute-done.2.y_ref = f32[152,128]{1,0:T(8,128)S(1)} collective-permute-done((f32[152,128]{1,0:T(8,128)S(1)}, f32[152,128]{1,0:T(8,128)S(1)}, u32[]{:S(2)}, u32[]{:S(2)}) %collective-permute-start.2) | collective-permute-done | bytes 77856 | tf_op jit(solution)/shard_map/ppermute | solution.py:1115
  11.4 0.2 %shard_map.72 = (f32[96,128]{1,0:T(8,128)S(1)}, f32[40,128]{1,0:T(8,128)S(1)}, f32[40,128]{1,0:T(8,128)S(1)}, f32[1,128]{1,0:T(1,128)S(1)}) custom-call(f32[64,128]{1,0:T(8,128)S(1)} %shard_map.70.main_ref, f32[72,128]{1,0:T(8,128)S(1)} %get-tuple-element.52.cols_ref, f32[376,128]{1,0:T(8,128)S(1)} %collective-permute-done.xa_ref, ...), custom_call_target="tpu_custom_call" | custom-call | bytes 180000 | tf_op jit(solution)/shard_map/pallas_call | solution.py:1059
  11.6 0.1 collective-permute-done.5
  11.7 3.7 %collective-permute-start.7 = (f32[40,128]{1,0:T(8,128)S(1)}, f32[40,128]{1,0:T(8,128)S(1)}, u32[]{:S(2)}, u32[]{:S(2)}) collective-permute-start(f32[40,128]{1,0:T(8,128)S(1)} %scatter.9), channel_id=1, source_target_pairs={{0,3},{1,2},{2,1},{3,0},{4,7},{5,6},{6,5},{7,4},{8,11},{9,10},{10,... | collective-permute-start | bytes 61448 | tf_op jit(solution)/shard_map/ppermute | solution.py:1147
  15.4 0.1 collective-permute-start.6
  15.5 0.8 %collective-permute-start.9 = (f32[1,128]{1,0:T(1,128)S(1)}, f32[1,128]{1,0:T(1,128)S(1)}, u32[]{:S(2)}, u32[]{:S(2)}) collective-permute-start(f32[1,128]{1,0:T(1,128)S(1)} %add.11.refs_0_), channel_id=1, source_target_pairs={{0,2},{1,3},{2,0},{3,1},{4,6},{5,7},{6,4},{7,5},{8,10},{9,11},{10,... | collective-permute-start | bytes 1544 | tf_op jit(solution)/shard_map/ppermute | solution.py:1167
  16.3 2.4 %shard_map.73 = (f32[19,4,16,128]{3,2,1,0:T(8,128)S(1)}, f32[4,16,128]{2,1,0:T(8,128)S(1)}, f32[4,16,128]{2,1,0:T(8,128)S(1)}, f32[19,16,128]{2,1,0:T(8,128)S(1)...) custom-call(f32[2,19,4,16,128]{4,3,2,1,0:T(8,128)S(1)} %copy-done.1, f32[19,4,16,128]{3,2,1,0:T(8,128)S(1)} %copy-done, ...), custom_call_target="tpu_custom_call" | custom-call | bytes 14400000 | tf_op jit(solution)/shard_map/pallas_call | solution.py:1059
  18.7 0.6 %collective-permute-done.6.za_ref = f32[40,128]{1,0:T(8,128)S(1)} collective-permute-done((f32[40,128]{1,0:T(8,128)S(1)}, f32[40,128]{1,0:T(8,128)S(1)}, u32[]{:S(2)}, u32[]{:S(2)}) %collective-permute-start.6) | collective-permute-done | bytes 20512 | tf_op jit(solution)/shard_map/ppermute | solution.py:1148
  19.3 0.6 %shard_map.74 = (f32[21,16,128]{2,1,0:T(8,128)S(1)}, f32[1,128]{1,0:T(1,128)S(1)}) custom-call(f32[96,128]{1,0:T(8,128)S(1)} %get-tuple-element.57.zown_ref, f32[40,128]{1,0:T(8,128)S(1)} %collective-permute-done.6.za_ref, f32[40,128]{1,0:T(8,128)S(1)} %collective-permute-done.7.zb_ref, f32[19,16,128]{2,1,0:T(8,128)S(1)} %get-tuple-element.62.pack_ref, ...), custom_call_target="tpu_custom_call" | custom-call | bytes 180000 | tf_op jit(solution)/shard_map/pallas_call | solution.py:1059
  19.9 0.1 collective-permute-done.9.refs_1_
  20.0 1.0 %shard_map.75 = (f32[19,4,16,128]{3,2,1,0:T(8,128)}, f32[4,16,128]{2,1,0:T(8,128)}, f32[1,1]{1,0:T(1,128)}) custom-call(s32[4,16,128]{2,1,0:T(8,128)S(1)} %copy-done.2, f32[21,16,128]{2,1,0:T(8,128)S(1)} %get-tuple-element.65.zout, f32[19,4,16,128]{3,2,1,0:T(8,128)S(1)} %get-tuple-element.66.inner_ref, f32[4,16,128]{2,1,0:T(8,128)S(1)} %get-tuple-element.67.grad1_ref, ...), custom_call_target="tpu_custom_call" | custom-call | bytes 180000 | tf_op jit(solution)/shard_map/pallas_call | solution.py:1059
  (16 shorter events, 0.1 us)
Async XLA Ops:
  0.6 1.4 %copy-start = (f32[19,4,16,128]{3,2,1,0:T(8,128)S(1)}, f32[19,4,16,128]{3,2,1,0:T(8,128)}, u32[]{:S(2)}) copy-start(f32[19,4,16,128]{3,2,1,0:T(8,128)} %adj_ref.7) | copy-start | bytes 1867780
  2.4 8.0 %collective-permute-start.1 = (f32[72,128]{1,0:T(8,128)S(1)}, f32[72,128]{1,0:T(8,128)S(1)}, u32[]{:S(2)}, u32[]{:S(2)}) collective-permute-start(f32[72,128]{1,0:T(8,128)S(1)} %get-tuple-element.52.cols_ref), channel_id=1, source_target_pairs={{0,24},{8,16},{16,8},{24,0},{1,25},{9,17},{17,9},{25,1},{2,26},{10... | collective-permute-start | bytes 110600 | tf_op jit(solution)/shard_map/ppermute | solution.py:1112
  4.9 4.2 %collective-permute-start.4 = (f32[48,128]{1,0:T(8,128)S(1)}, f32[48,128]{1,0:T(8,128)S(1)}, u32[]{:S(2)}, u32[]{:S(2)}) collective-permute-start(f32[48,128]{1,0:T(8,128)S(1)} %get-tuple-element.55), channel_id=1, source_target_pairs={{0,28},{4,24},{8,20},{12,16},{16,12},{20,8},{24,4},{28,0},{1,29},{... | collective-permute-start | bytes 73736 | tf_op jit(solution)/shard_map/ppermute | solution.py:1084
  6.6 4.7 %collective-permute-start.2 = (f32[152,128]{1,0:T(8,128)S(1)}, f32[152,128]{1,0:T(8,128)S(1)}, u32[]{:S(2)}, u32[]{:S(2)}) collective-permute-start(f32[152,128]{1,0:T(8,128)S(1)} %get-tuple-element.53), channel_id=1, source_target_pairs={{0,4},{4,0},{1,5},{5,1},{2,6},{6,2},{3,7},{7,3},{8,12},{12,8},{9,1... | collective-permute-start | bytes 233480 | tf_op jit(solution)/shard_map/ppermute | solution.py:1115
  6.6 9.6 %copy-start.1 = (f32[2,19,4,16,128]{4,3,2,1,0:T(8,128)S(1)}, f32[2,19,4,16,128]{4,3,2,1,0:T(8,128)}, u32[]{:S(2)}) copy-start(f32[2,19,4,16,128]{4,3,2,1,0:T(8,128)} %states_ref.1) | copy-start | bytes 3735556
  6.6 4.4 %collective-permute-start.3 = (f32[48,128]{1,0:T(8,128)S(1)}, f32[48,128]{1,0:T(8,128)S(1)}, u32[]{:S(2)}, u32[]{:S(2)}) collective-permute-start(f32[48,128]{1,0:T(8,128)S(1)} %get-tuple-element.54), channel_id=1, source_target_pairs={{0,12},{4,8},{8,4},{12,0},{16,28},{20,24},{24,20},{28,16},{1,13},{... | collective-permute-start | bytes 73736 | tf_op jit(solution)/shard_map/ppermute | solution.py:1084
  7.9 2.9 %collective-permute-start = (f32[376,128]{1,0:T(8,128)S(1)}, f32[376,128]{1,0:T(8,128)S(1)}, u32[]{:S(2)}, u32[]{:S(2)}) collective-permute-start(f32[376,128]{1,0:T(8,128)S(1)} %shard_map.69), channel_id=1, source_target_pairs={{0,8},{8,0},{16,24},{24,16},{1,9},{9,1},{17,25},{25,17},{2,10},{10... | collective-permute-start | bytes 577544 | tf_op jit(solution)/shard_map/ppermute | solution.py:1113
  9.0 7.3 %collective-permute-start.8 = (f32[232,128]{1,0:T(8,128)S(1)}, f32[232,128]{1,0:T(8,128)S(1)}, u32[]{:S(2)}, u32[]{:S(2)}) collective-permute-start(f32[232,128]{1,0:T(8,128)S(1)} %shard_map.71), channel_id=1, source_target_pairs={{0,24},{8,16},{16,8},{24,0},{1,25},{9,17},{17,9},{25,1},{2,26},{10... | collective-permute-start | bytes 356360 | tf_op jit(solution)/shard_map/ppermute | solution.py:1132
  10.4 1.3 %collective-permute-start.5 = (f32[1,128]{1,0:T(1,128)S(1)}, f32[1,128]{1,0:T(1,128)S(1)}, u32[]{:S(2)}, u32[]{:S(2)}) collective-permute-start(f32[1,128]{1,0:T(1,128)S(1)} %bitcast_add_fusion), channel_id=1, source_target_pairs={{0,8},{8,0},{16,24},{24,16},{1,9},{9,1},{17,25},{25,17},{2,10},{10... | collective-permute-start | bytes 1544 | tf_op jit(solution)/shard_map/ppermute | solution.py:1144
  11.7 6.9 %collective-permute-start.7 = (f32[40,128]{1,0:T(8,128)S(1)}, f32[40,128]{1,0:T(8,128)S(1)}, u32[]{:S(2)}, u32[]{:S(2)}) collective-permute-start(f32[40,128]{1,0:T(8,128)S(1)} %scatter.9), channel_id=1, source_target_pairs={{0,3},{1,2},{2,1},{3,0},{4,7},{5,6},{6,5},{7,4},{8,11},{9,10},{10,... | collective-permute-start | bytes 61448 | tf_op jit(solution)/shard_map/ppermute | solution.py:1147
  15.4 4.6 %copy-start.2 = (s32[4,16,128]{2,1,0:T(8,128)S(1)}, s32[4,16,128]{2,1,0:T(8,128)}, u32[]{:S(2)}) copy-start(s32[4,16,128]{2,1,0:T(8,128)} %mask_ref.1) | copy-start | bytes 98308
  15.4 3.9 %collective-permute-start.6 = (f32[40,128]{1,0:T(8,128)S(1)}, f32[40,128]{1,0:T(8,128)S(1)}, u32[]{:S(2)}, u32[]{:S(2)}) collective-permute-start(f32[40,128]{1,0:T(8,128)S(1)} %scatter.6), channel_id=1, source_target_pairs={{0,1},{1,0},{2,3},{3,2},{4,5},{5,4},{6,7},{7,6},{8,9},{9,8},{10,11... | collective-permute-start | bytes 61448 | tf_op jit(solution)/shard_map/ppermute | solution.py:1148
  15.5 4.5 %collective-permute-start.9 = (f32[1,128]{1,0:T(1,128)S(1)}, f32[1,128]{1,0:T(1,128)S(1)}, u32[]{:S(2)}, u32[]{:S(2)}) collective-permute-start(f32[1,128]{1,0:T(1,128)S(1)} %add.11.refs_0_), channel_id=1, source_target_pairs={{0,2},{1,3},{2,0},{3,1},{4,6},{5,7},{6,4},{7,5},{8,10},{9,11},{10,... | collective-permute-start | bytes 1544 | tf_op jit(solution)/shard_map/ppermute | solution.py:1167

commit v13 on v12

--- a/solution.py
+++ b/solution.py
@@ -660,7 +660,7 @@
     drag_ref[...] = jnp.sum(drag, axis=0, keepdims=True) + (ya_ref[row] + yb_ref[row])
 
 
-OUT_GROUPS = ((0, 5), (5, 10), (10, 15), (15, 19))
+OUT_GROUPS = ((0, 6), (6, 12), (12, 17), (17, 19))
 
 
 def turn(value, shift):
@@ -1011,17 +1011,6 @@
         copy.start()
         copies.append(copy)
 
-    for low, high in OUT_GROUPS:
-        for i in range(low, high):
-            for x in range(nx):
-                for t in range(tiles):
-                    rows = slice(8 * t, 8 * t + 8)
-                    out_ref[i, x, rows, :] = jnp.where(
-                        outer,
-                        turn(zout[i, rows, :], -2 - 4 * x),
-                        inner_ref[i, x, rows, :],
-                    )
-        send(out_ref.at[low:high], out_hbm.at[low:high])
     for x in range(nx):
         for t in range(tiles):
             rows = slice(8 * t, 8 * t + 8)
@@ -1037,6 +1026,17 @@
         total = total + jnp.sum(ref[...], axis=0, keepdims=True)
     drag_ref[...] = jnp.sum(total, axis=1, keepdims=True) / whole_cells
     send(drag_ref, drag_hbm)
+    for low, high in OUT_GROUPS:
+        for i in range(low, high):
+            for x in range(nx):
+                for t in range(tiles):
+                    rows = slice(8 * t, 8 * t + 8)
+                    out_ref[i, x, rows, :] = jnp.where(
+                        outer,
+                        turn(zout[i, rows, :], -2 - 4 * x),
+                        inner_ref[i, x, rows, :],
+                    )
+        send(out_ref.at[low:high], out_hbm.at[low:high])
     for copy in copies:
         copy.wait()
 

time: 21.1 us -> 21.2 us (level)
  no operation moved by 1% of the time
where the time goes in v13:
time: 21.2 us; the launch traced here: 21 us
  starting transfers between devices  12.8 us (60%)
  Pallas kernels  6.24 us (29%)
  waiting for transfers between devices  1.16 us (5%)
  between operations  0.74 us (3%)
    pallas_call x9, Pallas kernels, call(): pl.pallas_call(kernel, out_shape=[jax.ShapeDtypeStruct(s, jnp.float32) fo...  6.24 us
    ppermute x1, starting transfers between devices, body(): zb = lax.ppermute(zb, 'gz', z_second)  3.66 us
    ppermute x2, starting transfers between devices, diagonal(): return lax.ppermute(message, ('gx', 'gy'), pairs)  3.06 us
    ppermute x1, starting transfers between devices, body(): xc = lax.ppermute(cols, 'gx', x_second)  2.44 us
    ppermute x1, starting transfers between devices, body(): xb = lax.ppermute(xb, 'gx', x_second)  1.38 us
    ppermute x1, starting transfers between devices, body(): xa = lax.ppermute(xa, 'gx', x_first)  0.91 us
    ppermute x1, starting transfers between devices, body(): zhalf = lax.ppermute(drag_xy, 'gz', [(i, i ^ 2) for i in range(gz)])  0.77 us
    ppermute x1, waiting for transfers between devices, body(): za = lax.ppermute(za, 'gz', z_first)  0.59 us
  transfers between devices with their start and end apart: 10, of which 4 were waited for; matrix products, arithmetic and copies ran while one was open for 0% of the time, Pallas kernels for 17%

profile of v13, /device:TPU:0, one launch (start us, length us, event | category | flops | bytes accessed | tf_op | source)
XLA Modules:
  0.0 21.0 jit_solution(4328256398840313433)
XLA Ops:
  0.6 1.3 %shard_map.67 = (f32[4,4,16,128]{3,2,1,0:T(8,128)S(1)}, f32[8,128]{1,0:T(8,128)S(1)}) custom-call(f32[2,19,4,16,128]{4,3,2,1,0:T(8,128)} %states_ref.1, f32[4,16,128]{2,1,0:T(8,128)} %por_hbm.1, s32[4,16,128]{2,1,0:T(8,128)} %mask_ref.1), custom_call_target="tpu_custom_call" | custom-call | bytes 180000 | tf_op jit(solution)/shard_map/pallas_call | solution.py:1059
  2.0 0.0 copy-done
  2.0 0.4 %shard_map.68 = (f32[72,128]{1,0:T(8,128)S(1)}, f32[152,128]{1,0:T(8,128)S(1)}, f32[48,128]{1,0:T(8,128)S(1)}, f32[48,128]{1,0:T(8,128)S(1)}) custom-call(f32[19,4,16,128]{3,2,1,0:T(8,128)S(1)} %copy-done, f32[4,4,16,128]{3,2,1,0:T(8,128)S(1)} %get-tuple-element.50.ub_ref, f32[8,128]{1,0:T(8,128)S(1)} %get-tuple-element.51.drag_ref), custom_call_target="tpu_custom_call" | custom-call | bytes 14400000 | tf_op jit(solution)/shard_map/pallas_call | solution.py:1059
  2.4 2.4 %collective-permute-start.1 = (f32[72,128]{1,0:T(8,128)S(1)}, f32[72,128]{1,0:T(8,128)S(1)}, u32[]{:S(2)}, u32[]{:S(2)}) collective-permute-start(f32[72,128]{1,0:T(8,128)S(1)} %get-tuple-element.52.cols_ref), channel_id=1, source_target_pairs={{0,24},{8,16},{16,8},{24,0},{1,25},{9,17},{17,9},{25,1},{2,26},{10... | collective-permute-start | bytes 110600 | tf_op jit(solution)/shard_map/ppermute | solution.py:1112
  4.9 1.8 %collective-permute-start.4 = (f32[48,128]{1,0:T(8,128)S(1)}, f32[48,128]{1,0:T(8,128)S(1)}, u32[]{:S(2)}, u32[]{:S(2)}) collective-permute-start(f32[48,128]{1,0:T(8,128)S(1)} %get-tuple-element.55), channel_id=1, source_target_pairs={{0,28},{4,24},{8,20},{12,16},{16,12},{20,8},{24,4},{28,0},{1,29},{... | collective-permute-start | bytes 73736 | tf_op jit(solution)/shard_map/ppermute | solution.py:1084
  6.6 1.3 %collective-permute-start.3 = (f32[48,128]{1,0:T(8,128)S(1)}, f32[48,128]{1,0:T(8,128)S(1)}, u32[]{:S(2)}, u32[]{:S(2)}) collective-permute-start(f32[48,128]{1,0:T(8,128)S(1)} %get-tuple-element.54), channel_id=1, source_target_pairs={{0,12},{4,8},{8,4},{12,0},{16,28},{20,24},{24,20},{28,16},{1,13},{... | collective-permute-start | bytes 73736 | tf_op jit(solution)/shard_map/ppermute | solution.py:1084
  7.9 0.9 %collective-permute-start = (f32[376,128]{1,0:T(8,128)S(1)}, f32[376,128]{1,0:T(8,128)S(1)}, u32[]{:S(2)}, u32[]{:S(2)}) collective-permute-start(f32[376,128]{1,0:T(8,128)S(1)} %shard_map.69), channel_id=1, source_target_pairs={{0,8},{8,0},{16,24},{24,16},{1,9},{9,1},{17,25},{25,17},{2,10},{10... | collective-permute-start | bytes 577544 | tf_op jit(solution)/shard_map/ppermute | solution.py:1113
  8.9 0.1 shard_map.71
  9.0 0.0 collective-permute-done.4.yb_ref
  9.0 1.4 %collective-permute-start.8 = (f32[232,128]{1,0:T(8,128)S(1)}, f32[232,128]{1,0:T(8,128)S(1)}, u32[]{:S(2)}, u32[]{:S(2)}) collective-permute-start(f32[232,128]{1,0:T(8,128)S(1)} %shard_map.71), channel_id=1, source_target_pairs={{0,24},{8,16},{16,8},{24,0},{1,25},{9,17},{17,9},{25,1},{2,26},{10... | collective-permute-start | bytes 356360 | tf_op jit(solution)/shard_map/ppermute | solution.py:1132
  10.4 0.0 collective-permute-done.1.xc_ref
  10.4 0.5 %collective-permute-start.5 = (f32[1,128]{1,0:T(1,128)S(1)}, f32[1,128]{1,0:T(1,128)S(1)}, u32[]{:S(2)}, u32[]{:S(2)}) collective-permute-start(f32[1,128]{1,0:T(1,128)S(1)} %bitcast_add_fusion), channel_id=1, source_target_pairs={{0,8},{8,0},{16,24},{24,16},{1,9},{9,1},{17,25},{25,17},{2,10},{10... | collective-permute-start | bytes 1544 | tf_op jit(solution)/shard_map/ppermute | solution.py:1144
  10.9 0.1 shard_map.70.main_ref
  11.0 0.3 %collective-permute-done.2.y_ref = f32[152,128]{1,0:T(8,128)S(1)} collective-permute-done((f32[152,128]{1,0:T(8,128)S(1)}, f32[152,128]{1,0:T(8,128)S(1)}, u32[]{:S(2)}, u32[]{:S(2)}) %collective-permute-start.2) | collective-permute-done | bytes 77856 | tf_op jit(solution)/shard_map/ppermute | solution.py:1115
  11.4 0.2 %shard_map.72 = (f32[96,128]{1,0:T(8,128)S(1)}, f32[40,128]{1,0:T(8,128)S(1)}, f32[40,128]{1,0:T(8,128)S(1)}, f32[1,128]{1,0:T(1,128)S(1)}) custom-call(f32[64,128]{1,0:T(8,128)S(1)} %shard_map.70.main_ref, f32[72,128]{1,0:T(8,128)S(1)} %get-tuple-element.52.cols_ref, f32[376,128]{1,0:T(8,128)S(1)} %collective-permute-done.xa_ref, ...), custom_call_target="tpu_custom_call" | custom-call | bytes 180000 | tf_op jit(solution)/shard_map/pallas_call | solution.py:1059
  11.6 0.1 collective-permute-done.5
  11.7 3.7 %collective-permute-start.7 = (f32[40,128]{1,0:T(8,128)S(1)}, f32[40,128]{1,0:T(8,128)S(1)}, u32[]{:S(2)}, u32[]{:S(2)}) collective-permute-start(f32[40,128]{1,0:T(8,128)S(1)} %scatter.9), channel_id=1, source_target_pairs={{0,3},{1,2},{2,1},{3,0},{4,7},{5,6},{6,5},{7,4},{8,11},{9,10},{10,... | collective-permute-start | bytes 61448 | tf_op jit(solution)/shard_map/ppermute | solution.py:1147
  15.4 0.1 collective-permute-start.6
  15.5 0.8 %collective-permute-start.9 = (f32[1,128]{1,0:T(1,128)S(1)}, f32[1,128]{1,0:T(1,128)S(1)}, u32[]{:S(2)}, u32[]{:S(2)}) collective-permute-start(f32[1,128]{1,0:T(1,128)S(1)} %add.11.refs_0_), channel_id=1, source_target_pairs={{0,2},{1,3},{2,0},{3,1},{4,6},{5,7},{6,4},{7,5},{8,10},{9,11},{10,... | collective-permute-start | bytes 1544 | tf_op jit(solution)/shard_map/ppermute | solution.py:1167
  16.3 2.4 %shard_map.73 = (f32[19,4,16,128]{3,2,1,0:T(8,128)S(1)}, f32[4,16,128]{2,1,0:T(8,128)S(1)}, f32[4,16,128]{2,1,0:T(8,128)S(1)}, f32[19,16,128]{2,1,0:T(8,128)S(1)...) custom-call(f32[2,19,4,16,128]{4,3,2,1,0:T(8,128)S(1)} %copy-done.1, f32[19,4,16,128]{3,2,1,0:T(8,128)S(1)} %copy-done, ...), custom_call_target="tpu_custom_call" | custom-call | bytes 14400000 | tf_op jit(solution)/shard_map/pallas_call | solution.py:1059
  18.7 0.6 %collective-permute-done.6.za_ref = f32[40,128]{1,0:T(8,128)S(1)} collective-permute-done((f32[40,128]{1,0:T(8,128)S(1)}, f32[40,128]{1,0:T(8,128)S(1)}, u32[]{:S(2)}, u32[]{:S(2)}) %collective-permute-start.6) | collective-permute-done | bytes 20512 | tf_op jit(solution)/shard_map/ppermute | solution.py:1148
  19.3 0.6 %shard_map.74 = (f32[21,16,128]{2,1,0:T(8,128)S(1)}, f32[1,128]{1,0:T(1,128)S(1)}) custom-call(f32[96,128]{1,0:T(8,128)S(1)} %get-tuple-element.57.zown_ref, f32[40,128]{1,0:T(8,128)S(1)} %collective-permute-done.6.za_ref, f32[40,128]{1,0:T(8,128)S(1)} %collective-permute-done.7.zb_ref, f32[19,16,128]{2,1,0:T(8,128)S(1)} %get-tuple-element.62.pack_ref, ...), custom_call_target="tpu_custom_call" | custom-call | bytes 180000 | tf_op jit(solution)/shard_map/pallas_call | solution.py:1059
  19.9 0.1 collective-permute-done.9.refs_1_
  20.0 1.0 %shard_map.75 = (f32[19,4,16,128]{3,2,1,0:T(8,128)}, f32[4,16,128]{2,1,0:T(8,128)}, f32[1,1]{1,0:T(1,128)}) custom-call(s32[4,16,128]{2,1,0:T(8,128)S(1)} %copy-done.2, f32[21,16,128]{2,1,0:T(8,128)S(1)} %get-tuple-element.65.zout, f32[19,4,16,128]{3,2,1,0:T(8,128)S(1)} %get-tuple-element.66.inner_ref, f32[4,16,128]{2,1,0:T(8,128)S(1)} %get-tuple-element.67.grad1_ref, ...), custom_call_target="tpu_custom_call" | custom-call | bytes 180000 | tf_op jit(solution)/shard_map/pallas_call | solution.py:1059
  (16 shorter events, 0.1 us)
Async XLA Ops:
  0.6 1.4 %copy-start = (f32[19,4,16,128]{3,2,1,0:T(8,128)S(1)}, f32[19,4,16,128]{3,2,1,0:T(8,128)}, u32[]{:S(2)}) copy-start(f32[19,4,16,128]{3,2,1,0:T(8,128)} %adj_ref.7) | copy-start | bytes 1867780
  2.4 8.0 %collective-permute-start.1 = (f32[72,128]{1,0:T(8,128)S(1)}, f32[72,128]{1,0:T(8,128)S(1)}, u32[]{:S(2)}, u32[]{:S(2)}) collective-permute-start(f32[72,128]{1,0:T(8,128)S(1)} %get-tuple-element.52.cols_ref), channel_id=1, source_target_pairs={{0,24},{8,16},{16,8},{24,0},{1,25},{9,17},{17,9},{25,1},{2,26},{10... | collective-permute-start | bytes 110600 | tf_op jit(solution)/shard_map/ppermute | solution.py:1112
  4.9 4.2 %collective-permute-start.4 = (f32[48,128]{1,0:T(8,128)S(1)}, f32[48,128]{1,0:T(8,128)S(1)}, u32[]{:S(2)}, u32[]{:S(2)}) collective-permute-start(f32[48,128]{1,0:T(8,128)S(1)} %get-tuple-element.55), channel_id=1, source_target_pairs={{0,28},{4,24},{8,20},{12,16},{16,12},{20,8},{24,4},{28,0},{1,29},{... | collective-permute-start | bytes 73736 | tf_op jit(solution)/shard_map/ppermute | solution.py:1084
  6.6 4.7 %collective-permute-start.2 = (f32[152,128]{1,0:T(8,128)S(1)}, f32[152,128]{1,0:T(8,128)S(1)}, u32[]{:S(2)}, u32[]{:S(2)}) collective-permute-start(f32[152,128]{1,0:T(8,128)S(1)} %get-tuple-element.53), channel_id=1, source_target_pairs={{0,4},{4,0},{1,5},{5,1},{2,6},{6,2},{3,7},{7,3},{8,12},{12,8},{9,1... | collective-permute-start | bytes 233480 | tf_op jit(solution)/shard_map/ppermute | solution.py:1115
  6.6 9.6 %copy-start.1 = (f32[2,19,4,16,128]{4,3,2,1,0:T(8,128)S(1)}, f32[2,19,4,16,128]{4,3,2,1,0:T(8,128)}, u32[]{:S(2)}) copy-start(f32[2,19,4,16,128]{4,3,2,1,0:T(8,128)} %states_ref.1) | copy-start | bytes 3735556
  6.6 4.4 %collective-permute-start.3 = (f32[48,128]{1,0:T(8,128)S(1)}, f32[48,128]{1,0:T(8,128)S(1)}, u32[]{:S(2)}, u32[]{:S(2)}) collective-permute-start(f32[48,128]{1,0:T(8,128)S(1)} %get-tuple-element.54), channel_id=1, source_target_pairs={{0,12},{4,8},{8,4},{12,0},{16,28},{20,24},{24,20},{28,16},{1,13},{... | collective-permute-start | bytes 73736 | tf_op jit(solution)/shard_map/ppermute | solution.py:1084
  7.9 2.9 %collective-permute-start = (f32[376,128]{1,0:T(8,128)S(1)}, f32[376,128]{1,0:T(8,128)S(1)}, u32[]{:S(2)}, u32[]{:S(2)}) collective-permute-start(f32[376,128]{1,0:T(8,128)S(1)} %shard_map.69), channel_id=1, source_target_pairs={{0,8},{8,0},{16,24},{24,16},{1,9},{9,1},{17,25},{25,17},{2,10},{10... | collective-permute-start | bytes 577544 | tf_op jit(solution)/shard_map/ppermute | solution.py:1113
  9.0 7.3 %collective-permute-start.8 = (f32[232,128]{1,0:T(8,128)S(1)}, f32[232,128]{1,0:T(8,128)S(1)}, u32[]{:S(2)}, u32[]{:S(2)}) collective-permute-start(f32[232,128]{1,0:T(8,128)S(1)} %shard_map.71), channel_id=1, source_target_pairs={{0,24},{8,16},{16,8},{24,0},{1,25},{9,17},{17,9},{25,1},{2,26},{10... | collective-permute-start | bytes 356360 | tf_op jit(solution)/shard_map/ppermute | solution.py:1132
  10.4 1.3 %collective-permute-start.5 = (f32[1,128]{1,0:T(1,128)S(1)}, f32[1,128]{1,0:T(1,128)S(1)}, u32[]{:S(2)}, u32[]{:S(2)}) collective-permute-start(f32[1,128]{1,0:T(1,128)S(1)} %bitcast_add_fusion), channel_id=1, source_target_pairs={{0,8},{8,0},{16,24},{24,16},{1,9},{9,1},{17,25},{25,17},{2,10},{10... | collective-permute-start | bytes 1544 | tf_op jit(solution)/shard_map/ppermute | solution.py:1144
  11.7 6.9 %collective-permute-start.7 = (f32[40,128]{1,0:T(8,128)S(1)}, f32[40,128]{1,0:T(8,128)S(1)}, u32[]{:S(2)}, u32[]{:S(2)}) collective-permute-start(f32[40,128]{1,0:T(8,128)S(1)} %scatter.9), channel_id=1, source_target_pairs={{0,3},{1,2},{2,1},{3,0},{4,7},{5,6},{6,5},{7,4},{8,11},{9,10},{10,... | collective-permute-start | bytes 61448 | tf_op jit(solution)/shard_map/ppermute | solution.py:1147
  15.4 4.6 %copy-start.2 = (s32[4,16,128]{2,1,0:T(8,128)S(1)}, s32[4,16,128]{2,1,0:T(8,128)}, u32[]{:S(2)}) copy-start(s32[4,16,128]{2,1,0:T(8,128)} %mask_ref.1) | copy-start | bytes 98308
  15.4 3.9 %collective-permute-start.6 = (f32[40,128]{1,0:T(8,128)S(1)}, f32[40,128]{1,0:T(8,128)S(1)}, u32[]{:S(2)}, u32[]{:S(2)}) collective-permute-start(f32[40,128]{1,0:T(8,128)S(1)} %scatter.6), channel_id=1, source_target_pairs={{0,1},{1,0},{2,3},{3,2},{4,5},{5,4},{6,7},{7,6},{8,9},{9,8},{10,11... | collective-permute-start | bytes 61448 | tf_op jit(solution)/shard_map/ppermute | solution.py:1148
  15.5 4.5 %collective-permute-start.9 = (f32[1,128]{1,0:T(1,128)S(1)}, f32[1,128]{1,0:T(1,128)S(1)}, u32[]{:S(2)}, u32[]{:S(2)}) collective-permute-start(f32[1,128]{1,0:T(1,128)S(1)} %add.11.refs_0_), channel_id=1, source_target_pairs={{0,2},{1,3},{2,0},{3,1},{4,6},{5,7},{6,4},{7,5},{8,10},{9,11},{10,... | collective-permute-start | bytes 1544 | tf_op jit(solution)/shard_map/ppermute | solution.py:1167

commit v14 on v13

--- a/solution.py
+++ b/solution.py
@@ -694,6 +694,7 @@
     tiles = ny // 8
     lane = lax.broadcasted_iota(jnp.int32, (8, nz), 1)
     slot = lane // 4
+    slot0 = ((lane + 2) % nz) // 4
     sub = lax.broadcasted_iota(jnp.int32, (8, nz), 0)
     even_x = parity("gx") == 0
     even_y = parity("gy") == 0
@@ -852,7 +853,7 @@
                 value = z_shifted(mid[i, x + 1 + cx, low : low + 8, :], cz)
                 got.append(value)
                 pack_ref[i, rows, :] = jnp.where(
-                    slot == x, pltpu.roll(value, 4 * x + 2, 1), pack_ref[i, rows, :]
+                    slot0 == x, pltpu.roll(value, 4 * x, 1), pack_ref[i, rows, :]
                 )
             f0, fs, fd, fm, u = state_of(states_ref, (0, x, rows))
             b = ub_ref[3, x, rows, :]
@@ -880,7 +881,11 @@
                         else ub_ref[3, x, rows, :]
                     )
                     p = x + first
-                    acc = jnp.where(slot == p, pltpu.roll(value, 4 * p + 2, 1), acc)
+                    acc = jnp.where(
+                        (slot if level else slot0) == p,
+                        turn(value, 4 * p + 2 * level),
+                        acc,
+                    )
                 out_ref[i, rows, :] = acc
         return carry
 
@@ -964,9 +969,9 @@
             fs, fd = pairs_of(f)
             fm = moments(f[0], fs, fd)
             grad = gradient_cell(kept, f[0], fs, fd, fm, got[19:22])
-            slab_grad.append(turn(grad, -8))
-
-    at = lane % 4
+            slab_grad.append(turn(grad, -10))
+
+    at = (lane + 2) % 4
     for t in range(tiles):
         rows = slice(8 * t, 8 * t + 8)
         got = []
@@ -974,7 +979,7 @@
             cx, cy, cz = VEL[i]
             value = pack_ref[i, rows, :]
             edge = zmid[i, 8 + 8 * t + cy : 16 + 8 * t + cy, :]
-            back = -4 * (2 + cx)
+            back = -4 * (2 + cx) - 2
             if cz == 0:
                 value = jnp.where((at == 1) | (at == 2), turn(edge, back), value)
             else:
@@ -1015,9 +1020,9 @@
         for t in range(tiles):
             rows = slice(8 * t, 8 * t + 8)
             level1 = jnp.where(
-                ends, turn(zout[20, rows, :], -2 - 4 * x), grad1_ref[x, rows, :]
+                ends, turn(zout[20, rows, :], -4 * x), grad1_ref[x, rows, :]
             )
-            edge = turn(zout[19, rows, :], -2 - 4 * x) + level1
+            edge = turn(zout[19, rows, :], -4 * x) + level1
             grad = jnp.where(outer, edge, inner_grad_ref[x, rows, :])
             grad_ref[x, rows, :] = jnp.where(mask_ref[x, rows, :] == 0, grad, 0.0)
     send(grad_ref, grad_hbm)
@@ -1033,7 +1038,7 @@
                     rows = slice(8 * t, 8 * t + 8)
                     out_ref[i, x, rows, :] = jnp.where(
                         outer,
-                        turn(zout[i, rows, :], -2 - 4 * x),
+                        turn(zout[i, rows, :], -4 * x),
                         inner_ref[i, x, rows, :],
                     )
         send(out_ref.at[low:high], out_hbm.at[low:high])

time: 21.2 us -> 21.2 us (level)
  transfers between devices with their start and end apart: 10 -> 10, of which waited for: 4 -> 4; matrix products, arithmetic and copies ran while one was open for 0% -> 0% of each run, Pallas kernels for 17% -> 16%
where the time goes in v14:
time: 21.2 us; the launch traced here: 21 us
  starting transfers between devices  12.8 us (60%)
  Pallas kernels  6.18 us (29%)
  waiting for transfers between devices  1.2 us (6%)
  between operations  0.74 us (3%)
    pallas_call x9, Pallas kernels, call(): pl.pallas_call(kernel, out_shape=[jax.ShapeDtypeStruct(s, jnp.float32) fo...  6.18 us
    ppermute x1, starting transfers between devices, body(): zb = lax.ppermute(zb, 'gz', z_second)  3.66 us
    ppermute x2, starting transfers between devices, diagonal(): return lax.ppermute(message, ('gx', 'gy'), pairs)  3.06 us
    ppermute x1, starting transfers between devices, body(): xc = lax.ppermute(cols, 'gx', x_second)  2.44 us
    ppermute x1, starting transfers between devices, body(): xb = lax.ppermute(xb, 'gx', x_second)  1.38 us
    ppermute x1, starting transfers between devices, body(): xa = lax.ppermute(xa, 'gx', x_first)  0.91 us
    ppermute x1, starting transfers between devices, body(): zhalf = lax.ppermute(drag_xy, 'gz', [(i, i ^ 2) for i in range(gz)])  0.77 us
    ppermute x1, waiting for transfers between devices, body(): za = lax.ppermute(za, 'gz', z_first)  0.64 us
  transfers between devices with their start and end apart: 10, of which 4 were waited for; matrix products, arithmetic and copies ran while one was open for 0% of the time, Pallas kernels for 16%

profile of v14, /device:TPU:0, one launch (start us, length us, event | category | flops | bytes accessed | tf_op | source)
XLA Modules:
  0.0 21.0 jit_solution(921993993460760157)
XLA Ops:
  0.6 1.3 %shard_map.67 = (f32[4,4,16,128]{3,2,1,0:T(8,128)S(1)}, f32[8,128]{1,0:T(8,128)S(1)}) custom-call(f32[2,19,4,16,128]{4,3,2,1,0:T(8,128)} %states_ref.1, f32[4,16,128]{2,1,0:T(8,128)} %por_hbm.1, s32[4,16,128]{2,1,0:T(8,128)} %mask_ref.1), custom_call_target="tpu_custom_call" | custom-call | bytes 180000 | tf_op jit(solution)/shard_map/pallas_call | solution.py:1064
  2.0 0.0 copy-done
  2.0 0.4 %shard_map.68 = (f32[72,128]{1,0:T(8,128)S(1)}, f32[152,128]{1,0:T(8,128)S(1)}, f32[48,128]{1,0:T(8,128)S(1)}, f32[48,128]{1,0:T(8,128)S(1)}) custom-call(f32[19,4,16,128]{3,2,1,0:T(8,128)S(1)} %copy-done, f32[4,4,16,128]{3,2,1,0:T(8,128)S(1)} %get-tuple-element.50.ub_ref, f32[8,128]{1,0:T(8,128)S(1)} %get-tuple-element.51.drag_ref), custom_call_target="tpu_custom_call" | custom-call | bytes 14400000 | tf_op jit(solution)/shard_map/pallas_call | solution.py:1064
  2.4 2.4 %collective-permute-start.1 = (f32[72,128]{1,0:T(8,128)S(1)}, f32[72,128]{1,0:T(8,128)S(1)}, u32[]{:S(2)}, u32[]{:S(2)}) collective-permute-start(f32[72,128]{1,0:T(8,128)S(1)} %get-tuple-element.52.cols_ref), channel_id=1, source_target_pairs={{0,24},{8,16},{16,8},{24,0},{1,25},{9,17},{17,9},{25,1},{2,26},{10... | collective-permute-start | bytes 110600 | tf_op jit(solution)/shard_map/ppermute | solution.py:1117
  4.9 1.8 %collective-permute-start.4 = (f32[48,128]{1,0:T(8,128)S(1)}, f32[48,128]{1,0:T(8,128)S(1)}, u32[]{:S(2)}, u32[]{:S(2)}) collective-permute-start(f32[48,128]{1,0:T(8,128)S(1)} %get-tuple-element.55), channel_id=1, source_target_pairs={{0,28},{4,24},{8,20},{12,16},{16,12},{20,8},{24,4},{28,0},{1,29},{... | collective-permute-start | bytes 73736 | tf_op jit(solution)/shard_map/ppermute | solution.py:1089
  6.6 1.3 %collective-permute-start.3 = (f32[48,128]{1,0:T(8,128)S(1)}, f32[48,128]{1,0:T(8,128)S(1)}, u32[]{:S(2)}, u32[]{:S(2)}) collective-permute-start(f32[48,128]{1,0:T(8,128)S(1)} %get-tuple-element.54), channel_id=1, source_target_pairs={{0,12},{4,8},{8,4},{12,0},{16,28},{20,24},{24,20},{28,16},{1,13},{... | collective-permute-start | bytes 73736 | tf_op jit(solution)/shard_map/ppermute | solution.py:1089
  7.9 0.9 %collective-permute-start = (f32[376,128]{1,0:T(8,128)S(1)}, f32[376,128]{1,0:T(8,128)S(1)}, u32[]{:S(2)}, u32[]{:S(2)}) collective-permute-start(f32[376,128]{1,0:T(8,128)S(1)} %shard_map.69), channel_id=1, source_target_pairs={{0,8},{8,0},{16,24},{24,16},{1,9},{9,1},{17,25},{25,17},{2,10},{10... | collective-permute-start | bytes 577544 | tf_op jit(solution)/shard_map/ppermute | solution.py:1118
  8.9 0.1 shard_map.71
  9.0 0.0 collective-permute-done.4.yb_ref
  9.0 1.4 %collective-permute-start.8 = (f32[232,128]{1,0:T(8,128)S(1)}, f32[232,128]{1,0:T(8,128)S(1)}, u32[]{:S(2)}, u32[]{:S(2)}) collective-permute-start(f32[232,128]{1,0:T(8,128)S(1)} %shard_map.71), channel_id=1, source_target_pairs={{0,24},{8,16},{16,8},{24,0},{1,25},{9,17},{17,9},{25,1},{2,26},{10... | collective-permute-start | bytes 356360 | tf_op jit(solution)/shard_map/ppermute | solution.py:1137
  10.4 0.5 %collective-permute-start.5 = (f32[1,128]{1,0:T(1,128)S(1)}, f32[1,128]{1,0:T(1,128)S(1)}, u32[]{:S(2)}, u32[]{:S(2)}) collective-permute-start(f32[1,128]{1,0:T(1,128)S(1)} %bitcast_add_fusion), channel_id=1, source_target_pairs={{0,8},{8,0},{16,24},{24,16},{1,9},{9,1},{17,25},{25,17},{2,10},{10... | collective-permute-start | bytes 1544 | tf_op jit(solution)/shard_map/ppermute | solution.py:1149
  10.9 0.0 collective-permute-done.xa_ref
  10.9 0.1 shard_map.70.main_ref
  11.0 0.3 %collective-permute-done.2.y_ref = f32[152,128]{1,0:T(8,128)S(1)} collective-permute-done((f32[152,128]{1,0:T(8,128)S(1)}, f32[152,128]{1,0:T(8,128)S(1)}, u32[]{:S(2)}, u32[]{:S(2)}) %collective-permute-start.2) | collective-permute-done | bytes 77856 | tf_op jit(solution)/shard_map/ppermute | solution.py:1120
  11.4 0.2 %shard_map.72 = (f32[96,128]{1,0:T(8,128)S(1)}, f32[40,128]{1,0:T(8,128)S(1)}, f32[40,128]{1,0:T(8,128)S(1)}, f32[1,128]{1,0:T(1,128)S(1)}) custom-call(f32[64,128]{1,0:T(8,128)S(1)} %shard_map.70.main_ref, f32[72,128]{1,0:T(8,128)S(1)} %get-tuple-element.52.cols_ref, f32[376,128]{1,0:T(8,128)S(1)} %collective-permute-done.xa_ref, ...), custom_call_target="tpu_custom_call" | custom-call | bytes 180000 | tf_op jit(solution)/shard_map/pallas_call | solution.py:1064
  11.6 0.1 collective-permute-done.5
  11.7 3.7 %collective-permute-start.7 = (f32[40,128]{1,0:T(8,128)S(1)}, f32[40,128]{1,0:T(8,128)S(1)}, u32[]{:S(2)}, u32[]{:S(2)}) collective-permute-start(f32[40,128]{1,0:T(8,128)S(1)} %scatter.9), channel_id=1, source_target_pairs={{0,3},{1,2},{2,1},{3,0},{4,7},{5,6},{6,5},{7,4},{8,11},{9,10},{10,... | collective-permute-start | bytes 61448 | tf_op jit(solution)/shard_map/ppermute | solution.py:1152
  15.4 0.1 collective-permute-start.6
  15.5 0.8 %collective-permute-start.9 = (f32[1,128]{1,0:T(1,128)S(1)}, f32[1,128]{1,0:T(1,128)S(1)}, u32[]{:S(2)}, u32[]{:S(2)}) collective-permute-start(f32[1,128]{1,0:T(1,128)S(1)} %add.11.refs_0_), channel_id=1, source_target_pairs={{0,2},{1,3},{2,0},{3,1},{4,6},{5,7},{6,4},{7,5},{8,10},{9,11},{10,... | collective-permute-start | bytes 1544 | tf_op jit(solution)/shard_map/ppermute | solution.py:1172
  16.3 2.3 %shard_map.73 = (f32[19,4,16,128]{3,2,1,0:T(8,128)S(1)}, f32[4,16,128]{2,1,0:T(8,128)S(1)}, f32[4,16,128]{2,1,0:T(8,128)S(1)}, f32[19,16,128]{2,1,0:T(8,128)S(1)...) custom-call(f32[2,19,4,16,128]{4,3,2,1,0:T(8,128)S(1)} %copy-done.1, f32[19,4,16,128]{3,2,1,0:T(8,128)S(1)} %copy-done, ...), custom_call_target="tpu_custom_call" | custom-call | bytes 14400000 | tf_op jit(solution)/shard_map/pallas_call | solution.py:1064
  18.6 0.6 %collective-permute-done.6.za_ref = f32[40,128]{1,0:T(8,128)S(1)} collective-permute-done((f32[40,128]{1,0:T(8,128)S(1)}, f32[40,128]{1,0:T(8,128)S(1)}, u32[]{:S(2)}, u32[]{:S(2)}) %collective-permute-start.6) | collective-permute-done | bytes 20512 | tf_op jit(solution)/shard_map/ppermute | solution.py:1153
  19.3 0.6 %shard_map.74 = (f32[21,16,128]{2,1,0:T(8,128)S(1)}, f32[1,128]{1,0:T(1,128)S(1)}) custom-call(f32[96,128]{1,0:T(8,128)S(1)} %get-tuple-element.57.zown_ref, f32[40,128]{1,0:T(8,128)S(1)} %collective-permute-done.6.za_ref, f32[40,128]{1,0:T(8,128)S(1)} %collective-permute-done.7.zb_ref, f32[19,16,128]{2,1,0:T(8,128)S(1)} %get-tuple-element.62.pack_ref, ...), custom_call_target="tpu_custom_call" | custom-call | bytes 180000 | tf_op jit(solution)/shard_map/pallas_call | solution.py:1064
  19.9 0.1 collective-permute-done.9.refs_1_
  20.0 1.0 %shard_map.75 = (f32[19,4,16,128]{3,2,1,0:T(8,128)}, f32[4,16,128]{2,1,0:T(8,128)}, f32[1,1]{1,0:T(1,128)}) custom-call(s32[4,16,128]{2,1,0:T(8,128)S(1)} %copy-done.2, f32[21,16,128]{2,1,0:T(8,128)S(1)} %get-tuple-element.65.zout, f32[19,4,16,128]{3,2,1,0:T(8,128)S(1)} %get-tuple-element.66.inner_ref, f32[4,16,128]{2,1,0:T(8,128)S(1)} %get-tuple-element.67.grad1_ref, ...), custom_call_target="tpu_custom_call" | custom-call | bytes 180000 | tf_op jit(solution)/shard_map/pallas_call | solution.py:1064
  (16 shorter events, 0.1 us)
Async XLA Ops:
  0.6 1.4 %copy-start = (f32[19,4,16,128]{3,2,1,0:T(8,128)S(1)}, f32[19,4,16,128]{3,2,1,0:T(8,128)}, u32[]{:S(2)}) copy-start(f32[19,4,16,128]{3,2,1,0:T(8,128)} %adj_ref.7) | copy-start | bytes 1867780
  2.4 8.0 %collective-permute-start.1 = (f32[72,128]{1,0:T(8,128)S(1)}, f32[72,128]{1,0:T(8,128)S(1)}, u32[]{:S(2)}, u32[]{:S(2)}) collective-permute-start(f32[72,128]{1,0:T(8,128)S(1)} %get-tuple-element.52.cols_ref), channel_id=1, source_target_pairs={{0,24},{8,16},{16,8},{24,0},{1,25},{9,17},{17,9},{25,1},{2,26},{10... | collective-permute-start | bytes 110600 | tf_op jit(solution)/shard_map/ppermute | solution.py:1117
  4.9 4.2 %collective-permute-start.4 = (f32[48,128]{1,0:T(8,128)S(1)}, f32[48,128]{1,0:T(8,128)S(1)}, u32[]{:S(2)}, u32[]{:S(2)}) collective-permute-start(f32[48,128]{1,0:T(8,128)S(1)} %get-tuple-element.55), channel_id=1, source_target_pairs={{0,28},{4,24},{8,20},{12,16},{16,12},{20,8},{24,4},{28,0},{1,29},{... | collective-permute-start | bytes 73736 | tf_op jit(solution)/shard_map/ppermute | solution.py:1089
  6.6 4.7 %collective-permute-start.2 = (f32[152,128]{1,0:T(8,128)S(1)}, f32[152,128]{1,0:T(8,128)S(1)}, u32[]{:S(2)}, u32[]{:S(2)}) collective-permute-start(f32[152,128]{1,0:T(8,128)S(1)} %get-tuple-element.53), channel_id=1, source_target_pairs={{0,4},{4,0},{1,5},{5,1},{2,6},{6,2},{3,7},{7,3},{8,12},{12,8},{9,1... | collective-permute-start | bytes 233480 | tf_op jit(solution)/shard_map/ppermute | solution.py:1120
  6.6 9.6 %copy-start.1 = (f32[2,19,4,16,128]{4,3,2,1,0:T(8,128)S(1)}, f32[2,19,4,16,128]{4,3,2,1,0:T(8,128)}, u32[]{:S(2)}) copy-start(f32[2,19,4,16,128]{4,3,2,1,0:T(8,128)} %states_ref.1) | copy-start | bytes 3735556
  6.6 4.4 %collective-permute-start.3 = (f32[48,128]{1,0:T(8,128)S(1)}, f32[48,128]{1,0:T(8,128)S(1)}, u32[]{:S(2)}, u32[]{:S(2)}) collective-permute-start(f32[48,128]{1,0:T(8,128)S(1)} %get-tuple-element.54), channel_id=1, source_target_pairs={{0,12},{4,8},{8,4},{12,0},{16,28},{20,24},{24,20},{28,16},{1,13},{... | collective-permute-start | bytes 73736 | tf_op jit(solution)/shard_map/ppermute | solution.py:1089
  7.9 2.9 %collective-permute-start = (f32[376,128]{1,0:T(8,128)S(1)}, f32[376,128]{1,0:T(8,128)S(1)}, u32[]{:S(2)}, u32[]{:S(2)}) collective-permute-start(f32[376,128]{1,0:T(8,128)S(1)} %shard_map.69), channel_id=1, source_target_pairs={{0,8},{8,0},{16,24},{24,16},{1,9},{9,1},{17,25},{25,17},{2,10},{10... | collective-permute-start | bytes 577544 | tf_op jit(solution)/shard_map/ppermute | solution.py:1118
  9.0 7.3 %collective-permute-start.8 = (f32[232,128]{1,0:T(8,128)S(1)}, f32[232,128]{1,0:T(8,128)S(1)}, u32[]{:S(2)}, u32[]{:S(2)}) collective-permute-start(f32[232,128]{1,0:T(8,128)S(1)} %shard_map.71), channel_id=1, source_target_pairs={{0,24},{8,16},{16,8},{24,0},{1,25},{9,17},{17,9},{25,1},{2,26},{10... | collective-permute-start | bytes 356360 | tf_op jit(solution)/shard_map/ppermute | solution.py:1137
  10.4 1.3 %collective-permute-start.5 = (f32[1,128]{1,0:T(1,128)S(1)}, f32[1,128]{1,0:T(1,128)S(1)}, u32[]{:S(2)}, u32[]{:S(2)}) collective-permute-start(f32[1,128]{1,0:T(1,128)S(1)} %bitcast_add_fusion), channel_id=1, source_target_pairs={{0,8},{8,0},{16,24},{24,16},{1,9},{9,1},{17,25},{25,17},{2,10},{10... | collective-permute-start | bytes 1544 | tf_op jit(solution)/shard_map/ppermute | solution.py:1149
  11.7 6.9 %collective-permute-start.7 = (f32[40,128]{1,0:T(8,128)S(1)}, f32[40,128]{1,0:T(8,128)S(1)}, u32[]{:S(2)}, u32[]{:S(2)}) collective-permute-start(f32[40,128]{1,0:T(8,128)S(1)} %scatter.9), channel_id=1, source_target_pairs={{0,3},{1,2},{2,1},{3,0},{4,7},{5,6},{6,5},{7,4},{8,11},{9,10},{10,... | collective-permute-start | bytes 61448 | tf_op jit(solution)/shard_map/ppermute | solution.py:1152
  15.4 4.6 %copy-start.2 = (s32[4,16,128]{2,1,0:T(8,128)S(1)}, s32[4,16,128]{2,1,0:T(8,128)}, u32[]{:S(2)}) copy-start(s32[4,16,128]{2,1,0:T(8,128)} %mask_ref.1) | copy-start | bytes 98308
  15.4 3.9 %collective-permute-start.6 = (f32[40,128]{1,0:T(8,128)S(1)}, f32[40,128]{1,0:T(8,128)S(1)}, u32[]{:S(2)}, u32[]{:S(2)}) collective-permute-start(f32[40,128]{1,0:T(8,128)S(1)} %scatter.6), channel_id=1, source_target_pairs={{0,1},{1,0},{2,3},{3,2},{4,5},{5,4},{6,7},{7,6},{8,9},{9,8},{10,11... | collective-permute-start | bytes 61448 | tf_op jit(solution)/shard_map/ppermute | solution.py:1153
  15.5 4.5 %collective-permute-start.9 = (f32[1,128]{1,0:T(1,128)S(1)}, f32[1,128]{1,0:T(1,128)S(1)}, u32[]{:S(2)}, u32[]{:S(2)}) collective-permute-start(f32[1,128]{1,0:T(1,128)S(1)} %add.11.refs_0_), channel_id=1, source_target_pairs={{0,2},{1,3},{2,0},{3,1},{4,6},{5,7},{6,4},{7,5},{8,10},{9,11},{10,... | collective-permute-start | bytes 1544 | tf_op jit(solution)/shard_map/ppermute | solution.py:1172
